TPU v7x, 32 devices: a whole 2x2x4 slice. The times are simulated.
32 devices in a mesh: groups: 2 (over x), ctx: 8 (over z, y), head: 2 (over core).
Axes of the slice: x: 2, y: 2, z: 4, core: 2. Of those that a mesh axis runs over, the one named last changes fastest.
Arguments:
- queries: bfloat16 [1024, 128, 576], P(('groups', 'ctx'), 'head'), parts along dimension 0, may hold values from -10 to 10
- latent_cache: bfloat16 [65536, 576], P(('groups', 'ctx')), parts along dimension 0, may hold values from -8.5 to 8.5
- positions: int32 [1024], P(('groups', 'ctx')), parts along dimension 0, may hold values from 32256 to 32767, as said below
- block_ids: int32 [16, 32], P(('groups', 'ctx')), parts along dimension 0, may hold values from 0 to 511, as said below
Outputs:
- attn_latent: bfloat16 [1024, 128, 512], P(('groups', 'ctx'), 'head'), parts along dimension 0
There are 2 independent parts, one for each index of `groups`. A program takes and returns all parts, laid end to end along the dimension named above; each array names one. Nothing has to cross between parts.
Inputs may be any that keep to these rules, and one draw needn't show every extreme that they name: Rows c*64 to c*64 + 63 hold consecutive positions inside one key block; the 8 query blocks lie in the last 8 key blocks of the cache, one in each. `block_ids`: row c holds 32 different key blocks: the block that holds query block c's positions, which is the only one from its shard of 64 blocks, and otherwise blocks of earlier shards. In each row at most 8 blocks lie in one shard, and exactly 8 in some shard.
All inputs are finite; a program needn't handle non-finite values.
Results may differ from a plain program's by a relative error of at most 0.0034.
Values may be sent and summed in bfloat16 or wider, within the bound.
No kernel may reach another device: no remote copies, remote signals or barrier semaphores. Data moves between devices by JAX's collectives and lax.ppermute only.
A program may use at most 128 MiB of HBM per device.

v0:
```python
import jax
import jax.numpy as jnp
from jax import lax
from jax.sharding import PartitionSpec as P

KVL = 512
BLOCK = 64
SEL = 32


softmax_scale = 1.0 / 192.0**0.5


def rank_within(owners):
    places = jnp.arange(owners.shape[-1])
    matching = owners[..., :, None] == owners[..., None, :]
    before = places[None, :] < places[:, None]
    return jnp.sum(jnp.where(matching & before, 1, 0), axis=-1).astype(jnp.int32)


def attend(query_rows, query_pos, key_rows, key_pos):
    scores = (
        jnp.einsum("qhl,kl->qhk", query_rows, key_rows, preferred_element_type=jnp.float32)
        * softmax_scale
    )
    visible = key_pos[None, :] <= query_pos[:, None]
    scores = jnp.where(visible[:, None, :], scores, -jnp.inf)
    row_max = jnp.max(scores, axis=-1, keepdims=True)
    weights = jnp.exp(scores - row_max)
    denominator = jnp.sum(weights, axis=-1, keepdims=True)
    rounded = weights.astype(jnp.bfloat16)
    combined = jnp.einsum(
        "qhk,kv->qhv", rounded, key_rows[:, :KVL], preferred_element_type=jnp.float32
    )
    return (combined / denominator).astype(jnp.bfloat16)


def requested(request_table, slot_count, first_slot):
    my_requests = lax.dynamic_slice_in_dim(request_table, first_slot, slot_count, 1)
    return lax.all_to_all(my_requests, "ctx", split_axis=0, concat_axis=0, tiled=True)


def local(queries, latent_cache, positions, block_ids):
    owner_count = lax.axis_size("ctx")
    capacity = max(2, 2 * SEL // owner_count)
    width_all = latent_cache.shape[1]
    shard_blocks = latent_cache.shape[0] // BLOCK
    cache_blocks = latent_cache.reshape(shard_blocks, BLOCK, width_all)
    chosen = block_ids[0]
    owners = chosen // shard_blocks
    within = chosen % shard_blocks
    slot_index = owners * capacity + rank_within(owners)
    slot_ids = jnp.arange(owner_count * capacity, dtype=jnp.int32)
    matches = slot_ids[:, None] == slot_index[None, :]
    request_table = jnp.sum(jnp.where(matches, within[None, :] + 1, 0), axis=1) - 1
    request_table = request_table.reshape(owner_count, capacity)
    slot_count = capacity // 2
    wanted = requested(request_table, slot_count, lax.axis_index("head") * slot_count)
    outgoing = cache_blocks[jnp.maximum(wanted, 0)]
    arrived = lax.all_to_all(outgoing, "ctx", split_axis=0, concat_axis=0, tiled=True)
    fetched = lax.all_gather(arrived, "head", axis=1, tiled=True)
    slot_blocks = fetched.reshape(owner_count * capacity, BLOCK, width_all)
    key_rows = slot_blocks[slot_index].reshape(chosen.shape[0] * BLOCK, width_all)
    key_pos = (chosen[:, None] * BLOCK + jnp.arange(BLOCK, dtype=jnp.int32)[None, :]).reshape(
        chosen.shape[0] * BLOCK
    )
    return attend(queries, positions, key_rows, key_pos)


def solution(mesh):
    return jax.shard_map(
        local,
        mesh=mesh,
        in_specs=(
            P(("groups", "ctx"), "head", None),
            P(("groups", "ctx"), None),
            P(("groups", "ctx")),
            P(("groups", "ctx"), None),
        ),
        out_specs=P(("groups", "ctx"), "head", None),
        check_vma=False,
    )
```

profile of v0, /device:TPU:0, one launch (start us, length us, event | category | flops | bytes accessed | tf_op | source)
XLA Modules:
  0.0 170.4 jit_solution(661235737777343019)
XLA Ops:
  6.5 0.7 bitcast_multiply_fusion
  7.2 0.7 and_select_fusion.3
  7.9 0.2 select_reduce_fusion.1
  8.1 0.1 select_reduce_fusion
  8.2 0.1 sub.27
  8.2 0.7 constant_dynamic-slice_fusion
  8.9 7.3 %all-to-all-start = ((s32[8,1,4]{2,1,0:T(1,128)}), s32[8,1,4]{2,1,0:T(1,128)S(1)}, u32[]{:S(2)}, u32[]{:S(2)}) async-start(s32[8,1,4]{2,1,0:T(1,128)} %bitcast.16), calls=%async_computation | async-start | bytes 8192 | tf_op jit(solution)/shard_map/all_to_all | solution.py:40
  16.2 0.0 all-gather.2.cloned.1.call-start
  16.2 7.7 %copy.16 = bf16[4096,576]{1,0:T(8,128)(2,1)} copy(bf16[4096,576]{0,1:T(8,128)(2,1)} %param.5) | data formatting | bytes 9437184 | tf_op args[1]
  23.9 0.0 copy-start.1
  23.9 0.0 copy-start
  23.9 0.0 all-to-all-done
  23.9 0.1 reshape.178
  24.0 3.5 %gather_fusion = bf16[32,64,576]{2,1,0:T(8,128)(2,1)S(1)} fusion(bf16[64,64,576]{2,1,0:T(8,128)(2,1)} %bitcast.59, s32[1024]{0:T(1024)S(1)} %pad_clamp_fusion.1), kind=kCustom, calls=%fused_computation | custom fusion | bytes 4718720 | tf_op jit(solution)/shard_map/gather | solution.py:59
  27.5 64.9 %all_to_all.14 = bf16[8,4,64,576]{3,2,1,0:T(8,128)(2,1)} all-to-all(bf16[8,4,64,576]{3,2,1,0:T(8,128)(2,1)S(1)} %bitcast.60), channel_id=1, replica_groups=mesh['groups'=2,'ctx'=8,'head'=2] {'ctx'}, dimensions={0} | all-to-all | bytes 4718592 | tf_op jit(solution)/shard_map/all_to_all | solution.py:60
  92.4 0.0 all-gather.2.cloned.1.call-update
  92.5 0.1 iota_add_fusion
  92.5 0.1 add.81
  92.6 0.0 copy-done.1
  92.6 0.0 copy-done
  92.6 0.1 broadcast_compare_fusion
  92.8 13.9 %all-gather.2.cloned.1.call-done = bf16[8,8,64,576]{3,2,1,0:T(8,128)(2,1)} async-done(((bf16[8,4,64,576]{3,2,1,0:T(8,128)(2,1)}), bf16[8,8,64,576]{3,2,1,0:T(8,128)(2,1)}) %all-gather.2.cloned.1.call-update) | async-done | bytes 4718608 | tf_op jit(solution)/shard_map/all_gather | solution.py:61
  106.7 3.5 %gather_fusion.1 = bf16[32,64,576]{2,1,0:T(8,128)(2,1)S(1)} fusion(bf16[64,64,576]{2,1,0:T(8,128)(2,1)} %bitcast.63, s32[1024]{0:T(1024)S(1)} %pad_clamp_fusion), kind=kCustom, calls=%fused_computation.1 | custom fusion | bytes 4718720 | tf_op jit(solution)/shard_map/gather | solution.py:63
  110.2 20.9 %fusion.2 = (f32[64,64]{1,0:T(8,128)S(1)}, f32[2048,64,64]{0,2,1:T(8,128)}) fusion(pred[64,2048]{1,0:T(8,128)(4,1)S(1)} %broadcast_compare_fusion, bf16[2048,576,1]{1,0,2:T(8,128)(2,1)S(1)} %bitcast.61, bf16[64,64,576]{2,1,0:T(8,128)(2,1)} %param.4), kind=kOutput, calls=%fused_computation.6 | convolution fusion | flops 9688838144 | bytes 40779776 | tf_op jit(solution)/shard_map/qhl,kl->qhk/dot_general | solution.py:23
  131.1 14.9 %fusion = f32[64,64]{1,0:T(8,128)S(1)} fusion(f32[2048,64,64]{0,2,1:T(8,128)} %get-tuple-element.10, f32[64,64]{1,0:T(8,128)S(1)} %get-tuple-element.9, pred[64,2048]{1,0:T(8,128)(4,1)S(1)} %broadcast_compare_fusion), kind=kLoop, calls=%fused_computation.4 | loop fusion | flops 33550336 | bytes 33718272 | tf_op jit(solution)/shard_map/reduce_sum | solution.py:30
  146.0 17.5 %divide_convert_fusion = bf16[64,64,512]{2,1,0:T(8,128)(2,1)} fusion(f32[64,64]{1,0:T(8,128)S(1)} %fusion, f32[2048,64,64]{0,2,1:T(8,128)} %get-tuple-element.10, f32[64,64]{1,0:T(8,128)S(1)} %get-tuple-element.9, pred[64,2048]{1,0:T(8,128)(4,1)S(1)} %broadcast_compare_fusion, bf16[2048,576]{1,0:T(8,128)(2,1)S(1)} %bitcast.62), kind=kOutput, calls=%fused_computation.12 | convolution fusion | flops 8627683328 | bytes 40042496 | tf_op jit(solution)/shard_map/qhk,kv->qhv/dot_general | solution.py:32
  (6 shorter events, 0.1 us)
Async XLA Ops:
  8.9 15.0 %all-to-all-start = ((s32[8,1,4]{2,1,0:T(1,128)}), s32[8,1,4]{2,1,0:T(1,128)S(1)}, u32[]{:S(2)}, u32[]{:S(2)}) async-start(s32[8,1,4]{2,1,0:T(1,128)} %bitcast.16), calls=%async_computation | async-start | bytes 8192 | tf_op jit(solution)/shard_map/all_to_all | solution.py:40
  16.2 90.5 %all-gather.2.cloned.1.call-start = ((), (), s32[]{:S(2)}) async-start(), calls=%async_computation.2 | async-start | bytes 7864320 | tf_op jit(solution)/shard_map/all_gather | solution.py:61
  23.9 68.7 %copy-start.1 = (s32[1,32]{1,0:T(1,128)S(1)}, s32[1,32]{1,0:T(1,128)}, u32[]{:S(2)}) copy-start(s32[1,32]{1,0:T(1,128)} %param.7) | copy-start | bytes 388
  23.9 68.7 %copy-start = (s32[64]{0:T(128)S(1)}, s32[64]{0:T(128)}, u32[]{:S(2)}) copy-start(s32[64]{0:T(128)} %param.6) | copy-start | bytes 772
Sparse Core Ops, SparseCore 0:
  92.6 14.0 all-gather.1
where the time goes:
time: 171 us; the launch traced here: 170 us
  blocking collectives  64.9 us (38%)
  matrix products  38.4 us (22%)
  other arithmetic  16.8 us (10%)
  local copies, waits for them, and re-layouts  15.6 us (9%)
  waiting for transfers between devices  13.9 us (8%)
  between operations  13.5 us (8%)
  starting transfers between devices  7.32 us (4%)
    all_to_all x1, blocking collectives, local(): lax.all_to_all(outgoing, 'ctx', split_axis=0, concat_axis=0, tiled=True)  64.9 us
    dot_general x1, matrix products, attend(): jnp.einsum('qhl,kl->qhk', query_rows, key_rows, preferred_element_type=jn...  20.9 us
    dot_general x1, matrix products, attend(): jnp.einsum('qhk,kv->qhv', rounded, key_rows[:, :KVL], preferred_element_t...  17.5 us
    reduce_sum x1, other arithmetic, attend(): denominator = jnp.sum(weights, axis=-1, keepdims=True)  14.9 us
    all_gather x1, waiting for transfers between devices, local(): fetched = lax.all_gather(arrived, 'head', axis=1, tiled=True)  13.9 us
    unnamed x5, local copies, waits for them, and re-layouts  7.66 us
    all_to_all x1, starting transfers between devices, requested(): lax.all_to_all(my_requests, 'ctx', split_axis=0, concat_axis=0, tiled=True)  7.28 us
    gather x1, local copies, waits for them, and re-layouts, local(): outgoing = cache_blocks[jnp.maximum(wanted, 0)]  3.51 us
  transfers between devices with their start and end apart: 2, of which 1 were waited for; matrix products, arithmetic and copies ran while one was open for 5% of the time, Pallas kernels for 0%

commit v1 on v0

v1 whole, which is shorter than its diff:
```python
import functools

import jax
import jax.numpy as jnp
from jax import lax
from jax.experimental import pallas as pl
from jax.experimental.pallas import tpu as pltpu
from jax.sharding import PartitionSpec as P

KVL = 512
BLOCK = 64
SEL = 32
PAIR = 2 * BLOCK
GROUP = 2 * PAIR
SUB = 512
STEP = 2 * SUB
NEG = -1e30
SCALE = 1.4426950408889634 / 192.0**0.5
NT = (((1,), (1,)), ((), ()))
NN = (((1,), (0,)), ((), ()))


def log2(n):
    shift = n.bit_length() - 1
    assert 1 << shift == n
    return shift


def pack_kernel(capacity, phases, ids, cache, *refs):
    dests = ids.shape[0]
    count_out = len(phases) * (dests + 1)
    outs = [refs[p * (dests + 1) : (p + 1) * (dests + 1)] for p in range(len(phases))]
    table, rows, sems = refs[count_out:]
    _, half, tokens = rows.shape
    shift = log2(tokens // BLOCK)
    head = lax.axis_index("head")
    me = lax.axis_index("ctx")
    copies = []
    for i, start in enumerate((head, 1 - head)):
        from_rows = pl.ds(pl.multiple_of(start * half, 32), half)
        copies.append(pltpu.make_async_copy(cache.at[from_rows, :], rows.at[i], sems.at[i]))
        copies[i].start()

    @pl.loop(0, dests)
    def _(d):
        first = d * (capacity + 1)
        for slot in range(capacity + 1):
            table[first + slot] = 0
        at = first
        for j in range(SEL):
            block = ids[d, j]
            table[at] = block & ((1 << shift) - 1)
            at = at + (block >> shift == me).astype(jnp.int32)
        table[at] = 0

    left = lax.broadcasted_iota(jnp.int32, (half, PAIR), 1) < BLOCK

    def block_pair(part, d, chunk):
        first = d * (capacity + 1) + 2 * chunk
        a, b = table[first], table[first + 1]
        xa = rows[part, :, pl.ds(pl.multiple_of((a >> 1) * PAIR, PAIR), PAIR)].astype(jnp.float32)
        xb = rows[part, :, pl.ds(pl.multiple_of((b >> 1) * PAIR, PAIR), PAIR)].astype(jnp.float32)
        xa = pltpu.roll(xa, (a & 1) * BLOCK, 1)
        xb = pltpu.roll(xb, (1 - (b & 1)) * BLOCK, 1)
        return jnp.where(left, xa, xb).astype(jnp.bfloat16)

    copies[0].wait()
    for p, chunks in enumerate(phases):
        for c, chunk in enumerate(chunks):
            for k in range(dests):
                outs[p][k][c] = block_pair(0, me ^ k, chunk)
    copies[1].wait()
    for p, chunks in enumerate(phases):
        for c, chunk in enumerate(chunks):
            outs[p][dests][c] = block_pair(1, me, chunk)


def pack(all_ids, cache_t, capacity, phases):
    dests = all_ids.shape[0]
    lat, tokens = cache_t.shape
    half = lat // 2
    shapes = [(len(chunks), half, PAIR) for chunks in phases for _ in range(dests + 1)]
    return pl.pallas_call(
        functools.partial(pack_kernel, capacity, phases),
        out_shape=[jax.ShapeDtypeStruct(s, jnp.bfloat16) for s in shapes],
        grid_spec=pltpu.PrefetchScalarGridSpec(
            num_scalar_prefetch=1,
            grid=(1,),
            in_specs=[pl.BlockSpec(memory_space=pltpu.HBM)],
            out_specs=[pl.BlockSpec(s, lambda i, ids: (0, 0, 0)) for s in shapes],
            scratch_shapes=[
                pltpu.SMEM((dests * (capacity + 1),), jnp.int32),
                pltpu.VMEM((2, half, tokens), jnp.bfloat16),
                pltpu.SemaphoreType.DMA((2,)),
            ],
        ),
        compiler_params=pltpu.CompilerParams(vmem_limit_bytes=40 << 20),
        name="pack",
    )(all_ids, cache_t)


def slot_starts(ids, starts, owners, capacity, shift):
    for slot in range(owners * capacity):
        starts[slot] = -1
    for o in range(owners):
        starts[owners * capacity + o] = 0
    for j in range(SEL):
        block = ids[j]
        owner = block >> shift
        rank = starts[owners * capacity + owner]
        starts[owner * capacity + rank] = block * BLOCK
        starts[owners * capacity + owner] = rank + 1


def pair_copies(source, kt, at, head, half, sems):
    return [
        pltpu.make_async_copy(
            source[i], kt.at[pl.ds(pl.multiple_of(part * half, 32), half), pl.ds(at, PAIR)], sems.at[i]
        )
        for i, part in enumerate((head, 1 - head))
    ]


def pair_bias(bias, at, start_a, start_b):
    lane = lax.broadcasted_iota(jnp.int32, (8, PAIR), 1)
    start = jnp.where(lane < BLOCK, start_a, start_b)
    bias[:, pl.ds(at, PAIR)] = jnp.where(start >= 0, 0.0, NEG).astype(jnp.float32)


class Half:
    def __init__(self, base, q, kt, bias, scores, weights, keys, diagonal=None):
        self.base, self.q, self.kt, self.bias = base, q, kt, bias
        self.scores, self.weights, self.keys, self.diagonal = scores, weights, keys, diagonal

    def score(self, group):
        at = group * GROUP
        rows = pl.ds(self.base, SUB)
        part = lax.dot_general(
            self.q[rows, :], self.kt[:, at : at + GROUP], NN, preferred_element_type=jnp.float32
        )
        self.scores[:, at : at + GROUP] = part + self.bias[0:1, at : at + GROUP]
        if self.diagonal is not None:
            where, key, pos, first = self.diagonal
            if at <= where < at + GROUP:
                for s in range(SUB // BLOCK):
                    slab = pl.ds(s * BLOCK, BLOCK)
                    seen = key <= pos[first + (self.base // BLOCK) + s]
                    self.scores[slab, where : where + PAIR] = jnp.where(
                        seen, self.scores[slab, where : where + PAIR], NEG
                    )

    def weigh(self, slab, old=None):
        rows = pl.ds(slab * BLOCK, BLOCK)
        high = self.scores[rows, 0:PAIR]
        for at in range(PAIR, self.keys, PAIR):
            high = jnp.maximum(high, self.scores[rows, at : at + PAIR])
        top = jnp.max(high, axis=1, keepdims=True) * SCALE
        if old is not None:
            top = jnp.maximum(top, old)
        spread = jnp.broadcast_to(top, (BLOCK, PAIR))
        total = jnp.zeros((BLOCK, PAIR), jnp.float32)
        for at in range(0, self.keys, PAIR):
            part = jnp.exp2(self.scores[rows, at : at + PAIR] * SCALE - spread)
            total = total + part
            self.weights[rows, at : at + PAIR] = part.astype(jnp.bfloat16)
        return top, jnp.sum(total, axis=1, keepdims=True)

    def combine(self, column):
        return lax.dot_general(
            self.weights[:, 0 : self.keys],
            self.kt[column : column + GROUP, 0 : self.keys],
            NT,
            preferred_element_type=jnp.float32,
        )


def first_kernel(capacity, shift, chunks, final, ids, pos, q, *refs):
    owners = len(refs_pairs := refs[: len(refs) - (1 if final else 2) - 8]) // 2
    mine, other = refs_pairs[:owners], refs_pairs[owners:]
    outs = refs[2 * owners : len(refs) - 8]
    starts, kt, bias, scores_a, scores_b, weights_a, weights_b, sems = refs[len(refs) - 8 :]
    half = mine[0].shape[1]
    head = lax.axis_index("head")
    me = lax.axis_index("ctx")
    keys = owners * chunks * PAIR
    step = pl.program_id(0)

    @pl.when(step == 0)
    def _():
        copies = []
        for c in range(chunks):
            for k in range(owners):
                at = pl.multiple_of((c * owners + (me ^ k)) * PAIR, PAIR)
                copies += pair_copies((mine[k].at[c], other[k].at[c]), kt, at, head, half, sems.at[c * owners + k])
        for copy in copies:
            copy.start()
        slot_starts(ids, starts, owners, capacity, shift)
        for c in range(chunks):
            for o in range(owners):
                slot = o * capacity + 2 * c
                pair_bias(bias, (c * owners + o) * PAIR, starts[slot], starts[slot + 1])
        for copy in copies:
            copy.wait()

    key = starts[(owners - 1) * capacity] + lax.broadcasted_iota(jnp.int32, (1, PAIR), 1)
    diagonal = ((owners - 1) * PAIR, key, pos, step * (STEP // BLOCK))
    a = Half(0, q, kt, bias, scores_a, weights_a, keys, diagonal)
    b = Half(SUB, q, kt, bias, scores_b, weights_b, keys, diagonal)
    lane = lax.broadcasted_iota(jnp.int32, (BLOCK, PAIR), 1)
    groups, slabs = keys // GROUP, SUB // BLOCK
    sums = {}

    def weigh(part, slab):
        top, low = part.weigh(slab)
        sums[part.base, slab] = low
        if not final:
            outs[1][pl.ds(part.base + slab * BLOCK, BLOCK), :] = jnp.where(lane < BLOCK, top, low)

    def combine(part, column):
        summed = part.combine(column)
        if final:
            inverse = jnp.concatenate([1.0 / sums[part.base, s] for s in range(slabs)], axis=0)
            summed = (summed * inverse).astype(jnp.bfloat16)
        outs[0][pl.ds(part.base, SUB), column : column + GROUP] = summed

    for g in range(groups):
        a.score(g)
    for i in range(max(groups, slabs)):
        if i < groups:
            b.score(i)
        if i < slabs:
            weigh(a, i)
    for i, column in enumerate(range(0, KVL, GROUP)):
        combine(a, column)
        for s in range(i * slabs // 2, (i + 1) * slabs // 2):
            weigh(b, s)
    for column in range(0, KVL, GROUP):
        combine(b, column)


def rest_kernel(capacity, shift, chunks, skip, levels, ids, q, carry, stats, *refs):
    owners = (len(refs) - 9) // 2
    mine, other = refs[:owners], refs[owners : 2 * owners]
    out, starts, kt, bias, scores_a, scores_b, weights_a, weights_b, sems = refs[2 * owners :]
    half = mine[0].shape[1]
    head = lax.axis_index("head")
    me = lax.axis_index("ctx")
    live = owners * capacity + owners

    @pl.when(pl.program_id(0) == 0)
    def _():
        slot_starts(ids, starts, owners, capacity, shift)
        kt[...] = jnp.zeros(kt.shape, kt.dtype)
        bias[...] = jnp.full(bias.shape, NEG, bias.dtype)
        pairs = [(c, k) for c in range(chunks) for k in range(owners)]

        def each(act):
            starts[live] = 0
            for c, k in pairs:
                slot = (me ^ k) * capacity + 2 * (skip + c)
                @pl.when(starts[slot] >= 0)
                def _():
                    count = starts[live]
                    starts[live] = count + 1
                    at = pl.multiple_of(count * PAIR, PAIR)
                    source = (mine[k].at[c], other[k].at[c])
                    act(pair_copies(source, kt, at, head, half, sems.at[c * owners + k]), at, slot)

        def begin(copies, at, slot):
            for copy in copies:
                copy.start()
            pair_bias(bias, at, starts[slot], starts[slot + 1])

        def end(copies, at, slot):
            for copy in copies:
                copy.wait()

        each(begin)
        each(end)

    slabs = SUB // BLOCK

    def attend(groups):
        keys = groups * GROUP
        a = Half(0, q, kt, bias, scores_a, weights_a, keys)
        b = Half(SUB, q, kt, bias, scores_b, weights_b, keys)
        factors = {}

        def weigh(part, slab):
            rows = pl.ds(part.base + slab * BLOCK, BLOCK)
            old, low = stats[rows, 0:1], stats[rows, BLOCK : BLOCK + 1]
            top, more = part.weigh(slab, old)
            shrink = jnp.exp2(old - top)
            inverse = 1.0 / (low * shrink + more)
            factors[part.base, slab] = (shrink * inverse, inverse)

        def combine(part, column):
            rows = pl.ds(part.base, SUB)
            cols = slice(column, column + GROUP)
            summed = part.combine(column)
            for s in range(slabs):
                slab = pl.ds(part.base + s * BLOCK, BLOCK)
                before, now = factors[part.base, s]
                result = carry[slab, cols] * before + summed[s * BLOCK : (s + 1) * BLOCK] * now
                out[slab, cols] = result.astype(jnp.bfloat16)

        for g in range(groups):
            a.score(g)
        for i in range(max(groups, slabs)):
            if i < groups:
                b.score(i)
            if i < slabs:
                weigh(a, i)
        for i, column in enumerate(range(0, KVL, GROUP)):
            combine(a, column)
            for s in range(i * slabs // 2, (i + 1) * slabs // 2):
                weigh(b, s)
        for column in range(0, KVL, GROUP):
            combine(b, column)

    needed = (starts[live] + 1) // 2
    below = -1
    for level in levels:
        @pl.when(jnp.logical_and(needed > below, needed <= level))
        def _():
            attend(level)
        below = level


def anywhere(count):
    return [pl.BlockSpec(memory_space=pl.ANY)] * count


def scratch(owners, capacity, chunks, lat, keys):
    return [
        pltpu.SMEM((owners * capacity + owners + 1,), jnp.int32),
        pltpu.VMEM((lat, keys), jnp.bfloat16),
        pltpu.VMEM((8, keys), jnp.float32),
        pltpu.VMEM((SUB, keys), jnp.float32),
        pltpu.VMEM((SUB, keys), jnp.float32),
        pltpu.VMEM((SUB, keys), jnp.bfloat16),
        pltpu.VMEM((SUB, keys), jnp.bfloat16),
        pltpu.SemaphoreType.DMA((chunks * owners, 2)),
    ]


def attend_first(ids, pos, q, mine, other, capacity, shift, final):
    rows, lat = q.shape
    owners, chunks = len(mine), mine[0].shape[0]
    keys = owners * chunks * PAIR
    if final:
        out_shape = [jax.ShapeDtypeStruct((rows, KVL), jnp.bfloat16)]
    else:
        out_shape = [jax.ShapeDtypeStruct((rows, KVL), jnp.float32), jax.ShapeDtypeStruct((rows, PAIR), jnp.float32)]
    return pl.pallas_call(
        functools.partial(first_kernel, capacity, shift, chunks, final),
        out_shape=out_shape,
        grid_spec=pltpu.PrefetchScalarGridSpec(
            num_scalar_prefetch=2,
            grid=(rows // STEP,),
            in_specs=[pl.BlockSpec((STEP, lat), lambda i, *_: (i, 0))] + anywhere(2 * owners),
            out_specs=[pl.BlockSpec((STEP, s.shape[1]), lambda i, *_: (i, 0)) for s in out_shape],
            scratch_shapes=scratch(owners, capacity, chunks, lat, keys),
        ),
        compiler_params=pltpu.CompilerParams(vmem_limit_bytes=56 << 20),
        cost_estimate=pl.CostEstimate(
            flops=2 * rows * keys * (lat + KVL), bytes_accessed=rows * (lat + 2 * KVL) * 2, transcendentals=rows * keys
        ),
        name="attend_first",
    )(ids, pos, q, *mine, *other)


def attend_rest(ids, q, carry, stats, mine, other, capacity, shift, skip):
    rows, lat = q.shape
    owners, chunks = len(mine), mine[0].shape[0]
    keys = owners * chunks * PAIR
    most = keys // GROUP
    levels = [n for n in (2, 3, 4) if n < most] + [most]
    return pl.pallas_call(
        functools.partial(rest_kernel, capacity, shift, chunks, skip, levels),
        out_shape=jax.ShapeDtypeStruct((rows, KVL), jnp.bfloat16),
        grid_spec=pltpu.PrefetchScalarGridSpec(
            num_scalar_prefetch=1,
            grid=(rows // STEP,),
            in_specs=[
                pl.BlockSpec((STEP, lat), lambda i, *_: (i, 0)),
                pl.BlockSpec((STEP, KVL), lambda i, *_: (i, 0)),
                pl.BlockSpec((STEP, PAIR), lambda i, *_: (i, 0)),
            ]
            + anywhere(2 * owners),
            out_specs=pl.BlockSpec((STEP, KVL), lambda i, *_: (i, 0)),
            scratch_shapes=scratch(owners, capacity, chunks, lat, keys),
        ),
        compiler_params=pltpu.CompilerParams(vmem_limit_bytes=56 << 20),
        cost_estimate=pl.CostEstimate(
            flops=rows * keys * (lat + KVL), bytes_accessed=rows * (lat + 3 * KVL) * 2, transcendentals=rows * keys // 2
        ),
        name="attend_rest",
    )(ids, q, carry, stats, *mine, *other)


def local(queries, latent_cache, positions, block_ids):
    owners = lax.axis_size("ctx")
    capacity = max(2, 2 * SEL // owners)
    shift = log2(latent_cache.shape[0] // BLOCK)
    q_rows, heads, lat = queries.shape
    rows = q_rows * heads
    all_ids = lax.all_to_all(
        jnp.broadcast_to(block_ids, (owners, SEL)), "ctx", split_axis=0, concat_axis=0, tiled=True
    )
    chunks = list(range(capacity // 2))
    cut = (len(chunks) + 1) // 2
    phases = [part for part in (chunks[:cut], chunks[cut:]) if part]
    packed = pack(all_ids, latent_cache.T, capacity, phases)
    near_first = sorted(range(1, owners), reverse=True)
    mine, other = [], []
    for p in range(len(phases)):
        own = packed[p * (owners + 1) : (p + 1) * (owners + 1)]
        got, swapped = [own[0]] + [None] * (owners - 1), [own[owners]] + [None] * (owners - 1)
        for k in near_first:
            got[k] = lax.ppermute(own[k], "ctx", [(c, c ^ k) for c in range(owners)])
        for k in near_first:
            swapped[k] = lax.ppermute(got[k], "head", [(0, 1), (1, 0)])
        mine.append(got)
        other.append(swapped)
    q = queries.reshape(rows, lat)
    ids = block_ids[0]
    final = len(phases) == 1
    out = attend_first(ids, positions, q, mine[0], other[0], capacity, shift, final)
    if final:
        out = out[0]
    else:
        out = attend_rest(ids, q, *out, mine[1], other[1], capacity, shift, cut)
    return out.reshape(q_rows, heads, KVL)


def solution(mesh):
    return jax.shard_map(
        local,
        mesh=mesh,
        in_specs=(
            P(("groups", "ctx"), "head", None),
            P(("groups", "ctx"), None),
            P(("groups", "ctx")),
            P(("groups", "ctx"), None),
        ),
        out_specs=P(("groups", "ctx"), "head", None),
        check_vma=False,
    )
```

time: 171 us -> 136 us (0.80); the launches traced: 170 us -> 134 us
  Pallas kernels: 0 us -> 59.1 us
  blocking collectives: 64.9 us -> 13.5 us
  matrix products: 38.4 us -> 0 us
  starting transfers between devices: 7.32 us -> 33.1 us
  other arithmetic: 16.8 us -> 0 us
  between operations: 13.5 us -> 0.51 us
  local copies, waits for them, and re-layouts: 15.6 us -> 6.55 us
  waiting for transfers between devices: 13.9 us -> 20.8 us
    pallas_call x0 -> x3, Pallas kernels: none -> 59.1 us  [the longest x1 31.8 us: attend_first(): pl.pallas_call(functools.partial(first_kernel, capacity, shift, chunks, f...]
    all_to_all x1, blocking collectives: 64.9 us -> 13.5 us  [local(): lax.all_to_all(jnp.broadcast_to(block_ids, (owners, SEL)), 'ctx', split_a...]
    dot_general x2 -> x0, matrix products: 38.4 us -> none  [the longest x1 20.9 us: attend(): jnp.einsum('qhl,kl->qhk', query_rows, key_rows, preferred_element_type=jn...]
    ppermute x0 -> x28, starting transfers between devices: none -> 33.1 us  [the longest x14 29.8 us: local(): got[k] = lax.ppermute(own[k], 'ctx', [(c, c ^ k) for c in range(owners)])]
    ppermute x0 -> x28, waiting for transfers between devices: none -> 20.8 us  [the longest x14 20.5 us: local(): got[k] = lax.ppermute(own[k], 'ctx', [(c, c ^ k) for c in range(owners)])]
    reduce_sum x3 -> x0, other arithmetic: 15.2 us -> none  [the longest x1 14.9 us: attend(): denominator = jnp.sum(weights, axis=-1, keepdims=True)]
    all_gather x1 -> x0, waiting for transfers between devices: 13.9 us -> none  [local(): fetched = lax.all_gather(arrived, 'head', axis=1, tiled=True)]
    all_to_all x1 -> x0, starting transfers between devices: 7.28 us -> none  [requested(): lax.all_to_all(my_requests, 'ctx', split_axis=0, concat_axis=0, tiled=True)]
  transfers between devices with their start and end apart: 2 -> 28, of which waited for: 1 -> 7; matrix products, arithmetic and copies ran while one was open for 5% -> 0% of each run, Pallas kernels for 0% -> 24%
where the time goes in v1:
time: 136 us; the launch traced here: 134 us
  Pallas kernels  59.1 us (43%)
  starting transfers between devices  33.1 us (24%)
  waiting for transfers between devices  20.8 us (15%)
  blocking collectives  13.5 us (10%)
  local copies, waits for them, and re-layouts  6.55 us (5%)
    pallas_call x1, Pallas kernels, attend_first(): pl.pallas_call(functools.partial(first_kernel, capacity, shift, chunks, f...  31.8 us
    ppermute x14, starting transfers between devices, local(): got[k] = lax.ppermute(own[k], 'ctx', [(c, c ^ k) for c in range(owners)])  29.8 us
    pallas_call x1, Pallas kernels, attend_rest(): pl.pallas_call(functools.partial(rest_kernel, capacity, shift, chunks, sk...  23.8 us
    ppermute x14, waiting for transfers between devices, local(): got[k] = lax.ppermute(own[k], 'ctx', [(c, c ^ k) for c in range(owners)])  20.5 us
    all_to_all x1, blocking collectives, local(): lax.all_to_all(jnp.broadcast_to(block_ids, (owners, SEL)), 'ctx', split_a...  13.5 us
    unnamed x66, local copies, waits for them, and re-layouts  5.89 us
    pallas_call x1, Pallas kernels, pack(): pl.pallas_call(functools.partial(pack_kernel, capacity, phases), out_shap...  3.43 us
    ppermute x14, starting transfers between devices, local(): swapped[k] = lax.ppermute(got[k], 'head', [(0, 1), (1, 0)])  3.3 us
  transfers between devices with their start and end apart: 28, of which 7 were waited for; matrix products, arithmetic and copies ran while one was open for 0% of the time, Pallas kernels for 24%

profile of v1, /device:TPU:0, one launch (start us, length us, event | category | flops | bytes accessed | tf_op | source)
XLA Modules:
  0.0 133.6 jit_solution(17851083476310844157)
XLA Ops:
  0.0 0.7 broadcast_in_dim.2
  0.7 13.5 %all_to_all.8 = s32[8,1,32]{2,1,0:T(1,128)S(1)} all-to-all(s32[8,1,32]{2,1,0:T(1,128)S(1)} %broadcast_in_dim.2), channel_id=1, replica_groups=mesh['groups'=2,'ctx'=8,'head'=2] {'ctx'}, dimensions={0} | all-to-all | bytes 2048 | tf_op jit(solution)/shard_map/all_to_all | solution.py:408
  14.2 2.3 %copy-done = bf16[4096,576]{0,1:T(8,128)(2,1)S(1)} copy-done((bf16[4096,576]{0,1:T(8,128)(2,1)S(1)}, bf16[4096,576]{0,1:T(8,128)(2,1)}, u32[]{:S(2)}) %copy-start) | copy-done | bytes 4718616
  16.5 3.4 %pack.1 = (bf16[2,288,128]{2,1,0:T(8,128)(2,1)S(1)}, bf16[2,288,128]{2,1,0:T(8,128)(2,1)S(1)}, bf16[2,288,128]{2,1,0:T(8,128)(2,1)S(1)}, bf16[2,288,128]{2,1,0:T...) custom-call(s32[8,32]{1,0:T(8,128)S(1)} %bitcast.6, ...), custom_call_target="tpu_custom_call" | custom-call | tf_op jit(solution)/shard_map/pack/pallas_call | solution.py:83
  20.0 0.7 copy-done.1
  20.6 0.7 copy-done.2
  21.3 0.7 copy-done.3
  22.0 0.7 copy-done.4
  22.6 0.6 collective-permute-start
  23.2 0.6 collective-permute-start.1
  23.7 2.4 %collective-permute-start.2 = (bf16[2,288,128]{2,1,0:T(8,128)(2,1)S(1)}, bf16[2,288,128]{2,1,0:T(8,128)(2,1)S(1)}, u32[]{:S(2)}, u32[]{:S(2)}) collective-permute-start(bf16[2,288,128]{2,1,0:T(8,128)(2,1)S(1)} %get-tuple-element.28), channel_id=1, source_target_pairs={{0,6},{2,4},{4,2},{6,0},{8,14},{10,12},{12,10},{14,8},{1,7},{3,5},... | collective-permute-start | bytes 442376 | tf_op jit(solution)/shard_map/ppermute | solution.py:421
  26.1 0.6 collective-permute-start.3
  26.7 2.4 %collective-permute-start.4 = (bf16[2,288,128]{2,1,0:T(8,128)(2,1)S(1)}, bf16[2,288,128]{2,1,0:T(8,128)(2,1)S(1)}, u32[]{:S(2)}, u32[]{:S(2)}) collective-permute-start(bf16[2,288,128]{2,1,0:T(8,128)(2,1)S(1)} %get-tuple-element.30), channel_id=1, source_target_pairs={{0,10},{2,8},{4,14},{6,12},{8,2},{10,0},{12,6},{14,4},{1,11},{3,9}... | collective-permute-start | bytes 442376 | tf_op jit(solution)/shard_map/ppermute | solution.py:421
  29.0 0.0 collective-permute-done.refs_1_
  29.0 0.6 collective-permute-start.5
  29.6 0.8 collective-permute-done.1.refs_2_
  30.4 3.4 %collective-permute-start.6 = (bf16[2,288,128]{2,1,0:T(8,128)(2,1)S(1)}, bf16[2,288,128]{2,1,0:T(8,128)(2,1)S(1)}, u32[]{:S(2)}, u32[]{:S(2)}) collective-permute-start(bf16[2,288,128]{2,1,0:T(8,128)(2,1)S(1)} %get-tuple-element.32), channel_id=1, source_target_pairs={{0,14},{2,12},{4,10},{6,8},{8,6},{10,4},{12,2},{14,0},{1,15},{3,13... | collective-permute-start | bytes 442376 | tf_op jit(solution)/shard_map/ppermute | solution.py:421
  33.8 2.3 %collective-permute-done.2.refs_3_ = bf16[2,288,128]{2,1,0:T(8,128)(2,1)S(1)} collective-permute-done((bf16[2,288,128]{2,1,0:T(8,128)(2,1)S(1)}, bf16[2,288,128]{2,1,0:T(8,128)(2,1)S(1)}, u32[]{:S(2)}, u32[]{:S(2)}) %collective-permute-start.2) | collective-permute-done | bytes 147488 | tf_op jit(solution)/shard_map/ppermute | solution.py:421
  36.1 0.0 collective-permute-start.14
  36.1 7.8 %collective-permute-done.3.refs_4_ = bf16[2,288,128]{2,1,0:T(8,128)(2,1)S(1)} collective-permute-done((bf16[2,288,128]{2,1,0:T(8,128)(2,1)S(1)}, bf16[2,288,128]{2,1,0:T(8,128)(2,1)S(1)}, u32[]{:S(2)}, u32[]{:S(2)}) %collective-permute-start.3) | collective-permute-done | bytes 147488 | tf_op jit(solution)/shard_map/ppermute | solution.py:421
  43.9 0.0 collective-permute-start.15
  43.9 4.6 %collective-permute-done.4.refs_5_ = bf16[2,288,128]{2,1,0:T(8,128)(2,1)S(1)} collective-permute-done((bf16[2,288,128]{2,1,0:T(8,128)(2,1)S(1)}, bf16[2,288,128]{2,1,0:T(8,128)(2,1)S(1)}, u32[]{:S(2)}, u32[]{:S(2)}) %collective-permute-start.4) | collective-permute-done | bytes 147488 | tf_op jit(solution)/shard_map/ppermute | solution.py:421
  48.5 0.0 collective-permute-start.16
  48.5 0.0 collective-permute-done.5.refs_6_
  48.5 4.7 %collective-permute-start.17 = (bf16[2,288,128]{2,1,0:T(8,128)(2,1)S(1)}, bf16[2,288,128]{2,1,0:T(8,128)(2,1)S(1)}, u32[]{:S(2)}, u32[]{:S(2)}) collective-permute-start(bf16[2,288,128]{2,1,0:T(8,128)(2,1)S(1)} %get-tuple-element.40), channel_id=1, source_target_pairs={{0,8},{2,10},{4,12},{6,14},{8,0},{10,2},{12,4},{14,6},{1,9},{3,11}... | collective-permute-start | bytes 442376 | tf_op jit(solution)/shard_map/ppermute | solution.py:421
  53.2 0.0 collective-permute-done.6.refs_7_
  53.2 10.5 %collective-permute-start.18 = (bf16[2,288,128]{2,1,0:T(8,128)(2,1)S(1)}, bf16[2,288,128]{2,1,0:T(8,128)(2,1)S(1)}, u32[]{:S(2)}, u32[]{:S(2)}) collective-permute-start(bf16[2,288,128]{2,1,0:T(8,128)(2,1)S(1)} %get-tuple-element.41), channel_id=1, source_target_pairs={{0,10},{2,8},{4,14},{6,12},{8,2},{10,0},{12,6},{14,4},{1,11},{3,9}... | collective-permute-start | bytes 442376 | tf_op jit(solution)/shard_map/ppermute | solution.py:421
  63.7 2.3 %collective-permute-start.19 = (bf16[2,288,128]{2,1,0:T(8,128)(2,1)S(1)}, bf16[2,288,128]{2,1,0:T(8,128)(2,1)S(1)}, u32[]{:S(2)}, u32[]{:S(2)}) collective-permute-start(bf16[2,288,128]{2,1,0:T(8,128)(2,1)S(1)} %get-tuple-element.42), channel_id=1, source_target_pairs={{0,12},{2,14},{4,8},{6,10},{8,4},{10,6},{12,0},{14,2},{1,13},{3,15... | collective-permute-start | bytes 442376 | tf_op jit(solution)/shard_map/ppermute | solution.py:421
  66.0 0.0 collective-permute-done.15.refs_2_
  66.1 1.8 %collective-permute-start.20 = (bf16[2,288,128]{2,1,0:T(8,128)(2,1)S(1)}, bf16[2,288,128]{2,1,0:T(8,128)(2,1)S(1)}, u32[]{:S(2)}, u32[]{:S(2)}) collective-permute-start(bf16[2,288,128]{2,1,0:T(8,128)(2,1)S(1)} %get-tuple-element.43), channel_id=1, source_target_pairs={{0,14},{2,12},{4,10},{6,8},{8,6},{10,4},{12,2},{14,0},{1,15},{3,13... | collective-permute-start | bytes 442376 | tf_op jit(solution)/shard_map/ppermute | solution.py:421
  67.9 0.0 collective-permute-done.16.refs_3_
  67.9 0.0 collective-permute-done.17.refs_4_
  67.9 0.5 collective-permute-start.8
  68.4 3.7 %collective-permute-done.18.refs_5_ = bf16[2,288,128]{2,1,0:T(8,128)(2,1)S(1)} collective-permute-done((bf16[2,288,128]{2,1,0:T(8,128)(2,1)S(1)}, bf16[2,288,128]{2,1,0:T(8,128)(2,1)S(1)}, u32[]{:S(2)}, u32[]{:S(2)}) %collective-permute-start.18) | collective-permute-done | bytes 147488 | tf_op jit(solution)/shard_map/ppermute | solution.py:421
  72.2 0.5 collective-permute-start.10
  72.7 1.3 collective-permute-done.20.refs_7_
  74.0 0.0 collective-permute-start.11
  74.0 0.0 collective-permute-done.7.refs_9_
  74.0 0.5 collective-permute-start.12
  74.5 0.0 collective-permute-done.8.refs_10_
  74.5 0.1 collective-permute-start.13
  74.6 0.0 collective-permute-done.9.refs_11_
  74.6 0.4 collective-permute-start.21
  75.0 0.1 collective-permute-start.22
  75.1 0.2 collective-permute-done.11.refs_13_
  75.4 0.2 collective-permute-start.23
  75.6 0.0 collective-permute-done.12.refs_14_
  75.6 0.3 collective-permute-start.24
  75.9 0.0 collective-permute-done.13.refs_15_
  75.9 0.2 collective-permute-start.25
  76.1 0.0 collective-permute-done.21.refs_9_
  76.1 0.3 collective-permute-start.26
  76.4 0.0 collective-permute-done.22.refs_10_
  76.4 0.2 collective-permute-start.27
  76.7 31.8 %attend_first.1 = (f32[4096,512]{1,0:T(8,128)}, f32[4096,128]{1,0:T(8,128)}) custom-call(s32[32]{0:T(128)} %bitcast.8, s32[64]{0:T(128)} %pos.1, bf16[4096,576]{1,0:T(8,128)(2,1)} %bitcast.10, bf16[2,288,128]{2,1,0:T(8,128)(2,1)} %copy-done.3, bf16[2,288,128]{2,1,0:T(8,128)(2,1)} %copy-done.5, bf16[2,288,128]{2,1,0:T(8,128)(2,1)} %copy-done.6, ...), custom_call_target="tpu_custom_call" | custom-call | flops 18253611008 | bytes 13107200 | tf_op jit(solution)/shard_map/attend_first/pallas_call | solution.py:355
  108.7 0.0 collective-permute-done.23.refs_11_
  108.7 0.0 collective-permute-done.26.refs_14_
  108.8 0.0 collective-permute-done.27.refs_15_
  108.8 0.6 copy-done.26
  109.3 0.1 copy-done.28
  109.4 0.1 copy-done.30
  109.5 0.0 copy-done.31
  109.5 0.1 copy-done.32
  109.6 23.8 %attend_rest.1 = bf16[4096,512]{1,0:T(8,128)(2,1)} custom-call(s32[32]{0:T(128)} %bitcast.9, bf16[4096,576]{1,0:T(8,128)(2,1)} %bitcast.11, f32[4096,512]{1,0:T(8,128)} %get-tuple-element.34.carry, f32[4096,128]{1,0:T(8,128)} %get-tuple-element.35.stats, bf16[2,288,128]{2,1,0:T(8,128)(2,1)} %copy-done.1, bf16[2,288,128]{2,1,0:T(8,128)(2,1)} %copy-done.8, ...), custom_call_target="tpu_custom_call" | custom-call | flops 9126805504 | bytes 17301504 | tf_op jit(solution)/shard_map/attend_rest/pallas_call | solution.py:379
  (63 shorter events, 0.1 us)
Async XLA Ops:
  14.2 2.3 %copy-start = (bf16[4096,576]{0,1:T(8,128)(2,1)S(1)}, bf16[4096,576]{0,1:T(8,128)(2,1)}, u32[]{:S(2)}) copy-start(bf16[4096,576]{0,1:T(8,128)(2,1)} %param.5) | copy-start | bytes 14155780
  20.0 0.7 copy-start.1
  20.6 0.7 copy-start.2
  21.3 0.7 copy-start.3
  21.9 0.7 copy-start.4
  22.6 6.4 %collective-permute-start = (bf16[2,288,128]{2,1,0:T(8,128)(2,1)S(1)}, bf16[2,288,128]{2,1,0:T(8,128)(2,1)S(1)}, u32[]{:S(2)}, u32[]{:S(2)}) collective-permute-start(bf16[2,288,128]{2,1,0:T(8,128)(2,1)S(1)} %get-tuple-element.26), channel_id=1, source_target_pairs={{0,2},{2,0},{4,6},{6,4},{8,10},{10,8},{12,14},{14,12},{1,3},{3,1},... | collective-permute-start | bytes 442376 | tf_op jit(solution)/shard_map/ppermute | solution.py:421
  23.2 7.2 %collective-permute-start.1 = (bf16[2,288,128]{2,1,0:T(8,128)(2,1)S(1)}, bf16[2,288,128]{2,1,0:T(8,128)(2,1)S(1)}, u32[]{:S(2)}, u32[]{:S(2)}) collective-permute-start(bf16[2,288,128]{2,1,0:T(8,128)(2,1)S(1)} %get-tuple-element.27), channel_id=1, source_target_pairs={{0,4},{2,6},{4,0},{6,2},{8,12},{10,14},{12,8},{14,10},{1,5},{3,7},... | collective-permute-start | bytes 442376 | tf_op jit(solution)/shard_map/ppermute | solution.py:421
  23.7 12.3 %collective-permute-start.2 = (bf16[2,288,128]{2,1,0:T(8,128)(2,1)S(1)}, bf16[2,288,128]{2,1,0:T(8,128)(2,1)S(1)}, u32[]{:S(2)}, u32[]{:S(2)}) collective-permute-start(bf16[2,288,128]{2,1,0:T(8,128)(2,1)S(1)} %get-tuple-element.28), channel_id=1, source_target_pairs={{0,6},{2,4},{4,2},{6,0},{8,14},{10,12},{12,10},{14,8},{1,7},{3,5},... | collective-permute-start | bytes 442376 | tf_op jit(solution)/shard_map/ppermute | solution.py:421
  26.1 17.8 %collective-permute-start.3 = (bf16[2,288,128]{2,1,0:T(8,128)(2,1)S(1)}, bf16[2,288,128]{2,1,0:T(8,128)(2,1)S(1)}, u32[]{:S(2)}, u32[]{:S(2)}) collective-permute-start(bf16[2,288,128]{2,1,0:T(8,128)(2,1)S(1)} %get-tuple-element.29), channel_id=1, source_target_pairs={{0,8},{2,10},{4,12},{6,14},{8,0},{10,2},{12,4},{14,6},{1,9},{3,11}... | collective-permute-start | bytes 442376 | tf_op jit(solution)/shard_map/ppermute | solution.py:421
  26.7 21.8 %collective-permute-start.4 = (bf16[2,288,128]{2,1,0:T(8,128)(2,1)S(1)}, bf16[2,288,128]{2,1,0:T(8,128)(2,1)S(1)}, u32[]{:S(2)}, u32[]{:S(2)}) collective-permute-start(bf16[2,288,128]{2,1,0:T(8,128)(2,1)S(1)} %get-tuple-element.30), channel_id=1, source_target_pairs={{0,10},{2,8},{4,14},{6,12},{8,2},{10,0},{12,6},{14,4},{1,11},{3,9}... | collective-permute-start | bytes 442376 | tf_op jit(solution)/shard_map/ppermute | solution.py:421
  29.0 47.6 %copy-start.5 = (bf16[2,288,128]{2,1,0:T(8,128)(2,1)}, bf16[2,288,128]{2,1,0:T(8,128)(2,1)S(1)}, u32[]{:S(2)}) copy-start(bf16[2,288,128]{2,1,0:T(8,128)(2,1)S(1)} %collective-permute-done.refs_1_) | copy-start | bytes 442372
  29.0 19.4 %collective-permute-start.5 = (bf16[2,288,128]{2,1,0:T(8,128)(2,1)S(1)}, bf16[2,288,128]{2,1,0:T(8,128)(2,1)S(1)}, u32[]{:S(2)}, u32[]{:S(2)}) collective-permute-start(bf16[2,288,128]{2,1,0:T(8,128)(2,1)S(1)} %get-tuple-element.31), channel_id=1, source_target_pairs={{0,12},{2,14},{4,8},{6,10},{8,4},{10,6},{12,0},{14,2},{1,13},{3,15... | collective-permute-start | bytes 442376 | tf_op jit(solution)/shard_map/ppermute | solution.py:421
  30.4 46.2 %copy-start.6 = (bf16[2,288,128]{2,1,0:T(8,128)(2,1)}, bf16[2,288,128]{2,1,0:T(8,128)(2,1)S(1)}, u32[]{:S(2)}) copy-start(bf16[2,288,128]{2,1,0:T(8,128)(2,1)S(1)} %collective-permute-done.1.refs_2_) | copy-start | bytes 442372
  30.4 22.8 %collective-permute-start.6 = (bf16[2,288,128]{2,1,0:T(8,128)(2,1)S(1)}, bf16[2,288,128]{2,1,0:T(8,128)(2,1)S(1)}, u32[]{:S(2)}, u32[]{:S(2)}) collective-permute-start(bf16[2,288,128]{2,1,0:T(8,128)(2,1)S(1)} %get-tuple-element.32), channel_id=1, source_target_pairs={{0,14},{2,12},{4,10},{6,8},{8,6},{10,4},{12,2},{14,0},{1,15},{3,13... | collective-permute-start | bytes 442376 | tf_op jit(solution)/shard_map/ppermute | solution.py:421
  36.1 40.6 %copy-start.7 = (bf16[2,288,128]{2,1,0:T(8,128)(2,1)}, bf16[2,288,128]{2,1,0:T(8,128)(2,1)S(1)}, u32[]{:S(2)}) copy-start(bf16[2,288,128]{2,1,0:T(8,128)(2,1)S(1)} %collective-permute-done.2.refs_3_) | copy-start | bytes 442372
  36.1 27.6 %collective-permute-start.14 = (bf16[2,288,128]{2,1,0:T(8,128)(2,1)S(1)}, bf16[2,288,128]{2,1,0:T(8,128)(2,1)S(1)}, u32[]{:S(2)}, u32[]{:S(2)}) collective-permute-start(bf16[2,288,128]{2,1,0:T(8,128)(2,1)S(1)} %get-tuple-element.37), channel_id=1, source_target_pairs={{0,2},{2,0},{4,6},{6,4},{8,10},{10,8},{12,14},{14,12},{1,3},{3,1},... | collective-permute-start | bytes 442376 | tf_op jit(solution)/shard_map/ppermute | solution.py:421
  43.9 32.8 %copy-start.9 = (bf16[2,288,128]{2,1,0:T(8,128)(2,1)}, bf16[2,288,128]{2,1,0:T(8,128)(2,1)S(1)}, u32[]{:S(2)}) copy-start(bf16[2,288,128]{2,1,0:T(8,128)(2,1)S(1)} %collective-permute-done.3.refs_4_) | copy-start | bytes 442372
  43.9 22.2 %collective-permute-start.15 = (bf16[2,288,128]{2,1,0:T(8,128)(2,1)S(1)}, bf16[2,288,128]{2,1,0:T(8,128)(2,1)S(1)}, u32[]{:S(2)}, u32[]{:S(2)}) collective-permute-start(bf16[2,288,128]{2,1,0:T(8,128)(2,1)S(1)} %get-tuple-element.38), channel_id=1, source_target_pairs={{0,4},{2,6},{4,0},{6,2},{8,12},{10,14},{12,8},{14,10},{1,5},{3,7},... | collective-permute-start | bytes 442376 | tf_op jit(solution)/shard_map/ppermute | solution.py:421
  48.4 28.2 %copy-start.10 = (bf16[2,288,128]{2,1,0:T(8,128)(2,1)}, bf16[2,288,128]{2,1,0:T(8,128)(2,1)S(1)}, u32[]{:S(2)}) copy-start(bf16[2,288,128]{2,1,0:T(8,128)(2,1)S(1)} %collective-permute-done.4.refs_5_) | copy-start | bytes 442372
  48.5 19.5 %collective-permute-start.16 = (bf16[2,288,128]{2,1,0:T(8,128)(2,1)S(1)}, bf16[2,288,128]{2,1,0:T(8,128)(2,1)S(1)}, u32[]{:S(2)}, u32[]{:S(2)}) collective-permute-start(bf16[2,288,128]{2,1,0:T(8,128)(2,1)S(1)} %get-tuple-element.39), channel_id=1, source_target_pairs={{0,6},{2,4},{4,2},{6,0},{8,14},{10,12},{12,10},{14,8},{1,7},{3,5},... | collective-permute-start | bytes 442376 | tf_op jit(solution)/shard_map/ppermute | solution.py:421
  48.5 28.2 %copy-start.12 = (bf16[2,288,128]{2,1,0:T(8,128)(2,1)}, bf16[2,288,128]{2,1,0:T(8,128)(2,1)S(1)}, u32[]{:S(2)}) copy-start(bf16[2,288,128]{2,1,0:T(8,128)(2,1)S(1)} %collective-permute-done.5.refs_6_) | copy-start | bytes 442372
  48.5 19.4 %collective-permute-start.17 = (bf16[2,288,128]{2,1,0:T(8,128)(2,1)S(1)}, bf16[2,288,128]{2,1,0:T(8,128)(2,1)S(1)}, u32[]{:S(2)}, u32[]{:S(2)}) collective-permute-start(bf16[2,288,128]{2,1,0:T(8,128)(2,1)S(1)} %get-tuple-element.40), channel_id=1, source_target_pairs={{0,8},{2,10},{4,12},{6,14},{8,0},{10,2},{12,4},{14,6},{1,9},{3,11}... | collective-permute-start | bytes 442376 | tf_op jit(solution)/shard_map/ppermute | solution.py:421
  53.2 23.5 %copy-start.14 = (bf16[2,288,128]{2,1,0:T(8,128)(2,1)}, bf16[2,288,128]{2,1,0:T(8,128)(2,1)S(1)}, u32[]{:S(2)}) copy-start(bf16[2,288,128]{2,1,0:T(8,128)(2,1)S(1)} %collective-permute-done.6.refs_7_) | copy-start | bytes 442372
  53.2 19.0 %collective-permute-start.18 = (bf16[2,288,128]{2,1,0:T(8,128)(2,1)S(1)}, bf16[2,288,128]{2,1,0:T(8,128)(2,1)S(1)}, u32[]{:S(2)}, u32[]{:S(2)}) collective-permute-start(bf16[2,288,128]{2,1,0:T(8,128)(2,1)S(1)} %get-tuple-element.41), channel_id=1, source_target_pairs={{0,10},{2,8},{4,14},{6,12},{8,2},{10,0},{12,6},{14,4},{1,11},{3,9}... | collective-permute-start | bytes 442376 | tf_op jit(solution)/shard_map/ppermute | solution.py:421
  63.7 44.9 %copy-start.8 = (bf16[2,288,128]{2,1,0:T(8,128)(2,1)}, bf16[2,288,128]{2,1,0:T(8,128)(2,1)S(1)}, u32[]{:S(2)}) copy-start(bf16[2,288,128]{2,1,0:T(8,128)(2,1)S(1)} %collective-permute-done.14.refs_1_) | copy-start | bytes 442372
  63.7 8.4 %collective-permute-start.19 = (bf16[2,288,128]{2,1,0:T(8,128)(2,1)S(1)}, bf16[2,288,128]{2,1,0:T(8,128)(2,1)S(1)}, u32[]{:S(2)}, u32[]{:S(2)}) collective-permute-start(bf16[2,288,128]{2,1,0:T(8,128)(2,1)S(1)} %get-tuple-element.42), channel_id=1, source_target_pairs={{0,12},{2,14},{4,8},{6,10},{8,4},{10,6},{12,0},{14,2},{1,13},{3,15... | collective-permute-start | bytes 442376 | tf_op jit(solution)/shard_map/ppermute | solution.py:421
  66.0 42.5 %copy-start.11 = (bf16[2,288,128]{2,1,0:T(8,128)(2,1)}, bf16[2,288,128]{2,1,0:T(8,128)(2,1)S(1)}, u32[]{:S(2)}) copy-start(bf16[2,288,128]{2,1,0:T(8,128)(2,1)S(1)} %collective-permute-done.15.refs_2_) | copy-start | bytes 442372
  66.1 7.9 %collective-permute-start.20 = (bf16[2,288,128]{2,1,0:T(8,128)(2,1)S(1)}, bf16[2,288,128]{2,1,0:T(8,128)(2,1)S(1)}, u32[]{:S(2)}, u32[]{:S(2)}) collective-permute-start(bf16[2,288,128]{2,1,0:T(8,128)(2,1)S(1)} %get-tuple-element.43), channel_id=1, source_target_pairs={{0,14},{2,12},{4,10},{6,8},{8,6},{10,4},{12,2},{14,0},{1,15},{3,13... | collective-permute-start | bytes 442376 | tf_op jit(solution)/shard_map/ppermute | solution.py:421
  67.9 40.7 %copy-start.13 = (bf16[2,288,128]{2,1,0:T(8,128)(2,1)}, bf16[2,288,128]{2,1,0:T(8,128)(2,1)S(1)}, u32[]{:S(2)}) copy-start(bf16[2,288,128]{2,1,0:T(8,128)(2,1)S(1)} %collective-permute-done.16.refs_3_) | copy-start | bytes 442372
  67.9 6.1 %collective-permute-start.7 = (bf16[2,288,128]{2,1,0:T(8,128)(2,1)S(1)}, bf16[2,288,128]{2,1,0:T(8,128)(2,1)S(1)}, u32[]{:S(2)}, u32[]{:S(2)}) collective-permute-start(bf16[2,288,128]{2,1,0:T(8,128)(2,1)S(1)} %collective-permute-done.refs_1_), channel_id=1, source_target_pairs={{0,1},{1,0},{2,3},{3,2},{4,5},{5,4},{6,7},{7,6},{8,9},{9,8},{10,11... | collective-permute-start | bytes 442376 | tf_op jit(solution)/shard_map/ppermute | solution.py:423
  67.9 40.7 %copy-start.15 = (bf16[2,288,128]{2,1,0:T(8,128)(2,1)}, bf16[2,288,128]{2,1,0:T(8,128)(2,1)S(1)}, u32[]{:S(2)}) copy-start(bf16[2,288,128]{2,1,0:T(8,128)(2,1)S(1)} %collective-permute-done.17.refs_4_) | copy-start | bytes 442372
  67.9 6.6 %collective-permute-start.8 = (bf16[2,288,128]{2,1,0:T(8,128)(2,1)S(1)}, bf16[2,288,128]{2,1,0:T(8,128)(2,1)S(1)}, u32[]{:S(2)}, u32[]{:S(2)}) collective-permute-start(bf16[2,288,128]{2,1,0:T(8,128)(2,1)S(1)} %collective-permute-done.1.refs_2_), channel_id=1, source_target_pairs={{0,1},{1,0},{2,3},{3,2},{4,5},{5,4},{6,7},{7,6},{8,9},{9,8},{10,11... | collective-permute-start | bytes 442376 | tf_op jit(solution)/shard_map/ppermute | solution.py:423
  72.1 36.5 %copy-start.16 = (bf16[2,288,128]{2,1,0:T(8,128)(2,1)}, bf16[2,288,128]{2,1,0:T(8,128)(2,1)S(1)}, u32[]{:S(2)}) copy-start(bf16[2,288,128]{2,1,0:T(8,128)(2,1)S(1)} %collective-permute-done.18.refs_5_) | copy-start | bytes 442372
  72.1 2.5 %collective-permute-start.9 = (bf16[2,288,128]{2,1,0:T(8,128)(2,1)S(1)}, bf16[2,288,128]{2,1,0:T(8,128)(2,1)S(1)}, u32[]{:S(2)}, u32[]{:S(2)}) collective-permute-start(bf16[2,288,128]{2,1,0:T(8,128)(2,1)S(1)} %collective-permute-done.2.refs_3_), channel_id=1, source_target_pairs={{0,1},{1,0},{2,3},{3,2},{4,5},{5,4},{6,7},{7,6},{8,9},{9,8},{10,11... | collective-permute-start | bytes 442376 | tf_op jit(solution)/shard_map/ppermute | solution.py:423
  72.2 36.5 %copy-start.17 = (bf16[2,288,128]{2,1,0:T(8,128)(2,1)}, bf16[2,288,128]{2,1,0:T(8,128)(2,1)S(1)}, u32[]{:S(2)}) copy-start(bf16[2,288,128]{2,1,0:T(8,128)(2,1)S(1)} %collective-permute-done.19.refs_6_) | copy-start | bytes 442372
  72.2 2.9 %collective-permute-start.10 = (bf16[2,288,128]{2,1,0:T(8,128)(2,1)S(1)}, bf16[2,288,128]{2,1,0:T(8,128)(2,1)S(1)}, u32[]{:S(2)}, u32[]{:S(2)}) collective-permute-start(bf16[2,288,128]{2,1,0:T(8,128)(2,1)S(1)} %collective-permute-done.3.refs_4_), channel_id=1, source_target_pairs={{0,1},{1,0},{2,3},{3,2},{4,5},{5,4},{6,7},{7,6},{8,9},{9,8},{10,11... | collective-permute-start | bytes 442376 | tf_op jit(solution)/shard_map/ppermute | solution.py:423
  74.0 34.6 %copy-start.18 = (bf16[2,288,128]{2,1,0:T(8,128)(2,1)}, bf16[2,288,128]{2,1,0:T(8,128)(2,1)S(1)}, u32[]{:S(2)}) copy-start(bf16[2,288,128]{2,1,0:T(8,128)(2,1)S(1)} %collective-permute-done.20.refs_7_) | copy-start | bytes 442372
  74.0 1.4 %collective-permute-start.11 = (bf16[2,288,128]{2,1,0:T(8,128)(2,1)S(1)}, bf16[2,288,128]{2,1,0:T(8,128)(2,1)S(1)}, u32[]{:S(2)}, u32[]{:S(2)}) collective-permute-start(bf16[2,288,128]{2,1,0:T(8,128)(2,1)S(1)} %collective-permute-done.4.refs_5_), channel_id=1, source_target_pairs={{0,1},{1,0},{2,3},{3,2},{4,5},{5,4},{6,7},{7,6},{8,9},{9,8},{10,11... | collective-permute-start | bytes 442376 | tf_op jit(solution)/shard_map/ppermute | solution.py:423
  74.0 2.7 %copy-start.19 = (bf16[2,288,128]{2,1,0:T(8,128)(2,1)}, bf16[2,288,128]{2,1,0:T(8,128)(2,1)S(1)}, u32[]{:S(2)}) copy-start(bf16[2,288,128]{2,1,0:T(8,128)(2,1)S(1)} %collective-permute-done.7.refs_9_) | copy-start | bytes 442372
  74.0 1.6 %collective-permute-start.12 = (bf16[2,288,128]{2,1,0:T(8,128)(2,1)S(1)}, bf16[2,288,128]{2,1,0:T(8,128)(2,1)S(1)}, u32[]{:S(2)}, u32[]{:S(2)}) collective-permute-start(bf16[2,288,128]{2,1,0:T(8,128)(2,1)S(1)} %collective-permute-done.5.refs_6_), channel_id=1, source_target_pairs={{0,1},{1,0},{2,3},{3,2},{4,5},{5,4},{6,7},{7,6},{8,9},{9,8},{10,11... | collective-permute-start | bytes 442376 | tf_op jit(solution)/shard_map/ppermute | solution.py:423
  74.5 2.2 %copy-start.20 = (bf16[2,288,128]{2,1,0:T(8,128)(2,1)}, bf16[2,288,128]{2,1,0:T(8,128)(2,1)S(1)}, u32[]{:S(2)}) copy-start(bf16[2,288,128]{2,1,0:T(8,128)(2,1)S(1)} %collective-permute-done.8.refs_10_) | copy-start | bytes 442372
  74.5 1.4 %collective-permute-start.13 = (bf16[2,288,128]{2,1,0:T(8,128)(2,1)S(1)}, bf16[2,288,128]{2,1,0:T(8,128)(2,1)S(1)}, u32[]{:S(2)}, u32[]{:S(2)}) collective-permute-start(bf16[2,288,128]{2,1,0:T(8,128)(2,1)S(1)} %collective-permute-done.6.refs_7_), channel_id=1, source_target_pairs={{0,1},{1,0},{2,3},{3,2},{4,5},{5,4},{6,7},{7,6},{8,9},{9,8},{10,11... | collective-permute-start | bytes 442376 | tf_op jit(solution)/shard_map/ppermute | solution.py:423
  74.6 2.1 %copy-start.21 = (bf16[2,288,128]{2,1,0:T(8,128)(2,1)}, bf16[2,288,128]{2,1,0:T(8,128)(2,1)S(1)}, u32[]{:S(2)}) copy-start(bf16[2,288,128]{2,1,0:T(8,128)(2,1)S(1)} %collective-permute-done.9.refs_11_) | copy-start | bytes 442372
  74.6 1.5 %collective-permute-start.21 = (bf16[2,288,128]{2,1,0:T(8,128)(2,1)S(1)}, bf16[2,288,128]{2,1,0:T(8,128)(2,1)S(1)}, u32[]{:S(2)}, u32[]{:S(2)}) collective-permute-start(bf16[2,288,128]{2,1,0:T(8,128)(2,1)S(1)} %collective-permute-done.14.refs_1_), channel_id=1, source_target_pairs={{0,1},{1,0},{2,3},{3,2},{4,5},{5,4},{6,7},{7,6},{8,9},{9,8},{10,11... | collective-permute-start | bytes 442376 | tf_op jit(solution)/shard_map/ppermute | solution.py:423
  75.0 1.7 %copy-start.23 = (bf16[2,288,128]{2,1,0:T(8,128)(2,1)}, bf16[2,288,128]{2,1,0:T(8,128)(2,1)S(1)}, u32[]{:S(2)}) copy-start(bf16[2,288,128]{2,1,0:T(8,128)(2,1)S(1)} %collective-permute-done.10.refs_12_) | copy-start | bytes 442372
  75.0 1.4 %collective-permute-start.22 = (bf16[2,288,128]{2,1,0:T(8,128)(2,1)S(1)}, bf16[2,288,128]{2,1,0:T(8,128)(2,1)S(1)}, u32[]{:S(2)}, u32[]{:S(2)}) collective-permute-start(bf16[2,288,128]{2,1,0:T(8,128)(2,1)S(1)} %collective-permute-done.15.refs_2_), channel_id=1, source_target_pairs={{0,1},{1,0},{2,3},{3,2},{4,5},{5,4},{6,7},{7,6},{8,9},{9,8},{10,11... | collective-permute-start | bytes 442376 | tf_op jit(solution)/shard_map/ppermute | solution.py:423
  75.4 1.3 %copy-start.25 = (bf16[2,288,128]{2,1,0:T(8,128)(2,1)}, bf16[2,288,128]{2,1,0:T(8,128)(2,1)S(1)}, u32[]{:S(2)}) copy-start(bf16[2,288,128]{2,1,0:T(8,128)(2,1)S(1)} %collective-permute-done.11.refs_13_) | copy-start | bytes 442372
  75.4 33.3 %collective-permute-start.23 = (bf16[2,288,128]{2,1,0:T(8,128)(2,1)S(1)}, bf16[2,288,128]{2,1,0:T(8,128)(2,1)S(1)}, u32[]{:S(2)}, u32[]{:S(2)}) collective-permute-start(bf16[2,288,128]{2,1,0:T(8,128)(2,1)S(1)} %collective-permute-done.16.refs_3_), channel_id=1, source_target_pairs={{0,1},{1,0},{2,3},{3,2},{4,5},{5,4},{6,7},{7,6},{8,9},{9,8},{10,11... | collective-permute-start | bytes 442376 | tf_op jit(solution)/shard_map/ppermute | solution.py:423
  75.6 1.1 copy-start.27
  75.6 33.1 %collective-permute-start.24 = (bf16[2,288,128]{2,1,0:T(8,128)(2,1)S(1)}, bf16[2,288,128]{2,1,0:T(8,128)(2,1)S(1)}, u32[]{:S(2)}, u32[]{:S(2)}) collective-permute-start(bf16[2,288,128]{2,1,0:T(8,128)(2,1)S(1)} %collective-permute-done.17.refs_4_), channel_id=1, source_target_pairs={{0,1},{1,0},{2,3},{3,2},{4,5},{5,4},{6,7},{7,6},{8,9},{9,8},{10,11... | collective-permute-start | bytes 442376 | tf_op jit(solution)/shard_map/ppermute | solution.py:423
  75.9 0.8 copy-start.29
  75.9 32.8 %collective-permute-start.25 = (bf16[2,288,128]{2,1,0:T(8,128)(2,1)S(1)}, bf16[2,288,128]{2,1,0:T(8,128)(2,1)S(1)}, u32[]{:S(2)}, u32[]{:S(2)}) collective-permute-start(bf16[2,288,128]{2,1,0:T(8,128)(2,1)S(1)} %collective-permute-done.18.refs_5_), channel_id=1, source_target_pairs={{0,1},{1,0},{2,3},{3,2},{4,5},{5,4},{6,7},{7,6},{8,9},{9,8},{10,11... | collective-permute-start | bytes 442376 | tf_op jit(solution)/shard_map/ppermute | solution.py:423
  76.1 32.5 %copy-start.22 = (bf16[2,288,128]{2,1,0:T(8,128)(2,1)}, bf16[2,288,128]{2,1,0:T(8,128)(2,1)S(1)}, u32[]{:S(2)}) copy-start(bf16[2,288,128]{2,1,0:T(8,128)(2,1)S(1)} %collective-permute-done.21.refs_9_) | copy-start | bytes 442372
  76.1 32.6 %collective-permute-start.26 = (bf16[2,288,128]{2,1,0:T(8,128)(2,1)S(1)}, bf16[2,288,128]{2,1,0:T(8,128)(2,1)S(1)}, u32[]{:S(2)}, u32[]{:S(2)}) collective-permute-start(bf16[2,288,128]{2,1,0:T(8,128)(2,1)S(1)} %collective-permute-done.19.refs_6_), channel_id=1, source_target_pairs={{0,1},{1,0},{2,3},{3,2},{4,5},{5,4},{6,7},{7,6},{8,9},{9,8},{10,11... | collective-permute-start | bytes 442376 | tf_op jit(solution)/shard_map/ppermute | solution.py:423
  76.4 32.2 %copy-start.24 = (bf16[2,288,128]{2,1,0:T(8,128)(2,1)}, bf16[2,288,128]{2,1,0:T(8,128)(2,1)S(1)}, u32[]{:S(2)}) copy-start(bf16[2,288,128]{2,1,0:T(8,128)(2,1)S(1)} %collective-permute-done.22.refs_10_) | copy-start | bytes 442372
  76.4 32.3 %collective-permute-start.27 = (bf16[2,288,128]{2,1,0:T(8,128)(2,1)S(1)}, bf16[2,288,128]{2,1,0:T(8,128)(2,1)S(1)}, u32[]{:S(2)}, u32[]{:S(2)}) collective-permute-start(bf16[2,288,128]{2,1,0:T(8,128)(2,1)S(1)} %collective-permute-done.20.refs_7_), channel_id=1, source_target_pairs={{0,1},{1,0},{2,3},{3,2},{4,5},{5,4},{6,7},{7,6},{8,9},{9,8},{10,11... | collective-permute-start | bytes 442376 | tf_op jit(solution)/shard_map/ppermute | solution.py:423
  108.7 0.7 copy-start.26
  108.7 0.7 copy-start.28
  108.7 0.8 copy-start.30
  108.7 0.8 copy-start.31
  108.8 0.8 copy-start.32

commit v2 on v1

v2 whole, which is shorter than its diff:
```python
import functools

import jax
import jax.numpy as jnp
from jax import lax
from jax.experimental import pallas as pl
from jax.experimental.pallas import tpu as pltpu
from jax.sharding import PartitionSpec as P

KVL = 512
BLOCK = 64
SEL = 32
PAIR = 2 * BLOCK
GROUP = 2 * PAIR
SUB = 512
STEP = 2 * SUB
VMEM = 60 << 20
NEG = -1e30
SCALE = 1.4426950408889634 / 192.0**0.5
NT = (((1,), (1,)), ((), ()))
NN = (((1,), (0,)), ((), ()))


def log2(n):
    shift = n.bit_length() - 1
    assert 1 << shift == n
    return shift


def partners(owners):
    count = (owners - 2) // 2
    low, high = range(1, count + 1), range(count + 1, 2 * count + 1)
    return [(a, b) if i % 2 == 0 else (b, a) for i, (a, b) in enumerate(zip(low, high))]


def pack_kernel(capacity, phases, ids, cache, *refs):
    dests = ids.shape[0]
    pairs = partners(dests)
    each = len(pairs) + 2
    outs = [refs[p * each : (p + 1) * each] for p in range(len(phases))]
    table, rows, sem = refs[len(phases) * each :]
    lat, tokens = rows.shape
    half = lat // 2
    shift = log2(tokens // BLOCK)
    head = lax.axis_index("head")
    me = lax.axis_index("ctx")
    copy = pltpu.make_async_copy(cache, rows, sem)
    copy.start()

    @pl.loop(0, dests)
    def _(d):
        first = d * (capacity + 1)
        for slot in range(capacity + 1):
            table[first + slot] = 0
        at = first
        for j in range(SEL):
            block = ids[d, j]
            table[at] = block & ((1 << shift) - 1)
            at = at + (block >> shift == me).astype(jnp.int32)
        table[at] = 0

    def block_pair(d, chunk, start, size):
        first = d * (capacity + 1) + 2 * chunk
        a, b = table[first], table[first + 1]
        left = lax.broadcasted_iota(jnp.int32, (size, PAIR), 1) < BLOCK
        xa = rows[pl.ds(start, size), pl.ds(pl.multiple_of((a >> 1) * PAIR, PAIR), PAIR)].astype(jnp.float32)
        xb = rows[pl.ds(start, size), pl.ds(pl.multiple_of((b >> 1) * PAIR, PAIR), PAIR)].astype(jnp.float32)
        xa = pltpu.roll(xa, (a & 1) * BLOCK, 1)
        xb = pltpu.roll(xb, (1 - (b & 1)) * BLOCK, 1)
        return jnp.where(left, xa, xb).astype(jnp.bfloat16)

    copy.wait()
    for p, chunks in enumerate(phases):
        for c, chunk in enumerate(chunks):
            for j, (a, b) in enumerate(pairs):
                d = me ^ jnp.where(head == 0, a, b)
                outs[p][j][c] = block_pair(d, chunk, 0, lat)
            shared = pl.multiple_of(head * half, 32)
            outs[p][-2][c] = block_pair(me ^ (dests - 1), chunk, shared, half)
    for p, chunks in enumerate(phases):
        for c, chunk in enumerate(chunks):
            outs[p][-1][c] = block_pair(me, chunk, 0, lat)


def pack(all_ids, cache_t, capacity, phases):
    dests = all_ids.shape[0]
    lat, tokens = cache_t.shape
    sizes = [lat] * len(partners(dests)) + [lat // 2, lat]
    shapes = [(len(chunks), size, PAIR) for chunks in phases for size in sizes]
    packed = pl.pallas_call(
        functools.partial(pack_kernel, capacity, phases),
        out_shape=[jax.ShapeDtypeStruct(s, jnp.bfloat16) for s in shapes],
        grid_spec=pltpu.PrefetchScalarGridSpec(
            num_scalar_prefetch=1,
            grid=(1,),
            in_specs=[pl.BlockSpec(memory_space=pl.ANY)],
            out_specs=[pl.BlockSpec(s, lambda i, ids: (0, 0, 0)) for s in shapes],
            scratch_shapes=[
                pltpu.SMEM((dests * (capacity + 1),), jnp.int32),
                pltpu.VMEM((lat, tokens), jnp.bfloat16),
                pltpu.SemaphoreType.DMA,
            ],
        ),
        compiler_params=pltpu.CompilerParams(vmem_limit_bytes=VMEM),
        name="pack",
    )(all_ids, cache_t)
    return [packed[p * len(sizes) : (p + 1) * len(sizes)] for p in range(len(phases))]


def slot_starts(ids, starts, owners, capacity, shift):
    for slot in range(owners * capacity):
        starts[slot] = -1
    for o in range(owners):
        starts[owners * capacity + o] = 0
    for j in range(SEL):
        block = ids[j]
        owner = block >> shift
        rank = starts[owners * capacity + owner]
        starts[owner * capacity + rank] = block * BLOCK
        starts[owners * capacity + owner] = rank + 1


class Arrived:
    def __init__(self, owners, arrays, sems):
        pairs = partners(owners)
        count = len(pairs)
        head, me = lax.axis_index("head"), lax.axis_index("ctx")
        got, shared, own = arrays[:count], arrays[count], arrays[count + 1]
        swapped, shared_other = arrays[count + 2 : 2 * count + 2], arrays[2 * count + 2]
        self.chunks, lat, _ = own.shape
        half = lat // 2
        self.sems = sems
        self.parts = [(me, [(own, 0, lat)])]
        for (a, b), x, y in zip(pairs, got, swapped):
            self.parts.append((me ^ jnp.where(head == 0, a, b), [(x, 0, lat)]))
            self.parts.append((me ^ jnp.where(head == 0, b, a), [(y, 0, lat)]))
        split = [(x, pl.multiple_of(h * half, 32), half) for x, h in ((shared, head), (shared_other, 1 - head))]
        self.parts.append((me ^ (owners - 1), split))

    def owners(self):
        return [owner for owner, _ in self.parts]

    def copies(self, place, chunk, kt, at):
        sources = self.parts[place][1]
        return [
            pltpu.make_async_copy(
                x.at[chunk], kt.at[pl.ds(start, size), pl.ds(at, PAIR)], self.sems.at[chunk * len(self.parts) + place, i]
            )
            for i, (x, start, size) in enumerate(sources)
        ]


def pair_bias(bias, at, start_a, start_b):
    lane = lax.broadcasted_iota(jnp.int32, (8, PAIR), 1)
    start = jnp.where(lane < BLOCK, start_a, start_b)
    bias[:, pl.ds(at, PAIR)] = jnp.where(start >= 0, 0.0, NEG).astype(jnp.float32)


class Half:
    def __init__(self, base, q, kt, bias, scores, weights, tops, sums, keys, diagonal=None):
        self.base, self.q, self.kt, self.bias = base, q, kt, bias
        self.scores, self.weights, self.tops, self.sums = scores, weights, tops, sums
        self.keys, self.diagonal = keys, diagonal
        self.groups = -(-keys // GROUP)

    def score(self, group):
        at = group * GROUP
        end = min(at + GROUP, self.keys)
        part = lax.dot_general(
            self.q[pl.ds(self.base, SUB), :], self.kt[:, at:end], NN, preferred_element_type=jnp.float32
        )
        part = part + self.bias[0:1, at:end]
        columns = [part[:, c : c + PAIR] for c in range(0, end - at, PAIR)]
        if self.diagonal is not None:
            where, key, pos, first = self.diagonal
            if at <= where < end:
                seen = jnp.concatenate(
                    [
                        jnp.broadcast_to(key, (BLOCK, PAIR)) <= pos[first + self.base // BLOCK + s]
                        for s in range(SUB // BLOCK)
                    ],
                    axis=0,
                )
                index = (where - at) // PAIR
                columns[index] = jnp.where(seen, columns[index], NEG)
        high = columns[0]
        for i, column in enumerate(columns):
            self.scores[:, at + i * PAIR : at + (i + 1) * PAIR] = column
            high = jnp.maximum(high, column) if i else high
        self.tops[...] = high if group == 0 else jnp.maximum(self.tops[...], high)

    def settle(self, old=None):
        top = jnp.max(self.tops[...], axis=1, keepdims=True) * SCALE
        top = jnp.broadcast_to(top, (SUB, PAIR))
        self.tops[...] = top if old is None else jnp.maximum(top, old)

    def weigh(self, slab):
        rows = pl.ds(slab * BLOCK, BLOCK)
        top = self.tops[rows, :]
        total = jnp.zeros((BLOCK, PAIR), jnp.float32)
        for at in range(0, self.keys, PAIR):
            part = jnp.exp2(self.scores[rows, at : at + PAIR] * SCALE - top)
            total = total + part
            self.weights[rows, at : at + PAIR] = part.astype(jnp.bfloat16)
        self.sums[rows, :] = total

    def total(self):
        return jnp.broadcast_to(jnp.sum(self.sums[...], axis=1, keepdims=True), (SUB, PAIR))

    def combine(self, column):
        return lax.dot_general(
            self.weights[:, 0 : self.keys],
            self.kt[column : column + GROUP, 0 : self.keys],
            NT,
            preferred_element_type=jnp.float32,
        )


def run_halves(a, b, before, after, combine):
    slabs = SUB // BLOCK
    for g in range(a.groups):
        a.score(g)
    before(a)
    for i in range(max(a.groups, slabs)):
        if i < b.groups:
            b.score(i)
        if i < slabs:
            a.weigh(i)
    before(b)
    after(a)
    for i, column in enumerate(range(0, KVL, GROUP)):
        combine(a, column)
        for s in range(i * slabs // 2, (i + 1) * slabs // 2):
            b.weigh(s)
    after(b)
    for column in range(0, KVL, GROUP):
        combine(b, column)


SCRATCH = 12


def first_kernel(capacity, shift, owners, final, ids, pos, q, *refs):
    count = len(refs) - SCRATCH - (1 if final else 2)
    outs = refs[count : len(refs) - SCRATCH]
    starts, kt, bias, *work, sems = refs[len(refs) - SCRATCH :]
    arrived = Arrived(owners, refs[:count], sems)
    chunks = arrived.chunks
    keys = owners * chunks * PAIR
    step = pl.program_id(0)

    @pl.when(step == 0)
    def _():
        copies = []
        for c in range(chunks):
            for place, owner in enumerate(arrived.owners()):
                copies += arrived.copies(place, c, kt, pl.multiple_of((c * owners + owner) * PAIR, PAIR))
        for copy in copies:
            copy.start()
        slot_starts(ids, starts, owners, capacity, shift)
        for c in range(chunks):
            for o in range(owners):
                slot = o * capacity + 2 * c
                pair_bias(bias, (c * owners + o) * PAIR, starts[slot], starts[slot + 1])
        for copy in copies:
            copy.wait()

    key = starts[(owners - 1) * capacity] + lax.broadcasted_iota(jnp.int32, (1, PAIR), 1)
    diagonal = ((owners - 1) * PAIR, key, pos, step * (STEP // BLOCK))
    a = Half(0, q, kt, bias, *work[0::2], keys, diagonal)
    b = Half(SUB, q, kt, bias, *work[1::2], keys, diagonal)

    def after(part):
        total = part.total()
        part.sums[...] = 1.0 / total
        if not final:
            outs[1][pl.ds(part.base, SUB), :] = part.tops[...] + jnp.log2(total)

    def combine(part, column):
        summed = part.combine(column)
        for at in range(0, GROUP, PAIR):
            result = summed[:, at : at + PAIR] * part.sums[...]
            outs[0][pl.ds(part.base, SUB), column + at : column + at + PAIR] = result.astype(jnp.bfloat16)

    run_halves(a, b, lambda part: part.settle(), after, combine)


def rest_kernel(capacity, shift, owners, skip, levels, ids, q, carry, logs, *refs):
    count = len(refs) - SCRATCH - 1
    out = refs[count]
    starts, kt, bias, *work, sems = refs[len(refs) - SCRATCH :]
    arrived = Arrived(owners, refs[:count], sems)
    live = owners * capacity + owners

    @pl.when(pl.program_id(0) == 0)
    def _():
        slot_starts(ids, starts, owners, capacity, shift)
        kt[...] = jnp.zeros(kt.shape, kt.dtype)
        bias[...] = jnp.full(bias.shape, NEG, bias.dtype)

        def each(act):
            starts[live] = 0
            for c in range(arrived.chunks):
                for place, owner in enumerate(arrived.owners()):
                    slot = owner * capacity + 2 * (skip + c)
                    @pl.when(starts[slot] >= 0)
                    def _():
                        at = starts[live]
                        starts[live] = at + 1
                        at = pl.multiple_of(at * PAIR, PAIR)
                        act(arrived.copies(place, c, kt, at), at, slot)

        def begin(copies, at, slot):
            for copy in copies:
                copy.start()
            pair_bias(bias, at, starts[slot], starts[slot + 1])

        def end(copies, at, slot):
            for copy in copies:
                copy.wait()

        each(begin)
        each(end)

    def attend(keys):
        a = Half(0, q, kt, bias, *work[0::2], keys)
        b = Half(SUB, q, kt, bias, *work[1::2], keys)

        def before(part):
            part.settle(logs[pl.ds(part.base, SUB), :])

        def after(part):
            kept = jnp.exp2(logs[pl.ds(part.base, SUB), :] - part.tops[...])
            inverse = 1.0 / (kept + part.total())
            part.sums[...] = inverse
            part.tops[...] = kept * inverse

        def combine(part, column):
            summed = part.combine(column)
            rows = pl.ds(part.base, SUB)
            for at in range(0, GROUP, PAIR):
                cols = slice(column + at, column + at + PAIR)
                result = summed[:, at : at + PAIR] * part.sums[...]
                result = result + carry[rows, cols].astype(jnp.float32) * part.tops[...]
                out[rows, cols] = result.astype(jnp.bfloat16)

        run_halves(a, b, before, after, combine)

    needed = starts[live]
    below = -1
    for level in levels:
        @pl.when(jnp.logical_and(needed > below, needed <= level))
        def _():
            attend(level * PAIR)
        below = level


def anywhere(count):
    return [pl.BlockSpec(memory_space=pl.ANY)] * count


def scratch(owners, capacity, chunks, lat, keys):
    return [
        pltpu.SMEM((owners * capacity + owners + 1,), jnp.int32),
        pltpu.VMEM((lat, keys), jnp.bfloat16),
        pltpu.VMEM((8, keys), jnp.float32),
        *[pltpu.VMEM((SUB, keys), jnp.float32)] * 2,
        *[pltpu.VMEM((SUB, keys), jnp.bfloat16)] * 2,
        *[pltpu.VMEM((SUB, PAIR), jnp.float32)] * 4,
        pltpu.SemaphoreType.DMA((chunks * owners, 2)),
    ]


def attend_first(ids, pos, q, arrays, owners, capacity, shift, chunks, final):
    rows, lat = q.shape
    keys = owners * chunks * PAIR
    out_shape = [jax.ShapeDtypeStruct((rows, KVL), jnp.bfloat16), jax.ShapeDtypeStruct((rows, PAIR), jnp.float32)]
    if final:
        out_shape = out_shape[:1]
    return pl.pallas_call(
        functools.partial(first_kernel, capacity, shift, owners, final),
        out_shape=out_shape,
        grid_spec=pltpu.PrefetchScalarGridSpec(
            num_scalar_prefetch=2,
            grid=(rows // STEP,),
            in_specs=[pl.BlockSpec((STEP, lat), lambda i, *_: (i, 0))] + anywhere(len(arrays)),
            out_specs=[pl.BlockSpec((STEP, s.shape[1]), lambda i, *_: (i, 0)) for s in out_shape],
            scratch_shapes=scratch(owners, capacity, chunks, lat, keys),
        ),
        compiler_params=pltpu.CompilerParams(vmem_limit_bytes=VMEM),
        cost_estimate=pl.CostEstimate(
            flops=2 * rows * keys * (lat + KVL), bytes_accessed=rows * (lat + KVL) * 2, transcendentals=rows * keys
        ),
        name="attend_first",
    )(ids, pos, q, *arrays)


def attend_rest(ids, q, carry, logs, arrays, owners, capacity, shift, chunks, skip):
    rows, lat = q.shape
    keys = owners * chunks * PAIR
    most = owners * chunks
    levels = [n for n in (4, 5, 6, 8) if n < most] + [most]
    return pl.pallas_call(
        functools.partial(rest_kernel, capacity, shift, owners, skip, levels),
        out_shape=jax.ShapeDtypeStruct((rows, KVL), jnp.bfloat16),
        grid_spec=pltpu.PrefetchScalarGridSpec(
            num_scalar_prefetch=1,
            grid=(rows // STEP,),
            in_specs=[
                pl.BlockSpec((STEP, lat), lambda i, *_: (i, 0)),
                pl.BlockSpec((STEP, KVL), lambda i, *_: (i, 0)),
                pl.BlockSpec((STEP, PAIR), lambda i, *_: (i, 0)),
            ]
            + anywhere(len(arrays)),
            out_specs=pl.BlockSpec((STEP, KVL), lambda i, *_: (i, 0)),
            scratch_shapes=scratch(owners, capacity, chunks, lat, keys),
        ),
        compiler_params=pltpu.CompilerParams(vmem_limit_bytes=VMEM),
        cost_estimate=pl.CostEstimate(
            flops=rows * keys * (lat + KVL), bytes_accessed=rows * (lat + 2 * KVL) * 2, transcendentals=rows * keys // 2
        ),
        name="attend_rest",
    )(ids, q, carry, logs, *arrays)


def local(queries, latent_cache, positions, block_ids):
    owners = lax.axis_size("ctx")
    capacity = max(2, 2 * SEL // owners)
    shift = log2(latent_cache.shape[0] // BLOCK)
    q_rows, heads, lat = queries.shape
    rows = q_rows * heads
    all_ids = lax.all_to_all(
        jnp.broadcast_to(block_ids, (owners, SEL)), "ctx", split_axis=0, concat_axis=0, tiled=True
    )
    chunks = list(range(capacity // 2))
    cut = (len(chunks) + 1) // 2
    phases = [part for part in (chunks[:cut], chunks[cut:]) if part]
    packed = pack(all_ids, latent_cache.T, capacity, phases)
    steps = partners(owners) + [(owners - 1, owners - 1)]

    def send(own):
        got = []
        for x, ks in zip(own, steps):
            moves = [(2 * c + h, 2 * (c ^ k) + h) for c in range(owners) for h, k in enumerate(ks)]
            got.append(lax.ppermute(x, ("ctx", "head"), moves))
        return got

    def swap(got):
        return [lax.ppermute(x, "head", [(0, 1), (1, 0)]) for x in got]

    q = queries.reshape(rows, lat)
    ids = block_ids[0]
    final = len(phases) == 1
    got = [send(own) for own in packed]
    arrays = [*got[0], packed[0][-1], *swap(got[0])]
    out = attend_first(ids, positions, q, arrays, owners, capacity, shift, len(phases[0]), final)
    if final:
        out = out[0]
    else:
        carry, logs = out
        *late, logs = lax.optimization_barrier((*got[1], logs))
        arrays = [*late, packed[1][-1], *swap(late)]
        out = attend_rest(ids, q, carry, logs, arrays, owners, capacity, shift, len(phases[1]), cut)
    return out.reshape(q_rows, heads, KVL)


def solution(mesh):
    return jax.shard_map(
        local,
        mesh=mesh,
        in_specs=(
            P(("groups", "ctx"), "head", None),
            P(("groups", "ctx"), None),
            P(("groups", "ctx")),
            P(("groups", "ctx"), None),
        ),
        out_specs=P(("groups", "ctx"), "head", None),
        check_vma=False,
    )
```

time: 136 us -> 103 us (0.76)
  waiting for transfers between devices: 20.8 us -> 8.56 us
  Pallas kernels: 59.1 us -> 50.7 us
  starting transfers between devices: 33.1 us -> 25.6 us
  local copies, waits for them, and re-layouts: 6.55 us -> 2.43 us
    ppermute x28 -> x16, waiting for transfers between devices: 20.8 us -> 8.56 us  [the longest x8 6.83 us: send(): got.append(lax.ppermute(x, ('ctx', 'head'), moves))]
    pallas_call x2, Pallas kernels: 55.7 us -> 44.5 us  [the longest x1 31.1 us: attend_first(): pl.pallas_call(functools.partial(first_kernel, capacity, shift, owners, f...]
    ppermute x28 -> x16, starting transfers between devices: 33.1 us -> 25.6 us  [the longest x8 15.6 us: send(): got.append(lax.ppermute(x, ('ctx', 'head'), moves))]
    unnamed x66 -> x32, local copies, waits for them, and re-layouts: 5.89 us -> 1.78 us
    pallas_call x1, Pallas kernels: 3.43 us -> 6.17 us  [pack(): pl.pallas_call(functools.partial(pack_kernel, capacity, phases), out_shap...]
  transfers between devices with their start and end apart: 28 -> 16, of which waited for: 7 -> 4; matrix products, arithmetic and copies ran while one was open for 0% -> 0% of each run, Pallas kernels for 24% -> 31%
where the time goes in v2:
time: 103 us; the launch traced here: 101 us
  Pallas kernels  50.7 us (49%)
  starting transfers between devices  25.6 us (25%)
  blocking collectives  13.6 us (13%)
  waiting for transfers between devices  8.56 us (8%)
  local copies, waits for them, and re-layouts  2.43 us (2%)
    pallas_call x1, Pallas kernels, attend_first(): pl.pallas_call(functools.partial(first_kernel, capacity, shift, owners, f...  31.1 us
    ppermute x8, starting transfers between devices, send(): got.append(lax.ppermute(x, ('ctx', 'head'), moves))  15.6 us
    all_to_all x1, blocking collectives, local(): lax.all_to_all(jnp.broadcast_to(block_ids, (owners, SEL)), 'ctx', split_a...  13.6 us
    pallas_call x1, Pallas kernels, attend_rest(): pl.pallas_call(functools.partial(rest_kernel, capacity, shift, owners, sk...  13.4 us
    ppermute x8, starting transfers between devices, swap(): return [lax.ppermute(x, 'head', [(0, 1), (1, 0)]) for x in got]  10.1 us
    ppermute x8, waiting for transfers between devices, send(): got.append(lax.ppermute(x, ('ctx', 'head'), moves))  6.83 us
    pallas_call x1, Pallas kernels, pack(): pl.pallas_call(functools.partial(pack_kernel, capacity, phases), out_shap...  6.17 us
  transfers between devices with their start and end apart: 16, of which 4 were waited for; matrix products, arithmetic and copies ran while one was open for 0% of the time, Pallas kernels for 31%

profile of v2, /device:TPU:0, one launch (start us, length us, event | category | flops | bytes accessed | tf_op | source)
XLA Modules:
  0.0 101.3 jit_solution(13239951703788796674)
XLA Ops:
  0.0 0.7 broadcast_in_dim.2
  0.7 13.6 %all_to_all.8 = s32[8,1,32]{2,1,0:T(1,128)} all-to-all(s32[8,1,32]{2,1,0:T(1,128)S(1)} %broadcast_in_dim.2), channel_id=1, replica_groups=mesh['groups'=2,'ctx'=8,'head'=2] {'ctx'}, dimensions={0} | all-to-all | bytes 2048 | tf_op jit(solution)/shard_map/all_to_all | solution.py:432
  14.3 6.2 %pack.1 = (bf16[2,576,128]{2,1,0:T(8,128)(2,1)}, bf16[2,576,128]{2,1,0:T(8,128)(2,1)}, bf16[2,576,128]{2,1,0:T(8,128)(2,1)}, bf16[2,288,128]{2,1,0:T(8,128)(2,1)...) custom-call(s32[8,32]{1,0:T(8,128)} %bitcast.6, ...), custom_call_target="tpu_custom_call" | custom-call | tf_op jit(solution)/shard_map/pack/pallas_call | solution.py:90
  20.5 0.6 collective-permute-start
  21.1 1.5 %collective-permute-start.1 = (bf16[2,576,128]{2,1,0:T(8,128)(2,1)}, bf16[2,576,128]{2,1,0:T(8,128)(2,1)S(1)}, u32[]{:S(2)}, u32[]{:S(2)}) collective-permute-start(bf16[2,576,128]{2,1,0:T(8,128)(2,1)} %get-tuple-element.23), channel_id=1, source_target_pairs={{0,10},{1,5},{2,8},{3,7},{4,14},{5,1},{6,12},{7,3},{8,2},{9,13},{1... | collective-permute-start | bytes 884744 | tf_op jit(solution)/shard_map/ppermute | solution.py:445
  22.6 0.6 collective-permute-start.2
  23.1 4.2 %collective-permute-start.3 = (bf16[2,288,128]{2,1,0:T(8,128)(2,1)}, bf16[2,288,128]{2,1,0:T(8,128)(2,1)S(1)}, u32[]{:S(2)}, u32[]{:S(2)}) collective-permute-start(bf16[2,288,128]{2,1,0:T(8,128)(2,1)} %get-tuple-element.25), channel_id=1, source_target_pairs={{0,14},{1,15},{2,12},{3,13},{4,10},{5,11},{6,8},{7,9},{8,6},{9,7},... | collective-permute-start | bytes 442376 | tf_op jit(solution)/shard_map/ppermute | solution.py:445
  27.3 1.4 %collective-permute-done.refs_0_ = bf16[2,576,128]{2,1,0:T(8,128)(2,1)S(1)} collective-permute-done((bf16[2,576,128]{2,1,0:T(8,128)(2,1)}, bf16[2,576,128]{2,1,0:T(8,128)(2,1)S(1)}, u32[]{:S(2)}, u32[]{:S(2)}) %collective-permute-start) | collective-permute-done | bytes 294944 | tf_op jit(solution)/shard_map/ppermute | solution.py:445
  28.7 0.0 copy-start.1
  28.7 8.4 %collective-permute-start.4 = (bf16[2,576,128]{2,1,0:T(8,128)(2,1)S(1)}, bf16[2,576,128]{2,1,0:T(8,128)(2,1)S(1)}, u32[]{:S(2)}, u32[]{:S(2)}) collective-permute-start(bf16[2,576,128]{2,1,0:T(8,128)(2,1)S(1)} %collective-permute-done.refs_0_), channel_id=1, source_target_pairs={{0,1},{1,0},{2,3},{3,2},{4,5},{5,4},{6,7},{7,6},{8,9},{9,8},{10,11... | collective-permute-start | bytes 884744 | tf_op jit(solution)/shard_map/ppermute | solution.py:449
  37.1 5.4 %collective-permute-done.1.refs_1_ = bf16[2,576,128]{2,1,0:T(8,128)(2,1)S(1)} collective-permute-done((bf16[2,576,128]{2,1,0:T(8,128)(2,1)}, bf16[2,576,128]{2,1,0:T(8,128)(2,1)S(1)}, u32[]{:S(2)}, u32[]{:S(2)}) %collective-permute-start.1) | collective-permute-done | bytes 294944 | tf_op jit(solution)/shard_map/ppermute | solution.py:445
  42.5 0.0 copy-start.2
  42.5 0.0 collective-permute-start.5
  42.5 0.0 collective-permute-done.2.refs_2_
  42.5 0.0 copy-start.4
  42.5 0.5 collective-permute-start.6
  43.0 0.0 collective-permute-done.3.refs_3_
  43.0 0.0 copy-start.13
  43.0 0.1 collective-permute-start.7
  43.1 1.5 %collective-permute-start.11 = (bf16[2,288,128]{2,1,0:T(8,128)(2,1)}, bf16[2,288,128]{2,1,0:T(8,128)(2,1)S(1)}, u32[]{:S(2)}, u32[]{:S(2)}) collective-permute-start(bf16[2,288,128]{2,1,0:T(8,128)(2,1)} %get-tuple-element.31), channel_id=1, source_target_pairs={{0,14},{1,15},{2,12},{3,13},{4,10},{5,11},{6,8},{7,9},{8,6},{9,7},... | collective-permute-start | bytes 442376 | tf_op jit(solution)/shard_map/ppermute | solution.py:445
  44.6 0.1 collective-permute-done.7.refs_8_
  44.7 1.5 %collective-permute-start.8 = (bf16[2,576,128]{2,1,0:T(8,128)(2,1)}, bf16[2,576,128]{2,1,0:T(8,128)(2,1)S(1)}, u32[]{:S(2)}, u32[]{:S(2)}) collective-permute-start(bf16[2,576,128]{2,1,0:T(8,128)(2,1)} %get-tuple-element.28), channel_id=1, source_target_pairs={{0,2},{1,9},{2,0},{3,11},{4,6},{5,13},{6,4},{7,15},{8,10},{9,1},{1... | collective-permute-start | bytes 884744 | tf_op jit(solution)/shard_map/ppermute | solution.py:445
  46.2 0.0 collective-permute-done.4.refs_5_
  46.2 5.7 %collective-permute-start.9 = (bf16[2,576,128]{2,1,0:T(8,128)(2,1)}, bf16[2,576,128]{2,1,0:T(8,128)(2,1)S(1)}, u32[]{:S(2)}, u32[]{:S(2)}) collective-permute-start(bf16[2,576,128]{2,1,0:T(8,128)(2,1)} %get-tuple-element.29), channel_id=1, source_target_pairs={{0,10},{1,5},{2,8},{3,7},{4,14},{5,1},{6,12},{7,3},{8,2},{9,13},{1... | collective-permute-start | bytes 884744 | tf_op jit(solution)/shard_map/ppermute | solution.py:445
  52.0 0.0 collective-permute-done.5.refs_6_
  52.0 0.0 collective-permute-start.10
  52.0 0.0 collective-permute-done.6.refs_7_
  52.0 0.0 copy-start.8
  52.0 0.0 copy-done.1
  52.0 0.0 copy-done.2
  52.0 0.0 copy-done.4
  52.0 0.0 copy-done.13
  52.0 0.0 copy-done.14
  52.1 0.0 copy-done.6
  52.1 0.6 copy-done.7
  52.7 0.1 copy-done.8
  52.8 31.1 %attend_first.1 = (bf16[4096,512]{1,0:T(8,128)(2,1)}, f32[4096,128]{1,0:T(8,128)}) custom-call(s32[32]{0:T(128)} %bitcast.8, s32[64]{0:T(128)} %pos.1, bf16[4096,576]{1,0:T(8,128)(2,1)} %bitcast.10, bf16[2,576,128]{2,1,0:T(8,128)(2,1)} %copy-done.1, bf16[2,576,128]{2,1,0:T(8,128)(2,1)} %copy-done.2, bf16[2,576,128]{2,1,0:T(8,128)(2,1)} %copy-done.4, ...), custom_call_target="tpu_custom_call" | custom-call | flops 18253611008 | bytes 8912896 | tf_op jit(solution)/shard_map/attend_first/pallas_call | solution.py:380
  83.9 0.0 collective-permute-done.11.refs_3_
  84.0 0.0 copy-start.12
  84.0 0.0 collective-permute-done.8.refs_0_
  84.0 0.0 copy-start
  84.0 0.0 collective-permute-done.9.refs_1_
  84.0 0.0 copy-start.3
  84.0 0.0 collective-permute-done.10.refs_2_
  84.0 0.0 copy-start.5
  84.0 0.1 collective-permute-start.12
  84.1 0.5 collective-permute-start.13
  84.6 0.1 collective-permute-start.14
  84.7 0.4 collective-permute-start.15
  85.1 1.6 %collective-permute-done.15.refs_8_ = bf16[2,288,128]{2,1,0:T(8,128)(2,1)S(1)} collective-permute-done((bf16[2,288,128]{2,1,0:T(8,128)(2,1)S(1)}, bf16[2,288,128]{2,1,0:T(8,128)(2,1)S(1)}, u32[]{:S(2)}, u32[]{:S(2)}) %collective-permute-start.15) | collective-permute-done | bytes 147488 | tf_op jit(solution)/shard_map/ppermute | solution.py:449
  86.7 0.0 collective-permute-done.12.refs_5_
  86.7 0.0 collective-permute-done.13.refs_6_
  86.7 0.0 copy-start.10
  86.8 0.0 collective-permute-done.14.refs_7_
  86.8 0.0 copy-start.11
  86.8 0.0 copy-done.12
  86.8 0.0 copy-done
  86.8 0.0 copy-done.3
  86.8 0.0 copy-done.5
  86.8 0.6 copy-done.15
  87.4 0.1 copy-done.9
  87.5 0.1 copy-done.10
  87.6 0.1 copy-done.11
  87.8 13.4 %attend_rest.1 = bf16[4096,512]{1,0:T(8,128)(2,1)} custom-call(s32[32]{0:T(128)} %bitcast.9, bf16[4096,576]{1,0:T(8,128)(2,1)} %bitcast.11, bf16[4096,512]{1,0:T(8,128)(2,1)} %get-tuple-element.27.carry, f32[4096,128]{1,0:T(8,128)} %get-tuple-element.33.logs, bf16[2,576,128]{2,1,0:T(8,128)(2,1)} %copy-done, bf16[2,576,128]{2,1,0:T(8,128)(2,1)} %copy-done.3, ...), custom_call_target="tpu_custom_call" | custom-call | flops 9126805504 | bytes 13107200 | tf_op jit(solution)/shard_map/attend_rest/pallas_call | solution.py:403
  (5 shorter events, 0.0 us)
Async XLA Ops:
  20.5 8.2 %collective-permute-start = (bf16[2,576,128]{2,1,0:T(8,128)(2,1)}, bf16[2,576,128]{2,1,0:T(8,128)(2,1)S(1)}, u32[]{:S(2)}, u32[]{:S(2)}) collective-permute-start(bf16[2,576,128]{2,1,0:T(8,128)(2,1)} %get-tuple-element.22), channel_id=1, source_target_pairs={{0,2},{1,9},{2,0},{3,11},{4,6},{5,13},{6,4},{7,15},{8,10},{9,1},{1... | collective-permute-start | bytes 884744 | tf_op jit(solution)/shard_map/ppermute | solution.py:445
  21.1 21.4 %collective-permute-start.1 = (bf16[2,576,128]{2,1,0:T(8,128)(2,1)}, bf16[2,576,128]{2,1,0:T(8,128)(2,1)S(1)}, u32[]{:S(2)}, u32[]{:S(2)}) collective-permute-start(bf16[2,576,128]{2,1,0:T(8,128)(2,1)} %get-tuple-element.23), channel_id=1, source_target_pairs={{0,10},{1,5},{2,8},{3,7},{4,14},{5,1},{6,12},{7,3},{8,2},{9,13},{1... | collective-permute-start | bytes 884744 | tf_op jit(solution)/shard_map/ppermute | solution.py:445
  22.6 20.0 %collective-permute-start.2 = (bf16[2,576,128]{2,1,0:T(8,128)(2,1)}, bf16[2,576,128]{2,1,0:T(8,128)(2,1)S(1)}, u32[]{:S(2)}, u32[]{:S(2)}) collective-permute-start(bf16[2,576,128]{2,1,0:T(8,128)(2,1)} %get-tuple-element.24), channel_id=1, source_target_pairs={{0,6},{1,13},{2,4},{3,15},{4,2},{5,9},{6,0},{7,11},{8,14},{9,5},{1... | collective-permute-start | bytes 884744 | tf_op jit(solution)/shard_map/ppermute | solution.py:445
  23.1 19.9 %collective-permute-start.3 = (bf16[2,288,128]{2,1,0:T(8,128)(2,1)}, bf16[2,288,128]{2,1,0:T(8,128)(2,1)S(1)}, u32[]{:S(2)}, u32[]{:S(2)}) collective-permute-start(bf16[2,288,128]{2,1,0:T(8,128)(2,1)} %get-tuple-element.25), channel_id=1, source_target_pairs={{0,14},{1,15},{2,12},{3,13},{4,10},{5,11},{6,8},{7,9},{8,6},{9,7},... | collective-permute-start | bytes 442376 | tf_op jit(solution)/shard_map/ppermute | solution.py:445
  28.7 23.3 %copy-start.1 = (bf16[2,576,128]{2,1,0:T(8,128)(2,1)}, bf16[2,576,128]{2,1,0:T(8,128)(2,1)S(1)}, u32[]{:S(2)}) copy-start(bf16[2,576,128]{2,1,0:T(8,128)(2,1)S(1)} %collective-permute-done.refs_0_) | copy-start | bytes 884740
  28.7 17.5 %collective-permute-start.4 = (bf16[2,576,128]{2,1,0:T(8,128)(2,1)S(1)}, bf16[2,576,128]{2,1,0:T(8,128)(2,1)S(1)}, u32[]{:S(2)}, u32[]{:S(2)}) collective-permute-start(bf16[2,576,128]{2,1,0:T(8,128)(2,1)S(1)} %collective-permute-done.refs_0_), channel_id=1, source_target_pairs={{0,1},{1,0},{2,3},{3,2},{4,5},{5,4},{6,7},{7,6},{8,9},{9,8},{10,11... | collective-permute-start | bytes 884744 | tf_op jit(solution)/shard_map/ppermute | solution.py:449
  42.5 9.5 %copy-start.2 = (bf16[2,576,128]{2,1,0:T(8,128)(2,1)}, bf16[2,576,128]{2,1,0:T(8,128)(2,1)S(1)}, u32[]{:S(2)}) copy-start(bf16[2,576,128]{2,1,0:T(8,128)(2,1)S(1)} %collective-permute-done.1.refs_1_) | copy-start | bytes 884740
  42.5 9.5 %collective-permute-start.5 = (bf16[2,576,128]{2,1,0:T(8,128)(2,1)S(1)}, bf16[2,576,128]{2,1,0:T(8,128)(2,1)S(1)}, u32[]{:S(2)}, u32[]{:S(2)}) collective-permute-start(bf16[2,576,128]{2,1,0:T(8,128)(2,1)S(1)} %collective-permute-done.1.refs_1_), channel_id=1, source_target_pairs={{0,1},{1,0},{2,3},{3,2},{4,5},{5,4},{6,7},{7,6},{8,9},{9,8},{10,11... | collective-permute-start | bytes 884744 | tf_op jit(solution)/shard_map/ppermute | solution.py:449
  42.5 9.5 %copy-start.4 = (bf16[2,576,128]{2,1,0:T(8,128)(2,1)}, bf16[2,576,128]{2,1,0:T(8,128)(2,1)S(1)}, u32[]{:S(2)}) copy-start(bf16[2,576,128]{2,1,0:T(8,128)(2,1)S(1)} %collective-permute-done.2.refs_2_) | copy-start | bytes 884740
  42.5 9.4 %collective-permute-start.6 = (bf16[2,576,128]{2,1,0:T(8,128)(2,1)S(1)}, bf16[2,576,128]{2,1,0:T(8,128)(2,1)S(1)}, u32[]{:S(2)}, u32[]{:S(2)}) collective-permute-start(bf16[2,576,128]{2,1,0:T(8,128)(2,1)S(1)} %collective-permute-done.2.refs_2_), channel_id=1, source_target_pairs={{0,1},{1,0},{2,3},{3,2},{4,5},{5,4},{6,7},{7,6},{8,9},{9,8},{10,11... | collective-permute-start | bytes 884744 | tf_op jit(solution)/shard_map/ppermute | solution.py:449
  43.0 9.0 %copy-start.13 = (bf16[2,288,128]{2,1,0:T(8,128)(2,1)}, bf16[2,288,128]{2,1,0:T(8,128)(2,1)S(1)}, u32[]{:S(2)}) copy-start(bf16[2,288,128]{2,1,0:T(8,128)(2,1)S(1)} %collective-permute-done.3.refs_3_) | copy-start | bytes 442372
  43.0 1.7 %collective-permute-start.7 = (bf16[2,288,128]{2,1,0:T(8,128)(2,1)S(1)}, bf16[2,288,128]{2,1,0:T(8,128)(2,1)S(1)}, u32[]{:S(2)}, u32[]{:S(2)}) collective-permute-start(bf16[2,288,128]{2,1,0:T(8,128)(2,1)S(1)} %collective-permute-done.3.refs_3_), channel_id=1, source_target_pairs={{0,1},{1,0},{2,3},{3,2},{4,5},{5,4},{6,7},{7,6},{8,9},{9,8},{10,11... | collective-permute-start | bytes 442376 | tf_op jit(solution)/shard_map/ppermute | solution.py:449
  43.1 40.8 %collective-permute-start.11 = (bf16[2,288,128]{2,1,0:T(8,128)(2,1)}, bf16[2,288,128]{2,1,0:T(8,128)(2,1)S(1)}, u32[]{:S(2)}, u32[]{:S(2)}) collective-permute-start(bf16[2,288,128]{2,1,0:T(8,128)(2,1)} %get-tuple-element.31), channel_id=1, source_target_pairs={{0,14},{1,15},{2,12},{3,13},{4,10},{5,11},{6,8},{7,9},{8,6},{9,7},... | collective-permute-start | bytes 442376 | tf_op jit(solution)/shard_map/ppermute | solution.py:445
  44.7 7.3 %copy-start.14 = (bf16[2,288,128]{2,1,0:T(8,128)(2,1)}, bf16[2,288,128]{2,1,0:T(8,128)(2,1)S(1)}, u32[]{:S(2)}) copy-start(bf16[2,288,128]{2,1,0:T(8,128)(2,1)S(1)} %collective-permute-done.7.refs_8_) | copy-start | bytes 442372
  44.7 39.2 %collective-permute-start.8 = (bf16[2,576,128]{2,1,0:T(8,128)(2,1)}, bf16[2,576,128]{2,1,0:T(8,128)(2,1)S(1)}, u32[]{:S(2)}, u32[]{:S(2)}) collective-permute-start(bf16[2,576,128]{2,1,0:T(8,128)(2,1)} %get-tuple-element.28), channel_id=1, source_target_pairs={{0,2},{1,9},{2,0},{3,11},{4,6},{5,13},{6,4},{7,15},{8,10},{9,1},{1... | collective-permute-start | bytes 884744 | tf_op jit(solution)/shard_map/ppermute | solution.py:445
  46.2 5.8 %copy-start.6 = (bf16[2,576,128]{2,1,0:T(8,128)(2,1)}, bf16[2,576,128]{2,1,0:T(8,128)(2,1)S(1)}, u32[]{:S(2)}) copy-start(bf16[2,576,128]{2,1,0:T(8,128)(2,1)S(1)} %collective-permute-done.4.refs_5_) | copy-start | bytes 884740
  46.2 37.8 %collective-permute-start.9 = (bf16[2,576,128]{2,1,0:T(8,128)(2,1)}, bf16[2,576,128]{2,1,0:T(8,128)(2,1)S(1)}, u32[]{:S(2)}, u32[]{:S(2)}) collective-permute-start(bf16[2,576,128]{2,1,0:T(8,128)(2,1)} %get-tuple-element.29), channel_id=1, source_target_pairs={{0,10},{1,5},{2,8},{3,7},{4,14},{5,1},{6,12},{7,3},{8,2},{9,13},{1... | collective-permute-start | bytes 884744 | tf_op jit(solution)/shard_map/ppermute | solution.py:445
  52.0 0.7 copy-start.7
  52.0 32.0 %collective-permute-start.10 = (bf16[2,576,128]{2,1,0:T(8,128)(2,1)}, bf16[2,576,128]{2,1,0:T(8,128)(2,1)S(1)}, u32[]{:S(2)}, u32[]{:S(2)}) collective-permute-start(bf16[2,576,128]{2,1,0:T(8,128)(2,1)} %get-tuple-element.30), channel_id=1, source_target_pairs={{0,6},{1,13},{2,4},{3,15},{4,2},{5,9},{6,0},{7,11},{8,14},{9,5},{1... | collective-permute-start | bytes 884744 | tf_op jit(solution)/shard_map/ppermute | solution.py:445
  52.0 0.8 copy-start.8
  84.0 2.8 %copy-start.12 = (bf16[2,288,128]{2,1,0:T(8,128)(2,1)}, bf16[2,288,128]{2,1,0:T(8,128)(2,1)S(1)}, u32[]{:S(2)}) copy-start(bf16[2,288,128]{2,1,0:T(8,128)(2,1)S(1)} %collective-permute-done.11.refs_3_) | copy-start | bytes 442372
  84.0 2.8 %copy-start = (bf16[2,576,128]{2,1,0:T(8,128)(2,1)}, bf16[2,576,128]{2,1,0:T(8,128)(2,1)S(1)}, u32[]{:S(2)}) copy-start(bf16[2,576,128]{2,1,0:T(8,128)(2,1)S(1)} %collective-permute-done.8.refs_0_) | copy-start | bytes 884740
  84.0 2.8 %copy-start.3 = (bf16[2,576,128]{2,1,0:T(8,128)(2,1)}, bf16[2,576,128]{2,1,0:T(8,128)(2,1)S(1)}, u32[]{:S(2)}) copy-start(bf16[2,576,128]{2,1,0:T(8,128)(2,1)S(1)} %collective-permute-done.9.refs_1_) | copy-start | bytes 884740
  84.0 2.8 %copy-start.5 = (bf16[2,576,128]{2,1,0:T(8,128)(2,1)}, bf16[2,576,128]{2,1,0:T(8,128)(2,1)S(1)}, u32[]{:S(2)}) copy-start(bf16[2,576,128]{2,1,0:T(8,128)(2,1)S(1)} %collective-permute-done.10.refs_2_) | copy-start | bytes 884740
  84.0 2.7 %collective-permute-start.12 = (bf16[2,576,128]{2,1,0:T(8,128)(2,1)S(1)}, bf16[2,576,128]{2,1,0:T(8,128)(2,1)S(1)}, u32[]{:S(2)}, u32[]{:S(2)}) collective-permute-start(bf16[2,576,128]{2,1,0:T(8,128)(2,1)S(1)} %collective-permute-done.8.refs_0_), channel_id=1, source_target_pairs={{0,1},{1,0},{2,3},{3,2},{4,5},{5,4},{6,7},{7,6},{8,9},{9,8},{10,11... | collective-permute-start | bytes 884744 | tf_op jit(solution)/shard_map/ppermute | solution.py:449
  84.1 2.6 %collective-permute-start.13 = (bf16[2,576,128]{2,1,0:T(8,128)(2,1)S(1)}, bf16[2,576,128]{2,1,0:T(8,128)(2,1)S(1)}, u32[]{:S(2)}, u32[]{:S(2)}) collective-permute-start(bf16[2,576,128]{2,1,0:T(8,128)(2,1)S(1)} %collective-permute-done.9.refs_1_), channel_id=1, source_target_pairs={{0,1},{1,0},{2,3},{3,2},{4,5},{5,4},{6,7},{7,6},{8,9},{9,8},{10,11... | collective-permute-start | bytes 884744 | tf_op jit(solution)/shard_map/ppermute | solution.py:449
  84.6 2.2 %collective-permute-start.14 = (bf16[2,576,128]{2,1,0:T(8,128)(2,1)S(1)}, bf16[2,576,128]{2,1,0:T(8,128)(2,1)S(1)}, u32[]{:S(2)}, u32[]{:S(2)}) collective-permute-start(bf16[2,576,128]{2,1,0:T(8,128)(2,1)S(1)} %collective-permute-done.10.refs_2_), channel_id=1, source_target_pairs={{0,1},{1,0},{2,3},{3,2},{4,5},{5,4},{6,7},{7,6},{8,9},{9,8},{10,11... | collective-permute-start | bytes 884744 | tf_op jit(solution)/shard_map/ppermute | solution.py:449
  84.7 2.0 %collective-permute-start.15 = (bf16[2,288,128]{2,1,0:T(8,128)(2,1)S(1)}, bf16[2,288,128]{2,1,0:T(8,128)(2,1)S(1)}, u32[]{:S(2)}, u32[]{:S(2)}) collective-permute-start(bf16[2,288,128]{2,1,0:T(8,128)(2,1)S(1)} %collective-permute-done.11.refs_3_), channel_id=1, source_target_pairs={{0,1},{1,0},{2,3},{3,2},{4,5},{5,4},{6,7},{7,6},{8,9},{9,8},{10,11... | collective-permute-start | bytes 442376 | tf_op jit(solution)/shard_map/ppermute | solution.py:449
  86.7 0.7 copy-start.15
  86.7 0.8 copy-start.9
  86.7 0.9 copy-start.10
  86.8 1.0 %copy-start.11 = (bf16[2,576,128]{2,1,0:T(8,128)(2,1)}, bf16[2,576,128]{2,1,0:T(8,128)(2,1)S(1)}, u32[]{:S(2)}) copy-start(bf16[2,576,128]{2,1,0:T(8,128)(2,1)S(1)} %collective-permute-done.14.refs_7_) | copy-start | bytes 884740

commit v3 on v2

v3 whole, which is shorter than its diff:
```python
import functools

import jax
import jax.numpy as jnp
from jax import lax
from jax.experimental import pallas as pl
from jax.experimental.pallas import tpu as pltpu
from jax.sharding import PartitionSpec as P

KVL = 512
BLOCK = 64
SEL = 32
PAIR = 2 * BLOCK
GROUP = 2 * PAIR
SUB = 512
STEP = 2 * SUB
VMEM = 60 << 20
NEG = -1e30
SCALE = 1.4426950408889634 / 192.0**0.5
NT = (((1,), (1,)), ((), ()))
NN = (((1,), (0,)), ((), ()))


def log2(n):
    shift = n.bit_length() - 1
    assert 1 << shift == n
    return shift


def partners(owners):
    count = (owners - 2) // 2
    low, high = range(1, count + 1), range(count + 1, 2 * count + 1)
    return [(a, b) if i % 2 == 0 else (b, a) for i, (a, b) in enumerate(zip(low, high))]


def pack_kernel(capacity, chunks, ids, cache, *refs):
    dests = ids.shape[0]
    pairs = partners(dests)
    outs = refs[: len(pairs) + 2]
    table, rows, sem = refs[len(pairs) + 2 :]
    lat, tokens = rows.shape
    half = lat // 2
    shift = log2(tokens // BLOCK)
    head = lax.axis_index("head")
    me = lax.axis_index("ctx")
    copy = pltpu.make_async_copy(cache, rows, sem)
    copy.start()

    @pl.loop(0, dests)
    def _(d):
        first = d * (capacity + 1)
        for slot in range(capacity + 1):
            table[first + slot] = 0
        at = first
        for j in range(SEL):
            block = ids[d, j]
            table[at] = block & ((1 << shift) - 1)
            at = at + (block >> shift == me).astype(jnp.int32)
        table[at] = 0

    def block_pair(d, chunk, start, size):
        first = d * (capacity + 1) + 2 * chunk
        a, b = table[first], table[first + 1]
        left = lax.broadcasted_iota(jnp.int32, (size, PAIR), 1) < BLOCK
        xa = rows[pl.ds(start, size), pl.ds(pl.multiple_of((a >> 1) * PAIR, PAIR), PAIR)].astype(jnp.float32)
        xb = rows[pl.ds(start, size), pl.ds(pl.multiple_of((b >> 1) * PAIR, PAIR), PAIR)].astype(jnp.float32)
        xa = pltpu.roll(xa, (a & 1) * BLOCK, 1)
        xb = pltpu.roll(xb, (1 - (b & 1)) * BLOCK, 1)
        return jnp.where(left, xa, xb).astype(jnp.bfloat16)

    copy.wait()
    for c, chunk in enumerate(chunks):
        for j, (a, b) in enumerate(pairs):
            d = me ^ jnp.where(head == 0, a, b)
            outs[j][c] = block_pair(d, chunk, 0, lat)
        shared = pl.multiple_of(head * half, 32)
        outs[-2][c] = block_pair(me ^ (dests - 1), chunk, shared, half)
        outs[-1][c] = block_pair(me, chunk, 0, lat)


def pack(all_ids, cache_t, capacity, phases):
    dests = all_ids.shape[0]
    lat, tokens = cache_t.shape
    chunks = [chunk for phase in phases for chunk in phase]
    sizes = [lat] * len(partners(dests)) + [lat // 2, lat]
    shapes = [(len(phase), size, PAIR) for phase in phases for size in sizes]

    def kernel(ids, cache, *refs):
        scratch = refs[len(shapes) :]
        joined = []
        for j in range(len(sizes)):
            views = [refs[p * len(sizes) + j].at[i] for p, phase in enumerate(phases) for i in range(len(phase))]
            joined.append(Views(views))
        pack_kernel(capacity, chunks, ids, cache, *joined, *scratch)

    packed = pl.pallas_call(
        kernel,
        out_shape=[jax.ShapeDtypeStruct(s, jnp.bfloat16) for s in shapes],
        grid_spec=pltpu.PrefetchScalarGridSpec(
            num_scalar_prefetch=1,
            grid=(1,),
            in_specs=[pl.BlockSpec(memory_space=pl.ANY)],
            out_specs=[pl.BlockSpec(s, lambda i, ids: (0, 0, 0)) for s in shapes],
            scratch_shapes=[
                pltpu.SMEM((dests * (capacity + 1),), jnp.int32),
                pltpu.VMEM((lat, tokens), jnp.bfloat16),
                pltpu.SemaphoreType.DMA,
            ],
        ),
        compiler_params=pltpu.CompilerParams(vmem_limit_bytes=VMEM),
        cost_estimate=pl.CostEstimate(flops=0, bytes_accessed=8 * lat * tokens, transcendentals=0),
        name="pack",
    )(all_ids, cache_t)
    return [list(packed[p * len(sizes) : (p + 1) * len(sizes)]) for p in range(len(phases))]


class Views:
    def __init__(self, refs):
        self.refs = refs

    def __setitem__(self, i, value):
        self.refs[i][...] = value


def pair_bias(bias, at, start_a, start_b):
    lane = lax.broadcasted_iota(jnp.int32, (8, PAIR), 1)
    start = jnp.where(lane < BLOCK, start_a, start_b)
    bias[:, pl.ds(at, PAIR)] = jnp.where(start >= 0, 0.0, NEG).astype(jnp.float32)


def plan_kernel(owners, capacity, shift, phases, ids, table, *rest):
    biases, count = rest[:-1], rest[-1]
    for slot in range(owners * capacity):
        table[slot] = -1
    for o in range(owners):
        count[o] = 0
    for j in range(SEL):
        block = ids[j]
        owner = block >> shift
        rank = count[owner]
        table[owner * capacity + rank] = block * BLOCK
        count[owner] = rank + 1
    for p, (bias, phase) in enumerate(zip(biases, phases)):
        last = p > 0 and p == len(phases) - 1
        if last:
            bias[...] = jnp.full(bias.shape, NEG, bias.dtype)
            live = jnp.int32(0)
        for c, chunk in enumerate(phase):
            for o in range(owners if p == 0 else owners - 1):
                slot = o * capacity + 2 * chunk
                a, b = table[slot], table[slot + 1]
                if last:
                    used = a >= 0
                    table[owners * capacity + c * owners + o] = jnp.where(used, live, -1)
                    pair_bias(bias, pl.multiple_of(live * PAIR, PAIR), a, b)
                    live = live + used.astype(jnp.int32)
                else:
                    pair_bias(bias, (c * (owners if p == 0 else owners - 1) + o) * PAIR, a, b)
            if last:
                table[owners * capacity + c * owners + owners - 1] = -1
        if last:
            table[owners * capacity + len(phase) * owners] = live


def plan(ids, owners, capacity, shift, phases):
    shapes = [(8, len(phase) * (owners if p == 0 else owners - 1) * PAIR) for p, phase in enumerate(phases)]
    if len(phases) > 1:
        shapes[-1] = (8, shapes[-1][1] + PAIR)
    entries = owners * capacity + len(phases[-1]) * owners + 1
    return pl.pallas_call(
        functools.partial(plan_kernel, owners, capacity, shift, phases),
        out_shape=[jax.ShapeDtypeStruct((entries,), jnp.int32)]
        + [jax.ShapeDtypeStruct(s, jnp.float32) for s in shapes],
        grid_spec=pltpu.PrefetchScalarGridSpec(
            num_scalar_prefetch=1,
            grid=(1,),
            in_specs=[],
            out_specs=[pl.BlockSpec(memory_space=pltpu.SMEM)] + [pl.BlockSpec(s, lambda i, ids: (0, 0)) for s in shapes],
            scratch_shapes=[pltpu.SMEM((owners,), jnp.int32)],
        ),
        cost_estimate=pl.CostEstimate(flops=0, bytes_accessed=1 << 20, transcendentals=0),
        name="plan",
    )(ids)


class Arrived:
    def __init__(self, owners, arrays):
        pairs = partners(owners)
        count = len(pairs)
        head, me = lax.axis_index("head"), lax.axis_index("ctx")
        got, shared, own = arrays[:count], arrays[count], arrays[count + 1]
        swapped, shared_other = arrays[count + 2 : 2 * count + 2], arrays[2 * count + 2]
        self.chunks, lat, _ = own.shape
        half = lat // 2
        self.parts = [(me, [(own, 0, lat)])]
        for (a, b), x, y in zip(pairs, got, swapped):
            self.parts.append((me ^ jnp.where(head == 0, a, b), [(x, 0, lat)]))
            self.parts.append((me ^ jnp.where(head == 0, b, a), [(y, 0, lat)]))
        split = [(x, pl.multiple_of(h * half, 32), half) for x, h in ((shared, head), (shared_other, 1 - head))]
        self.parts.append((me ^ (owners - 1), split))

    def place(self, chunk, part, kt, at):
        for x, start, size in self.parts[part][1]:
            kt[pl.ds(start, size), pl.ds(pl.multiple_of(at, PAIR), PAIR)] = x[chunk]


class Half:
    def __init__(self, base, q, kt, bias, scores, weights, tops, sums, keys, diagonal=None):
        self.base, self.q, self.kt, self.bias = base, q, kt, bias
        self.scores, self.weights, self.tops, self.sums = scores, weights, tops, sums
        self.keys, self.diagonal = keys, diagonal
        self.groups = -(-keys // GROUP)

    def score(self, group):
        at = group * GROUP
        end = min(at + GROUP, self.keys)
        part = lax.dot_general(
            self.q[pl.ds(self.base, SUB), :], self.kt[:, at:end], NN, preferred_element_type=jnp.float32
        )
        part = part + self.bias[0:1, at:end]
        columns = [part[:, c : c + PAIR] for c in range(0, end - at, PAIR)]
        if self.diagonal is not None:
            where, key, pos, first = self.diagonal
            if at <= where < end:
                seen = jnp.concatenate(
                    [
                        jnp.broadcast_to(key, (BLOCK, PAIR)) <= pos[first + self.base // BLOCK + s]
                        for s in range(SUB // BLOCK)
                    ],
                    axis=0,
                )
                index = (where - at) // PAIR
                columns[index] = jnp.where(seen, columns[index], NEG)
        high = columns[0]
        for i, column in enumerate(columns):
            self.scores[:, at + i * PAIR : at + (i + 1) * PAIR] = column
            high = jnp.maximum(high, column) if i else high
        self.tops[...] = high if group == 0 else jnp.maximum(self.tops[...], high)

    def settle(self, old=None):
        top = jnp.max(self.tops[...], axis=1, keepdims=True) * SCALE
        top = jnp.broadcast_to(top, (SUB, PAIR))
        self.tops[...] = top if old is None else jnp.maximum(top, old)

    def weigh(self, slab):
        rows = pl.ds(slab * BLOCK, BLOCK)
        top = self.tops[rows, :]
        total = jnp.zeros((BLOCK, PAIR), jnp.float32)
        for at in range(0, self.keys, PAIR):
            part = jnp.exp2(self.scores[rows, at : at + PAIR] * SCALE - top)
            total = total + part
            self.weights[rows, at : at + PAIR] = part.astype(jnp.bfloat16)
        self.sums[rows, :] = total

    def total(self):
        return jnp.broadcast_to(jnp.sum(self.sums[...], axis=1, keepdims=True), (SUB, PAIR))

    def combine(self, column):
        return lax.dot_general(
            self.weights[:, 0 : self.keys],
            self.kt[column : column + GROUP, 0 : self.keys],
            NT,
            preferred_element_type=jnp.float32,
        )


def run_halves(a, b, before, after, combine):
    slabs = SUB // BLOCK
    for g in range(a.groups):
        a.score(g)
    before(a)
    for i in range(max(a.groups, slabs)):
        if i < b.groups:
            b.score(i)
        if i < slabs:
            a.weigh(i)
    before(b)
    after(a)
    for i, column in enumerate(range(0, KVL, GROUP)):
        combine(a, column)
        for s in range(i * slabs // 2, (i + 1) * slabs // 2):
            b.weigh(s)
    after(b)
    for column in range(0, KVL, GROUP):
        combine(b, column)


SCRATCH = 9


def attend_kernel(owners, capacity, kind, levels, table, pos, q, bias, *refs):
    start, end = kind in ("first", "only"), kind in ("last", "only")
    if not start:
        carry, logs, *refs = refs
    outs = refs[len(refs) - SCRATCH - (1 if end else 2) : len(refs) - SCRATCH]
    kt, *work = refs[len(refs) - SCRATCH :]
    arrived = Arrived(owners, refs[: len(refs) - SCRATCH - len(outs)])
    chunks = arrived.chunks
    step = pl.program_id(0)
    index = owners * capacity
    needed = table[index + chunks * owners] if kind == "last" else None

    @pl.when(step == 0)
    def _():
        for c in range(chunks):
            for part, (owner, _) in enumerate(arrived.parts):
                if kind == "last":
                    at = table[index + c * owners + owner]
                    pl.when(at >= 0)(functools.partial(arrived.place, c, part, kt, at * PAIR))
                elif start:
                    arrived.place(c, part, kt, (c * owners + owner) * PAIR)
                else:
                    at = (c * (owners - 1) + owner) * PAIR
                    pl.when(owner < owners - 1)(functools.partial(arrived.place, c, part, kt, at))
        if kind == "last":
            fill = jnp.int32(levels[-1])
            for level in reversed(levels[:-1]):
                fill = jnp.where(needed <= level, level, fill)

            @pl.loop(needed, fill)
            def _(i):
                kt[:, pl.ds(pl.multiple_of(i * PAIR, PAIR), PAIR)] = jnp.zeros((kt.shape[0], PAIR), kt.dtype)

    def attend(keys):
        diagonal = None
        if start:
            key = table[(owners - 1) * capacity] + lax.broadcasted_iota(jnp.int32, (1, PAIR), 1)
            diagonal = ((owners - 1) * PAIR, key, pos, step * (STEP // BLOCK))
        a = Half(0, q, kt, bias, *work[0::2], keys, diagonal)
        b = Half(SUB, q, kt, bias, *work[1::2], keys, diagonal)

        def before(part):
            part.settle(None if start else logs[pl.ds(part.base, SUB), :])

        def after(part):
            rows = pl.ds(part.base, SUB)
            total = part.total()
            if not start:
                kept = jnp.exp2(logs[rows, :] - part.tops[...])
                total = total + kept
            inverse = 1.0 / total
            part.sums[...] = inverse
            if not end:
                outs[1][rows, :] = part.tops[...] + jnp.log2(total)
            if not start:
                part.tops[...] = kept * inverse

        def combine(part, column):
            summed = part.combine(column)
            rows = pl.ds(part.base, SUB)
            for at in range(0, GROUP, PAIR):
                cols = slice(column + at, column + at + PAIR)
                result = summed[:, at : at + PAIR] * part.sums[...]
                if not start:
                    result = result + carry[rows, cols] * part.tops[...]
                outs[0][rows, cols] = result.astype(outs[0].dtype)

        run_halves(a, b, before, after, combine)

    if kind != "last":
        attend(kt.shape[1])
        return
    below = -1
    for level in levels:
        pl.when(jnp.logical_and(needed > below, needed <= level))(functools.partial(attend, level * PAIR))
        below = level


def attend(table, pos, q, bias, state, arrays, owners, capacity, kind, chunks):
    rows, lat = q.shape
    pairs = chunks * (owners if kind in ("first", "only") else owners - 1)
    keys = pairs * PAIR
    levels = [n for n in (4, 5, 6, 8) if n < pairs] + [pairs]
    out_shape = [jax.ShapeDtypeStruct((rows, KVL), jnp.float32), jax.ShapeDtypeStruct((rows, PAIR), jnp.float32)]
    if kind in ("last", "only"):
        out_shape = [jax.ShapeDtypeStruct((rows, KVL), jnp.bfloat16)]

    def whole(x):
        return pl.BlockSpec(x.shape, lambda i, *_: (0,) * x.ndim)

    def row_block(x):
        return pl.BlockSpec((STEP, x.shape[1]), lambda i, *_: (i, 0))

    return pl.pallas_call(
        functools.partial(attend_kernel, owners, capacity, kind, levels),
        out_shape=out_shape,
        grid_spec=pltpu.PrefetchScalarGridSpec(
            num_scalar_prefetch=2,
            grid=(rows // STEP,),
            in_specs=[row_block(q), whole(bias)] + [row_block(x) for x in state] + [whole(x) for x in arrays],
            out_specs=[row_block(x) for x in out_shape],
            scratch_shapes=[
                pltpu.VMEM((lat, keys), jnp.bfloat16),
                *[pltpu.VMEM((SUB, keys), jnp.float32)] * 2,
                *[pltpu.VMEM((SUB, keys), jnp.bfloat16)] * 2,
                *[pltpu.VMEM((SUB, PAIR), jnp.float32)] * 4,
            ],
        ),
        compiler_params=pltpu.CompilerParams(vmem_limit_bytes=VMEM),
        cost_estimate=pl.CostEstimate(
            flops=2 * rows * keys * (lat + KVL), bytes_accessed=rows * (lat + 2 * KVL) * 2, transcendentals=rows * keys
        ),
        name="attend_" + kind,
    )(table, pos, q, bias, *state, *arrays)


def split_phases(chunks):
    if chunks < 3:
        return [[c] for c in range(chunks)]
    return [[0], [1], list(range(2, chunks))]


def local(queries, latent_cache, positions, block_ids):
    owners = lax.axis_size("ctx")
    capacity = max(2, 2 * SEL // owners)
    shift = log2(latent_cache.shape[0] // BLOCK)
    q_rows, heads, lat = queries.shape
    rows = q_rows * heads
    all_ids = lax.all_to_all(
        jnp.broadcast_to(block_ids, (owners, SEL)), "ctx", split_axis=0, concat_axis=0, tiled=True
    )
    phases = split_phases(capacity // 2)
    packed = pack(all_ids, latent_cache.T, capacity, phases[:1])
    if len(phases) > 1:
        packed += pack(all_ids, latent_cache.T, capacity, phases[1:])
    table, *biases = plan(block_ids[0], owners, capacity, shift, phases)
    steps = partners(owners) + [(owners - 1, owners - 1)]

    def send(own):
        got = []
        for x, ks in zip(own, steps):
            moves = [(2 * c + h, 2 * (c ^ k) + h) for c in range(owners) for h, k in enumerate(ks)]
            got.append(lax.ppermute(x, ("ctx", "head"), moves))
        return got

    def swap(got):
        return [lax.ppermute(x, "head", [(0, 1), (1, 0)]) for x in got]

    q = queries.reshape(rows, lat)
    got = [send(own) for own in packed]
    if len(phases) > 1:
        *got[0], packed[1][-1], table = lax.optimization_barrier((*got[0], packed[1][-1], table))
    state = []
    for p, phase in enumerate(phases):
        late = got[p]
        if state:
            *late, logs = lax.optimization_barrier((*late, state[1]))
            state = [state[0], logs]
        arrays = [*late, packed[p][-1], *swap(late)]
        kind = "only" if len(phases) == 1 else "first" if p == 0 else "last" if p == len(phases) - 1 else "middle"
        state = attend(table, positions, q, biases[p], state, arrays, owners, capacity, kind, len(phase))
    return state[0].reshape(q_rows, heads, KVL)


def solution(mesh):
    return jax.shard_map(
        local,
        mesh=mesh,
        in_specs=(
            P(("groups", "ctx"), "head", None),
            P(("groups", "ctx"), None),
            P(("groups", "ctx")),
            P(("groups", "ctx"), None),
        ),
        out_specs=P(("groups", "ctx"), "head", None),
        check_vma=False,
    )
```

time: 103 us -> 106 us (1.029)
  Pallas kernels: 50.7 us -> 60.6 us
  waiting for transfers between devices: 8.56 us -> 2.74 us
  starting transfers between devices: 25.6 us -> 23.7 us
    pallas_call x3 -> x6, Pallas kernels: 50.7 us -> 60.6 us  [the longest x3 49.1 us: attend(): pl.pallas_call(functools.partial(attend_kernel, owners, capacity, kind, l...]
    ppermute x8 -> x12, starting transfers between devices: 10.1 us -> 3.23 us  [swap(): return [lax.ppermute(x, 'head', [(0, 1), (1, 0)]) for x in got]]
    ppermute x8 -> x12, waiting for transfers between devices: 6.83 us -> 1.09 us  [send(): got.append(lax.ppermute(x, ('ctx', 'head'), moves))]
    ppermute x8 -> x12, starting transfers between devices: 15.6 us -> 20.5 us  [send(): got.append(lax.ppermute(x, ('ctx', 'head'), moves))]
    unnamed x32 -> x56, local copies, waits for them, and re-layouts: 1.78 us -> 2.16 us
  transfers between devices with their start and end apart: 16 -> 24, of which waited for: 4 -> 2; matrix products, arithmetic and copies ran while one was open for 0% -> 0% of each run, Pallas kernels for 31% -> 41%
where the time goes in v3:
time: 106 us; the launch traced here: 104 us
  Pallas kernels  60.6 us (57%)
  starting transfers between devices  23.7 us (22%)
  blocking collectives  13.5 us (13%)
  local copies, waits for them, and re-layouts  2.81 us (3%)
  waiting for transfers between devices  2.74 us (3%)
    pallas_call x3, Pallas kernels, attend(): pl.pallas_call(functools.partial(attend_kernel, owners, capacity, kind, l...  49.1 us
    ppermute x12, starting transfers between devices, send(): got.append(lax.ppermute(x, ('ctx', 'head'), moves))  20.5 us
    all_to_all x1, blocking collectives, local(): lax.all_to_all(jnp.broadcast_to(block_ids, (owners, SEL)), 'ctx', split_a...  13.5 us
    pallas_call x2, Pallas kernels, pack(): pl.pallas_call(kernel, out_shape=[jax.ShapeDtypeStruct(s, jnp.bfloat16) f...  9.88 us
    ppermute x12, starting transfers between devices, swap(): return [lax.ppermute(x, 'head', [(0, 1), (1, 0)]) for x in got]  3.23 us
    unnamed x56, local copies, waits for them, and re-layouts  2.16 us
  transfers between devices with their start and end apart: 24, of which 2 were waited for; matrix products, arithmetic and copies ran while one was open for 0% of the time, Pallas kernels for 41%

profile of v3, /device:TPU:0, one launch (start us, length us, event | category | flops | bytes accessed | tf_op | source)
XLA Modules:
  0.0 103.7 jit_solution(4415969479802453958)
XLA Ops:
  0.0 0.7 broadcast_in_dim.2
  0.7 13.5 %all_to_all.8 = s32[8,1,32]{2,1,0:T(1,128)} all-to-all(s32[8,1,32]{2,1,0:T(1,128)S(1)} %broadcast_in_dim.2), channel_id=1, replica_groups=mesh['groups'=2,'ctx'=8,'head'=2] {'ctx'}, dimensions={0} | all-to-all | bytes 2048 | tf_op jit(solution)/shard_map/all_to_all | solution.py:419
  14.1 4.2 %pack.2 = (bf16[1,576,128]{2,1,0:T(8,128)(2,1)}, bf16[1,576,128]{2,1,0:T(8,128)(2,1)}, bf16[1,576,128]{2,1,0:T(8,128)(2,1)}, bf16[1,288,128]{2,1,0:T(8,128)(2,1)}, bf16[1,576,128]{2,1,0:T(8,128)(2,1)}) custom-call(s32[8,32]{1,0:T(8,128)} %bitcast.7, bf16[576,4096]{1,0:T(8,128)(2,1)} %bitcast.5), custom_call_target="tpu_custom_call" | custom-call | bytes 18874368 | tf_op jit(solution)/shard_map/pack/pallas_call | solution.py:96
  18.4 0.6 collective-permute-start
  19.0 1.5 %collective-permute-start.1 = (bf16[1,576,128]{2,1,0:T(8,128)(2,1)}, bf16[1,576,128]{2,1,0:T(8,128)(2,1)S(1)}, u32[]{:S(2)}, u32[]{:S(2)}) collective-permute-start(bf16[1,576,128]{2,1,0:T(8,128)(2,1)} %get-tuple-element.45), channel_id=1, source_target_pairs={{0,10},{1,5},{2,8},{3,7},{4,14},{5,1},{6,12},{7,3},{8,2},{9,13},{1... | collective-permute-start | bytes 442376 | tf_op jit(solution)/shard_map/ppermute | solution.py:433
  20.5 0.7 collective-permute-start.2
  21.2 4.0 %collective-permute-start.3 = (bf16[1,288,128]{2,1,0:T(8,128)(2,1)}, bf16[1,288,128]{2,1,0:T(8,128)(2,1)S(1)}, u32[]{:S(2)}, u32[]{:S(2)}) collective-permute-start(bf16[1,288,128]{2,1,0:T(8,128)(2,1)} %get-tuple-element.47), channel_id=1, source_target_pairs={{0,14},{1,15},{2,12},{3,13},{4,10},{5,11},{6,8},{7,9},{8,6},{9,7},... | collective-permute-start | bytes 221192 | tf_op jit(solution)/shard_map/ppermute | solution.py:433
  25.2 1.6 %plan.1 = (s32[81]{0:T(128)}, f32[8,1024]{1,0:T(8,128)}, f32[8,896]{1,0:T(8,128)}, f32[8,1920]{1,0:T(8,128)}) custom-call(s32[32]{0:T(128)} %bitcast.10), custom_call_target="tpu_custom_call" | custom-call | bytes 1048576 | tf_op jit(solution)/shard_map/plan/pallas_call | solution.py:170
  26.8 5.6 %pack.3 = (bf16[1,576,128]{2,1,0:T(8,128)(2,1)}, bf16[1,576,128]{2,1,0:T(8,128)(2,1)}, bf16[1,576,128]{2,1,0:T(8,128)(2,1)}, bf16[1,288,128]{2,1,0:T(8,128)(2,1)...) custom-call(s32[8,32]{1,0:T(8,128)} %bitcast.8, ...), custom_call_target="tpu_custom_call" | custom-call | bytes 18874368 | tf_op jit(solution)/shard_map/pack/pallas_call | solution.py:96
  32.4 0.0 collective-permute-done.3.refs_3_
  32.4 0.0 copy-start.25
  32.4 0.0 collective-permute-done.refs_0_
  32.5 0.0 collective-permute-done.1.refs_1_
  32.5 0.0 collective-permute-done.2.refs_2_
  32.5 0.0 copy-start.15
  32.5 0.1 collective-permute-start.4
  32.6 0.5 collective-permute-start.5
  33.1 0.1 collective-permute-start.6
  33.2 0.4 collective-permute-start.7
  33.6 1.5 %collective-permute-start.11 = (bf16[1,288,128]{2,1,0:T(8,128)(2,1)}, bf16[1,288,128]{2,1,0:T(8,128)(2,1)S(1)}, u32[]{:S(2)}, u32[]{:S(2)}) collective-permute-start(bf16[1,288,128]{2,1,0:T(8,128)(2,1)} %get-tuple-element.63), channel_id=1, source_target_pairs={{0,14},{1,15},{2,12},{3,13},{4,10},{5,11},{6,8},{7,9},{8,6},{9,7},... | collective-permute-start | bytes 221192 | tf_op jit(solution)/shard_map/ppermute | solution.py:433
  35.1 0.0 collective-permute-done.7.refs_8_
  35.1 0.7 collective-permute-start.8
  35.8 0.0 collective-permute-done.4.refs_5_
  35.8 3.1 %collective-permute-start.9 = (bf16[1,576,128]{2,1,0:T(8,128)(2,1)}, bf16[1,576,128]{2,1,0:T(8,128)(2,1)S(1)}, u32[]{:S(2)}, u32[]{:S(2)}) collective-permute-start(bf16[1,576,128]{2,1,0:T(8,128)(2,1)} %get-tuple-element.61), channel_id=1, source_target_pairs={{0,10},{1,5},{2,8},{3,7},{4,14},{5,1},{6,12},{7,3},{8,2},{9,13},{1... | collective-permute-start | bytes 442376 | tf_op jit(solution)/shard_map/ppermute | solution.py:433
  38.9 0.0 collective-permute-done.5.refs_6_
  38.9 1.5 %collective-permute-start.10 = (bf16[1,576,128]{2,1,0:T(8,128)(2,1)}, bf16[1,576,128]{2,1,0:T(8,128)(2,1)S(1)}, u32[]{:S(2)}, u32[]{:S(2)}) collective-permute-start(bf16[1,576,128]{2,1,0:T(8,128)(2,1)} %get-tuple-element.62), channel_id=1, source_target_pairs={{0,6},{1,13},{2,4},{3,15},{4,2},{5,9},{6,0},{7,11},{8,14},{9,5},{1... | collective-permute-start | bytes 442376 | tf_op jit(solution)/shard_map/ppermute | solution.py:433
  40.4 0.0 collective-permute-done.6.refs_7_
  40.4 0.6 copy-done.22
  41.0 17.5 %attend_first.1 = (f32[4096,512]{1,0:T(8,128)}, f32[4096,128]{1,0:T(8,128)}) custom-call(s32[81]{0:T(128)} %get-tuple-element.50.table, s32[64]{0:T(128)} %pos.5, bf16[4096,576]{1,0:T(8,128)(2,1)} %bitcast.11, f32[8,1024]{1,0:T(8,128)} %get-tuple-element.53.bias, bf16[1,576,128]{2,1,0:T(8,128)(2,1)} %copy-done.11, bf16[1,576,128]{2,1,0:T(8,128)(2,1)} %copy-done.13, ...), custom_call_target="tpu_custom_call" | custom-call | flops 9126805504 | bytes 13107200 | tf_op jit(solution)/shard_map/attend_first/pallas_call | solution.py:384
  58.5 0.0 collective-permute-done.11.refs_5_
  58.6 0.0 collective-permute-done.8.refs_2_
  58.6 0.0 collective-permute-done.9.refs_3_
  58.6 0.0 collective-permute-done.10.refs_4_
  58.6 0.1 collective-permute-start.12
  58.7 0.5 collective-permute-start.13
  59.2 0.1 collective-permute-start.14
  59.3 0.4 collective-permute-start.15
  59.7 1.5 %collective-permute-start.19 = (bf16[2,288,128]{2,1,0:T(8,128)(2,1)S(1)}, bf16[2,288,128]{2,1,0:T(8,128)(2,1)S(1)}, u32[]{:S(2)}, u32[]{:S(2)}) collective-permute-start(bf16[2,288,128]{2,1,0:T(8,128)(2,1)S(1)} %copy-done.9), channel_id=1, source_target_pairs={{0,14},{1,15},{2,12},{3,13},{4,10},{5,11},{6,8},{7,9},{8,6},{9,7},... | collective-permute-start | bytes 442376 | tf_op jit(solution)/shard_map/ppermute | solution.py:433
  61.2 0.0 collective-permute-done.15.refs_10_
  61.2 0.7 collective-permute-start.16
  62.0 0.0 collective-permute-done.12.refs_7_
  62.0 2.2 %collective-permute-start.17 = (bf16[2,576,128]{2,1,0:T(8,128)(2,1)S(1)}, bf16[2,576,128]{2,1,0:T(8,128)(2,1)S(1)}, u32[]{:S(2)}, u32[]{:S(2)}) collective-permute-start(bf16[2,576,128]{2,1,0:T(8,128)(2,1)S(1)} %copy-done.1), channel_id=1, source_target_pairs={{0,10},{1,5},{2,8},{3,7},{4,14},{5,1},{6,12},{7,3},{8,2},{9,13},{1... | collective-permute-start | bytes 884744 | tf_op jit(solution)/shard_map/ppermute | solution.py:433
  64.2 0.0 collective-permute-done.13.refs_8_
  64.2 2.5 %collective-permute-start.18 = (bf16[2,576,128]{2,1,0:T(8,128)(2,1)S(1)}, bf16[2,576,128]{2,1,0:T(8,128)(2,1)S(1)}, u32[]{:S(2)}, u32[]{:S(2)}) collective-permute-start(bf16[2,576,128]{2,1,0:T(8,128)(2,1)S(1)} %copy-done), channel_id=1, source_target_pairs={{0,6},{1,13},{2,4},{3,15},{4,2},{5,9},{6,0},{7,11},{8,14},{9,5},{1... | collective-permute-start | bytes 884744 | tf_op jit(solution)/shard_map/ppermute | solution.py:433
  66.7 0.0 collective-permute-done.14.refs_9_
  66.7 0.6 copy-done.21
  67.3 17.8 %attend_middle.1 = (f32[4096,512]{1,0:T(8,128)}, f32[4096,128]{1,0:T(8,128)}) custom-call(s32[81]{0:T(128)} %get-tuple-element.50.table, s32[64]{0:T(128)} %pos.5, bf16[4096,576]{1,0:T(8,128)(2,1)} %bitcast.12, f32[8,896]{1,0:T(8,128)} %get-tuple-element.52.bias, f32[4096,512]{1,0:T(8,128)} %get-tuple-element.59.refs_0_, ...), custom_call_target="tpu_custom_call" | custom-call | flops 7985954816 | bytes 13107200 | tf_op jit(solution)/shard_map/attend_middle/pallas_call | solution.py:384
  85.2 0.0 collective-permute-done.19.refs_5_
  85.2 0.0 collective-permute-done.16.refs_2_
  85.2 1.1 %collective-permute-done.17.refs_3_ = bf16[2,576,128]{2,1,0:T(8,128)(2,1)S(1)} collective-permute-done((bf16[2,576,128]{2,1,0:T(8,128)(2,1)S(1)}, bf16[2,576,128]{2,1,0:T(8,128)(2,1)S(1)}, u32[]{:S(2)}, u32[]{:S(2)}) %collective-permute-start.17) | collective-permute-done | bytes 294944 | tf_op jit(solution)/shard_map/ppermute | solution.py:433
  86.3 0.0 collective-permute-done.18.refs_4_
  86.3 0.1 collective-permute-start.20
  86.3 0.5 collective-permute-start.21
  86.8 0.1 collective-permute-start.22
  86.9 0.4 collective-permute-start.23
  87.3 1.6 %collective-permute-done.23.refs_10_ = bf16[2,288,128]{2,1,0:T(8,128)(2,1)S(1)} collective-permute-done((bf16[2,288,128]{2,1,0:T(8,128)(2,1)S(1)}, bf16[2,288,128]{2,1,0:T(8,128)(2,1)S(1)}, u32[]{:S(2)}, u32[]{:S(2)}) %collective-permute-start.23) | collective-permute-done | bytes 147488 | tf_op jit(solution)/shard_map/ppermute | solution.py:437
  89.0 0.0 collective-permute-done.20.refs_7_
  89.0 0.0 collective-permute-done.21.refs_8_
  89.0 0.0 collective-permute-done.22.refs_9_
  89.0 0.6 copy-done.23
  89.6 0.1 copy-done.6
  89.7 0.1 copy-done.7
  89.8 0.1 copy-done.8
  89.9 13.8 %attend_last.1 = bf16[4096,512]{1,0:T(8,128)(2,1)} custom-call(s32[81]{0:T(128)} %get-tuple-element.50.table, s32[64]{0:T(128)} %pos.5, bf16[4096,576]{1,0:T(8,128)(2,1)} %bitcast.13, f32[8,1920]{1,0:T(8,128)} %get-tuple-element.51.bias, f32[4096,512]{1,0:T(8,128)} %get-tuple-element.71.refs_0_, f32[4096,128]{1,0:T(8,128)} %get-tuple-element.77.refs_1_, ...), custom_call_target="tpu_custom_call" | custom-call | flops 15971909632 | bytes 13107200 | tf_op jit(solution)/shard_map/attend_last/pallas_call | solution.py:384
  (48 shorter events, 0.1 us)
Async XLA Ops:
  18.4 14.1 %collective-permute-start = (bf16[1,576,128]{2,1,0:T(8,128)(2,1)}, bf16[1,576,128]{2,1,0:T(8,128)(2,1)S(1)}, u32[]{:S(2)}, u32[]{:S(2)}) collective-permute-start(bf16[1,576,128]{2,1,0:T(8,128)(2,1)} %get-tuple-element.44), channel_id=1, source_target_pairs={{0,2},{1,9},{2,0},{3,11},{4,6},{5,13},{6,4},{7,15},{8,10},{9,1},{1... | collective-permute-start | bytes 442376 | tf_op jit(solution)/shard_map/ppermute | solution.py:433
  19.0 13.5 %collective-permute-start.1 = (bf16[1,576,128]{2,1,0:T(8,128)(2,1)}, bf16[1,576,128]{2,1,0:T(8,128)(2,1)S(1)}, u32[]{:S(2)}, u32[]{:S(2)}) collective-permute-start(bf16[1,576,128]{2,1,0:T(8,128)(2,1)} %get-tuple-element.45), channel_id=1, source_target_pairs={{0,10},{1,5},{2,8},{3,7},{4,14},{5,1},{6,12},{7,3},{8,2},{9,13},{1... | collective-permute-start | bytes 442376 | tf_op jit(solution)/shard_map/ppermute | solution.py:433
  20.5 12.0 %collective-permute-start.2 = (bf16[1,576,128]{2,1,0:T(8,128)(2,1)}, bf16[1,576,128]{2,1,0:T(8,128)(2,1)S(1)}, u32[]{:S(2)}, u32[]{:S(2)}) collective-permute-start(bf16[1,576,128]{2,1,0:T(8,128)(2,1)} %get-tuple-element.46), channel_id=1, source_target_pairs={{0,6},{1,13},{2,4},{3,15},{4,2},{5,9},{6,0},{7,11},{8,14},{9,5},{1... | collective-permute-start | bytes 442376 | tf_op jit(solution)/shard_map/ppermute | solution.py:433
  21.2 11.2 %collective-permute-start.3 = (bf16[1,288,128]{2,1,0:T(8,128)(2,1)}, bf16[1,288,128]{2,1,0:T(8,128)(2,1)S(1)}, u32[]{:S(2)}, u32[]{:S(2)}) collective-permute-start(bf16[1,288,128]{2,1,0:T(8,128)(2,1)} %get-tuple-element.47), channel_id=1, source_target_pairs={{0,14},{1,15},{2,12},{3,13},{4,10},{5,11},{6,8},{7,9},{8,6},{9,7},... | collective-permute-start | bytes 221192 | tf_op jit(solution)/shard_map/ppermute | solution.py:433
  32.4 7.9 %copy-start.25 = (bf16[1,288,128]{2,1,0:T(8,128)(2,1)}, bf16[1,288,128]{2,1,0:T(8,128)(2,1)S(1)}, u32[]{:S(2)}) copy-start(bf16[1,288,128]{2,1,0:T(8,128)(2,1)S(1)} %collective-permute-done.3.refs_3_) | copy-start | bytes 221188
  32.5 7.9 %copy-start.11 = (bf16[1,576,128]{2,1,0:T(8,128)(2,1)}, bf16[1,576,128]{2,1,0:T(8,128)(2,1)S(1)}, u32[]{:S(2)}) copy-start(bf16[1,576,128]{2,1,0:T(8,128)(2,1)S(1)} %collective-permute-done.refs_0_) | copy-start | bytes 442372
  32.5 7.9 %copy-start.13 = (bf16[1,576,128]{2,1,0:T(8,128)(2,1)}, bf16[1,576,128]{2,1,0:T(8,128)(2,1)S(1)}, u32[]{:S(2)}) copy-start(bf16[1,576,128]{2,1,0:T(8,128)(2,1)S(1)} %collective-permute-done.1.refs_1_) | copy-start | bytes 442372
  32.5 7.9 %copy-start.15 = (bf16[1,576,128]{2,1,0:T(8,128)(2,1)}, bf16[1,576,128]{2,1,0:T(8,128)(2,1)S(1)}, u32[]{:S(2)}) copy-start(bf16[1,576,128]{2,1,0:T(8,128)(2,1)S(1)} %collective-permute-done.2.refs_2_) | copy-start | bytes 442372
  32.5 3.3 %collective-permute-start.4 = (bf16[1,576,128]{2,1,0:T(8,128)(2,1)S(1)}, bf16[1,576,128]{2,1,0:T(8,128)(2,1)S(1)}, u32[]{:S(2)}, u32[]{:S(2)}) collective-permute-start(bf16[1,576,128]{2,1,0:T(8,128)(2,1)S(1)} %collective-permute-done.refs_0_), channel_id=1, source_target_pairs={{0,1},{1,0},{2,3},{3,2},{4,5},{5,4},{6,7},{7,6},{8,9},{9,8},{10,11... | collective-permute-start | bytes 442376 | tf_op jit(solution)/shard_map/ppermute | solution.py:437
  32.6 6.3 %collective-permute-start.5 = (bf16[1,576,128]{2,1,0:T(8,128)(2,1)S(1)}, bf16[1,576,128]{2,1,0:T(8,128)(2,1)S(1)}, u32[]{:S(2)}, u32[]{:S(2)}) collective-permute-start(bf16[1,576,128]{2,1,0:T(8,128)(2,1)S(1)} %collective-permute-done.1.refs_1_), channel_id=1, source_target_pairs={{0,1},{1,0},{2,3},{3,2},{4,5},{5,4},{6,7},{7,6},{8,9},{9,8},{10,11... | collective-permute-start | bytes 442376 | tf_op jit(solution)/shard_map/ppermute | solution.py:437
  33.1 7.3 %collective-permute-start.6 = (bf16[1,576,128]{2,1,0:T(8,128)(2,1)S(1)}, bf16[1,576,128]{2,1,0:T(8,128)(2,1)S(1)}, u32[]{:S(2)}, u32[]{:S(2)}) collective-permute-start(bf16[1,576,128]{2,1,0:T(8,128)(2,1)S(1)} %collective-permute-done.2.refs_2_), channel_id=1, source_target_pairs={{0,1},{1,0},{2,3},{3,2},{4,5},{5,4},{6,7},{7,6},{8,9},{9,8},{10,11... | collective-permute-start | bytes 442376 | tf_op jit(solution)/shard_map/ppermute | solution.py:437
  33.2 2.0 %collective-permute-start.7 = (bf16[1,288,128]{2,1,0:T(8,128)(2,1)S(1)}, bf16[1,288,128]{2,1,0:T(8,128)(2,1)S(1)}, u32[]{:S(2)}, u32[]{:S(2)}) collective-permute-start(bf16[1,288,128]{2,1,0:T(8,128)(2,1)S(1)} %collective-permute-done.3.refs_3_), channel_id=1, source_target_pairs={{0,1},{1,0},{2,3},{3,2},{4,5},{5,4},{6,7},{7,6},{8,9},{9,8},{10,11... | collective-permute-start | bytes 221192 | tf_op jit(solution)/shard_map/ppermute | solution.py:437
  33.6 24.9 %collective-permute-start.11 = (bf16[1,288,128]{2,1,0:T(8,128)(2,1)}, bf16[1,288,128]{2,1,0:T(8,128)(2,1)S(1)}, u32[]{:S(2)}, u32[]{:S(2)}) collective-permute-start(bf16[1,288,128]{2,1,0:T(8,128)(2,1)} %get-tuple-element.63), channel_id=1, source_target_pairs={{0,14},{1,15},{2,12},{3,13},{4,10},{5,11},{6,8},{7,9},{8,6},{9,7},... | collective-permute-start | bytes 221192 | tf_op jit(solution)/shard_map/ppermute | solution.py:433
  35.1 5.3 %copy-start.27 = (bf16[1,288,128]{2,1,0:T(8,128)(2,1)}, bf16[1,288,128]{2,1,0:T(8,128)(2,1)S(1)}, u32[]{:S(2)}) copy-start(bf16[1,288,128]{2,1,0:T(8,128)(2,1)S(1)} %collective-permute-done.7.refs_8_) | copy-start | bytes 221188
  35.1 23.4 %collective-permute-start.8 = (bf16[1,576,128]{2,1,0:T(8,128)(2,1)}, bf16[1,576,128]{2,1,0:T(8,128)(2,1)S(1)}, u32[]{:S(2)}, u32[]{:S(2)}) collective-permute-start(bf16[1,576,128]{2,1,0:T(8,128)(2,1)} %get-tuple-element.60), channel_id=1, source_target_pairs={{0,2},{1,9},{2,0},{3,11},{4,6},{5,13},{6,4},{7,15},{8,10},{9,1},{1... | collective-permute-start | bytes 442376 | tf_op jit(solution)/shard_map/ppermute | solution.py:433
  35.8 4.6 %copy-start.18 = (bf16[1,576,128]{2,1,0:T(8,128)(2,1)}, bf16[1,576,128]{2,1,0:T(8,128)(2,1)S(1)}, u32[]{:S(2)}) copy-start(bf16[1,576,128]{2,1,0:T(8,128)(2,1)S(1)} %collective-permute-done.4.refs_5_) | copy-start | bytes 442372
  35.8 22.8 %collective-permute-start.9 = (bf16[1,576,128]{2,1,0:T(8,128)(2,1)}, bf16[1,576,128]{2,1,0:T(8,128)(2,1)S(1)}, u32[]{:S(2)}, u32[]{:S(2)}) collective-permute-start(bf16[1,576,128]{2,1,0:T(8,128)(2,1)} %get-tuple-element.61), channel_id=1, source_target_pairs={{0,10},{1,5},{2,8},{3,7},{4,14},{5,1},{6,12},{7,3},{8,2},{9,13},{1... | collective-permute-start | bytes 442376 | tf_op jit(solution)/shard_map/ppermute | solution.py:433
  38.9 1.5 %copy-start.20 = (bf16[1,576,128]{2,1,0:T(8,128)(2,1)}, bf16[1,576,128]{2,1,0:T(8,128)(2,1)S(1)}, u32[]{:S(2)}) copy-start(bf16[1,576,128]{2,1,0:T(8,128)(2,1)S(1)} %collective-permute-done.5.refs_6_) | copy-start | bytes 442372
  38.9 19.7 %collective-permute-start.10 = (bf16[1,576,128]{2,1,0:T(8,128)(2,1)}, bf16[1,576,128]{2,1,0:T(8,128)(2,1)S(1)}, u32[]{:S(2)}, u32[]{:S(2)}) collective-permute-start(bf16[1,576,128]{2,1,0:T(8,128)(2,1)} %get-tuple-element.62), channel_id=1, source_target_pairs={{0,6},{1,13},{2,4},{3,15},{4,2},{5,9},{6,0},{7,11},{8,14},{9,5},{1... | collective-permute-start | bytes 442376 | tf_op jit(solution)/shard_map/ppermute | solution.py:433
  40.4 0.7 copy-start.22
  41.0 18.7 %copy-start.9 = (bf16[2,288,128]{2,1,0:T(8,128)(2,1)S(1)}, bf16[2,288,128]{2,1,0:T(8,128)(2,1)}, u32[]{:S(2)}) copy-start(bf16[2,288,128]{2,1,0:T(8,128)(2,1)} %get-tuple-element.75) | copy-start | bytes 442372
  41.0 20.2 %copy-start.2 = (bf16[2,576,128]{2,1,0:T(8,128)(2,1)S(1)}, bf16[2,576,128]{2,1,0:T(8,128)(2,1)}, u32[]{:S(2)}) copy-start(bf16[2,576,128]{2,1,0:T(8,128)(2,1)} %get-tuple-element.72) | copy-start | bytes 884740
  41.0 20.9 %copy-start.1 = (bf16[2,576,128]{2,1,0:T(8,128)(2,1)S(1)}, bf16[2,576,128]{2,1,0:T(8,128)(2,1)}, u32[]{:S(2)}) copy-start(bf16[2,576,128]{2,1,0:T(8,128)(2,1)} %get-tuple-element.73) | copy-start | bytes 884740
  41.0 23.2 %copy-start = (bf16[2,576,128]{2,1,0:T(8,128)(2,1)S(1)}, bf16[2,576,128]{2,1,0:T(8,128)(2,1)}, u32[]{:S(2)}) copy-start(bf16[2,576,128]{2,1,0:T(8,128)(2,1)} %get-tuple-element.74) | copy-start | bytes 884740
  58.5 8.1 %copy-start.24 = (bf16[1,288,128]{2,1,0:T(8,128)(2,1)}, bf16[1,288,128]{2,1,0:T(8,128)(2,1)S(1)}, u32[]{:S(2)}) copy-start(bf16[1,288,128]{2,1,0:T(8,128)(2,1)S(1)} %collective-permute-done.11.refs_5_) | copy-start | bytes 221188
  58.6 8.1 %copy-start.10 = (bf16[1,576,128]{2,1,0:T(8,128)(2,1)}, bf16[1,576,128]{2,1,0:T(8,128)(2,1)S(1)}, u32[]{:S(2)}) copy-start(bf16[1,576,128]{2,1,0:T(8,128)(2,1)S(1)} %collective-permute-done.8.refs_2_) | copy-start | bytes 442372
  58.6 8.1 %copy-start.12 = (bf16[1,576,128]{2,1,0:T(8,128)(2,1)}, bf16[1,576,128]{2,1,0:T(8,128)(2,1)S(1)}, u32[]{:S(2)}) copy-start(bf16[1,576,128]{2,1,0:T(8,128)(2,1)S(1)} %collective-permute-done.9.refs_3_) | copy-start | bytes 442372
  58.6 8.1 %copy-start.16 = (bf16[1,576,128]{2,1,0:T(8,128)(2,1)}, bf16[1,576,128]{2,1,0:T(8,128)(2,1)S(1)}, u32[]{:S(2)}) copy-start(bf16[1,576,128]{2,1,0:T(8,128)(2,1)S(1)} %collective-permute-done.10.refs_4_) | copy-start | bytes 442372
  58.6 3.3 %collective-permute-start.12 = (bf16[1,576,128]{2,1,0:T(8,128)(2,1)S(1)}, bf16[1,576,128]{2,1,0:T(8,128)(2,1)S(1)}, u32[]{:S(2)}, u32[]{:S(2)}) collective-permute-start(bf16[1,576,128]{2,1,0:T(8,128)(2,1)S(1)} %collective-permute-done.8.refs_2_), channel_id=1, source_target_pairs={{0,1},{1,0},{2,3},{3,2},{4,5},{5,4},{6,7},{7,6},{8,9},{9,8},{10,11... | collective-permute-start | bytes 442376 | tf_op jit(solution)/shard_map/ppermute | solution.py:437
  58.7 5.5 %collective-permute-start.13 = (bf16[1,576,128]{2,1,0:T(8,128)(2,1)S(1)}, bf16[1,576,128]{2,1,0:T(8,128)(2,1)S(1)}, u32[]{:S(2)}, u32[]{:S(2)}) collective-permute-start(bf16[1,576,128]{2,1,0:T(8,128)(2,1)S(1)} %collective-permute-done.9.refs_3_), channel_id=1, source_target_pairs={{0,1},{1,0},{2,3},{3,2},{4,5},{5,4},{6,7},{7,6},{8,9},{9,8},{10,11... | collective-permute-start | bytes 442376 | tf_op jit(solution)/shard_map/ppermute | solution.py:437
  59.2 7.5 %collective-permute-start.14 = (bf16[1,576,128]{2,1,0:T(8,128)(2,1)S(1)}, bf16[1,576,128]{2,1,0:T(8,128)(2,1)S(1)}, u32[]{:S(2)}, u32[]{:S(2)}) collective-permute-start(bf16[1,576,128]{2,1,0:T(8,128)(2,1)S(1)} %collective-permute-done.10.refs_4_), channel_id=1, source_target_pairs={{0,1},{1,0},{2,3},{3,2},{4,5},{5,4},{6,7},{7,6},{8,9},{9,8},{10,11... | collective-permute-start | bytes 442376 | tf_op jit(solution)/shard_map/ppermute | solution.py:437
  59.3 2.0 %collective-permute-start.15 = (bf16[1,288,128]{2,1,0:T(8,128)(2,1)S(1)}, bf16[1,288,128]{2,1,0:T(8,128)(2,1)S(1)}, u32[]{:S(2)}, u32[]{:S(2)}) collective-permute-start(bf16[1,288,128]{2,1,0:T(8,128)(2,1)S(1)} %collective-permute-done.11.refs_5_), channel_id=1, source_target_pairs={{0,1},{1,0},{2,3},{3,2},{4,5},{5,4},{6,7},{7,6},{8,9},{9,8},{10,11... | collective-permute-start | bytes 221192 | tf_op jit(solution)/shard_map/ppermute | solution.py:437
  59.7 25.4 %collective-permute-start.19 = (bf16[2,288,128]{2,1,0:T(8,128)(2,1)S(1)}, bf16[2,288,128]{2,1,0:T(8,128)(2,1)S(1)}, u32[]{:S(2)}, u32[]{:S(2)}) collective-permute-start(bf16[2,288,128]{2,1,0:T(8,128)(2,1)S(1)} %copy-done.9), channel_id=1, source_target_pairs={{0,14},{1,15},{2,12},{3,13},{4,10},{5,11},{6,8},{7,9},{8,6},{9,7},... | collective-permute-start | bytes 442376 | tf_op jit(solution)/shard_map/ppermute | solution.py:433
  61.2 5.5 %copy-start.26 = (bf16[1,288,128]{2,1,0:T(8,128)(2,1)}, bf16[1,288,128]{2,1,0:T(8,128)(2,1)S(1)}, u32[]{:S(2)}) copy-start(bf16[1,288,128]{2,1,0:T(8,128)(2,1)S(1)} %collective-permute-done.15.refs_10_) | copy-start | bytes 221188
  61.2 23.9 %collective-permute-start.16 = (bf16[2,576,128]{2,1,0:T(8,128)(2,1)S(1)}, bf16[2,576,128]{2,1,0:T(8,128)(2,1)S(1)}, u32[]{:S(2)}, u32[]{:S(2)}) collective-permute-start(bf16[2,576,128]{2,1,0:T(8,128)(2,1)S(1)} %copy-done.2), channel_id=1, source_target_pairs={{0,2},{1,9},{2,0},{3,11},{4,6},{5,13},{6,4},{7,15},{8,10},{9,1},{1... | collective-permute-start | bytes 884744 | tf_op jit(solution)/shard_map/ppermute | solution.py:433
  62.0 4.8 %copy-start.17 = (bf16[1,576,128]{2,1,0:T(8,128)(2,1)}, bf16[1,576,128]{2,1,0:T(8,128)(2,1)S(1)}, u32[]{:S(2)}) copy-start(bf16[1,576,128]{2,1,0:T(8,128)(2,1)S(1)} %collective-permute-done.12.refs_7_) | copy-start | bytes 442372
  62.0 24.3 %collective-permute-start.17 = (bf16[2,576,128]{2,1,0:T(8,128)(2,1)S(1)}, bf16[2,576,128]{2,1,0:T(8,128)(2,1)S(1)}, u32[]{:S(2)}, u32[]{:S(2)}) collective-permute-start(bf16[2,576,128]{2,1,0:T(8,128)(2,1)S(1)} %copy-done.1), channel_id=1, source_target_pairs={{0,10},{1,5},{2,8},{3,7},{4,14},{5,1},{6,12},{7,3},{8,2},{9,13},{1... | collective-permute-start | bytes 884744 | tf_op jit(solution)/shard_map/ppermute | solution.py:433
  64.2 2.5 %copy-start.19 = (bf16[1,576,128]{2,1,0:T(8,128)(2,1)}, bf16[1,576,128]{2,1,0:T(8,128)(2,1)S(1)}, u32[]{:S(2)}) copy-start(bf16[1,576,128]{2,1,0:T(8,128)(2,1)S(1)} %collective-permute-done.13.refs_8_) | copy-start | bytes 442372
  64.2 22.0 %collective-permute-start.18 = (bf16[2,576,128]{2,1,0:T(8,128)(2,1)S(1)}, bf16[2,576,128]{2,1,0:T(8,128)(2,1)S(1)}, u32[]{:S(2)}, u32[]{:S(2)}) collective-permute-start(bf16[2,576,128]{2,1,0:T(8,128)(2,1)S(1)} %copy-done), channel_id=1, source_target_pairs={{0,6},{1,13},{2,4},{3,15},{4,2},{5,9},{6,0},{7,11},{8,14},{9,5},{1... | collective-permute-start | bytes 884744 | tf_op jit(solution)/shard_map/ppermute | solution.py:433
  66.7 0.7 copy-start.21
  85.2 3.8 %copy-start.14 = (bf16[2,288,128]{2,1,0:T(8,128)(2,1)}, bf16[2,288,128]{2,1,0:T(8,128)(2,1)S(1)}, u32[]{:S(2)}) copy-start(bf16[2,288,128]{2,1,0:T(8,128)(2,1)S(1)} %collective-permute-done.19.refs_5_) | copy-start | bytes 442372
  85.2 3.8 %copy-start.3 = (bf16[2,576,128]{2,1,0:T(8,128)(2,1)}, bf16[2,576,128]{2,1,0:T(8,128)(2,1)S(1)}, u32[]{:S(2)}) copy-start(bf16[2,576,128]{2,1,0:T(8,128)(2,1)S(1)} %collective-permute-done.16.refs_2_) | copy-start | bytes 884740
  86.3 2.8 %copy-start.4 = (bf16[2,576,128]{2,1,0:T(8,128)(2,1)}, bf16[2,576,128]{2,1,0:T(8,128)(2,1)S(1)}, u32[]{:S(2)}) copy-start(bf16[2,576,128]{2,1,0:T(8,128)(2,1)S(1)} %collective-permute-done.17.refs_3_) | copy-start | bytes 884740
  86.3 2.8 %copy-start.5 = (bf16[2,576,128]{2,1,0:T(8,128)(2,1)}, bf16[2,576,128]{2,1,0:T(8,128)(2,1)S(1)}, u32[]{:S(2)}) copy-start(bf16[2,576,128]{2,1,0:T(8,128)(2,1)S(1)} %collective-permute-done.18.refs_4_) | copy-start | bytes 884740
  86.3 2.7 %collective-permute-start.20 = (bf16[2,576,128]{2,1,0:T(8,128)(2,1)S(1)}, bf16[2,576,128]{2,1,0:T(8,128)(2,1)S(1)}, u32[]{:S(2)}, u32[]{:S(2)}) collective-permute-start(bf16[2,576,128]{2,1,0:T(8,128)(2,1)S(1)} %collective-permute-done.16.refs_2_), channel_id=1, source_target_pairs={{0,1},{1,0},{2,3},{3,2},{4,5},{5,4},{6,7},{7,6},{8,9},{9,8},{10,11... | collective-permute-start | bytes 884744 | tf_op jit(solution)/shard_map/ppermute | solution.py:437
  86.3 2.6 %collective-permute-start.21 = (bf16[2,576,128]{2,1,0:T(8,128)(2,1)S(1)}, bf16[2,576,128]{2,1,0:T(8,128)(2,1)S(1)}, u32[]{:S(2)}, u32[]{:S(2)}) collective-permute-start(bf16[2,576,128]{2,1,0:T(8,128)(2,1)S(1)} %collective-permute-done.17.refs_3_), channel_id=1, source_target_pairs={{0,1},{1,0},{2,3},{3,2},{4,5},{5,4},{6,7},{7,6},{8,9},{9,8},{10,11... | collective-permute-start | bytes 884744 | tf_op jit(solution)/shard_map/ppermute | solution.py:437
  86.8 2.2 %collective-permute-start.22 = (bf16[2,576,128]{2,1,0:T(8,128)(2,1)S(1)}, bf16[2,576,128]{2,1,0:T(8,128)(2,1)S(1)}, u32[]{:S(2)}, u32[]{:S(2)}) collective-permute-start(bf16[2,576,128]{2,1,0:T(8,128)(2,1)S(1)} %collective-permute-done.18.refs_4_), channel_id=1, source_target_pairs={{0,1},{1,0},{2,3},{3,2},{4,5},{5,4},{6,7},{7,6},{8,9},{9,8},{10,11... | collective-permute-start | bytes 884744 | tf_op jit(solution)/shard_map/ppermute | solution.py:437
  86.9 2.0 %collective-permute-start.23 = (bf16[2,288,128]{2,1,0:T(8,128)(2,1)S(1)}, bf16[2,288,128]{2,1,0:T(8,128)(2,1)S(1)}, u32[]{:S(2)}, u32[]{:S(2)}) collective-permute-start(bf16[2,288,128]{2,1,0:T(8,128)(2,1)S(1)} %collective-permute-done.19.refs_5_), channel_id=1, source_target_pairs={{0,1},{1,0},{2,3},{3,2},{4,5},{5,4},{6,7},{7,6},{8,9},{9,8},{10,11... | collective-permute-start | bytes 442376 | tf_op jit(solution)/shard_map/ppermute | solution.py:437
  89.0 0.7 copy-start.23
  89.0 0.8 copy-start.6
  89.0 0.9 copy-start.7
  89.0 0.9 copy-start.8

commit v4 on v3

--- a/solution.py
+++ b/solution.py
@@ -34,7 +34,7 @@
 
 
 def pack_kernel(capacity, chunks, ids, cache, *refs):
-    dests = ids.shape[0]
+    dests = len(ids)
     pairs = partners(dests)
     outs = refs[: len(pairs) + 2]
     table, rows, sem = refs[len(pairs) + 2 :]
@@ -45,21 +45,18 @@
     me = lax.axis_index("ctx")
     copy = pltpu.make_async_copy(cache, rows, sem)
     copy.start()
-
-    @pl.loop(0, dests)
-    def _(d):
-        first = d * (capacity + 1)
+    for k in range(dests):
+        at = jnp.int32(k * (capacity + 1))
         for slot in range(capacity + 1):
-            table[first + slot] = 0
-        at = first
+            table[k * (capacity + 1) + slot] = 0
         for j in range(SEL):
-            block = ids[d, j]
+            block = ids[k][0, j]
             table[at] = block & ((1 << shift) - 1)
             at = at + (block >> shift == me).astype(jnp.int32)
         table[at] = 0
 
-    def block_pair(d, chunk, start, size):
-        first = d * (capacity + 1) + 2 * chunk
+    def block_pair(k, chunk, start, size):
+        first = k * (capacity + 1) + 2 * chunk
         a, b = table[first], table[first + 1]
         left = lax.broadcasted_iota(jnp.int32, (size, PAIR), 1) < BLOCK
         xa = rows[pl.ds(start, size), pl.ds(pl.multiple_of((a >> 1) * PAIR, PAIR), PAIR)].astype(jnp.float32)
@@ -71,36 +68,28 @@
     copy.wait()
     for c, chunk in enumerate(chunks):
         for j, (a, b) in enumerate(pairs):
-            d = me ^ jnp.where(head == 0, a, b)
-            outs[j][c] = block_pair(d, chunk, 0, lat)
-        shared = pl.multiple_of(head * half, 32)
-        outs[-2][c] = block_pair(me ^ (dests - 1), chunk, shared, half)
-        outs[-1][c] = block_pair(me, chunk, 0, lat)
-
-
-def pack(all_ids, cache_t, capacity, phases):
-    dests = all_ids.shape[0]
+            outs[j][c] = block_pair(jnp.where(head == 0, a, b), chunk, 0, lat)
+        outs[-2][c] = block_pair(dests - 1, chunk, pl.multiple_of(head * half, 32), half)
+        outs[-1][c] = block_pair(0, chunk, 0, lat)
+
+
+def pack(ids, cache_t, capacity, chunks):
+    dests = len(ids)
     lat, tokens = cache_t.shape
-    chunks = [chunk for phase in phases for chunk in phase]
     sizes = [lat] * len(partners(dests)) + [lat // 2, lat]
-    shapes = [(len(phase), size, PAIR) for phase in phases for size in sizes]
-
-    def kernel(ids, cache, *refs):
-        scratch = refs[len(shapes) :]
-        joined = []
-        for j in range(len(sizes)):
-            views = [refs[p * len(sizes) + j].at[i] for p, phase in enumerate(phases) for i in range(len(phase))]
-            joined.append(Views(views))
-        pack_kernel(capacity, chunks, ids, cache, *joined, *scratch)
+    shapes = [(len(chunks), size, PAIR) for size in sizes]
+
+    def kernel(*refs):
+        pack_kernel(capacity, chunks, refs[:dests], *refs[dests:])
 
     packed = pl.pallas_call(
         kernel,
         out_shape=[jax.ShapeDtypeStruct(s, jnp.bfloat16) for s in shapes],
         grid_spec=pltpu.PrefetchScalarGridSpec(
-            num_scalar_prefetch=1,
+            num_scalar_prefetch=dests,
             grid=(1,),
             in_specs=[pl.BlockSpec(memory_space=pl.ANY)],
-            out_specs=[pl.BlockSpec(s, lambda i, ids: (0, 0, 0)) for s in shapes],
+            out_specs=[pl.BlockSpec(s, lambda i, *_: (0, 0, 0)) for s in shapes],
             scratch_shapes=[
                 pltpu.SMEM((dests * (capacity + 1),), jnp.int32),
                 pltpu.VMEM((lat, tokens), jnp.bfloat16),
@@ -110,22 +99,21 @@
         compiler_params=pltpu.CompilerParams(vmem_limit_bytes=VMEM),
         cost_estimate=pl.CostEstimate(flops=0, bytes_accessed=8 * lat * tokens, transcendentals=0),
         name="pack",
-    )(all_ids, cache_t)
-    return [list(packed[p * len(sizes) : (p + 1) * len(sizes)]) for p in range(len(phases))]
-
-
-class Views:
-    def __init__(self, refs):
-        self.refs = refs
-
-    def __setitem__(self, i, value):
-        self.refs[i][...] = value
+    )(*ids, cache_t)
+    return list(packed)
 
 
 def pair_bias(bias, at, start_a, start_b):
     lane = lax.broadcasted_iota(jnp.int32, (8, PAIR), 1)
     start = jnp.where(lane < BLOCK, start_a, start_b)
     bias[:, pl.ds(at, PAIR)] = jnp.where(start >= 0, 0.0, NEG).astype(jnp.float32)
+
+
+def pair_places(owners, phase, first):
+    return {
+        (c, o): i
+        for i, (c, o) in enumerate((c, o) for c in range(phase) for o in range(owners) if o < owners - 1 or first and c == 0)
+    }
 
 
 def plan_kernel(owners, capacity, shift, phases, ids, table, *rest):
@@ -145,25 +133,24 @@
         if last:
             bias[...] = jnp.full(bias.shape, NEG, bias.dtype)
             live = jnp.int32(0)
-        for c, chunk in enumerate(phase):
-            for o in range(owners if p == 0 else owners - 1):
-                slot = o * capacity + 2 * chunk
-                a, b = table[slot], table[slot + 1]
-                if last:
-                    used = a >= 0
-                    table[owners * capacity + c * owners + o] = jnp.where(used, live, -1)
-                    pair_bias(bias, pl.multiple_of(live * PAIR, PAIR), a, b)
-                    live = live + used.astype(jnp.int32)
-                else:
-                    pair_bias(bias, (c * (owners if p == 0 else owners - 1) + o) * PAIR, a, b)
+        for (c, o), i in pair_places(owners, len(phase), p == 0).items():
+            slot = o * capacity + 2 * phase[c]
+            a, b = table[slot], table[slot + 1]
             if last:
+                used = a >= 0
+                table[owners * capacity + c * owners + o] = jnp.where(used, live, -1)
+                pair_bias(bias, pl.multiple_of(live * PAIR, PAIR), a, b)
+                live = live + used.astype(jnp.int32)
+            else:
+                pair_bias(bias, i * PAIR, a, b)
+        if last:
+            for c in range(len(phase)):
                 table[owners * capacity + c * owners + owners - 1] = -1
-        if last:
             table[owners * capacity + len(phase) * owners] = live
 
 
 def plan(ids, owners, capacity, shift, phases):
-    shapes = [(8, len(phase) * (owners if p == 0 else owners - 1) * PAIR) for p, phase in enumerate(phases)]
+    shapes = [(8, len(pair_places(owners, len(phase), p == 0)) * PAIR) for p, phase in enumerate(phases)]
     if len(phases) > 1:
         shapes[-1] = (8, shapes[-1][1] + PAIR)
     entries = owners * capacity + len(phases[-1]) * owners + 1
@@ -307,10 +294,10 @@
                 if kind == "last":
                     at = table[index + c * owners + owner]
                     pl.when(at >= 0)(functools.partial(arrived.place, c, part, kt, at * PAIR))
-                elif start:
-                    arrived.place(c, part, kt, (c * owners + owner) * PAIR)
+                elif start and c == 0:
+                    arrived.place(c, part, kt, owner * PAIR)
                 else:
-                    at = (c * (owners - 1) + owner) * PAIR
+                    at = (c * (owners - 1) + owner + int(start)) * PAIR
                     pl.when(owner < owners - 1)(functools.partial(arrived.place, c, part, kt, at))
         if kind == "last":
             fill = jnp.int32(levels[-1])
@@ -368,7 +355,7 @@
 
 def attend(table, pos, q, bias, state, arrays, owners, capacity, kind, chunks):
     rows, lat = q.shape
-    pairs = chunks * (owners if kind in ("first", "only") else owners - 1)
+    pairs = len(pair_places(owners, chunks, kind in ("first", "only")))
     keys = pairs * PAIR
     levels = [n for n in (4, 5, 6, 8) if n < pairs] + [pairs]
     out_shape = [jax.ShapeDtypeStruct((rows, KVL), jnp.float32), jax.ShapeDtypeStruct((rows, PAIR), jnp.float32)]
@@ -405,9 +392,8 @@
 
 
 def split_phases(chunks):
-    if chunks < 3:
-        return [[c] for c in range(chunks)]
-    return [[0], [1], list(range(2, chunks))]
+    cut = (chunks + 1) // 2
+    return [phase for phase in (list(range(cut)), list(range(cut, chunks))) if phase]
 
 
 def local(queries, latent_cache, positions, block_ids):
@@ -416,13 +402,11 @@
     shift = log2(latent_cache.shape[0] // BLOCK)
     q_rows, heads, lat = queries.shape
     rows = q_rows * heads
-    all_ids = lax.all_to_all(
-        jnp.broadcast_to(block_ids, (owners, SEL)), "ctx", split_axis=0, concat_axis=0, tiled=True
-    )
+    lists = [block_ids] + [
+        lax.ppermute(block_ids, "ctx", [(c, c ^ k) for c in range(owners)]) for k in range(1, owners)
+    ]
     phases = split_phases(capacity // 2)
-    packed = pack(all_ids, latent_cache.T, capacity, phases[:1])
-    if len(phases) > 1:
-        packed += pack(all_ids, latent_cache.T, capacity, phases[1:])
+    packed = [pack(lists, latent_cache.T, capacity, phase) for phase in phases]
     table, *biases = plan(block_ids[0], owners, capacity, shift, phases)
     steps = partners(owners) + [(owners - 1, owners - 1)]
 
@@ -437,9 +421,11 @@
         return [lax.ppermute(x, "head", [(0, 1), (1, 0)]) for x in got]
 
     q = queries.reshape(rows, lat)
-    got = [send(own) for own in packed]
-    if len(phases) > 1:
-        *got[0], packed[1][-1], table = lax.optimization_barrier((*got[0], packed[1][-1], table))
+    got = [send(packed[0])]
+    for own in packed[1:]:
+        both = lax.optimization_barrier((*got[-1], *own[:-1], table))
+        got[-1], own[:-1], table = list(both[: len(got[-1])]), both[len(got[-1]) : -1], both[-1]
+        got.append(send(own))
     state = []
     for p, phase in enumerate(phases):
         late = got[p]

time: 106 us -> 104 us (0.981); the launches traced: 104 us -> 104 us
  blocking collectives: 13.5 us -> 0 us
  waiting for transfers between devices: 2.74 us -> 13.5 us
  starting transfers between devices: 23.7 us -> 30.6 us
  Pallas kernels: 60.6 us -> 57.2 us
    all_to_all x1 -> x0, blocking collectives: 13.5 us -> none  [local(): lax.all_to_all(jnp.broadcast_to(block_ids, (owners, SEL)), 'ctx', split_a...]
    ppermute x0 -> x7, starting transfers between devices: none -> 12.4 us  [local(): lax.ppermute(block_ids, 'ctx', [(c, c ^ k) for c in range(owners)])]
    ppermute x12 -> x8, waiting for transfers between devices: 1.09 us -> 8.55 us  [send(): got.append(lax.ppermute(x, ('ctx', 'head'), moves))]
    ppermute x12 -> x8, starting transfers between devices: 20.5 us -> 16.1 us  [send(): got.append(lax.ppermute(x, ('ctx', 'head'), moves))]
    pallas_call x3 -> x2, Pallas kernels: 49.1 us -> 45.8 us  [attend(): pl.pallas_call(functools.partial(attend_kernel, owners, capacity, kind, l...]
    ppermute x0 -> x7, waiting for transfers between devices: none -> 3.31 us  [local(): lax.ppermute(block_ids, 'ctx', [(c, c ^ k) for c in range(owners)])]
    ppermute x12 -> x8, starting transfers between devices: 3.23 us -> 2.16 us  [swap(): return [lax.ppermute(x, 'head', [(0, 1), (1, 0)]) for x in got]]
    unnamed x56 -> x46, local copies, waits for them, and re-layouts: 2.16 us -> 2.18 us
  transfers between devices with their start and end apart: 24 -> 23, of which waited for: 2 -> 6; matrix products, arithmetic and copies ran while one was open for 0% -> 0% of each run, Pallas kernels for 41% -> 35%
where the time goes in v4:
time: 104 us
  Pallas kernels  57.2 us (55%)
  starting transfers between devices  30.6 us (29%)
  waiting for transfers between devices  13.5 us (13%)
  local copies, waits for them, and re-layouts  2.18 us (2%)
    pallas_call x2, Pallas kernels, attend(): pl.pallas_call(functools.partial(attend_kernel, owners, capacity, kind, l...  45.8 us
    ppermute x8, starting transfers between devices, send(): got.append(lax.ppermute(x, ('ctx', 'head'), moves))  16.1 us
    ppermute x7, starting transfers between devices, local(): lax.ppermute(block_ids, 'ctx', [(c, c ^ k) for c in range(owners)])  12.4 us
    pallas_call x2, Pallas kernels, pack(): pl.pallas_call(kernel, out_shape=[jax.ShapeDtypeStruct(s, jnp.bfloat16) f...  9.82 us
    ppermute x8, waiting for transfers between devices, send(): got.append(lax.ppermute(x, ('ctx', 'head'), moves))  8.55 us
    ppermute x7, waiting for transfers between devices, local(): lax.ppermute(block_ids, 'ctx', [(c, c ^ k) for c in range(owners)])  3.31 us
    unnamed x46, local copies, waits for them, and re-layouts  2.18 us
    ppermute x8, starting transfers between devices, swap(): return [lax.ppermute(x, 'head', [(0, 1), (1, 0)]) for x in got]  2.16 us
  transfers between devices with their start and end apart: 23, of which 6 were waited for; matrix products, arithmetic and copies ran while one was open for 0% of the time, Pallas kernels for 35%

profile of v4, /device:TPU:0, one launch (start us, length us, event | category | flops | bytes accessed | tf_op | source)
XLA Modules:
  0.0 103.8 jit_solution(663054124011861)
XLA Ops:
  0.0 6.0 %collective-permute-start.6 = (s32[1,32]{1,0:T(1,128)}, s32[1,32]{1,0:T(1,128)S(1)}, u32[]{:S(2)}, u32[]{:S(2)}) collective-permute-start(s32[1,32]{1,0:T(1,128)} %refs_0_.3), channel_id=1, source_target_pairs={{0,14},{2,12},{4,10},{6,8},{8,6},{10,4},{12,2},{14,0},{1,15},{3,13... | collective-permute-start | bytes 392 | tf_op jit(solution)/shard_map/ppermute | solution.py:406
  6.0 0.2 collective-permute-start.5
  6.2 0.7 collective-permute-start.4
  7.0 2.0 %collective-permute-start.3 = (s32[1,32]{1,0:T(1,128)}, s32[1,32]{1,0:T(1,128)S(1)}, u32[]{:S(2)}, u32[]{:S(2)}) collective-permute-start(s32[1,32]{1,0:T(1,128)} %refs_0_.3), channel_id=1, source_target_pairs={{0,8},{2,10},{4,12},{6,14},{8,0},{10,2},{12,4},{14,6},{1,9},{3,11}... | collective-permute-start | bytes 392 | tf_op jit(solution)/shard_map/ppermute | solution.py:406
  8.9 2.4 %collective-permute-start.2 = (s32[1,32]{1,0:T(1,128)}, s32[1,32]{1,0:T(1,128)S(1)}, u32[]{:S(2)}, u32[]{:S(2)}) collective-permute-start(s32[1,32]{1,0:T(1,128)} %refs_0_.3), channel_id=1, source_target_pairs={{0,6},{2,4},{4,2},{6,0},{8,14},{10,12},{12,10},{14,8},{1,7},{3,5},... | collective-permute-start | bytes 392 | tf_op jit(solution)/shard_map/ppermute | solution.py:406
  11.3 0.0 collective-permute-done.6.refs_7_
  11.3 0.8 collective-permute-start.1
  12.1 0.0 collective-permute-done.5.refs_6_
  12.1 0.3 collective-permute-start
  12.4 0.0 collective-permute-done.4.refs_5_
  12.4 0.0 collective-permute-done.3.refs_4_
  12.4 0.0 copy-start.3
  12.5 1.1 %collective-permute-done.2.refs_3_ = s32[1,32]{1,0:T(1,128)S(1)} collective-permute-done((s32[1,32]{1,0:T(1,128)}, s32[1,32]{1,0:T(1,128)S(1)}, u32[]{:S(2)}, u32[]{:S(2)}) %collective-permute-start.2) | collective-permute-done | bytes 160 | tf_op jit(solution)/shard_map/ppermute | solution.py:406
  13.5 1.5 %collective-permute-done.1.refs_2_ = s32[1,32]{1,0:T(1,128)S(1)} collective-permute-done((s32[1,32]{1,0:T(1,128)}, s32[1,32]{1,0:T(1,128)S(1)}, u32[]{:S(2)}, u32[]{:S(2)}) %collective-permute-start.1) | collective-permute-done | bytes 160 | tf_op jit(solution)/shard_map/ppermute | solution.py:406
  15.0 0.8 collective-permute-done.refs_1_
  15.8 0.0 copy-done
  15.8 0.0 copy-done.1
  15.8 0.0 copy-done.2
  15.8 0.0 copy-done.3
  15.8 0.5 copy-done.6
  16.3 4.9 %pack.2 = (bf16[2,576,128]{2,1,0:T(8,128)(2,1)}, bf16[2,576,128]{2,1,0:T(8,128)(2,1)}, bf16[2,576,128]{2,1,0:T(8,128)(2,1)}, bf16[2,288,128]{2,1,0:T(8,128)(2,1)}, bf16[2,576,128]{2,1,0:T(8,128)(2,1)}) custom-call(s32[1,32]{1,0:T(1,128)} %refs_0_.3, s32[1,32]{1,0:T(1,128)} %copy-done.6, s32[1,32]{1,0:T(1,128)} %copy-done.5, s32[1,32]{1,0:T(1,128)} %copy-done.4, ...), custom_call_target="tpu_custom_call" | custom-call | bytes 18874368 | tf_op jit(solution)/shard_map/pack/pallas_call | solution.py:85
  21.2 0.4 collective-permute-start.7
  21.6 3.3 %collective-permute-start.8 = (bf16[2,576,128]{2,1,0:T(8,128)(2,1)}, bf16[2,576,128]{2,1,0:T(8,128)(2,1)S(1)}, u32[]{:S(2)}, u32[]{:S(2)}) collective-permute-start(bf16[2,576,128]{2,1,0:T(8,128)(2,1)} %get-tuple-element.35), channel_id=1, source_target_pairs={{0,10},{1,5},{2,8},{3,7},{4,14},{5,1},{6,12},{7,3},{8,2},{9,13},{1... | collective-permute-start | bytes 884744 | tf_op jit(solution)/shard_map/ppermute | solution.py:417
  24.9 1.9 %collective-permute-start.9 = (bf16[2,576,128]{2,1,0:T(8,128)(2,1)}, bf16[2,576,128]{2,1,0:T(8,128)(2,1)S(1)}, u32[]{:S(2)}, u32[]{:S(2)}) collective-permute-start(bf16[2,576,128]{2,1,0:T(8,128)(2,1)} %get-tuple-element.36), channel_id=1, source_target_pairs={{0,6},{1,13},{2,4},{3,15},{4,2},{5,9},{6,0},{7,11},{8,14},{9,5},{1... | collective-permute-start | bytes 884744 | tf_op jit(solution)/shard_map/ppermute | solution.py:417
  26.8 1.2 %collective-permute-start.10 = (bf16[2,288,128]{2,1,0:T(8,128)(2,1)}, bf16[2,288,128]{2,1,0:T(8,128)(2,1)S(1)}, u32[]{:S(2)}, u32[]{:S(2)}) collective-permute-start(bf16[2,288,128]{2,1,0:T(8,128)(2,1)} %get-tuple-element.37), channel_id=1, source_target_pairs={{0,14},{1,15},{2,12},{3,13},{4,10},{5,11},{6,8},{7,9},{8,6},{9,7},... | collective-permute-start | bytes 442376 | tf_op jit(solution)/shard_map/ppermute | solution.py:417
  28.0 1.6 %plan.1 = (s32[81]{0:T(128)}, f32[8,1920]{1,0:T(8,128)}, f32[8,1920]{1,0:T(8,128)}) custom-call(s32[32]{0:T(128)} %bitcast.6), custom_call_target="tpu_custom_call" | custom-call | bytes 1048576 | tf_op jit(solution)/shard_map/plan/pallas_call | solution.py:157
  29.6 4.9 %pack.3 = (bf16[2,576,128]{2,1,0:T(8,128)(2,1)}, bf16[2,576,128]{2,1,0:T(8,128)(2,1)}, bf16[2,576,128]{2,1,0:T(8,128)(2,1)}, bf16[2,288,128]{2,1,0:T(8,128)(2,1)}, bf16[2,576,128]{2,1,0:T(8,128)(2,1)}) custom-call(s32[1,32]{1,0:T(1,128)} %refs_0_.3, s32[1,32]{1,0:T(1,128)} %copy-done.6, s32[1,32]{1,0:T(1,128)} %copy-done.5, s32[1,32]{1,0:T(1,128)} %copy-done.4, ...), custom_call_target="tpu_custom_call" | custom-call | bytes 18874368 | tf_op jit(solution)/shard_map/pack/pallas_call | solution.py:85
  34.5 7.5 %collective-permute-done.10.refs_3_ = bf16[2,288,128]{2,1,0:T(8,128)(2,1)S(1)} collective-permute-done((bf16[2,288,128]{2,1,0:T(8,128)(2,1)}, bf16[2,288,128]{2,1,0:T(8,128)(2,1)S(1)}, u32[]{:S(2)}, u32[]{:S(2)}) %collective-permute-start.10) | collective-permute-done | bytes 147488 | tf_op jit(solution)/shard_map/ppermute | solution.py:417
  42.0 0.0 collective-permute-done.7.refs_0_
  42.0 1.1 %collective-permute-done.8.refs_1_ = bf16[2,576,128]{2,1,0:T(8,128)(2,1)S(1)} collective-permute-done((bf16[2,576,128]{2,1,0:T(8,128)(2,1)}, bf16[2,576,128]{2,1,0:T(8,128)(2,1)S(1)}, u32[]{:S(2)}, u32[]{:S(2)}) %collective-permute-start.8) | collective-permute-done | bytes 294944 | tf_op jit(solution)/shard_map/ppermute | solution.py:417
  43.1 0.0 collective-permute-done.9.refs_2_
  43.1 0.1 collective-permute-start.11
  43.1 0.5 collective-permute-start.12
  43.6 0.1 collective-permute-start.13
  43.7 0.4 collective-permute-start.14
  44.1 4.5 %collective-permute-start.18 = (bf16[2,288,128]{2,1,0:T(8,128)(2,1)}, bf16[2,288,128]{2,1,0:T(8,128)(2,1)S(1)}, u32[]{:S(2)}, u32[]{:S(2)}) collective-permute-start(bf16[2,288,128]{2,1,0:T(8,128)(2,1)} %get-tuple-element.55), channel_id=1, source_target_pairs={{0,14},{1,15},{2,12},{3,13},{4,10},{5,11},{6,8},{7,9},{8,6},{9,7},... | collective-permute-start | bytes 442376 | tf_op jit(solution)/shard_map/ppermute | solution.py:417
  48.6 0.0 collective-permute-done.14.refs_8_
  48.6 0.5 collective-permute-start.15
  49.2 0.0 collective-permute-done.11.refs_5_
  49.2 4.2 %collective-permute-start.16 = (bf16[2,576,128]{2,1,0:T(8,128)(2,1)}, bf16[2,576,128]{2,1,0:T(8,128)(2,1)S(1)}, u32[]{:S(2)}, u32[]{:S(2)}) collective-permute-start(bf16[2,576,128]{2,1,0:T(8,128)(2,1)} %get-tuple-element.53), channel_id=1, source_target_pairs={{0,10},{1,5},{2,8},{3,7},{4,14},{5,1},{6,12},{7,3},{8,2},{9,13},{1... | collective-permute-start | bytes 884744 | tf_op jit(solution)/shard_map/ppermute | solution.py:417
  53.4 0.0 collective-permute-done.12.refs_6_
  53.4 0.0 collective-permute-start.17
  53.4 0.0 collective-permute-done.13.refs_7_
  53.5 0.6 copy-done.14
  54.1 0.1 copy-done.15
  54.2 30.3 %attend_first.1 = (f32[4096,512]{1,0:T(8,128)}, f32[4096,128]{1,0:T(8,128)}) custom-call(s32[81]{0:T(128)} %get-tuple-element.43.table, s32[64]{0:T(128)} %pos.3, bf16[4096,576]{1,0:T(8,128)(2,1)} %bitcast.7, f32[8,1920]{1,0:T(8,128)} %get-tuple-element.45.bias, bf16[2,576,128]{2,1,0:T(8,128)(2,1)} %copy-done.7, bf16[2,576,128]{2,1,0:T(8,128)(2,1)} %copy-done.8, ...), custom_call_target="tpu_custom_call" | custom-call | flops 17112760320 | bytes 13107200 | tf_op jit(solution)/shard_map/attend_first/pallas_call | solution.py:371
  84.5 0.0 collective-permute-done.18.refs_5_
  84.5 0.0 collective-permute-done.15.refs_2_
  84.6 0.0 copy-start.10
  84.6 0.0 collective-permute-done.16.refs_3_
  84.6 0.0 collective-permute-done.17.refs_4_
  84.6 0.4 collective-permute-start.19
  85.0 0.2 collective-permute-start.20
  85.2 0.3 collective-permute-start.21
  85.5 0.2 collective-permute-start.22
  85.7 1.6 %collective-permute-done.22.refs_10_ = bf16[2,288,128]{2,1,0:T(8,128)(2,1)S(1)} collective-permute-done((bf16[2,288,128]{2,1,0:T(8,128)(2,1)S(1)}, bf16[2,288,128]{2,1,0:T(8,128)(2,1)S(1)}, u32[]{:S(2)}, u32[]{:S(2)}) %collective-permute-start.22) | collective-permute-done | bytes 147488 | tf_op jit(solution)/shard_map/ppermute | solution.py:421
  87.3 0.0 collective-permute-done.19.refs_7_
  87.3 0.0 collective-permute-done.20.refs_8_
  87.3 0.0 collective-permute-done.21.refs_9_
  87.4 0.6 copy-done.22
  88.0 0.1 copy-done.16
  88.1 0.1 copy-done.17
  88.2 0.1 copy-done.18
  88.3 15.5 %attend_last.1 = bf16[4096,512]{1,0:T(8,128)(2,1)} custom-call(s32[81]{0:T(128)} %get-tuple-element.43.table, s32[64]{0:T(128)} %pos.3, bf16[4096,576]{1,0:T(8,128)(2,1)} %bitcast.8, f32[8,1920]{1,0:T(8,128)} %get-tuple-element.44.bias, f32[4096,512]{1,0:T(8,128)} %get-tuple-element.51.refs_0_, f32[4096,128]{1,0:T(8,128)} %get-tuple-element.57.refs_1_, ...), custom_call_target="tpu_custom_call" | custom-call | flops 15971909632 | bytes 13107200 | tf_op jit(solution)/shard_map/attend_last/pallas_call | solution.py:371
  (33 shorter events, 0.1 us)
Async XLA Ops:
  0.0 11.3 %collective-permute-start.6 = (s32[1,32]{1,0:T(1,128)}, s32[1,32]{1,0:T(1,128)S(1)}, u32[]{:S(2)}, u32[]{:S(2)}) collective-permute-start(s32[1,32]{1,0:T(1,128)} %refs_0_.3), channel_id=1, source_target_pairs={{0,14},{2,12},{4,10},{6,8},{8,6},{10,4},{12,2},{14,0},{1,15},{3,13... | collective-permute-start | bytes 392 | tf_op jit(solution)/shard_map/ppermute | solution.py:406
  6.0 6.1 %collective-permute-start.5 = (s32[1,32]{1,0:T(1,128)}, s32[1,32]{1,0:T(1,128)S(1)}, u32[]{:S(2)}, u32[]{:S(2)}) collective-permute-start(s32[1,32]{1,0:T(1,128)} %refs_0_.3), channel_id=1, source_target_pairs={{0,12},{2,14},{4,8},{6,10},{8,4},{10,6},{12,0},{14,2},{1,13},{3,15... | collective-permute-start | bytes 392 | tf_op jit(solution)/shard_map/ppermute | solution.py:406
  6.2 6.2 %collective-permute-start.4 = (s32[1,32]{1,0:T(1,128)}, s32[1,32]{1,0:T(1,128)S(1)}, u32[]{:S(2)}, u32[]{:S(2)}) collective-permute-start(s32[1,32]{1,0:T(1,128)} %refs_0_.3), channel_id=1, source_target_pairs={{0,10},{2,8},{4,14},{6,12},{8,2},{10,0},{12,6},{14,4},{1,11},{3,9}... | collective-permute-start | bytes 392 | tf_op jit(solution)/shard_map/ppermute | solution.py:406
  7.0 5.5 %collective-permute-start.3 = (s32[1,32]{1,0:T(1,128)}, s32[1,32]{1,0:T(1,128)S(1)}, u32[]{:S(2)}, u32[]{:S(2)}) collective-permute-start(s32[1,32]{1,0:T(1,128)} %refs_0_.3), channel_id=1, source_target_pairs={{0,8},{2,10},{4,12},{6,14},{8,0},{10,2},{12,4},{14,6},{1,9},{3,11}... | collective-permute-start | bytes 392 | tf_op jit(solution)/shard_map/ppermute | solution.py:406
  8.9 4.6 %collective-permute-start.2 = (s32[1,32]{1,0:T(1,128)}, s32[1,32]{1,0:T(1,128)S(1)}, u32[]{:S(2)}, u32[]{:S(2)}) collective-permute-start(s32[1,32]{1,0:T(1,128)} %refs_0_.3), channel_id=1, source_target_pairs={{0,6},{2,4},{4,2},{6,0},{8,14},{10,12},{12,10},{14,8},{1,7},{3,5},... | collective-permute-start | bytes 392 | tf_op jit(solution)/shard_map/ppermute | solution.py:406
  11.3 4.5 %copy-start = (s32[1,32]{1,0:T(1,128)}, s32[1,32]{1,0:T(1,128)S(1)}, u32[]{:S(2)}) copy-start(s32[1,32]{1,0:T(1,128)S(1)} %collective-permute-done.6.refs_7_) | copy-start | bytes 388
  11.3 3.7 %collective-permute-start.1 = (s32[1,32]{1,0:T(1,128)}, s32[1,32]{1,0:T(1,128)S(1)}, u32[]{:S(2)}, u32[]{:S(2)}) collective-permute-start(s32[1,32]{1,0:T(1,128)} %refs_0_.3), channel_id=1, source_target_pairs={{0,4},{2,6},{4,0},{6,2},{8,12},{10,14},{12,8},{14,10},{1,5},{3,7},... | collective-permute-start | bytes 392 | tf_op jit(solution)/shard_map/ppermute | solution.py:406
  12.1 3.7 %copy-start.1 = (s32[1,32]{1,0:T(1,128)}, s32[1,32]{1,0:T(1,128)S(1)}, u32[]{:S(2)}) copy-start(s32[1,32]{1,0:T(1,128)S(1)} %collective-permute-done.5.refs_6_) | copy-start | bytes 388
  12.1 3.7 %collective-permute-start = (s32[1,32]{1,0:T(1,128)}, s32[1,32]{1,0:T(1,128)S(1)}, u32[]{:S(2)}, u32[]{:S(2)}) collective-permute-start(s32[1,32]{1,0:T(1,128)} %refs_0_.3), channel_id=1, source_target_pairs={{0,2},{2,0},{4,6},{6,4},{8,10},{10,8},{12,14},{14,12},{1,3},{3,1},... | collective-permute-start | bytes 392 | tf_op jit(solution)/shard_map/ppermute | solution.py:406
  12.4 3.3 %copy-start.2 = (s32[1,32]{1,0:T(1,128)}, s32[1,32]{1,0:T(1,128)S(1)}, u32[]{:S(2)}) copy-start(s32[1,32]{1,0:T(1,128)S(1)} %collective-permute-done.4.refs_5_) | copy-start | bytes 388
  12.4 3.3 %copy-start.3 = (s32[1,32]{1,0:T(1,128)}, s32[1,32]{1,0:T(1,128)S(1)}, u32[]{:S(2)}) copy-start(s32[1,32]{1,0:T(1,128)S(1)} %collective-permute-done.3.refs_4_) | copy-start | bytes 388
  13.5 2.3 %copy-start.4 = (s32[1,32]{1,0:T(1,128)}, s32[1,32]{1,0:T(1,128)S(1)}, u32[]{:S(2)}) copy-start(s32[1,32]{1,0:T(1,128)S(1)} %collective-permute-done.2.refs_3_) | copy-start | bytes 388
  15.0 0.8 copy-start.5
  15.8 0.5 copy-start.6
  21.2 20.8 %collective-permute-start.7 = (bf16[2,576,128]{2,1,0:T(8,128)(2,1)}, bf16[2,576,128]{2,1,0:T(8,128)(2,1)S(1)}, u32[]{:S(2)}, u32[]{:S(2)}) collective-permute-start(bf16[2,576,128]{2,1,0:T(8,128)(2,1)} %get-tuple-element.34), channel_id=1, source_target_pairs={{0,2},{1,9},{2,0},{3,11},{4,6},{5,13},{6,4},{7,15},{8,10},{9,1},{1... | collective-permute-start | bytes 884744 | tf_op jit(solution)/shard_map/ppermute | solution.py:417
  21.6 21.4 %collective-permute-start.8 = (bf16[2,576,128]{2,1,0:T(8,128)(2,1)}, bf16[2,576,128]{2,1,0:T(8,128)(2,1)S(1)}, u32[]{:S(2)}, u32[]{:S(2)}) collective-permute-start(bf16[2,576,128]{2,1,0:T(8,128)(2,1)} %get-tuple-element.35), channel_id=1, source_target_pairs={{0,10},{1,5},{2,8},{3,7},{4,14},{5,1},{6,12},{7,3},{8,2},{9,13},{1... | collective-permute-start | bytes 884744 | tf_op jit(solution)/shard_map/ppermute | solution.py:417
  24.9 18.1 %collective-permute-start.9 = (bf16[2,576,128]{2,1,0:T(8,128)(2,1)}, bf16[2,576,128]{2,1,0:T(8,128)(2,1)S(1)}, u32[]{:S(2)}, u32[]{:S(2)}) collective-permute-start(bf16[2,576,128]{2,1,0:T(8,128)(2,1)} %get-tuple-element.36), channel_id=1, source_target_pairs={{0,6},{1,13},{2,4},{3,15},{4,2},{5,9},{6,0},{7,11},{8,14},{9,5},{1... | collective-permute-start | bytes 884744 | tf_op jit(solution)/shard_map/ppermute | solution.py:417
  26.8 15.1 %collective-permute-start.10 = (bf16[2,288,128]{2,1,0:T(8,128)(2,1)}, bf16[2,288,128]{2,1,0:T(8,128)(2,1)S(1)}, u32[]{:S(2)}, u32[]{:S(2)}) collective-permute-start(bf16[2,288,128]{2,1,0:T(8,128)(2,1)} %get-tuple-element.37), channel_id=1, source_target_pairs={{0,14},{1,15},{2,12},{3,13},{4,10},{5,11},{6,8},{7,9},{8,6},{9,7},... | collective-permute-start | bytes 442376 | tf_op jit(solution)/shard_map/ppermute | solution.py:417
  42.0 11.5 %copy-start.20 = (bf16[2,288,128]{2,1,0:T(8,128)(2,1)}, bf16[2,288,128]{2,1,0:T(8,128)(2,1)S(1)}, u32[]{:S(2)}) copy-start(bf16[2,288,128]{2,1,0:T(8,128)(2,1)S(1)} %collective-permute-done.10.refs_3_) | copy-start | bytes 442372
  42.0 11.5 %copy-start.7 = (bf16[2,576,128]{2,1,0:T(8,128)(2,1)}, bf16[2,576,128]{2,1,0:T(8,128)(2,1)S(1)}, u32[]{:S(2)}) copy-start(bf16[2,576,128]{2,1,0:T(8,128)(2,1)S(1)} %collective-permute-done.7.refs_0_) | copy-start | bytes 884740
  43.1 10.4 %copy-start.8 = (bf16[2,576,128]{2,1,0:T(8,128)(2,1)}, bf16[2,576,128]{2,1,0:T(8,128)(2,1)S(1)}, u32[]{:S(2)}) copy-start(bf16[2,576,128]{2,1,0:T(8,128)(2,1)S(1)} %collective-permute-done.8.refs_1_) | copy-start | bytes 884740
  43.1 10.4 %copy-start.9 = (bf16[2,576,128]{2,1,0:T(8,128)(2,1)}, bf16[2,576,128]{2,1,0:T(8,128)(2,1)S(1)}, u32[]{:S(2)}) copy-start(bf16[2,576,128]{2,1,0:T(8,128)(2,1)S(1)} %collective-permute-done.9.refs_2_) | copy-start | bytes 884740
  43.1 6.1 %collective-permute-start.11 = (bf16[2,576,128]{2,1,0:T(8,128)(2,1)S(1)}, bf16[2,576,128]{2,1,0:T(8,128)(2,1)S(1)}, u32[]{:S(2)}, u32[]{:S(2)}) collective-permute-start(bf16[2,576,128]{2,1,0:T(8,128)(2,1)S(1)} %collective-permute-done.7.refs_0_), channel_id=1, source_target_pairs={{0,1},{1,0},{2,3},{3,2},{4,5},{5,4},{6,7},{7,6},{8,9},{9,8},{10,11... | collective-permute-start | bytes 884744 | tf_op jit(solution)/shard_map/ppermute | solution.py:421
  43.1 10.3 %collective-permute-start.12 = (bf16[2,576,128]{2,1,0:T(8,128)(2,1)S(1)}, bf16[2,576,128]{2,1,0:T(8,128)(2,1)S(1)}, u32[]{:S(2)}, u32[]{:S(2)}) collective-permute-start(bf16[2,576,128]{2,1,0:T(8,128)(2,1)S(1)} %collective-permute-done.8.refs_1_), channel_id=1, source_target_pairs={{0,1},{1,0},{2,3},{3,2},{4,5},{5,4},{6,7},{7,6},{8,9},{9,8},{10,11... | collective-permute-start | bytes 884744 | tf_op jit(solution)/shard_map/ppermute | solution.py:421
  43.6 9.8 %collective-permute-start.13 = (bf16[2,576,128]{2,1,0:T(8,128)(2,1)S(1)}, bf16[2,576,128]{2,1,0:T(8,128)(2,1)S(1)}, u32[]{:S(2)}, u32[]{:S(2)}) collective-permute-start(bf16[2,576,128]{2,1,0:T(8,128)(2,1)S(1)} %collective-permute-done.9.refs_2_), channel_id=1, source_target_pairs={{0,1},{1,0},{2,3},{3,2},{4,5},{5,4},{6,7},{7,6},{8,9},{9,8},{10,11... | collective-permute-start | bytes 884744 | tf_op jit(solution)/shard_map/ppermute | solution.py:421
  43.7 4.9 %collective-permute-start.14 = (bf16[2,288,128]{2,1,0:T(8,128)(2,1)S(1)}, bf16[2,288,128]{2,1,0:T(8,128)(2,1)S(1)}, u32[]{:S(2)}, u32[]{:S(2)}) collective-permute-start(bf16[2,288,128]{2,1,0:T(8,128)(2,1)S(1)} %collective-permute-done.10.refs_3_), channel_id=1, source_target_pairs={{0,1},{1,0},{2,3},{3,2},{4,5},{5,4},{6,7},{7,6},{8,9},{9,8},{10,11... | collective-permute-start | bytes 442376 | tf_op jit(solution)/shard_map/ppermute | solution.py:421
  44.1 40.4 %collective-permute-start.18 = (bf16[2,288,128]{2,1,0:T(8,128)(2,1)}, bf16[2,288,128]{2,1,0:T(8,128)(2,1)S(1)}, u32[]{:S(2)}, u32[]{:S(2)}) collective-permute-start(bf16[2,288,128]{2,1,0:T(8,128)(2,1)} %get-tuple-element.55), channel_id=1, source_target_pairs={{0,14},{1,15},{2,12},{3,13},{4,10},{5,11},{6,8},{7,9},{8,6},{9,7},... | collective-permute-start | bytes 442376 | tf_op jit(solution)/shard_map/ppermute | solution.py:417
  48.6 4.8 %copy-start.21 = (bf16[2,288,128]{2,1,0:T(8,128)(2,1)}, bf16[2,288,128]{2,1,0:T(8,128)(2,1)S(1)}, u32[]{:S(2)}) copy-start(bf16[2,288,128]{2,1,0:T(8,128)(2,1)S(1)} %collective-permute-done.14.refs_8_) | copy-start | bytes 442372
  48.6 35.9 %collective-permute-start.15 = (bf16[2,576,128]{2,1,0:T(8,128)(2,1)}, bf16[2,576,128]{2,1,0:T(8,128)(2,1)S(1)}, u32[]{:S(2)}, u32[]{:S(2)}) collective-permute-start(bf16[2,576,128]{2,1,0:T(8,128)(2,1)} %get-tuple-element.52), channel_id=1, source_target_pairs={{0,2},{1,9},{2,0},{3,11},{4,6},{5,13},{6,4},{7,15},{8,10},{9,1},{1... | collective-permute-start | bytes 884744 | tf_op jit(solution)/shard_map/ppermute | solution.py:417
  49.2 4.3 %copy-start.13 = (bf16[2,576,128]{2,1,0:T(8,128)(2,1)}, bf16[2,576,128]{2,1,0:T(8,128)(2,1)S(1)}, u32[]{:S(2)}) copy-start(bf16[2,576,128]{2,1,0:T(8,128)(2,1)S(1)} %collective-permute-done.11.refs_5_) | copy-start | bytes 884740
  49.2 35.4 %collective-permute-start.16 = (bf16[2,576,128]{2,1,0:T(8,128)(2,1)}, bf16[2,576,128]{2,1,0:T(8,128)(2,1)S(1)}, u32[]{:S(2)}, u32[]{:S(2)}) collective-permute-start(bf16[2,576,128]{2,1,0:T(8,128)(2,1)} %get-tuple-element.53), channel_id=1, source_target_pairs={{0,10},{1,5},{2,8},{3,7},{4,14},{5,1},{6,12},{7,3},{8,2},{9,13},{1... | collective-permute-start | bytes 884744 | tf_op jit(solution)/shard_map/ppermute | solution.py:417
  53.4 0.7 copy-start.14
  53.4 31.2 %collective-permute-start.17 = (bf16[2,576,128]{2,1,0:T(8,128)(2,1)}, bf16[2,576,128]{2,1,0:T(8,128)(2,1)S(1)}, u32[]{:S(2)}, u32[]{:S(2)}) collective-permute-start(bf16[2,576,128]{2,1,0:T(8,128)(2,1)} %get-tuple-element.54), channel_id=1, source_target_pairs={{0,6},{1,13},{2,4},{3,15},{4,2},{5,9},{6,0},{7,11},{8,14},{9,5},{1... | collective-permute-start | bytes 884744 | tf_op jit(solution)/shard_map/ppermute | solution.py:417
  53.4 0.8 copy-start.15
  84.5 2.8 %copy-start.19 = (bf16[2,288,128]{2,1,0:T(8,128)(2,1)}, bf16[2,288,128]{2,1,0:T(8,128)(2,1)S(1)}, u32[]{:S(2)}) copy-start(bf16[2,288,128]{2,1,0:T(8,128)(2,1)S(1)} %collective-permute-done.18.refs_5_) | copy-start | bytes 442372
  84.6 2.8 %copy-start.10 = (bf16[2,576,128]{2,1,0:T(8,128)(2,1)}, bf16[2,576,128]{2,1,0:T(8,128)(2,1)S(1)}, u32[]{:S(2)}) copy-start(bf16[2,576,128]{2,1,0:T(8,128)(2,1)S(1)} %collective-permute-done.15.refs_2_) | copy-start | bytes 884740
  84.6 2.8 %copy-start.11 = (bf16[2,576,128]{2,1,0:T(8,128)(2,1)}, bf16[2,576,128]{2,1,0:T(8,128)(2,1)S(1)}, u32[]{:S(2)}) copy-start(bf16[2,576,128]{2,1,0:T(8,128)(2,1)S(1)} %collective-permute-done.16.refs_3_) | copy-start | bytes 884740
  84.6 2.8 %copy-start.12 = (bf16[2,576,128]{2,1,0:T(8,128)(2,1)}, bf16[2,576,128]{2,1,0:T(8,128)(2,1)S(1)}, u32[]{:S(2)}) copy-start(bf16[2,576,128]{2,1,0:T(8,128)(2,1)S(1)} %collective-permute-done.17.refs_4_) | copy-start | bytes 884740
  84.6 2.7 %collective-permute-start.19 = (bf16[2,576,128]{2,1,0:T(8,128)(2,1)S(1)}, bf16[2,576,128]{2,1,0:T(8,128)(2,1)S(1)}, u32[]{:S(2)}, u32[]{:S(2)}) collective-permute-start(bf16[2,576,128]{2,1,0:T(8,128)(2,1)S(1)} %collective-permute-done.15.refs_2_), channel_id=1, source_target_pairs={{0,1},{1,0},{2,3},{3,2},{4,5},{5,4},{6,7},{7,6},{8,9},{9,8},{10,11... | collective-permute-start | bytes 884744 | tf_op jit(solution)/shard_map/ppermute | solution.py:421
  85.0 2.3 %collective-permute-start.20 = (bf16[2,576,128]{2,1,0:T(8,128)(2,1)S(1)}, bf16[2,576,128]{2,1,0:T(8,128)(2,1)S(1)}, u32[]{:S(2)}, u32[]{:S(2)}) collective-permute-start(bf16[2,576,128]{2,1,0:T(8,128)(2,1)S(1)} %collective-permute-done.16.refs_3_), channel_id=1, source_target_pairs={{0,1},{1,0},{2,3},{3,2},{4,5},{5,4},{6,7},{7,6},{8,9},{9,8},{10,11... | collective-permute-start | bytes 884744 | tf_op jit(solution)/shard_map/ppermute | solution.py:421
  85.2 2.2 %collective-permute-start.21 = (bf16[2,576,128]{2,1,0:T(8,128)(2,1)S(1)}, bf16[2,576,128]{2,1,0:T(8,128)(2,1)S(1)}, u32[]{:S(2)}, u32[]{:S(2)}) collective-permute-start(bf16[2,576,128]{2,1,0:T(8,128)(2,1)S(1)} %collective-permute-done.17.refs_4_), channel_id=1, source_target_pairs={{0,1},{1,0},{2,3},{3,2},{4,5},{5,4},{6,7},{7,6},{8,9},{9,8},{10,11... | collective-permute-start | bytes 884744 | tf_op jit(solution)/shard_map/ppermute | solution.py:421
  85.5 1.8 %collective-permute-start.22 = (bf16[2,288,128]{2,1,0:T(8,128)(2,1)S(1)}, bf16[2,288,128]{2,1,0:T(8,128)(2,1)S(1)}, u32[]{:S(2)}, u32[]{:S(2)}) collective-permute-start(bf16[2,288,128]{2,1,0:T(8,128)(2,1)S(1)} %collective-permute-done.18.refs_5_), channel_id=1, source_target_pairs={{0,1},{1,0},{2,3},{3,2},{4,5},{5,4},{6,7},{7,6},{8,9},{9,8},{10,11... | collective-permute-start | bytes 442376 | tf_op jit(solution)/shard_map/ppermute | solution.py:421
  87.3 0.7 copy-start.22
  87.3 0.8 copy-start.16
  87.3 0.9 copy-start.17
  87.3 1.0 copy-start.18

commit v5 on v4

--- a/solution.py
+++ b/solution.py
@@ -12,8 +12,6 @@
 SEL = 32
 PAIR = 2 * BLOCK
 GROUP = 2 * PAIR
-SUB = 512
-STEP = 2 * SUB
 VMEM = 60 << 20
 NEG = -1e30
 SCALE = 1.4426950408889634 / 192.0**0.5
@@ -34,7 +32,7 @@
 
 
 def pack_kernel(capacity, chunks, ids, cache, *refs):
-    dests = len(ids)
+    dests = ids.shape[0]
     pairs = partners(dests)
     outs = refs[: len(pairs) + 2]
     table, rows, sem = refs[len(pairs) + 2 :]
@@ -50,7 +48,7 @@
         for slot in range(capacity + 1):
             table[k * (capacity + 1) + slot] = 0
         for j in range(SEL):
-            block = ids[k][0, j]
+            block = ids[me ^ k, j]
             table[at] = block & ((1 << shift) - 1)
             at = at + (block >> shift == me).astype(jnp.int32)
         table[at] = 0
@@ -74,19 +72,16 @@
 
 
 def pack(ids, cache_t, capacity, chunks):
-    dests = len(ids)
+    dests = ids.shape[0]
     lat, tokens = cache_t.shape
     sizes = [lat] * len(partners(dests)) + [lat // 2, lat]
     shapes = [(len(chunks), size, PAIR) for size in sizes]
 
-    def kernel(*refs):
-        pack_kernel(capacity, chunks, refs[:dests], *refs[dests:])
-
     packed = pl.pallas_call(
-        kernel,
+        functools.partial(pack_kernel, capacity, chunks),
         out_shape=[jax.ShapeDtypeStruct(s, jnp.bfloat16) for s in shapes],
         grid_spec=pltpu.PrefetchScalarGridSpec(
-            num_scalar_prefetch=dests,
+            num_scalar_prefetch=1,
             grid=(1,),
             in_specs=[pl.BlockSpec(memory_space=pl.ANY)],
             out_specs=[pl.BlockSpec(s, lambda i, *_: (0, 0, 0)) for s in shapes],
@@ -99,7 +94,7 @@
         compiler_params=pltpu.CompilerParams(vmem_limit_bytes=VMEM),
         cost_estimate=pl.CostEstimate(flops=0, bytes_accessed=8 * lat * tokens, transcendentals=0),
         name="pack",
-    )(*ids, cache_t)
+    )(ids, cache_t)
     return list(packed)
 
 
@@ -197,12 +192,13 @@
         self.scores, self.weights, self.tops, self.sums = scores, weights, tops, sums
         self.keys, self.diagonal = keys, diagonal
         self.groups = -(-keys // GROUP)
+        self.size = scores.shape[0]
 
     def score(self, group):
         at = group * GROUP
         end = min(at + GROUP, self.keys)
         part = lax.dot_general(
-            self.q[pl.ds(self.base, SUB), :], self.kt[:, at:end], NN, preferred_element_type=jnp.float32
+            self.q[pl.ds(self.base, self.size), :], self.kt[:, at:end], NN, preferred_element_type=jnp.float32
         )
         part = part + self.bias[0:1, at:end]
         columns = [part[:, c : c + PAIR] for c in range(0, end - at, PAIR)]
@@ -212,7 +208,7 @@
                 seen = jnp.concatenate(
                     [
                         jnp.broadcast_to(key, (BLOCK, PAIR)) <= pos[first + self.base // BLOCK + s]
-                        for s in range(SUB // BLOCK)
+                        for s in range(self.size // BLOCK)
                     ],
                     axis=0,
                 )
@@ -226,7 +222,7 @@
 
     def settle(self, old=None):
         top = jnp.max(self.tops[...], axis=1, keepdims=True) * SCALE
-        top = jnp.broadcast_to(top, (SUB, PAIR))
+        top = jnp.broadcast_to(top, (self.size, PAIR))
         self.tops[...] = top if old is None else jnp.maximum(top, old)
 
     def weigh(self, slab):
@@ -240,7 +236,7 @@
         self.sums[rows, :] = total
 
     def total(self):
-        return jnp.broadcast_to(jnp.sum(self.sums[...], axis=1, keepdims=True), (SUB, PAIR))
+        return jnp.broadcast_to(jnp.sum(self.sums[...], axis=1, keepdims=True), (self.size, PAIR))
 
     def combine(self, column):
         return lax.dot_general(
@@ -252,7 +248,7 @@
 
 
 def run_halves(a, b, before, after, combine):
-    slabs = SUB // BLOCK
+    slabs = a.size // BLOCK
     for g in range(a.groups):
         a.score(g)
     before(a)
@@ -284,6 +280,7 @@
     arrived = Arrived(owners, refs[: len(refs) - SCRATCH - len(outs)])
     chunks = arrived.chunks
     step = pl.program_id(0)
+    sub = work[0].shape[0]
     index = owners * capacity
     needed = table[index + chunks * owners] if kind == "last" else None
 
@@ -312,15 +309,15 @@
         diagonal = None
         if start:
             key = table[(owners - 1) * capacity] + lax.broadcasted_iota(jnp.int32, (1, PAIR), 1)
-            diagonal = ((owners - 1) * PAIR, key, pos, step * (STEP // BLOCK))
+            diagonal = ((owners - 1) * PAIR, key, pos, step * (2 * sub // BLOCK))
         a = Half(0, q, kt, bias, *work[0::2], keys, diagonal)
-        b = Half(SUB, q, kt, bias, *work[1::2], keys, diagonal)
+        b = Half(sub, q, kt, bias, *work[1::2], keys, diagonal)
 
         def before(part):
-            part.settle(None if start else logs[pl.ds(part.base, SUB), :])
+            part.settle(None if start else logs[pl.ds(part.base, sub), :])
 
         def after(part):
-            rows = pl.ds(part.base, SUB)
+            rows = pl.ds(part.base, sub)
             total = part.total()
             if not start:
                 kept = jnp.exp2(logs[rows, :] - part.tops[...])
@@ -334,7 +331,7 @@
 
         def combine(part, column):
             summed = part.combine(column)
-            rows = pl.ds(part.base, SUB)
+            rows = pl.ds(part.base, sub)
             for at in range(0, GROUP, PAIR):
                 cols = slice(column + at, column + at + PAIR)
                 result = summed[:, at : at + PAIR] * part.sums[...]
@@ -358,6 +355,8 @@
     pairs = len(pair_places(owners, chunks, kind in ("first", "only")))
     keys = pairs * PAIR
     levels = [n for n in (4, 5, 6, 8) if n < pairs] + [pairs]
+    sub = 1024 if keys <= 2048 and rows % 2048 == 0 else 512
+    step = 2 * sub
     out_shape = [jax.ShapeDtypeStruct((rows, KVL), jnp.float32), jax.ShapeDtypeStruct((rows, PAIR), jnp.float32)]
     if kind in ("last", "only"):
         out_shape = [jax.ShapeDtypeStruct((rows, KVL), jnp.bfloat16)]
@@ -366,21 +365,21 @@
         return pl.BlockSpec(x.shape, lambda i, *_: (0,) * x.ndim)
 
     def row_block(x):
-        return pl.BlockSpec((STEP, x.shape[1]), lambda i, *_: (i, 0))
+        return pl.BlockSpec((step, x.shape[1]), lambda i, *_: (i, 0))
 
     return pl.pallas_call(
         functools.partial(attend_kernel, owners, capacity, kind, levels),
         out_shape=out_shape,
         grid_spec=pltpu.PrefetchScalarGridSpec(
             num_scalar_prefetch=2,
-            grid=(rows // STEP,),
+            grid=(rows // step,),
             in_specs=[row_block(q), whole(bias)] + [row_block(x) for x in state] + [whole(x) for x in arrays],
             out_specs=[row_block(x) for x in out_shape],
             scratch_shapes=[
                 pltpu.VMEM((lat, keys), jnp.bfloat16),
-                *[pltpu.VMEM((SUB, keys), jnp.float32)] * 2,
-                *[pltpu.VMEM((SUB, keys), jnp.bfloat16)] * 2,
-                *[pltpu.VMEM((SUB, PAIR), jnp.float32)] * 4,
+                *[pltpu.VMEM((sub, keys), jnp.float32)] * 2,
+                *[pltpu.VMEM((sub, keys), jnp.bfloat16)] * 2,
+                *[pltpu.VMEM((sub, PAIR), jnp.float32)] * 4,
             ],
         ),
         compiler_params=pltpu.CompilerParams(vmem_limit_bytes=VMEM),
@@ -402,9 +401,9 @@
     shift = log2(latent_cache.shape[0] // BLOCK)
     q_rows, heads, lat = queries.shape
     rows = q_rows * heads
-    lists = [block_ids] + [
-        lax.ppermute(block_ids, "ctx", [(c, c ^ k) for c in range(owners)]) for k in range(1, owners)
-    ]
+    lists = lax.all_to_all(
+        jnp.broadcast_to(block_ids, (owners, SEL)), "ctx", split_axis=0, concat_axis=0, tiled=True
+    )
     phases = split_phases(capacity // 2)
     packed = [pack(lists, latent_cache.T, capacity, phase) for phase in phases]
     table, *biases = plan(block_ids[0], owners, capacity, shift, phases)

time: 104 us -> 116 us (1.12)
  the two profiles are of different devices: /device:TPU:0 before, /device:TPU:11 now
where the time goes in v5:
time: 116 us; the launch traced here: 118 us
  Pallas kernels  73.7 us (64%)
  waiting for transfers between devices  22.3 us (19%)
  blocking collectives  9.57 us (8%)
  starting transfers between devices  9.54 us (8%)
  local copies, waits for them, and re-layouts  2.28 us (2%)
    pallas_call x2, Pallas kernels, attend(): pl.pallas_call(functools.partial(attend_kernel, owners, capacity, kind, l...  62.3 us
    ppermute x8, waiting for transfers between devices, send(): got.append(lax.ppermute(x, ('ctx', 'head'), moves))  19.3 us
    pallas_call x2, Pallas kernels, pack(): pl.pallas_call(functools.partial(pack_kernel, capacity, chunks), out_shap...  9.86 us
    all_to_all x1, blocking collectives, local(): lax.all_to_all(jnp.broadcast_to(block_ids, (owners, SEL)), 'ctx', split_a...  9.57 us
    ppermute x8, starting transfers between devices, send(): got.append(lax.ppermute(x, ('ctx', 'head'), moves))  6.14 us
    ppermute x8, starting transfers between devices, swap(): return [lax.ppermute(x, 'head', [(0, 1), (1, 0)]) for x in got]  3.4 us
    ppermute x8, waiting for transfers between devices, swap(): return [lax.ppermute(x, 'head', [(0, 1), (1, 0)]) for x in got]  2.95 us
  transfers between devices with their start and end apart: 16, of which 3 were waited for; matrix products, arithmetic and copies ran while one was open for 0% of the time, Pallas kernels for 32%

profile of v5, /device:TPU:11, one launch (start us, length us, event | category | flops | bytes accessed | tf_op | source)
XLA Modules:
  0.0 117.8 jit_solution(16859199414342427061)
XLA Ops:
  0.0 0.7 broadcast_in_dim.2
  0.7 9.6 %all_to_all.8 = s32[8,1,32]{2,1,0:T(1,128)} all-to-all(s32[8,1,32]{2,1,0:T(1,128)S(1)} %broadcast_in_dim.2), channel_id=1, replica_groups=mesh['groups'=2,'ctx'=8,'head'=2] {'ctx'}, dimensions={0} | all-to-all | bytes 2048 | tf_op jit(solution)/shard_map/all_to_all | solution.py:404
  10.2 4.9 %pack.2 = (bf16[2,576,128]{2,1,0:T(8,128)(2,1)}, bf16[2,576,128]{2,1,0:T(8,128)(2,1)}, bf16[2,576,128]{2,1,0:T(8,128)(2,1)}, bf16[2,288,128]{2,1,0:T(8,128)(2,1)}, bf16[2,576,128]{2,1,0:T(8,128)(2,1)}) custom-call(s32[8,32]{1,0:T(8,128)} %bitcast.7, bf16[576,4096]{1,0:T(8,128)(2,1)} %bitcast.5), custom_call_target="tpu_custom_call" | custom-call | bytes 18874368 | tf_op jit(solution)/shard_map/pack/pallas_call | solution.py:80
  15.1 0.5 collective-permute-start
  15.7 1.0 collective-permute-start.1
  16.7 1.2 collective-permute-start.2
  17.9 0.4 collective-permute-start.3
  18.3 1.6 %plan.1 = (s32[81]{0:T(128)}, f32[8,1920]{1,0:T(8,128)}, f32[8,1920]{1,0:T(8,128)}) custom-call(s32[32]{0:T(128)} %bitcast.10), custom_call_target="tpu_custom_call" | custom-call | bytes 1048576 | tf_op jit(solution)/shard_map/plan/pallas_call | solution.py:152
  19.9 5.0 %pack.3 = (bf16[2,576,128]{2,1,0:T(8,128)(2,1)}, bf16[2,576,128]{2,1,0:T(8,128)(2,1)}, bf16[2,576,128]{2,1,0:T(8,128)(2,1)}, bf16[2,288,128]{2,1,0:T(8,128)(2,1)}, bf16[2,576,128]{2,1,0:T(8,128)(2,1)}) custom-call(s32[8,32]{1,0:T(8,128)} %bitcast.8, bf16[576,4096]{1,0:T(8,128)(2,1)} %bitcast.6), custom_call_target="tpu_custom_call" | custom-call | bytes 18874368 | tf_op jit(solution)/shard_map/pack/pallas_call | solution.py:80
  24.9 19.3 %collective-permute-done.3.refs_3_ = bf16[2,288,128]{2,1,0:T(8,128)(2,1)S(1)} collective-permute-done((bf16[2,288,128]{2,1,0:T(8,128)(2,1)}, bf16[2,288,128]{2,1,0:T(8,128)(2,1)S(1)}, u32[]{:S(2)}, u32[]{:S(2)}) %collective-permute-start.3) | collective-permute-done | bytes 147488 | tf_op jit(solution)/shard_map/ppermute | solution.py:416
  44.2 0.0 collective-permute-done.refs_0_
  44.2 0.0 collective-permute-done.1.refs_1_
  44.2 0.0 copy-start.1
  44.2 0.0 collective-permute-done.2.refs_2_
  44.2 0.0 copy-start.3
  44.2 0.1 collective-permute-start.4
  44.3 0.5 collective-permute-start.5
  44.8 0.1 collective-permute-start.6
  44.9 0.4 collective-permute-start.7
  45.3 0.4 collective-permute-start.11
  45.6 1.3 %collective-permute-done.7.refs_8_ = bf16[2,288,128]{2,1,0:T(8,128)(2,1)S(1)} collective-permute-done((bf16[2,288,128]{2,1,0:T(8,128)(2,1)S(1)}, bf16[2,288,128]{2,1,0:T(8,128)(2,1)S(1)}, u32[]{:S(2)}, u32[]{:S(2)}) %collective-permute-start.7) | collective-permute-done | bytes 147488 | tf_op jit(solution)/shard_map/ppermute | solution.py:420
  46.9 0.0 collective-permute-start.8
  46.9 0.0 collective-permute-done.4.refs_5_
  46.9 0.0 copy-start.6
  46.9 1.8 %collective-permute-start.9 = (bf16[2,576,128]{2,1,0:T(8,128)(2,1)}, bf16[2,576,128]{2,1,0:T(8,128)(2,1)S(1)}, u32[]{:S(2)}, u32[]{:S(2)}) collective-permute-start(bf16[2,576,128]{2,1,0:T(8,128)(2,1)} %get-tuple-element.53), channel_id=1, source_target_pairs={{0,10},{1,5},{2,8},{3,7},{4,14},{5,1},{6,12},{7,3},{8,2},{9,13},{1... | collective-permute-start | bytes 884744 | tf_op jit(solution)/shard_map/ppermute | solution.py:416
  48.7 0.0 collective-permute-done.5.refs_6_
  48.7 0.9 collective-permute-start.10
  49.6 0.0 collective-permute-done.6.refs_7_
  49.6 0.0 copy-done.13
  49.6 0.0 copy-done
  49.6 0.0 copy-done.1
  49.6 0.0 copy-done.3
  49.6 0.0 copy-done.14
  49.6 0.0 copy-done.6
  49.6 0.0 copy-done.7
  49.6 0.6 copy-done.8
  50.3 31.3 %attend_first.1 = (f32[4096,512]{1,0:T(8,128)}, f32[4096,128]{1,0:T(8,128)}) custom-call(s32[81]{0:T(128)} %get-tuple-element.43.table, s32[64]{0:T(128)} %pos.3, bf16[4096,576]{1,0:T(8,128)(2,1)} %bitcast.11, f32[8,1920]{1,0:T(8,128)} %get-tuple-element.45.bias, bf16[2,576,128]{2,1,0:T(8,128)(2,1)} %copy-done, bf16[2,576,128]{2,1,0:T(8,128)(2,1)} %copy-done.1, ...), custom_call_target="tpu_custom_call" | custom-call | flops 17112760320 | bytes 13107200 | tf_op jit(solution)/shard_map/attend_first/pallas_call | solution.py:370
  81.6 0.0 collective-permute-done.11.refs_5_
  81.6 0.0 copy-start.12
  81.6 0.0 collective-permute-done.8.refs_2_
  81.6 0.0 copy-start.2
  81.6 0.0 collective-permute-done.9.refs_3_
  81.6 0.0 copy-start.4
  81.6 0.0 collective-permute-done.10.refs_4_
  81.6 0.0 copy-start.5
  81.6 1.7 %collective-permute-start.12 = (bf16[2,576,128]{2,1,0:T(8,128)(2,1)S(1)}, bf16[2,576,128]{2,1,0:T(8,128)(2,1)S(1)}, u32[]{:S(2)}, u32[]{:S(2)}) collective-permute-start(bf16[2,576,128]{2,1,0:T(8,128)(2,1)S(1)} %collective-permute-done.8.refs_2_), channel_id=1, source_target_pairs={{0,1},{1,0},{2,3},{3,2},{4,5},{5,4},{6,7},{7,6},{8,9},{9,8},{10,11... | collective-permute-start | bytes 884744 | tf_op jit(solution)/shard_map/ppermute | solution.py:420
  83.4 0.1 collective-permute-start.13
  83.4 0.4 collective-permute-start.14
  83.9 0.1 collective-permute-start.15
  84.0 1.7 %collective-permute-done.15.refs_10_ = bf16[2,288,128]{2,1,0:T(8,128)(2,1)S(1)} collective-permute-done((bf16[2,288,128]{2,1,0:T(8,128)(2,1)S(1)}, bf16[2,288,128]{2,1,0:T(8,128)(2,1)S(1)}, u32[]{:S(2)}, u32[]{:S(2)}) %collective-permute-start.15) | collective-permute-done | bytes 147488 | tf_op jit(solution)/shard_map/ppermute | solution.py:420
  85.6 0.0 collective-permute-done.12.refs_7_
  85.6 0.0 collective-permute-done.13.refs_8_
  85.6 0.0 copy-start.10
  85.7 0.0 collective-permute-done.14.refs_9_
  85.7 0.0 copy-start.11
  85.7 0.0 copy-done.12
  85.7 0.0 copy-done.2
  85.7 0.0 copy-done.4
  85.7 0.0 copy-done.5
  85.7 0.6 copy-done.15
  86.3 0.1 copy-done.9
  86.4 0.1 copy-done.10
  86.5 0.1 copy-done.11
  86.6 31.0 %attend_last.1 = bf16[4096,512]{1,0:T(8,128)(2,1)} custom-call(s32[81]{0:T(128)} %get-tuple-element.43.table, s32[64]{0:T(128)} %pos.3, bf16[4096,576]{1,0:T(8,128)(2,1)} %bitcast.12, f32[8,1920]{1,0:T(8,128)} %get-tuple-element.44.bias, f32[4096,512]{1,0:T(8,128)} %get-tuple-element.51.refs_0_, f32[4096,128]{1,0:T(8,128)} %get-tuple-element.57.refs_1_, ...), custom_call_target="tpu_custom_call" | custom-call | flops 15971909632 | bytes 13107200 | tf_op jit(solution)/shard_map/attend_last/pallas_call | solution.py:370
  (7 shorter events, 0.0 us)
Async XLA Ops:
  15.1 29.0 %collective-permute-start = (bf16[2,576,128]{2,1,0:T(8,128)(2,1)}, bf16[2,576,128]{2,1,0:T(8,128)(2,1)S(1)}, u32[]{:S(2)}, u32[]{:S(2)}) collective-permute-start(bf16[2,576,128]{2,1,0:T(8,128)(2,1)} %get-tuple-element.34), channel_id=1, source_target_pairs={{0,2},{1,9},{2,0},{3,11},{4,6},{5,13},{6,4},{7,15},{8,10},{9,1},{1... | collective-permute-start | bytes 884744 | tf_op jit(solution)/shard_map/ppermute | solution.py:416
  15.7 28.5 %collective-permute-start.1 = (bf16[2,576,128]{2,1,0:T(8,128)(2,1)}, bf16[2,576,128]{2,1,0:T(8,128)(2,1)S(1)}, u32[]{:S(2)}, u32[]{:S(2)}) collective-permute-start(bf16[2,576,128]{2,1,0:T(8,128)(2,1)} %get-tuple-element.35), channel_id=1, source_target_pairs={{0,10},{1,5},{2,8},{3,7},{4,14},{5,1},{6,12},{7,3},{8,2},{9,13},{1... | collective-permute-start | bytes 884744 | tf_op jit(solution)/shard_map/ppermute | solution.py:416
  16.7 27.5 %collective-permute-start.2 = (bf16[2,576,128]{2,1,0:T(8,128)(2,1)}, bf16[2,576,128]{2,1,0:T(8,128)(2,1)S(1)}, u32[]{:S(2)}, u32[]{:S(2)}) collective-permute-start(bf16[2,576,128]{2,1,0:T(8,128)(2,1)} %get-tuple-element.36), channel_id=1, source_target_pairs={{0,6},{1,13},{2,4},{3,15},{4,2},{5,9},{6,0},{7,11},{8,14},{9,5},{1... | collective-permute-start | bytes 884744 | tf_op jit(solution)/shard_map/ppermute | solution.py:416
  17.9 26.3 %collective-permute-start.3 = (bf16[2,288,128]{2,1,0:T(8,128)(2,1)}, bf16[2,288,128]{2,1,0:T(8,128)(2,1)S(1)}, u32[]{:S(2)}, u32[]{:S(2)}) collective-permute-start(bf16[2,288,128]{2,1,0:T(8,128)(2,1)} %get-tuple-element.37), channel_id=1, source_target_pairs={{0,14},{1,15},{2,12},{3,13},{4,10},{5,11},{6,8},{7,9},{8,6},{9,7},... | collective-permute-start | bytes 442376 | tf_op jit(solution)/shard_map/ppermute | solution.py:416
  44.2 5.4 %copy-start.13 = (bf16[2,288,128]{2,1,0:T(8,128)(2,1)}, bf16[2,288,128]{2,1,0:T(8,128)(2,1)S(1)}, u32[]{:S(2)}) copy-start(bf16[2,288,128]{2,1,0:T(8,128)(2,1)S(1)} %collective-permute-done.3.refs_3_) | copy-start | bytes 442372
  44.2 5.4 %copy-start = (bf16[2,576,128]{2,1,0:T(8,128)(2,1)}, bf16[2,576,128]{2,1,0:T(8,128)(2,1)S(1)}, u32[]{:S(2)}) copy-start(bf16[2,576,128]{2,1,0:T(8,128)(2,1)S(1)} %collective-permute-done.refs_0_) | copy-start | bytes 884740
  44.2 5.4 %copy-start.1 = (bf16[2,576,128]{2,1,0:T(8,128)(2,1)}, bf16[2,576,128]{2,1,0:T(8,128)(2,1)S(1)}, u32[]{:S(2)}) copy-start(bf16[2,576,128]{2,1,0:T(8,128)(2,1)S(1)} %collective-permute-done.1.refs_1_) | copy-start | bytes 884740
  44.2 5.4 %copy-start.3 = (bf16[2,576,128]{2,1,0:T(8,128)(2,1)}, bf16[2,576,128]{2,1,0:T(8,128)(2,1)S(1)}, u32[]{:S(2)}) copy-start(bf16[2,576,128]{2,1,0:T(8,128)(2,1)S(1)} %collective-permute-done.2.refs_2_) | copy-start | bytes 884740
  44.2 2.7 %collective-permute-start.4 = (bf16[2,576,128]{2,1,0:T(8,128)(2,1)S(1)}, bf16[2,576,128]{2,1,0:T(8,128)(2,1)S(1)}, u32[]{:S(2)}, u32[]{:S(2)}) collective-permute-start(bf16[2,576,128]{2,1,0:T(8,128)(2,1)S(1)} %collective-permute-done.refs_0_), channel_id=1, source_target_pairs={{0,1},{1,0},{2,3},{3,2},{4,5},{5,4},{6,7},{7,6},{8,9},{9,8},{10,11... | collective-permute-start | bytes 884744 | tf_op jit(solution)/shard_map/ppermute | solution.py:420
  44.3 4.4 %collective-permute-start.5 = (bf16[2,576,128]{2,1,0:T(8,128)(2,1)S(1)}, bf16[2,576,128]{2,1,0:T(8,128)(2,1)S(1)}, u32[]{:S(2)}, u32[]{:S(2)}) collective-permute-start(bf16[2,576,128]{2,1,0:T(8,128)(2,1)S(1)} %collective-permute-done.1.refs_1_), channel_id=1, source_target_pairs={{0,1},{1,0},{2,3},{3,2},{4,5},{5,4},{6,7},{7,6},{8,9},{9,8},{10,11... | collective-permute-start | bytes 884744 | tf_op jit(solution)/shard_map/ppermute | solution.py:420
  44.8 4.8 %collective-permute-start.6 = (bf16[2,576,128]{2,1,0:T(8,128)(2,1)S(1)}, bf16[2,576,128]{2,1,0:T(8,128)(2,1)S(1)}, u32[]{:S(2)}, u32[]{:S(2)}) collective-permute-start(bf16[2,576,128]{2,1,0:T(8,128)(2,1)S(1)} %collective-permute-done.2.refs_2_), channel_id=1, source_target_pairs={{0,1},{1,0},{2,3},{3,2},{4,5},{5,4},{6,7},{7,6},{8,9},{9,8},{10,11... | collective-permute-start | bytes 884744 | tf_op jit(solution)/shard_map/ppermute | solution.py:420
  44.9 2.0 %collective-permute-start.7 = (bf16[2,288,128]{2,1,0:T(8,128)(2,1)S(1)}, bf16[2,288,128]{2,1,0:T(8,128)(2,1)S(1)}, u32[]{:S(2)}, u32[]{:S(2)}) collective-permute-start(bf16[2,288,128]{2,1,0:T(8,128)(2,1)S(1)} %collective-permute-done.3.refs_3_), channel_id=1, source_target_pairs={{0,1},{1,0},{2,3},{3,2},{4,5},{5,4},{6,7},{7,6},{8,9},{9,8},{10,11... | collective-permute-start | bytes 442376 | tf_op jit(solution)/shard_map/ppermute | solution.py:420
  45.3 36.3 %collective-permute-start.11 = (bf16[2,288,128]{2,1,0:T(8,128)(2,1)}, bf16[2,288,128]{2,1,0:T(8,128)(2,1)S(1)}, u32[]{:S(2)}, u32[]{:S(2)}) collective-permute-start(bf16[2,288,128]{2,1,0:T(8,128)(2,1)} %get-tuple-element.55), channel_id=1, source_target_pairs={{0,14},{1,15},{2,12},{3,13},{4,10},{5,11},{6,8},{7,9},{8,6},{9,7},... | collective-permute-start | bytes 442376 | tf_op jit(solution)/shard_map/ppermute | solution.py:416
  46.9 2.7 %copy-start.14 = (bf16[2,288,128]{2,1,0:T(8,128)(2,1)}, bf16[2,288,128]{2,1,0:T(8,128)(2,1)S(1)}, u32[]{:S(2)}) copy-start(bf16[2,288,128]{2,1,0:T(8,128)(2,1)S(1)} %collective-permute-done.7.refs_8_) | copy-start | bytes 442372
  46.9 34.7 %collective-permute-start.8 = (bf16[2,576,128]{2,1,0:T(8,128)(2,1)}, bf16[2,576,128]{2,1,0:T(8,128)(2,1)S(1)}, u32[]{:S(2)}, u32[]{:S(2)}) collective-permute-start(bf16[2,576,128]{2,1,0:T(8,128)(2,1)} %get-tuple-element.52), channel_id=1, source_target_pairs={{0,2},{1,9},{2,0},{3,11},{4,6},{5,13},{6,4},{7,15},{8,10},{9,1},{1... | collective-permute-start | bytes 884744 | tf_op jit(solution)/shard_map/ppermute | solution.py:416
  46.9 2.7 %copy-start.6 = (bf16[2,576,128]{2,1,0:T(8,128)(2,1)}, bf16[2,576,128]{2,1,0:T(8,128)(2,1)S(1)}, u32[]{:S(2)}) copy-start(bf16[2,576,128]{2,1,0:T(8,128)(2,1)S(1)} %collective-permute-done.4.refs_5_) | copy-start | bytes 884740
  46.9 34.7 %collective-permute-start.9 = (bf16[2,576,128]{2,1,0:T(8,128)(2,1)}, bf16[2,576,128]{2,1,0:T(8,128)(2,1)S(1)}, u32[]{:S(2)}, u32[]{:S(2)}) collective-permute-start(bf16[2,576,128]{2,1,0:T(8,128)(2,1)} %get-tuple-element.53), channel_id=1, source_target_pairs={{0,10},{1,5},{2,8},{3,7},{4,14},{5,1},{6,12},{7,3},{8,2},{9,13},{1... | collective-permute-start | bytes 884744 | tf_op jit(solution)/shard_map/ppermute | solution.py:416
  48.7 0.9 copy-start.7
  48.7 32.9 %collective-permute-start.10 = (bf16[2,576,128]{2,1,0:T(8,128)(2,1)}, bf16[2,576,128]{2,1,0:T(8,128)(2,1)S(1)}, u32[]{:S(2)}, u32[]{:S(2)}) collective-permute-start(bf16[2,576,128]{2,1,0:T(8,128)(2,1)} %get-tuple-element.54), channel_id=1, source_target_pairs={{0,6},{1,13},{2,4},{3,15},{4,2},{5,9},{6,0},{7,11},{8,14},{9,5},{1... | collective-permute-start | bytes 884744 | tf_op jit(solution)/shard_map/ppermute | solution.py:416
  49.6 0.7 copy-start.8
  81.6 4.1 %copy-start.12 = (bf16[2,288,128]{2,1,0:T(8,128)(2,1)}, bf16[2,288,128]{2,1,0:T(8,128)(2,1)S(1)}, u32[]{:S(2)}) copy-start(bf16[2,288,128]{2,1,0:T(8,128)(2,1)S(1)} %collective-permute-done.11.refs_5_) | copy-start | bytes 442372
  81.6 4.1 %copy-start.2 = (bf16[2,576,128]{2,1,0:T(8,128)(2,1)}, bf16[2,576,128]{2,1,0:T(8,128)(2,1)S(1)}, u32[]{:S(2)}) copy-start(bf16[2,576,128]{2,1,0:T(8,128)(2,1)S(1)} %collective-permute-done.8.refs_2_) | copy-start | bytes 884740
  81.6 4.1 %copy-start.4 = (bf16[2,576,128]{2,1,0:T(8,128)(2,1)}, bf16[2,576,128]{2,1,0:T(8,128)(2,1)S(1)}, u32[]{:S(2)}) copy-start(bf16[2,576,128]{2,1,0:T(8,128)(2,1)S(1)} %collective-permute-done.9.refs_3_) | copy-start | bytes 884740
  81.6 4.1 %copy-start.5 = (bf16[2,576,128]{2,1,0:T(8,128)(2,1)}, bf16[2,576,128]{2,1,0:T(8,128)(2,1)S(1)}, u32[]{:S(2)}) copy-start(bf16[2,576,128]{2,1,0:T(8,128)(2,1)S(1)} %collective-permute-done.10.refs_4_) | copy-start | bytes 884740
  81.6 4.0 %collective-permute-start.12 = (bf16[2,576,128]{2,1,0:T(8,128)(2,1)S(1)}, bf16[2,576,128]{2,1,0:T(8,128)(2,1)S(1)}, u32[]{:S(2)}, u32[]{:S(2)}) collective-permute-start(bf16[2,576,128]{2,1,0:T(8,128)(2,1)S(1)} %collective-permute-done.8.refs_2_), channel_id=1, source_target_pairs={{0,1},{1,0},{2,3},{3,2},{4,5},{5,4},{6,7},{7,6},{8,9},{9,8},{10,11... | collective-permute-start | bytes 884744 | tf_op jit(solution)/shard_map/ppermute | solution.py:420
  83.4 2.3 %collective-permute-start.13 = (bf16[2,576,128]{2,1,0:T(8,128)(2,1)S(1)}, bf16[2,576,128]{2,1,0:T(8,128)(2,1)S(1)}, u32[]{:S(2)}, u32[]{:S(2)}) collective-permute-start(bf16[2,576,128]{2,1,0:T(8,128)(2,1)S(1)} %collective-permute-done.9.refs_3_), channel_id=1, source_target_pairs={{0,1},{1,0},{2,3},{3,2},{4,5},{5,4},{6,7},{7,6},{8,9},{9,8},{10,11... | collective-permute-start | bytes 884744 | tf_op jit(solution)/shard_map/ppermute | solution.py:420
  83.4 2.2 %collective-permute-start.14 = (bf16[2,576,128]{2,1,0:T(8,128)(2,1)S(1)}, bf16[2,576,128]{2,1,0:T(8,128)(2,1)S(1)}, u32[]{:S(2)}, u32[]{:S(2)}) collective-permute-start(bf16[2,576,128]{2,1,0:T(8,128)(2,1)S(1)} %collective-permute-done.10.refs_4_), channel_id=1, source_target_pairs={{0,1},{1,0},{2,3},{3,2},{4,5},{5,4},{6,7},{7,6},{8,9},{9,8},{10,11... | collective-permute-start | bytes 884744 | tf_op jit(solution)/shard_map/ppermute | solution.py:420
  83.9 1.8 %collective-permute-start.15 = (bf16[2,288,128]{2,1,0:T(8,128)(2,1)S(1)}, bf16[2,288,128]{2,1,0:T(8,128)(2,1)S(1)}, u32[]{:S(2)}, u32[]{:S(2)}) collective-permute-start(bf16[2,288,128]{2,1,0:T(8,128)(2,1)S(1)} %collective-permute-done.11.refs_5_), channel_id=1, source_target_pairs={{0,1},{1,0},{2,3},{3,2},{4,5},{5,4},{6,7},{7,6},{8,9},{9,8},{10,11... | collective-permute-start | bytes 442376 | tf_op jit(solution)/shard_map/ppermute | solution.py:420
  85.6 0.7 copy-start.15
  85.6 0.8 copy-start.9
  85.6 0.9 copy-start.10
  85.7 1.0 copy-start.11

commit v6 on v5

--- a/solution.py
+++ b/solution.py
@@ -11,7 +11,8 @@
 BLOCK = 64
 SEL = 32
 PAIR = 2 * BLOCK
-GROUP = 2 * PAIR
+SUB = 512
+STEP = 2 * SUB
 VMEM = 60 << 20
 NEG = -1e30
 SCALE = 1.4426950408889634 / 192.0**0.5
@@ -105,10 +106,10 @@
 
 
 def pair_places(owners, phase, first):
-    return {
-        (c, o): i
-        for i, (c, o) in enumerate((c, o) for c in range(phase) for o in range(owners) if o < owners - 1 or first and c == 0)
-    }
+    pairs = [(c, o) for c in range(phase) for o in range(owners - 1)]
+    if first:
+        pairs.insert(0, (0, owners - 1))
+    return {pair: i for i, pair in enumerate(pairs)}
 
 
 def plan_kernel(owners, capacity, shift, phases, ids, table, *rest):
@@ -124,10 +125,9 @@
         table[owner * capacity + rank] = block * BLOCK
         count[owner] = rank + 1
     for p, (bias, phase) in enumerate(zip(biases, phases)):
-        last = p > 0 and p == len(phases) - 1
-        if last:
-            bias[...] = jnp.full(bias.shape, NEG, bias.dtype)
-            live = jnp.int32(0)
+        last = p > 0
+        live = jnp.int32(0)
+        bias[...] = jnp.full(bias.shape, NEG, bias.dtype)
         for (c, o), i in pair_places(owners, len(phase), p == 0).items():
             slot = o * capacity + 2 * phase[c]
             a, b = table[slot], table[slot + 1]
@@ -145,9 +145,11 @@
 
 
 def plan(ids, owners, capacity, shift, phases):
-    shapes = [(8, len(pair_places(owners, len(phase), p == 0)) * PAIR) for p, phase in enumerate(phases)]
-    if len(phases) > 1:
-        shapes[-1] = (8, shapes[-1][1] + PAIR)
+    shapes = []
+    for p, phase in enumerate(phases):
+        each = group_width(phase_kind(p, phases)) // PAIR
+        pairs = len(pair_places(owners, len(phase), p == 0)) + int(p > 0)
+        shapes.append((8, -(-pairs // each) * each * PAIR))
     entries = owners * capacity + len(phases[-1]) * owners + 1
     return pl.pallas_call(
         functools.partial(plan_kernel, owners, capacity, shift, phases),
@@ -187,91 +189,103 @@
 
 
 class Half:
-    def __init__(self, base, q, kt, bias, scores, weights, tops, sums, keys, diagonal=None):
-        self.base, self.q, self.kt, self.bias = base, q, kt, bias
-        self.scores, self.weights, self.tops, self.sums = scores, weights, tops, sums
-        self.keys, self.diagonal = keys, diagonal
-        self.groups = -(-keys // GROUP)
-        self.size = scores.shape[0]
-
-    def score(self, group):
-        at = group * GROUP
-        end = min(at + GROUP, self.keys)
+    def __init__(self, base, q, kt, bias, width, scores, weights, tops, sums, acc):
+        self.base, self.q, self.kt, self.bias, self.width = base, q, kt, bias, width
+        self.scores, self.weights, self.tops, self.sums, self.acc = scores, weights, tops, sums, acc
+
+    def start(self):
+        self.tops[...] = jnp.full(self.tops.shape, NEG, jnp.float32)
+        self.sums[...] = jnp.zeros(self.sums.shape, jnp.float32)
+        self.acc[...] = jnp.zeros(self.acc.shape, jnp.float32)
+
+    def group(self, g):
+        return pl.multiple_of(g * self.width, self.width)
+
+    def score(self, g, visible=None):
+        at = self.group(g)
         part = lax.dot_general(
-            self.q[pl.ds(self.base, self.size), :], self.kt[:, at:end], NN, preferred_element_type=jnp.float32
+            self.q[pl.ds(self.base, SUB), :],
+            self.kt[:, pl.ds(at, self.width)],
+            NN,
+            preferred_element_type=jnp.float32,
         )
-        part = part + self.bias[0:1, at:end]
-        columns = [part[:, c : c + PAIR] for c in range(0, end - at, PAIR)]
-        if self.diagonal is not None:
-            where, key, pos, first = self.diagonal
-            if at <= where < end:
-                seen = jnp.concatenate(
-                    [
-                        jnp.broadcast_to(key, (BLOCK, PAIR)) <= pos[first + self.base // BLOCK + s]
-                        for s in range(self.size // BLOCK)
-                    ],
-                    axis=0,
-                )
-                index = (where - at) // PAIR
-                columns[index] = jnp.where(seen, columns[index], NEG)
-        high = columns[0]
-        for i, column in enumerate(columns):
-            self.scores[:, at + i * PAIR : at + (i + 1) * PAIR] = column
-            high = jnp.maximum(high, column) if i else high
-        self.tops[...] = high if group == 0 else jnp.maximum(self.tops[...], high)
+        part = part + self.bias[0:1, pl.ds(at, self.width)]
+        high = self.tops[...]
+        for c in range(0, self.width, PAIR):
+            column = part[:, c : c + PAIR]
+            if c == 0 and visible is not None:
+                column = visible(g, self.base, column)
+            self.scores[:, pl.ds(at + c, PAIR)] = column
+            high = jnp.maximum(high, column)
+        self.tops[...] = high
 
     def settle(self, old=None):
         top = jnp.max(self.tops[...], axis=1, keepdims=True) * SCALE
-        top = jnp.broadcast_to(top, (self.size, PAIR))
+        top = jnp.broadcast_to(top, (SUB, PAIR))
         self.tops[...] = top if old is None else jnp.maximum(top, old)
 
-    def weigh(self, slab):
-        rows = pl.ds(slab * BLOCK, BLOCK)
-        top = self.tops[rows, :]
-        total = jnp.zeros((BLOCK, PAIR), jnp.float32)
-        for at in range(0, self.keys, PAIR):
-            part = jnp.exp2(self.scores[rows, at : at + PAIR] * SCALE - top)
-            total = total + part
-            self.weights[rows, at : at + PAIR] = part.astype(jnp.bfloat16)
-        self.sums[rows, :] = total
+    def weigh(self, g):
+        at = self.group(g)
+        for slab in range(0, SUB, BLOCK):
+            rows = pl.ds(slab, BLOCK)
+            top = self.tops[rows, :]
+            total = self.sums[rows, :]
+            for c in range(0, self.width, PAIR):
+                part = jnp.exp2(self.scores[rows, pl.ds(at + c, PAIR)] * SCALE - top)
+                total = total + part
+                self.weights[rows, pl.ds(at + c, PAIR)] = part.astype(jnp.bfloat16)
+            self.sums[rows, :] = total
 
     def total(self):
-        return jnp.broadcast_to(jnp.sum(self.sums[...], axis=1, keepdims=True), (self.size, PAIR))
-
-    def combine(self, column):
-        return lax.dot_general(
-            self.weights[:, 0 : self.keys],
-            self.kt[column : column + GROUP, 0 : self.keys],
+        return jnp.broadcast_to(jnp.sum(self.sums[...], axis=1, keepdims=True), (SUB, PAIR))
+
+    def combine(self, g):
+        at = self.group(g)
+        self.acc[...] += lax.dot_general(
+            self.weights[:, pl.ds(at, self.width)],
+            self.kt[0:KVL, pl.ds(at, self.width)],
             NT,
             preferred_element_type=jnp.float32,
         )
 
 
-def run_halves(a, b, before, after, combine):
-    slabs = a.size // BLOCK
-    for g in range(a.groups):
-        a.score(g)
+def run_halves(a, b, groups, visible, before, after, finish):
+    a.start()
+    b.start()
+
+    @pl.loop(0, groups)
+    def _(g):
+        a.score(g, visible)
+
     before(a)
-    for i in range(max(a.groups, slabs)):
-        if i < b.groups:
-            b.score(i)
-        if i < slabs:
-            a.weigh(i)
+
+    @pl.loop(0, groups)
+    def _(g):
+        a.weigh(g)
+        b.score(g, visible)
+
     before(b)
     after(a)
-    for i, column in enumerate(range(0, KVL, GROUP)):
-        combine(a, column)
-        for s in range(i * slabs // 2, (i + 1) * slabs // 2):
-            b.weigh(s)
+
+    @pl.loop(0, groups)
+    def _(g):
+        b.weigh(g)
+        a.combine(g)
+
     after(b)
-    for column in range(0, KVL, GROUP):
-        combine(b, column)
-
-
-SCRATCH = 9
-
-
-def attend_kernel(owners, capacity, kind, levels, table, pos, q, bias, *refs):
+
+    @pl.loop(0, groups)
+    def _(g):
+        b.combine(g)
+
+    finish(a)
+    finish(b)
+
+
+SCRATCH = 11
+
+
+def attend_kernel(owners, capacity, kind, width, table, pos, q, bias, *refs):
     start, end = kind in ("first", "only"), kind in ("last", "only")
     if not start:
         carry, logs, *refs = refs
@@ -280,83 +294,82 @@
     arrived = Arrived(owners, refs[: len(refs) - SCRATCH - len(outs)])
     chunks = arrived.chunks
     step = pl.program_id(0)
-    sub = work[0].shape[0]
     index = owners * capacity
-    needed = table[index + chunks * owners] if kind == "last" else None
+    each = width // PAIR
+    if start:
+        needed = len(pair_places(owners, chunks, True))
+        groups = kt.shape[1] // width
+    else:
+        needed = table[index + chunks * owners]
+        groups = (needed + each - 1) // each
 
     @pl.when(step == 0)
     def _():
         for c in range(chunks):
             for part, (owner, _) in enumerate(arrived.parts):
-                if kind == "last":
+                if not start:
                     at = table[index + c * owners + owner]
                     pl.when(at >= 0)(functools.partial(arrived.place, c, part, kt, at * PAIR))
-                elif start and c == 0:
-                    arrived.place(c, part, kt, owner * PAIR)
+                elif c == 0:
+                    arrived.place(c, part, kt, lax.rem(owner + 1, owners) * PAIR)
                 else:
-                    at = (c * (owners - 1) + owner + int(start)) * PAIR
+                    at = (c * (owners - 1) + owner + 1) * PAIR
                     pl.when(owner < owners - 1)(functools.partial(arrived.place, c, part, kt, at))
-        if kind == "last":
-            fill = jnp.int32(levels[-1])
-            for level in reversed(levels[:-1]):
-                fill = jnp.where(needed <= level, level, fill)
-
-            @pl.loop(needed, fill)
-            def _(i):
-                kt[:, pl.ds(pl.multiple_of(i * PAIR, PAIR), PAIR)] = jnp.zeros((kt.shape[0], PAIR), kt.dtype)
-
-    def attend(keys):
-        diagonal = None
-        if start:
-            key = table[(owners - 1) * capacity] + lax.broadcasted_iota(jnp.int32, (1, PAIR), 1)
-            diagonal = ((owners - 1) * PAIR, key, pos, step * (2 * sub // BLOCK))
-        a = Half(0, q, kt, bias, *work[0::2], keys, diagonal)
-        b = Half(sub, q, kt, bias, *work[1::2], keys, diagonal)
-
-        def before(part):
-            part.settle(None if start else logs[pl.ds(part.base, sub), :])
-
-        def after(part):
-            rows = pl.ds(part.base, sub)
-            total = part.total()
-            if not start:
-                kept = jnp.exp2(logs[rows, :] - part.tops[...])
-                total = total + kept
-            inverse = 1.0 / total
-            part.sums[...] = inverse
-            if not end:
-                outs[1][rows, :] = part.tops[...] + jnp.log2(total)
-            if not start:
-                part.tops[...] = kept * inverse
-
-        def combine(part, column):
-            summed = part.combine(column)
-            rows = pl.ds(part.base, sub)
-            for at in range(0, GROUP, PAIR):
-                cols = slice(column + at, column + at + PAIR)
-                result = summed[:, at : at + PAIR] * part.sums[...]
+
+        @pl.loop(needed, groups * each)
+        def _(i):
+            kt[:, pl.ds(pl.multiple_of(i * PAIR, PAIR), PAIR)] = jnp.zeros((kt.shape[0], PAIR), kt.dtype)
+
+    visible = None
+    if start:
+        own = table[(owners - 1) * capacity] + lax.broadcasted_iota(jnp.int32, (1, PAIR), 1)
+
+        def visible(g, base, column):
+            key = jnp.broadcast_to(jnp.where(g == 0, own, 0), (BLOCK, PAIR))
+            first = (step * STEP + base) // BLOCK
+            slabs = [
+                jnp.where(key <= pos[first + s], column[s * BLOCK : (s + 1) * BLOCK], NEG) for s in range(SUB // BLOCK)
+            ]
+            return jnp.concatenate(slabs, axis=0)
+
+    a = Half(0, q, kt, bias, width, *work[0::2])
+    b = Half(SUB, q, kt, bias, width, *work[1::2])
+
+    def before(part):
+        part.settle(None if start else logs[pl.ds(part.base, SUB), :])
+
+    def after(part):
+        rows = pl.ds(part.base, SUB)
+        total = part.total()
+        if not start:
+            kept = jnp.exp2(logs[rows, :] - part.tops[...])
+            total = total + kept
+        inverse = 1.0 / total
+        part.sums[...] = inverse
+        if not end:
+            outs[1][rows, :] = part.tops[...] + jnp.log2(total)
+        if not start:
+            part.tops[...] = kept * inverse
+
+    def finish(part):
+        @pl.loop(0, SUB // BLOCK)
+        def _(s):
+            here = pl.ds(pl.multiple_of(s * BLOCK, BLOCK), BLOCK)
+            rows = pl.ds(pl.multiple_of(part.base + s * BLOCK, BLOCK), BLOCK)
+            for at in range(0, KVL, PAIR):
+                cols = slice(at, at + PAIR)
+                result = part.acc[here, cols] * part.sums[here, :]
                 if not start:
-                    result = result + carry[rows, cols] * part.tops[...]
+                    result = result + carry[rows, cols] * part.tops[here, :]
                 outs[0][rows, cols] = result.astype(outs[0].dtype)
 
-        run_halves(a, b, before, after, combine)
-
-    if kind != "last":
-        attend(kt.shape[1])
-        return
-    below = -1
-    for level in levels:
-        pl.when(jnp.logical_and(needed > below, needed <= level))(functools.partial(attend, level * PAIR))
-        below = level
-
-
-def attend(table, pos, q, bias, state, arrays, owners, capacity, kind, chunks):
+    run_halves(a, b, groups, visible, before, after, finish)
+
+
+def attend(table, pos, q, bias, state, arrays, owners, capacity, kind):
     rows, lat = q.shape
-    pairs = len(pair_places(owners, chunks, kind in ("first", "only")))
-    keys = pairs * PAIR
-    levels = [n for n in (4, 5, 6, 8) if n < pairs] + [pairs]
-    sub = 1024 if keys <= 2048 and rows % 2048 == 0 else 512
-    step = 2 * sub
+    keys = bias.shape[1]
+    width = group_width(kind)
     out_shape = [jax.ShapeDtypeStruct((rows, KVL), jnp.float32), jax.ShapeDtypeStruct((rows, PAIR), jnp.float32)]
     if kind in ("last", "only"):
         out_shape = [jax.ShapeDtypeStruct((rows, KVL), jnp.bfloat16)]
@@ -365,21 +378,22 @@
         return pl.BlockSpec(x.shape, lambda i, *_: (0,) * x.ndim)
 
     def row_block(x):
-        return pl.BlockSpec((step, x.shape[1]), lambda i, *_: (i, 0))
+        return pl.BlockSpec((STEP, x.shape[1]), lambda i, *_: (i, 0))
 
     return pl.pallas_call(
-        functools.partial(attend_kernel, owners, capacity, kind, levels),
+        functools.partial(attend_kernel, owners, capacity, kind, width),
         out_shape=out_shape,
         grid_spec=pltpu.PrefetchScalarGridSpec(
             num_scalar_prefetch=2,
-            grid=(rows // step,),
+            grid=(rows // STEP,),
             in_specs=[row_block(q), whole(bias)] + [row_block(x) for x in state] + [whole(x) for x in arrays],
             out_specs=[row_block(x) for x in out_shape],
             scratch_shapes=[
                 pltpu.VMEM((lat, keys), jnp.bfloat16),
-                *[pltpu.VMEM((sub, keys), jnp.float32)] * 2,
-                *[pltpu.VMEM((sub, keys), jnp.bfloat16)] * 2,
-                *[pltpu.VMEM((sub, PAIR), jnp.float32)] * 4,
+                *[pltpu.VMEM((SUB, keys), jnp.float32)] * 2,
+                *[pltpu.VMEM((SUB, keys), jnp.bfloat16)] * 2,
+                *[pltpu.VMEM((SUB, PAIR), jnp.float32)] * 4,
+                *[pltpu.VMEM((SUB, KVL), jnp.float32)] * 2,
             ],
         ),
         compiler_params=pltpu.CompilerParams(vmem_limit_bytes=VMEM),
@@ -388,6 +402,14 @@
         ),
         name="attend_" + kind,
     )(table, pos, q, bias, *state, *arrays)
+
+
+def phase_kind(p, phases):
+    return "only" if len(phases) == 1 else "first" if p == 0 else "last"
+
+
+def group_width(kind):
+    return 2 * PAIR if kind == "last" else 4 * PAIR
 
 
 def split_phases(chunks):
@@ -432,8 +454,8 @@
             *late, logs = lax.optimization_barrier((*late, state[1]))
             state = [state[0], logs]
         arrays = [*late, packed[p][-1], *swap(late)]
-        kind = "only" if len(phases) == 1 else "first" if p == 0 else "last" if p == len(phases) - 1 else "middle"
-        state = attend(table, positions, q, biases[p], state, arrays, owners, capacity, kind, len(phase))
+        kind = phase_kind(p, phases)
+        state = attend(table, positions, q, biases[p], state, arrays, owners, capacity, kind)
     return state[0].reshape(q_rows, heads, KVL)
 
 

time: 116 us -> 138 us (1.19)
  the two profiles are of different devices: /device:TPU:11 before, /device:TPU:15 now
where the time goes in v6:
time: 138 us; the launch traced here: 137 us
  Pallas kernels  93.6 us (68%)
  waiting for transfers between devices  22.6 us (16%)
  starting transfers between devices  9.78 us (7%)
  blocking collectives  8.79 us (6%)
  local copies, waits for them, and re-layouts  2.28 us (2%)
    pallas_call x2, Pallas kernels, attend(): pl.pallas_call(functools.partial(attend_kernel, owners, capacity, kind, w...  82.2 us
    ppermute x8, waiting for transfers between devices, send(): got.append(lax.ppermute(x, ('ctx', 'head'), moves))  19.3 us
    pallas_call x2, Pallas kernels, pack(): pl.pallas_call(functools.partial(pack_kernel, capacity, chunks), out_shap...  9.86 us
    all_to_all x1, blocking collectives, local(): lax.all_to_all(jnp.broadcast_to(block_ids, (owners, SEL)), 'ctx', split_a...  8.79 us
    ppermute x8, starting transfers between devices, send(): got.append(lax.ppermute(x, ('ctx', 'head'), moves))  6.38 us
    ppermute x8, starting transfers between devices, swap(): return [lax.ppermute(x, 'head', [(0, 1), (1, 0)]) for x in got]  3.4 us
    ppermute x8, waiting for transfers between devices, swap(): return [lax.ppermute(x, 'head', [(0, 1), (1, 0)]) for x in got]  3.3 us
  transfers between devices with their start and end apart: 16, of which 3 were waited for; matrix products, arithmetic and copies ran while one was open for 0% of the time, Pallas kernels for 43%

profile of v6, /device:TPU:15, one launch (start us, length us, event | category | flops | bytes accessed | tf_op | source)
XLA Modules:
  0.0 137.3 jit_solution(17789600160596083781)
XLA Ops:
  0.0 0.7 broadcast_in_dim.2
  0.7 8.8 %all_to_all.8 = s32[8,1,32]{2,1,0:T(1,128)} all-to-all(s32[8,1,32]{2,1,0:T(1,128)S(1)} %broadcast_in_dim.2), channel_id=1, replica_groups=mesh['groups'=2,'ctx'=8,'head'=2] {'ctx'}, dimensions={0} | all-to-all | bytes 2048 | tf_op jit(solution)/shard_map/all_to_all | solution.py:426
  9.4 4.9 %pack.2 = (bf16[2,576,128]{2,1,0:T(8,128)(2,1)}, bf16[2,576,128]{2,1,0:T(8,128)(2,1)}, bf16[2,576,128]{2,1,0:T(8,128)(2,1)}, bf16[2,288,128]{2,1,0:T(8,128)(2,1)}, bf16[2,576,128]{2,1,0:T(8,128)(2,1)}) custom-call(s32[8,32]{1,0:T(8,128)} %bitcast.7, bf16[576,4096]{1,0:T(8,128)(2,1)} %bitcast.5), custom_call_target="tpu_custom_call" | custom-call | bytes 18874368 | tf_op jit(solution)/shard_map/pack/pallas_call | solution.py:81
  14.4 0.4 collective-permute-start
  14.7 1.1 collective-permute-start.1
  15.9 1.2 collective-permute-start.2
  17.1 1.0 collective-permute-start.3
  18.1 1.6 %plan.1 = (s32[81]{0:T(128)}, f32[8,2048]{1,0:T(8,128)}, f32[8,2048]{1,0:T(8,128)}) custom-call(s32[32]{0:T(128)} %bitcast.10), custom_call_target="tpu_custom_call" | custom-call | bytes 1048576 | tf_op jit(solution)/shard_map/plan/pallas_call | solution.py:154
  19.7 5.0 %pack.3 = (bf16[2,576,128]{2,1,0:T(8,128)(2,1)}, bf16[2,576,128]{2,1,0:T(8,128)(2,1)}, bf16[2,576,128]{2,1,0:T(8,128)(2,1)}, bf16[2,288,128]{2,1,0:T(8,128)(2,1)}, bf16[2,576,128]{2,1,0:T(8,128)(2,1)}) custom-call(s32[8,32]{1,0:T(8,128)} %bitcast.8, bf16[576,4096]{1,0:T(8,128)(2,1)} %bitcast.6), custom_call_target="tpu_custom_call" | custom-call | bytes 18874368 | tf_op jit(solution)/shard_map/pack/pallas_call | solution.py:81
  24.7 19.3 %collective-permute-done.3.refs_3_ = bf16[2,288,128]{2,1,0:T(8,128)(2,1)S(1)} collective-permute-done((bf16[2,288,128]{2,1,0:T(8,128)(2,1)}, bf16[2,288,128]{2,1,0:T(8,128)(2,1)S(1)}, u32[]{:S(2)}, u32[]{:S(2)}) %collective-permute-start.3) | collective-permute-done | bytes 147488 | tf_op jit(solution)/shard_map/ppermute | solution.py:438
  44.0 0.0 collective-permute-done.refs_0_
  44.0 0.0 collective-permute-done.1.refs_1_
  44.0 0.0 copy-start.1
  44.0 0.0 collective-permute-done.2.refs_2_
  44.0 0.0 copy-start.3
  44.0 0.1 collective-permute-start.4
  44.1 0.5 collective-permute-start.5
  44.6 0.1 collective-permute-start.6
  44.7 0.4 collective-permute-start.7
  45.1 0.0 collective-permute-start.11
  45.1 1.6 %collective-permute-done.7.refs_8_ = bf16[2,288,128]{2,1,0:T(8,128)(2,1)S(1)} collective-permute-done((bf16[2,288,128]{2,1,0:T(8,128)(2,1)S(1)}, bf16[2,288,128]{2,1,0:T(8,128)(2,1)S(1)}, u32[]{:S(2)}, u32[]{:S(2)}) %collective-permute-start.7) | collective-permute-done | bytes 147488 | tf_op jit(solution)/shard_map/ppermute | solution.py:442
  46.7 0.0 collective-permute-start.8
  46.7 0.0 collective-permute-done.4.refs_5_
  46.7 0.0 copy-start.6
  46.7 1.2 collective-permute-start.9
  47.9 0.0 collective-permute-done.5.refs_6_
  47.9 1.4 %collective-permute-start.10 = (bf16[2,576,128]{2,1,0:T(8,128)(2,1)}, bf16[2,576,128]{2,1,0:T(8,128)(2,1)S(1)}, u32[]{:S(2)}, u32[]{:S(2)}) collective-permute-start(bf16[2,576,128]{2,1,0:T(8,128)(2,1)} %get-tuple-element.54), channel_id=1, source_target_pairs={{0,6},{1,13},{2,4},{3,15},{4,2},{5,9},{6,0},{7,11},{8,14},{9,5},{1... | collective-permute-start | bytes 884744 | tf_op jit(solution)/shard_map/ppermute | solution.py:438
  49.4 0.0 collective-permute-done.6.refs_7_
  49.4 0.0 copy-done.13
  49.4 0.0 copy-done
  49.4 0.0 copy-done.1
  49.4 0.0 copy-done.3
  49.4 0.0 copy-done.14
  49.4 0.0 copy-done.6
  49.4 0.0 copy-done.7
  49.4 0.6 copy-done.8
  50.1 51.9 %attend_first.1 = (f32[4096,512]{1,0:T(8,128)}, f32[4096,128]{1,0:T(8,128)}) custom-call(s32[81]{0:T(128)} %get-tuple-element.43.table, s32[64]{0:T(128)} %pos.3, bf16[4096,576]{1,0:T(8,128)(2,1)} %bitcast.11, f32[8,2048]{1,0:T(8,128)} %get-tuple-element.45.bias, bf16[2,576,128]{2,1,0:T(8,128)(2,1)} %copy-done, bf16[2,576,128]{2,1,0:T(8,128)(2,1)} %copy-done.1, ...), custom_call_target="tpu_custom_call" | custom-call | flops 18253611008 | bytes 13107200 | tf_op jit(solution)/shard_map/attend_first/pallas_call | solution.py:383
  101.9 0.0 collective-permute-done.11.refs_5_
  101.9 0.0 copy-start.12
  102.0 0.0 collective-permute-done.8.refs_2_
  102.0 0.0 copy-start.2
  102.0 0.0 collective-permute-done.9.refs_3_
  102.0 0.0 copy-start.4
  102.0 0.0 collective-permute-done.10.refs_4_
  102.0 0.0 copy-start.5
  102.0 1.7 %collective-permute-start.12 = (bf16[2,576,128]{2,1,0:T(8,128)(2,1)S(1)}, bf16[2,576,128]{2,1,0:T(8,128)(2,1)S(1)}, u32[]{:S(2)}, u32[]{:S(2)}) collective-permute-start(bf16[2,576,128]{2,1,0:T(8,128)(2,1)S(1)} %collective-permute-done.8.refs_2_), channel_id=1, source_target_pairs={{0,1},{1,0},{2,3},{3,2},{4,5},{5,4},{6,7},{7,6},{8,9},{9,8},{10,11... | collective-permute-start | bytes 884744 | tf_op jit(solution)/shard_map/ppermute | solution.py:442
  103.7 0.1 collective-permute-start.13
  103.8 0.4 collective-permute-start.14
  104.3 0.1 collective-permute-start.15
  104.3 1.7 %collective-permute-done.15.refs_10_ = bf16[2,288,128]{2,1,0:T(8,128)(2,1)S(1)} collective-permute-done((bf16[2,288,128]{2,1,0:T(8,128)(2,1)S(1)}, bf16[2,288,128]{2,1,0:T(8,128)(2,1)S(1)}, u32[]{:S(2)}, u32[]{:S(2)}) %collective-permute-start.15) | collective-permute-done | bytes 147488 | tf_op jit(solution)/shard_map/ppermute | solution.py:442
  106.0 0.0 collective-permute-done.12.refs_7_
  106.0 0.0 collective-permute-done.13.refs_8_
  106.0 0.0 copy-start.10
  106.0 0.0 collective-permute-done.14.refs_9_
  106.0 0.0 copy-start.11
  106.1 0.0 copy-done.12
  106.1 0.0 copy-done.2
  106.1 0.0 copy-done.4
  106.1 0.0 copy-done.5
  106.1 0.6 copy-done.15
  106.7 0.1 copy-done.9
  106.8 0.1 copy-done.10
  106.9 0.1 copy-done.11
  107.0 30.3 %attend_last.1 = bf16[4096,512]{1,0:T(8,128)(2,1)} custom-call(s32[81]{0:T(128)} %get-tuple-element.43.table, s32[64]{0:T(128)} %pos.3, bf16[4096,576]{1,0:T(8,128)(2,1)} %bitcast.12, f32[8,2048]{1,0:T(8,128)} %get-tuple-element.44.bias, f32[4096,512]{1,0:T(8,128)} %get-tuple-element.51.refs_0_, f32[4096,128]{1,0:T(8,128)} %get-tuple-element.57.refs_1_, ...), custom_call_target="tpu_custom_call" | custom-call | flops 18253611008 | bytes 13107200 | tf_op jit(solution)/shard_map/attend_last/pallas_call | solution.py:383
  (7 shorter events, 0.0 us)
Async XLA Ops:
  14.4 29.6 %collective-permute-start = (bf16[2,576,128]{2,1,0:T(8,128)(2,1)}, bf16[2,576,128]{2,1,0:T(8,128)(2,1)S(1)}, u32[]{:S(2)}, u32[]{:S(2)}) collective-permute-start(bf16[2,576,128]{2,1,0:T(8,128)(2,1)} %get-tuple-element.34), channel_id=1, source_target_pairs={{0,2},{1,9},{2,0},{3,11},{4,6},{5,13},{6,4},{7,15},{8,10},{9,1},{1... | collective-permute-start | bytes 884744 | tf_op jit(solution)/shard_map/ppermute | solution.py:438
  14.7 29.2 %collective-permute-start.1 = (bf16[2,576,128]{2,1,0:T(8,128)(2,1)}, bf16[2,576,128]{2,1,0:T(8,128)(2,1)S(1)}, u32[]{:S(2)}, u32[]{:S(2)}) collective-permute-start(bf16[2,576,128]{2,1,0:T(8,128)(2,1)} %get-tuple-element.35), channel_id=1, source_target_pairs={{0,10},{1,5},{2,8},{3,7},{4,14},{5,1},{6,12},{7,3},{8,2},{9,13},{1... | collective-permute-start | bytes 884744 | tf_op jit(solution)/shard_map/ppermute | solution.py:438
  15.9 28.1 %collective-permute-start.2 = (bf16[2,576,128]{2,1,0:T(8,128)(2,1)}, bf16[2,576,128]{2,1,0:T(8,128)(2,1)S(1)}, u32[]{:S(2)}, u32[]{:S(2)}) collective-permute-start(bf16[2,576,128]{2,1,0:T(8,128)(2,1)} %get-tuple-element.36), channel_id=1, source_target_pairs={{0,6},{1,13},{2,4},{3,15},{4,2},{5,9},{6,0},{7,11},{8,14},{9,5},{1... | collective-permute-start | bytes 884744 | tf_op jit(solution)/shard_map/ppermute | solution.py:438
  17.1 26.9 %collective-permute-start.3 = (bf16[2,288,128]{2,1,0:T(8,128)(2,1)}, bf16[2,288,128]{2,1,0:T(8,128)(2,1)S(1)}, u32[]{:S(2)}, u32[]{:S(2)}) collective-permute-start(bf16[2,288,128]{2,1,0:T(8,128)(2,1)} %get-tuple-element.37), channel_id=1, source_target_pairs={{0,14},{1,15},{2,12},{3,13},{4,10},{5,11},{6,8},{7,9},{8,6},{9,7},... | collective-permute-start | bytes 442376 | tf_op jit(solution)/shard_map/ppermute | solution.py:438
  44.0 5.4 %copy-start.13 = (bf16[2,288,128]{2,1,0:T(8,128)(2,1)}, bf16[2,288,128]{2,1,0:T(8,128)(2,1)S(1)}, u32[]{:S(2)}) copy-start(bf16[2,288,128]{2,1,0:T(8,128)(2,1)S(1)} %collective-permute-done.3.refs_3_) | copy-start | bytes 442372
  44.0 5.4 %copy-start = (bf16[2,576,128]{2,1,0:T(8,128)(2,1)}, bf16[2,576,128]{2,1,0:T(8,128)(2,1)S(1)}, u32[]{:S(2)}) copy-start(bf16[2,576,128]{2,1,0:T(8,128)(2,1)S(1)} %collective-permute-done.refs_0_) | copy-start | bytes 884740
  44.0 5.4 %copy-start.1 = (bf16[2,576,128]{2,1,0:T(8,128)(2,1)}, bf16[2,576,128]{2,1,0:T(8,128)(2,1)S(1)}, u32[]{:S(2)}) copy-start(bf16[2,576,128]{2,1,0:T(8,128)(2,1)S(1)} %collective-permute-done.1.refs_1_) | copy-start | bytes 884740
  44.0 5.4 %copy-start.3 = (bf16[2,576,128]{2,1,0:T(8,128)(2,1)}, bf16[2,576,128]{2,1,0:T(8,128)(2,1)S(1)}, u32[]{:S(2)}) copy-start(bf16[2,576,128]{2,1,0:T(8,128)(2,1)S(1)} %collective-permute-done.2.refs_2_) | copy-start | bytes 884740
  44.0 2.7 %collective-permute-start.4 = (bf16[2,576,128]{2,1,0:T(8,128)(2,1)S(1)}, bf16[2,576,128]{2,1,0:T(8,128)(2,1)S(1)}, u32[]{:S(2)}, u32[]{:S(2)}) collective-permute-start(bf16[2,576,128]{2,1,0:T(8,128)(2,1)S(1)} %collective-permute-done.refs_0_), channel_id=1, source_target_pairs={{0,1},{1,0},{2,3},{3,2},{4,5},{5,4},{6,7},{7,6},{8,9},{9,8},{10,11... | collective-permute-start | bytes 884744 | tf_op jit(solution)/shard_map/ppermute | solution.py:442
  44.1 3.8 %collective-permute-start.5 = (bf16[2,576,128]{2,1,0:T(8,128)(2,1)S(1)}, bf16[2,576,128]{2,1,0:T(8,128)(2,1)S(1)}, u32[]{:S(2)}, u32[]{:S(2)}) collective-permute-start(bf16[2,576,128]{2,1,0:T(8,128)(2,1)S(1)} %collective-permute-done.1.refs_1_), channel_id=1, source_target_pairs={{0,1},{1,0},{2,3},{3,2},{4,5},{5,4},{6,7},{7,6},{8,9},{9,8},{10,11... | collective-permute-start | bytes 884744 | tf_op jit(solution)/shard_map/ppermute | solution.py:442
  44.6 4.8 %collective-permute-start.6 = (bf16[2,576,128]{2,1,0:T(8,128)(2,1)S(1)}, bf16[2,576,128]{2,1,0:T(8,128)(2,1)S(1)}, u32[]{:S(2)}, u32[]{:S(2)}) collective-permute-start(bf16[2,576,128]{2,1,0:T(8,128)(2,1)S(1)} %collective-permute-done.2.refs_2_), channel_id=1, source_target_pairs={{0,1},{1,0},{2,3},{3,2},{4,5},{5,4},{6,7},{7,6},{8,9},{9,8},{10,11... | collective-permute-start | bytes 884744 | tf_op jit(solution)/shard_map/ppermute | solution.py:442
  44.7 2.0 %collective-permute-start.7 = (bf16[2,288,128]{2,1,0:T(8,128)(2,1)S(1)}, bf16[2,288,128]{2,1,0:T(8,128)(2,1)S(1)}, u32[]{:S(2)}, u32[]{:S(2)}) collective-permute-start(bf16[2,288,128]{2,1,0:T(8,128)(2,1)S(1)} %collective-permute-done.3.refs_3_), channel_id=1, source_target_pairs={{0,1},{1,0},{2,3},{3,2},{4,5},{5,4},{6,7},{7,6},{8,9},{9,8},{10,11... | collective-permute-start | bytes 442376 | tf_op jit(solution)/shard_map/ppermute | solution.py:442
  45.1 56.9 %collective-permute-start.11 = (bf16[2,288,128]{2,1,0:T(8,128)(2,1)}, bf16[2,288,128]{2,1,0:T(8,128)(2,1)S(1)}, u32[]{:S(2)}, u32[]{:S(2)}) collective-permute-start(bf16[2,288,128]{2,1,0:T(8,128)(2,1)} %get-tuple-element.55), channel_id=1, source_target_pairs={{0,14},{1,15},{2,12},{3,13},{4,10},{5,11},{6,8},{7,9},{8,6},{9,7},... | collective-permute-start | bytes 442376 | tf_op jit(solution)/shard_map/ppermute | solution.py:438
  46.7 2.7 %copy-start.14 = (bf16[2,288,128]{2,1,0:T(8,128)(2,1)}, bf16[2,288,128]{2,1,0:T(8,128)(2,1)S(1)}, u32[]{:S(2)}) copy-start(bf16[2,288,128]{2,1,0:T(8,128)(2,1)S(1)} %collective-permute-done.7.refs_8_) | copy-start | bytes 442372
  46.7 55.3 %collective-permute-start.8 = (bf16[2,576,128]{2,1,0:T(8,128)(2,1)}, bf16[2,576,128]{2,1,0:T(8,128)(2,1)S(1)}, u32[]{:S(2)}, u32[]{:S(2)}) collective-permute-start(bf16[2,576,128]{2,1,0:T(8,128)(2,1)} %get-tuple-element.52), channel_id=1, source_target_pairs={{0,2},{1,9},{2,0},{3,11},{4,6},{5,13},{6,4},{7,15},{8,10},{9,1},{1... | collective-permute-start | bytes 884744 | tf_op jit(solution)/shard_map/ppermute | solution.py:438
  46.7 2.7 %copy-start.6 = (bf16[2,576,128]{2,1,0:T(8,128)(2,1)}, bf16[2,576,128]{2,1,0:T(8,128)(2,1)S(1)}, u32[]{:S(2)}) copy-start(bf16[2,576,128]{2,1,0:T(8,128)(2,1)S(1)} %collective-permute-done.4.refs_5_) | copy-start | bytes 884740
  46.7 55.3 %collective-permute-start.9 = (bf16[2,576,128]{2,1,0:T(8,128)(2,1)}, bf16[2,576,128]{2,1,0:T(8,128)(2,1)S(1)}, u32[]{:S(2)}, u32[]{:S(2)}) collective-permute-start(bf16[2,576,128]{2,1,0:T(8,128)(2,1)} %get-tuple-element.53), channel_id=1, source_target_pairs={{0,10},{1,5},{2,8},{3,7},{4,14},{5,1},{6,12},{7,3},{8,2},{9,13},{1... | collective-permute-start | bytes 884744 | tf_op jit(solution)/shard_map/ppermute | solution.py:438
  47.9 1.5 %copy-start.7 = (bf16[2,576,128]{2,1,0:T(8,128)(2,1)}, bf16[2,576,128]{2,1,0:T(8,128)(2,1)S(1)}, u32[]{:S(2)}) copy-start(bf16[2,576,128]{2,1,0:T(8,128)(2,1)S(1)} %collective-permute-done.5.refs_6_) | copy-start | bytes 884740
  47.9 54.1 %collective-permute-start.10 = (bf16[2,576,128]{2,1,0:T(8,128)(2,1)}, bf16[2,576,128]{2,1,0:T(8,128)(2,1)S(1)}, u32[]{:S(2)}, u32[]{:S(2)}) collective-permute-start(bf16[2,576,128]{2,1,0:T(8,128)(2,1)} %get-tuple-element.54), channel_id=1, source_target_pairs={{0,6},{1,13},{2,4},{3,15},{4,2},{5,9},{6,0},{7,11},{8,14},{9,5},{1... | collective-permute-start | bytes 884744 | tf_op jit(solution)/shard_map/ppermute | solution.py:438
  49.4 0.7 copy-start.8
  101.9 4.1 %copy-start.12 = (bf16[2,288,128]{2,1,0:T(8,128)(2,1)}, bf16[2,288,128]{2,1,0:T(8,128)(2,1)S(1)}, u32[]{:S(2)}) copy-start(bf16[2,288,128]{2,1,0:T(8,128)(2,1)S(1)} %collective-permute-done.11.refs_5_) | copy-start | bytes 442372
  102.0 4.1 %copy-start.2 = (bf16[2,576,128]{2,1,0:T(8,128)(2,1)}, bf16[2,576,128]{2,1,0:T(8,128)(2,1)S(1)}, u32[]{:S(2)}) copy-start(bf16[2,576,128]{2,1,0:T(8,128)(2,1)S(1)} %collective-permute-done.8.refs_2_) | copy-start | bytes 884740
  102.0 4.1 %copy-start.4 = (bf16[2,576,128]{2,1,0:T(8,128)(2,1)}, bf16[2,576,128]{2,1,0:T(8,128)(2,1)S(1)}, u32[]{:S(2)}) copy-start(bf16[2,576,128]{2,1,0:T(8,128)(2,1)S(1)} %collective-permute-done.9.refs_3_) | copy-start | bytes 884740
  102.0 4.1 %copy-start.5 = (bf16[2,576,128]{2,1,0:T(8,128)(2,1)}, bf16[2,576,128]{2,1,0:T(8,128)(2,1)S(1)}, u32[]{:S(2)}) copy-start(bf16[2,576,128]{2,1,0:T(8,128)(2,1)S(1)} %collective-permute-done.10.refs_4_) | copy-start | bytes 884740
  102.0 4.0 %collective-permute-start.12 = (bf16[2,576,128]{2,1,0:T(8,128)(2,1)S(1)}, bf16[2,576,128]{2,1,0:T(8,128)(2,1)S(1)}, u32[]{:S(2)}, u32[]{:S(2)}) collective-permute-start(bf16[2,576,128]{2,1,0:T(8,128)(2,1)S(1)} %collective-permute-done.8.refs_2_), channel_id=1, source_target_pairs={{0,1},{1,0},{2,3},{3,2},{4,5},{5,4},{6,7},{7,6},{8,9},{9,8},{10,11... | collective-permute-start | bytes 884744 | tf_op jit(solution)/shard_map/ppermute | solution.py:442
  103.7 2.3 %collective-permute-start.13 = (bf16[2,576,128]{2,1,0:T(8,128)(2,1)S(1)}, bf16[2,576,128]{2,1,0:T(8,128)(2,1)S(1)}, u32[]{:S(2)}, u32[]{:S(2)}) collective-permute-start(bf16[2,576,128]{2,1,0:T(8,128)(2,1)S(1)} %collective-permute-done.9.refs_3_), channel_id=1, source_target_pairs={{0,1},{1,0},{2,3},{3,2},{4,5},{5,4},{6,7},{7,6},{8,9},{9,8},{10,11... | collective-permute-start | bytes 884744 | tf_op jit(solution)/shard_map/ppermute | solution.py:442
  103.8 2.2 %collective-permute-start.14 = (bf16[2,576,128]{2,1,0:T(8,128)(2,1)S(1)}, bf16[2,576,128]{2,1,0:T(8,128)(2,1)S(1)}, u32[]{:S(2)}, u32[]{:S(2)}) collective-permute-start(bf16[2,576,128]{2,1,0:T(8,128)(2,1)S(1)} %collective-permute-done.10.refs_4_), channel_id=1, source_target_pairs={{0,1},{1,0},{2,3},{3,2},{4,5},{5,4},{6,7},{7,6},{8,9},{9,8},{10,11... | collective-permute-start | bytes 884744 | tf_op jit(solution)/shard_map/ppermute | solution.py:442
  104.3 1.8 %collective-permute-start.15 = (bf16[2,288,128]{2,1,0:T(8,128)(2,1)S(1)}, bf16[2,288,128]{2,1,0:T(8,128)(2,1)S(1)}, u32[]{:S(2)}, u32[]{:S(2)}) collective-permute-start(bf16[2,288,128]{2,1,0:T(8,128)(2,1)S(1)} %collective-permute-done.11.refs_5_), channel_id=1, source_target_pairs={{0,1},{1,0},{2,3},{3,2},{4,5},{5,4},{6,7},{7,6},{8,9},{9,8},{10,11... | collective-permute-start | bytes 442376 | tf_op jit(solution)/shard_map/ppermute | solution.py:442
  106.0 0.7 copy-start.15
  106.0 0.8 copy-start.9
  106.0 0.9 copy-start.10
  106.0 1.0 copy-start.11

commit v7 on v5

--- a/solution.py
+++ b/solution.py
@@ -31,11 +31,10 @@
     return [(a, b) if i % 2 == 0 else (b, a) for i, (a, b) in enumerate(zip(low, high))]
 
 
-def pack_kernel(capacity, chunks, ids, cache, *refs):
+def pack_kernel(capacity, chunks, spread, ids, cache, *refs):
     dests = ids.shape[0]
     pairs = partners(dests)
-    outs = refs[: len(pairs) + 2]
-    table, rows, sem = refs[len(pairs) + 2 :]
+    outs, (table, rows, sem) = refs[:-3], refs[-3:]
     lat, tokens = rows.shape
     half = lat // 2
     shift = log2(tokens // BLOCK)
@@ -48,7 +47,7 @@
         for slot in range(capacity + 1):
             table[k * (capacity + 1) + slot] = 0
         for j in range(SEL):
-            block = ids[me ^ k, j]
+            block = ids[k if spread else me ^ k, j]
             table[at] = block & ((1 << shift) - 1)
             at = at + (block >> shift == me).astype(jnp.int32)
         table[at] = 0
@@ -64,6 +63,11 @@
         return jnp.where(left, xa, xb).astype(jnp.bfloat16)
 
     copy.wait()
+    if spread:
+        for c, chunk in enumerate(chunks):
+            for d in range(dests):
+                outs[0][d, c] = block_pair(d, chunk, pl.multiple_of(head * half, 32), half)
+        return
     for c, chunk in enumerate(chunks):
         for j, (a, b) in enumerate(pairs):
             outs[j][c] = block_pair(jnp.where(head == 0, a, b), chunk, 0, lat)
@@ -71,20 +75,22 @@
         outs[-1][c] = block_pair(0, chunk, 0, lat)
 
 
-def pack(ids, cache_t, capacity, chunks):
+def pack(ids, cache_t, capacity, chunks, spread=False):
     dests = ids.shape[0]
     lat, tokens = cache_t.shape
     sizes = [lat] * len(partners(dests)) + [lat // 2, lat]
     shapes = [(len(chunks), size, PAIR) for size in sizes]
+    if spread:
+        shapes = [(dests, len(chunks), lat // 2, PAIR)]
 
     packed = pl.pallas_call(
-        functools.partial(pack_kernel, capacity, chunks),
+        functools.partial(pack_kernel, capacity, chunks, spread),
         out_shape=[jax.ShapeDtypeStruct(s, jnp.bfloat16) for s in shapes],
         grid_spec=pltpu.PrefetchScalarGridSpec(
             num_scalar_prefetch=1,
             grid=(1,),
             in_specs=[pl.BlockSpec(memory_space=pl.ANY)],
-            out_specs=[pl.BlockSpec(s, lambda i, *_: (0, 0, 0)) for s in shapes],
+            out_specs=[pl.BlockSpec(s, lambda i, *_, n=len(s): (0,) * n) for s in shapes],
             scratch_shapes=[
                 pltpu.SMEM((dests * (capacity + 1),), jnp.int32),
                 pltpu.VMEM((lat, tokens), jnp.bfloat16),
@@ -170,6 +176,13 @@
         pairs = partners(owners)
         count = len(pairs)
         head, me = lax.axis_index("head"), lax.axis_index("ctx")
+        if len(arrays) == 2:
+            _, self.chunks, half, _ = arrays[0].shape
+            starts = [pl.multiple_of(h * half, 32) for h in (head, 1 - head)]
+            self.parts = [
+                (o, [(x.at[o], start, half) for x, start in zip(arrays, starts)]) for o in range(owners)
+            ]
+            return
         got, shared, own = arrays[:count], arrays[count], arrays[count + 1]
         swapped, shared_other = arrays[count + 2 : 2 * count + 2], arrays[2 * count + 2]
         self.chunks, lat, _ = own.shape
@@ -355,7 +368,7 @@
     pairs = len(pair_places(owners, chunks, kind in ("first", "only")))
     keys = pairs * PAIR
     levels = [n for n in (4, 5, 6, 8) if n < pairs] + [pairs]
-    sub = 1024 if keys <= 2048 and rows % 2048 == 0 else 512
+    sub = 512
     step = 2 * sub
     out_shape = [jax.ShapeDtypeStruct((rows, KVL), jnp.float32), jax.ShapeDtypeStruct((rows, PAIR), jnp.float32)]
     if kind in ("last", "only"):
@@ -405,7 +418,7 @@
         jnp.broadcast_to(block_ids, (owners, SEL)), "ctx", split_axis=0, concat_axis=0, tiled=True
     )
     phases = split_phases(capacity // 2)
-    packed = [pack(lists, latent_cache.T, capacity, phase) for phase in phases]
+    packed = pack(lists, latent_cache.T, capacity, phases[0])
     table, *biases = plan(block_ids[0], owners, capacity, shift, phases)
     steps = partners(owners) + [(owners - 1, owners - 1)]
 
@@ -420,20 +433,19 @@
         return [lax.ppermute(x, "head", [(0, 1), (1, 0)]) for x in got]
 
     q = queries.reshape(rows, lat)
-    got = [send(packed[0])]
-    for own in packed[1:]:
-        both = lax.optimization_barrier((*got[-1], *own[:-1], table))
-        got[-1], own[:-1], table = list(both[: len(got[-1])]), both[len(got[-1]) : -1], both[-1]
-        got.append(send(own))
-    state = []
-    for p, phase in enumerate(phases):
-        late = got[p]
-        if state:
-            *late, logs = lax.optimization_barrier((*late, state[1]))
-            state = [state[0], logs]
-        arrays = [*late, packed[p][-1], *swap(late)]
-        kind = "only" if len(phases) == 1 else "first" if p == 0 else "last" if p == len(phases) - 1 else "middle"
-        state = attend(table, positions, q, biases[p], state, arrays, owners, capacity, kind, len(phase))
+    got = send(packed)
+    if len(phases) == 1:
+        arrays = [*got, packed[-1], *swap(got)]
+        state = attend(table, positions, q, biases[0], [], arrays, owners, capacity, "only", len(phases[0]))
+        return state[0].reshape(q_rows, heads, KVL)
+    (more,) = pack(lists, latent_cache.T, capacity, phases[1], spread=True)
+    *got, more, table = lax.optimization_barrier((*got, more, table))
+    late = lax.all_to_all(more, "ctx", split_axis=0, concat_axis=0, tiled=True)
+    arrays = [*got, packed[-1], *swap(got)]
+    carry, logs = attend(table, positions, q, biases[0], [], arrays, owners, capacity, "first", len(phases[0]))
+    late, logs = lax.optimization_barrier((late, logs))
+    arrays = [late, *swap([late])]
+    state = attend(table, positions, q, biases[1], [carry, logs], arrays, owners, capacity, "last", len(phases[1]))
     return state[0].reshape(q_rows, heads, KVL)
 
 

time: 116 us -> 102 us (0.88)
  the two profiles are of different devices: /device:TPU:11 before, /device:TPU:0 now
where the time goes in v7:
time: 102 us; the launch traced here: 100 us
  Pallas kernels  55.4 us (54%)
  starting transfers between devices  15.7 us (15%)
  blocking collectives  13.5 us (13%)
  waiting for transfers between devices  13 us (13%)
  local copies, waits for them, and re-layouts  2.64 us (3%)
    pallas_call x2, Pallas kernels, attend(): pl.pallas_call(functools.partial(attend_kernel, owners, capacity, kind, l...  44.1 us
    all_to_all x1, blocking collectives, local(): lax.all_to_all(jnp.broadcast_to(block_ids, (owners, SEL)), 'ctx', split_a...  13.5 us
    pallas_call x2, Pallas kernels, pack(): pl.pallas_call(functools.partial(pack_kernel, capacity, chunks, spread),...  9.79 us
    ppermute x4, waiting for transfers between devices, send(): got.append(lax.ppermute(x, ('ctx', 'head'), moves))  8.8 us
    ppermute x4, starting transfers between devices, send(): got.append(lax.ppermute(x, ('ctx', 'head'), moves))  6.81 us
    all_to_all x1, starting transfers between devices, local(): late = lax.all_to_all(more, 'ctx', split_axis=0, concat_axis=0, tiled=True)  5.95 us
    ppermute x5, waiting for transfers between devices, swap(): return [lax.ppermute(x, 'head', [(0, 1), (1, 0)]) for x in got]  4.16 us
    ppermute x5, starting transfers between devices, swap(): return [lax.ppermute(x, 'head', [(0, 1), (1, 0)]) for x in got]  2.94 us
  transfers between devices with their start and end apart: 10, of which 4 were waited for; matrix products, arithmetic and copies ran while one was open for 0% of the time, Pallas kernels for 37%

profile of v7, /device:TPU:0, one launch (start us, length us, event | category | flops | bytes accessed | tf_op | source)
XLA Modules:
  0.0 100.3 jit_solution(3150494608270854547)
XLA Ops:
  0.0 0.7 broadcast_in_dim.2
  0.7 13.5 %all_to_all.13 = s32[8,1,32]{2,1,0:T(1,128)} all-to-all(s32[8,1,32]{2,1,0:T(1,128)S(1)} %broadcast_in_dim.2), channel_id=1, replica_groups=mesh['groups'=2,'ctx'=8,'head'=2] {'ctx'}, dimensions={0} | all-to-all | bytes 2048 | tf_op jit(solution)/shard_map/all_to_all | solution.py:417
  14.1 4.9 %pack.2 = (bf16[2,576,128]{2,1,0:T(8,128)(2,1)}, bf16[2,576,128]{2,1,0:T(8,128)(2,1)}, bf16[2,576,128]{2,1,0:T(8,128)(2,1)}, bf16[2,288,128]{2,1,0:T(8,128)(2,1)}, bf16[2,576,128]{2,1,0:T(8,128)(2,1)}) custom-call(s32[8,32]{1,0:T(8,128)} %bitcast.7, bf16[576,4096]{1,0:T(8,128)(2,1)} %bitcast.5), custom_call_target="tpu_custom_call" | custom-call | bytes 18874368 | tf_op jit(solution)/shard_map/pack/pallas_call | solution.py:86
  19.1 0.6 collective-permute-start
  19.7 1.5 %collective-permute-start.1 = (bf16[2,576,128]{2,1,0:T(8,128)(2,1)}, bf16[2,576,128]{2,1,0:T(8,128)(2,1)S(1)}, u32[]{:S(2)}, u32[]{:S(2)}) collective-permute-start(bf16[2,576,128]{2,1,0:T(8,128)(2,1)} %get-tuple-element.24), channel_id=1, source_target_pairs={{0,10},{1,5},{2,8},{3,7},{4,14},{5,1},{6,12},{7,3},{8,2},{9,13},{1... | collective-permute-start | bytes 884744 | tf_op jit(solution)/shard_map/ppermute | solution.py:429
  21.2 0.7 collective-permute-start.2
  21.9 4.0 %collective-permute-start.3 = (bf16[2,288,128]{2,1,0:T(8,128)(2,1)}, bf16[2,288,128]{2,1,0:T(8,128)(2,1)S(1)}, u32[]{:S(2)}, u32[]{:S(2)}) collective-permute-start(bf16[2,288,128]{2,1,0:T(8,128)(2,1)} %get-tuple-element.26), channel_id=1, source_target_pairs={{0,14},{1,15},{2,12},{3,13},{4,10},{5,11},{6,8},{7,9},{8,6},{9,7},... | collective-permute-start | bytes 442376 | tf_op jit(solution)/shard_map/ppermute | solution.py:429
  25.9 1.6 %plan.1 = (s32[81]{0:T(128)}, f32[8,1920]{1,0:T(8,128)}, f32[8,1920]{1,0:T(8,128)}) custom-call(s32[32]{0:T(128)} %bitcast.10), custom_call_target="tpu_custom_call" | custom-call | bytes 1048576 | tf_op jit(solution)/shard_map/plan/pallas_call | solution.py:158
  27.5 4.9 %pack.3 = bf16[8,2,288,128]{3,2,1,0:T(8,128)(2,1)} custom-call(s32[8,32]{1,0:T(8,128)} %bitcast.8, bf16[576,4096]{1,0:T(8,128)(2,1)} %bitcast.6), custom_call_target="tpu_custom_call" | custom-call | bytes 18874368 | tf_op jit(solution)/shard_map/pack/pallas_call | solution.py:86
  32.3 8.1 %collective-permute-done.3.refs_3_ = bf16[2,288,128]{2,1,0:T(8,128)(2,1)S(1)} collective-permute-done((bf16[2,288,128]{2,1,0:T(8,128)(2,1)}, bf16[2,288,128]{2,1,0:T(8,128)(2,1)S(1)}, u32[]{:S(2)}, u32[]{:S(2)}) %collective-permute-start.3) | collective-permute-done | bytes 147488 | tf_op jit(solution)/shard_map/ppermute | solution.py:429
  40.5 0.0 copy-start.8
  40.5 0.0 collective-permute-done.refs_0_
  40.5 0.0 copy-start.2
  40.5 0.7 collective-permute-done.1.refs_1_
  41.1 0.0 copy-start.3
  41.1 0.0 collective-permute-done.2.refs_2_
  41.2 0.0 copy-start.4
  41.2 5.9 %all-to-all-start.1 = ((bf16[8,2,288,128]{3,2,1,0:T(8,128)(2,1)}), bf16[8,2,288,128]{3,2,1,0:T(8,128)(2,1)S(1)}, u32[]{:S(2)}, u32[]{:S(2)}) async-start(bf16[8,2,288,128]{3,2,1,0:T(8,128)(2,1)} %pack.3), calls=%async_computation.1 | async-start | bytes 2359296 | tf_op jit(solution)/shard_map/all_to_all | solution.py:443
  47.1 1.9 %collective-permute-start.4 = (bf16[2,576,128]{2,1,0:T(8,128)(2,1)S(1)}, bf16[2,576,128]{2,1,0:T(8,128)(2,1)S(1)}, u32[]{:S(2)}, u32[]{:S(2)}) collective-permute-start(bf16[2,576,128]{2,1,0:T(8,128)(2,1)S(1)} %collective-permute-done.refs_0_), channel_id=1, source_target_pairs={{0,1},{1,0},{2,3},{3,2},{4,5},{5,4},{6,7},{7,6},{8,9},{9,8},{10,11... | collective-permute-start | bytes 884744 | tf_op jit(solution)/shard_map/ppermute | solution.py:433
  49.0 0.1 collective-permute-start.5
  49.1 0.4 collective-permute-start.6
  49.5 0.1 collective-permute-start.7
  49.6 1.7 %collective-permute-done.7.refs_8_ = bf16[2,288,128]{2,1,0:T(8,128)(2,1)S(1)} collective-permute-done((bf16[2,288,128]{2,1,0:T(8,128)(2,1)S(1)}, bf16[2,288,128]{2,1,0:T(8,128)(2,1)S(1)}, u32[]{:S(2)}, u32[]{:S(2)}) %collective-permute-start.7) | collective-permute-done | bytes 147488 | tf_op jit(solution)/shard_map/ppermute | solution.py:433
  51.3 0.0 copy-start.9
  51.3 0.0 collective-permute-done.4.refs_5_
  51.3 0.0 copy-start.5
  51.3 0.0 collective-permute-done.5.refs_6_
  51.3 0.0 copy-start.6
  51.3 0.0 collective-permute-done.6.refs_7_
  51.3 0.0 copy-start.7
  51.3 0.0 copy-done.8
  51.3 0.0 copy-done.2
  51.3 0.0 copy-done.3
  51.4 0.0 copy-done.4
  51.4 0.6 copy-done.9
  51.9 0.1 copy-done.5
  52.1 0.1 copy-done.6
  52.2 0.1 copy-done.7
  52.3 30.3 %attend_first.1 = (f32[4096,512]{1,0:T(8,128)}, f32[4096,128]{1,0:T(8,128)}) custom-call(s32[81]{0:T(128)} %get-tuple-element.28.table, s32[64]{0:T(128)} %pos.3, bf16[4096,576]{1,0:T(8,128)(2,1)} %bitcast.11, f32[8,1920]{1,0:T(8,128)} %get-tuple-element.30.bias, bf16[2,576,128]{2,1,0:T(8,128)(2,1)} %copy-done.2, bf16[2,576,128]{2,1,0:T(8,128)(2,1)} %copy-done.3, ...), custom_call_target="tpu_custom_call" | custom-call | flops 17112760320 | bytes 13107200 | tf_op jit(solution)/shard_map/attend_first/pallas_call | solution.py:383
  82.5 0.0 all-to-all-done.1.refs_2_
  82.5 0.0 copy-start
  82.5 0.4 collective-permute-start.8
  83.0 2.5 %collective-permute-done.8.refs_3_ = bf16[8,2,288,128]{3,2,1,0:T(8,128)(2,1)S(1)} collective-permute-done((bf16[8,2,288,128]{3,2,1,0:T(8,128)(2,1)S(1)}, bf16[8,2,288,128]{3,2,1,0:T(8,128)(2,1)S(1)}, u32[]{:S(2)}, u32[]{:S(2)}) %collective-permute-start.8) | collective-permute-done | bytes 1179680 | tf_op jit(solution)/shard_map/ppermute | solution.py:433
  85.5 0.0 copy-start.1
  85.5 0.0 copy-done
  85.5 1.1 %copy-done.1 = bf16[8,2,288,128]{3,2,1,0:T(8,128)(2,1)} copy-done((bf16[8,2,288,128]{3,2,1,0:T(8,128)(2,1)}, bf16[8,2,288,128]{3,2,1,0:T(8,128)(2,1)S(1)}, u32[]{:S(2)}) %copy-start.1) | copy-done | bytes 1179672
  86.5 13.8 %attend_last.1 = bf16[4096,512]{1,0:T(8,128)(2,1)} custom-call(s32[81]{0:T(128)} %get-tuple-element.28.table, s32[64]{0:T(128)} %pos.3, bf16[4096,576]{1,0:T(8,128)(2,1)} %bitcast.12, f32[8,1920]{1,0:T(8,128)} %get-tuple-element.29.bias, f32[4096,512]{1,0:T(8,128)} %get-tuple-element.36.refs_0_, f32[4096,128]{1,0:T(8,128)} %get-tuple-element.39.refs_1_, ...), custom_call_target="tpu_custom_call" | custom-call | flops 15971909632 | bytes 13107200 | tf_op jit(solution)/shard_map/attend_last/pallas_call | solution.py:383
Async XLA Ops:
  19.1 21.4 %collective-permute-start = (bf16[2,576,128]{2,1,0:T(8,128)(2,1)}, bf16[2,576,128]{2,1,0:T(8,128)(2,1)S(1)}, u32[]{:S(2)}, u32[]{:S(2)}) collective-permute-start(bf16[2,576,128]{2,1,0:T(8,128)(2,1)} %get-tuple-element.23), channel_id=1, source_target_pairs={{0,2},{1,9},{2,0},{3,11},{4,6},{5,13},{6,4},{7,15},{8,10},{9,1},{1... | collective-permute-start | bytes 884744 | tf_op jit(solution)/shard_map/ppermute | solution.py:429
  19.7 21.4 %collective-permute-start.1 = (bf16[2,576,128]{2,1,0:T(8,128)(2,1)}, bf16[2,576,128]{2,1,0:T(8,128)(2,1)S(1)}, u32[]{:S(2)}, u32[]{:S(2)}) collective-permute-start(bf16[2,576,128]{2,1,0:T(8,128)(2,1)} %get-tuple-element.24), channel_id=1, source_target_pairs={{0,10},{1,5},{2,8},{3,7},{4,14},{5,1},{6,12},{7,3},{8,2},{9,13},{1... | collective-permute-start | bytes 884744 | tf_op jit(solution)/shard_map/ppermute | solution.py:429
  21.2 20.0 %collective-permute-start.2 = (bf16[2,576,128]{2,1,0:T(8,128)(2,1)}, bf16[2,576,128]{2,1,0:T(8,128)(2,1)S(1)}, u32[]{:S(2)}, u32[]{:S(2)}) collective-permute-start(bf16[2,576,128]{2,1,0:T(8,128)(2,1)} %get-tuple-element.25), channel_id=1, source_target_pairs={{0,6},{1,13},{2,4},{3,15},{4,2},{5,9},{6,0},{7,11},{8,14},{9,5},{1... | collective-permute-start | bytes 884744 | tf_op jit(solution)/shard_map/ppermute | solution.py:429
  21.9 18.6 %collective-permute-start.3 = (bf16[2,288,128]{2,1,0:T(8,128)(2,1)}, bf16[2,288,128]{2,1,0:T(8,128)(2,1)S(1)}, u32[]{:S(2)}, u32[]{:S(2)}) collective-permute-start(bf16[2,288,128]{2,1,0:T(8,128)(2,1)} %get-tuple-element.26), channel_id=1, source_target_pairs={{0,14},{1,15},{2,12},{3,13},{4,10},{5,11},{6,8},{7,9},{8,6},{9,7},... | collective-permute-start | bytes 442376 | tf_op jit(solution)/shard_map/ppermute | solution.py:429
  40.5 10.9 %copy-start.8 = (bf16[2,288,128]{2,1,0:T(8,128)(2,1)}, bf16[2,288,128]{2,1,0:T(8,128)(2,1)S(1)}, u32[]{:S(2)}) copy-start(bf16[2,288,128]{2,1,0:T(8,128)(2,1)S(1)} %collective-permute-done.3.refs_3_) | copy-start | bytes 442372
  40.5 10.9 %copy-start.2 = (bf16[2,576,128]{2,1,0:T(8,128)(2,1)}, bf16[2,576,128]{2,1,0:T(8,128)(2,1)S(1)}, u32[]{:S(2)}) copy-start(bf16[2,576,128]{2,1,0:T(8,128)(2,1)S(1)} %collective-permute-done.refs_0_) | copy-start | bytes 884740
  41.1 10.2 %copy-start.3 = (bf16[2,576,128]{2,1,0:T(8,128)(2,1)}, bf16[2,576,128]{2,1,0:T(8,128)(2,1)S(1)}, u32[]{:S(2)}) copy-start(bf16[2,576,128]{2,1,0:T(8,128)(2,1)S(1)} %collective-permute-done.1.refs_1_) | copy-start | bytes 884740
  41.2 10.2 %copy-start.4 = (bf16[2,576,128]{2,1,0:T(8,128)(2,1)}, bf16[2,576,128]{2,1,0:T(8,128)(2,1)S(1)}, u32[]{:S(2)}) copy-start(bf16[2,576,128]{2,1,0:T(8,128)(2,1)S(1)} %collective-permute-done.2.refs_2_) | copy-start | bytes 884740
  41.2 41.4 %all-to-all-start.1 = ((bf16[8,2,288,128]{3,2,1,0:T(8,128)(2,1)}), bf16[8,2,288,128]{3,2,1,0:T(8,128)(2,1)S(1)}, u32[]{:S(2)}, u32[]{:S(2)}) async-start(bf16[8,2,288,128]{3,2,1,0:T(8,128)(2,1)} %pack.3), calls=%async_computation.1 | async-start | bytes 2359296 | tf_op jit(solution)/shard_map/all_to_all | solution.py:443
  47.1 4.2 %collective-permute-start.4 = (bf16[2,576,128]{2,1,0:T(8,128)(2,1)S(1)}, bf16[2,576,128]{2,1,0:T(8,128)(2,1)S(1)}, u32[]{:S(2)}, u32[]{:S(2)}) collective-permute-start(bf16[2,576,128]{2,1,0:T(8,128)(2,1)S(1)} %collective-permute-done.refs_0_), channel_id=1, source_target_pairs={{0,1},{1,0},{2,3},{3,2},{4,5},{5,4},{6,7},{7,6},{8,9},{9,8},{10,11... | collective-permute-start | bytes 884744 | tf_op jit(solution)/shard_map/ppermute | solution.py:433
  49.0 2.3 %collective-permute-start.5 = (bf16[2,576,128]{2,1,0:T(8,128)(2,1)S(1)}, bf16[2,576,128]{2,1,0:T(8,128)(2,1)S(1)}, u32[]{:S(2)}, u32[]{:S(2)}) collective-permute-start(bf16[2,576,128]{2,1,0:T(8,128)(2,1)S(1)} %collective-permute-done.1.refs_1_), channel_id=1, source_target_pairs={{0,1},{1,0},{2,3},{3,2},{4,5},{5,4},{6,7},{7,6},{8,9},{9,8},{10,11... | collective-permute-start | bytes 884744 | tf_op jit(solution)/shard_map/ppermute | solution.py:433
  49.1 2.2 %collective-permute-start.6 = (bf16[2,576,128]{2,1,0:T(8,128)(2,1)S(1)}, bf16[2,576,128]{2,1,0:T(8,128)(2,1)S(1)}, u32[]{:S(2)}, u32[]{:S(2)}) collective-permute-start(bf16[2,576,128]{2,1,0:T(8,128)(2,1)S(1)} %collective-permute-done.2.refs_2_), channel_id=1, source_target_pairs={{0,1},{1,0},{2,3},{3,2},{4,5},{5,4},{6,7},{7,6},{8,9},{9,8},{10,11... | collective-permute-start | bytes 884744 | tf_op jit(solution)/shard_map/ppermute | solution.py:433
  49.5 1.8 %collective-permute-start.7 = (bf16[2,288,128]{2,1,0:T(8,128)(2,1)S(1)}, bf16[2,288,128]{2,1,0:T(8,128)(2,1)S(1)}, u32[]{:S(2)}, u32[]{:S(2)}) collective-permute-start(bf16[2,288,128]{2,1,0:T(8,128)(2,1)S(1)} %collective-permute-done.3.refs_3_), channel_id=1, source_target_pairs={{0,1},{1,0},{2,3},{3,2},{4,5},{5,4},{6,7},{7,6},{8,9},{9,8},{10,11... | collective-permute-start | bytes 442376 | tf_op jit(solution)/shard_map/ppermute | solution.py:433
  51.3 0.7 copy-start.9
  51.3 0.8 copy-start.5
  51.3 0.9 copy-start.6
  51.3 0.9 copy-start.7
  82.5 2.9 %copy-start = (bf16[8,2,288,128]{3,2,1,0:T(8,128)(2,1)}, bf16[8,2,288,128]{3,2,1,0:T(8,128)(2,1)S(1)}, u32[]{:S(2)}) copy-start(bf16[8,2,288,128]{3,2,1,0:T(8,128)(2,1)S(1)} %all-to-all-done.1.refs_2_) | copy-start | bytes 3538948
  82.5 2.9 %collective-permute-start.8 = (bf16[8,2,288,128]{3,2,1,0:T(8,128)(2,1)S(1)}, bf16[8,2,288,128]{3,2,1,0:T(8,128)(2,1)S(1)}, u32[]{:S(2)}, u32[]{:S(2)}) collective-permute-start(bf16[8,2,288,128]{3,2,1,0:T(8,128)(2,1)S(1)} %all-to-all-done.1.refs_2_), channel_id=1, source_target_pairs={{0,1},{1,0},{2,3},{3,2},{4,5},{5,4},{6,7},{7,6},{8,9},{9,8},{10,11... | collective-permute-start | bytes 3538952 | tf_op jit(solution)/shard_map/ppermute | solution.py:433
  85.5 1.1 %copy-start.1 = (bf16[8,2,288,128]{3,2,1,0:T(8,128)(2,1)}, bf16[8,2,288,128]{3,2,1,0:T(8,128)(2,1)S(1)}, u32[]{:S(2)}) copy-start(bf16[8,2,288,128]{3,2,1,0:T(8,128)(2,1)S(1)} %collective-permute-done.8.refs_3_) | copy-start | bytes 3538948

commit v8 on v7

--- a/solution.py
+++ b/solution.py
@@ -56,32 +56,33 @@
         first = k * (capacity + 1) + 2 * chunk
         a, b = table[first], table[first + 1]
         left = lax.broadcasted_iota(jnp.int32, (size, PAIR), 1) < BLOCK
-        xa = rows[pl.ds(start, size), pl.ds(pl.multiple_of((a >> 1) * PAIR, PAIR), PAIR)].astype(jnp.float32)
-        xb = rows[pl.ds(start, size), pl.ds(pl.multiple_of((b >> 1) * PAIR, PAIR), PAIR)].astype(jnp.float32)
-        xa = pltpu.roll(xa, (a & 1) * BLOCK, 1)
-        xb = pltpu.roll(xb, (1 - (b & 1)) * BLOCK, 1)
-        return jnp.where(left, xa, xb).astype(jnp.bfloat16)
+        xa = rows[pl.ds(start, size), pl.ds(pl.multiple_of((a >> 1) * PAIR, PAIR), PAIR)]
+        xb = rows[pl.ds(start, size), pl.ds(pl.multiple_of((b >> 1) * PAIR, PAIR), PAIR)]
+        xa = jnp.where((a & 1) == 0, xa, pltpu.roll(xa, BLOCK, 1))
+        xb = jnp.where((b & 1) == 1, xb, pltpu.roll(xb, BLOCK, 1))
+        return jnp.where(left, xa, xb)
 
     copy.wait()
     if spread:
+        for c, chunk in enumerate(spread):
+            outs[0][c] = block_pair(me, chunk, 0, lat)
         for c, chunk in enumerate(chunks):
             for d in range(dests):
-                outs[0][d, c] = block_pair(d, chunk, pl.multiple_of(head * half, 32), half)
+                outs[1][d, c] = block_pair(d, chunk, pl.multiple_of(head * half, 32), half)
         return
     for c, chunk in enumerate(chunks):
         for j, (a, b) in enumerate(pairs):
             outs[j][c] = block_pair(jnp.where(head == 0, a, b), chunk, 0, lat)
-        outs[-2][c] = block_pair(dests - 1, chunk, pl.multiple_of(head * half, 32), half)
-        outs[-1][c] = block_pair(0, chunk, 0, lat)
-
-
-def pack(ids, cache_t, capacity, chunks, spread=False):
+        outs[-1][c] = block_pair(dests - 1, chunk, pl.multiple_of(head * half, 32), half)
+
+
+def pack(ids, cache_t, capacity, chunks, spread=None):
     dests = ids.shape[0]
     lat, tokens = cache_t.shape
-    sizes = [lat] * len(partners(dests)) + [lat // 2, lat]
+    sizes = [lat] * len(partners(dests)) + [lat // 2]
     shapes = [(len(chunks), size, PAIR) for size in sizes]
     if spread:
-        shapes = [(dests, len(chunks), lat // 2, PAIR)]
+        shapes = [(len(spread), lat, PAIR)] + ([(dests, len(chunks), lat // 2, PAIR)] if chunks else [])
 
     packed = pl.pallas_call(
         functools.partial(pack_kernel, capacity, chunks, spread),
@@ -395,7 +396,7 @@
                 *[pltpu.VMEM((sub, PAIR), jnp.float32)] * 4,
             ],
         ),
-        compiler_params=pltpu.CompilerParams(vmem_limit_bytes=VMEM),
+        compiler_params=pltpu.CompilerParams(vmem_limit_bytes=min(VMEM, (18 << 20) + keys * 10240)),
         cost_estimate=pl.CostEstimate(
             flops=2 * rows * keys * (lat + KVL), bytes_accessed=rows * (lat + 2 * KVL) * 2, transcendentals=rows * keys
         ),
@@ -435,13 +436,16 @@
     q = queries.reshape(rows, lat)
     got = send(packed)
     if len(phases) == 1:
-        arrays = [*got, packed[-1], *swap(got)]
+        (own,) = pack(lists, latent_cache.T, capacity, [], spread=phases[0])
+        arrays = [*got, own, *swap(got)]
         state = attend(table, positions, q, biases[0], [], arrays, owners, capacity, "only", len(phases[0]))
         return state[0].reshape(q_rows, heads, KVL)
-    (more,) = pack(lists, latent_cache.T, capacity, phases[1], spread=True)
+    *own, more = pack(lists, latent_cache.T, capacity, phases[1], spread=phases[0])
+    got[-1], more = lax.optimization_barrier((got[-1], more))
+    swapped = swap(got)
     *got, more, table = lax.optimization_barrier((*got, more, table))
     late = lax.all_to_all(more, "ctx", split_axis=0, concat_axis=0, tiled=True)
-    arrays = [*got, packed[-1], *swap(got)]
+    arrays = [*got, *own, *swapped]
     carry, logs = attend(table, positions, q, biases[0], [], arrays, owners, capacity, "first", len(phases[0]))
     late, logs = lax.optimization_barrier((late, logs))
     arrays = [late, *swap([late])]

time: 102 us -> 108 us (1.059)
  the two profiles are of different devices: /device:TPU:0 before, /device:TPU:11 now
where the time goes in v8:
time: 108 us; the launch traced here: 107 us
  Pallas kernels  53.7 us (50%)
  waiting for transfers between devices  22.8 us (21%)
  local copies, waits for them, and re-layouts  12.9 us (12%)
  blocking collectives  9.57 us (9%)
  starting transfers between devices  7.87 us (7%)
    pallas_call x2, Pallas kernels, attend(): pl.pallas_call(functools.partial(attend_kernel, owners, capacity, kind, l...  41.3 us
    ppermute x4, waiting for transfers between devices, send(): got.append(lax.ppermute(x, ('ctx', 'head'), moves))  18.4 us
    unnamed x20, local copies, waits for them, and re-layouts  12.2 us
    pallas_call x2, Pallas kernels, pack(): pl.pallas_call(functools.partial(pack_kernel, capacity, chunks, spread),...  10.8 us
    all_to_all x1, blocking collectives, local(): lax.all_to_all(jnp.broadcast_to(block_ids, (owners, SEL)), 'ctx', split_a...  9.57 us
    ppermute x5, waiting for transfers between devices, swap(): return [lax.ppermute(x, 'head', [(0, 1), (1, 0)]) for x in got]  4.34 us
    all_to_all x1, starting transfers between devices, local(): late = lax.all_to_all(more, 'ctx', split_axis=0, concat_axis=0, tiled=True)  3.53 us
    ppermute x4, starting transfers between devices, send(): got.append(lax.ppermute(x, ('ctx', 'head'), moves))  3.14 us
  transfers between devices with their start and end apart: 10, of which 3 were waited for; matrix products, arithmetic and copies ran while one was open for 0% of the time, Pallas kernels for 34%

profile of v8, /device:TPU:11, one launch (start us, length us, event | category | flops | bytes accessed | tf_op | source)
XLA Modules:
  0.0 107.0 jit_solution(2945497573497265631)
XLA Ops:
  0.0 0.7 broadcast_in_dim.2
  0.7 9.6 %all_to_all.13 = s32[8,1,32]{2,1,0:T(1,128)} all-to-all(s32[8,1,32]{2,1,0:T(1,128)S(1)} %broadcast_in_dim.2), channel_id=1, replica_groups=mesh['groups'=2,'ctx'=8,'head'=2] {'ctx'}, dimensions={0} | all-to-all | bytes 2048 | tf_op jit(solution)/shard_map/all_to_all | solution.py:418
  10.2 5.0 %pack.2 = (bf16[2,576,128]{2,1,0:T(8,128)(2,1)}, bf16[2,576,128]{2,1,0:T(8,128)(2,1)}, bf16[2,576,128]{2,1,0:T(8,128)(2,1)}, bf16[2,288,128]{2,1,0:T(8,128)(2,1)}) custom-call(s32[8,32]{1,0:T(8,128)} %bitcast.9, bf16[576,4096]{1,0:T(8,128)(2,1)} %bitcast.7), custom_call_target="tpu_custom_call" | custom-call | bytes 18874368 | tf_op jit(solution)/shard_map/pack/pallas_call | solution.py:87
  15.2 0.0 copy-start.3
  15.2 0.5 collective-permute-start
  15.7 1.0 collective-permute-start.1
  16.8 1.2 %collective-permute-start.2 = (bf16[2,576,128]{2,1,0:T(8,128)(2,1)}, bf16[2,576,128]{2,1,0:T(8,128)(2,1)S(1)}, u32[]{:S(2)}, u32[]{:S(2)}) collective-permute-start(bf16[2,576,128]{2,1,0:T(8,128)(2,1)} %get-tuple-element.28), channel_id=1, source_target_pairs={{0,6},{1,13},{2,4},{3,15},{4,2},{5,9},{6,0},{7,11},{8,14},{9,5},{1... | collective-permute-start | bytes 884744 | tf_op jit(solution)/shard_map/ppermute | solution.py:430
  17.9 0.4 collective-permute-start.3
  18.4 1.6 %plan.1 = (s32[81]{0:T(128)}, f32[8,1920]{1,0:T(8,128)}, f32[8,1920]{1,0:T(8,128)}) custom-call(s32[32]{0:T(128)} %bitcast.12), custom_call_target="tpu_custom_call" | custom-call | bytes 1048576 | tf_op jit(solution)/shard_map/plan/pallas_call | solution.py:159
  19.9 0.0 copy-start.5
  20.0 0.0 copy-start.6
  20.0 5.9 %pack.3 = (bf16[2,576,128]{2,1,0:T(8,128)(2,1)}, bf16[8,2,288,128]{3,2,1,0:T(8,128)(2,1)}) custom-call(s32[8,32]{1,0:T(8,128)} %bitcast.10, bf16[576,4096]{1,0:T(8,128)(2,1)} %bitcast.8), custom_call_target="tpu_custom_call" | custom-call | bytes 18874368 | tf_op jit(solution)/shard_map/pack/pallas_call | solution.py:87
  25.8 18.4 %collective-permute-done.3.refs_3_ = bf16[2,288,128]{2,1,0:T(8,128)(2,1)S(1)} collective-permute-done((bf16[2,288,128]{2,1,0:T(8,128)(2,1)}, bf16[2,288,128]{2,1,0:T(8,128)(2,1)S(1)}, u32[]{:S(2)}, u32[]{:S(2)}) %collective-permute-start.3) | collective-permute-done | bytes 147488 | tf_op jit(solution)/shard_map/ppermute | solution.py:430
  44.2 0.0 collective-permute-done.refs_0_
  44.3 0.0 collective-permute-done.1.refs_1_
  44.3 0.0 collective-permute-done.2.refs_2_
  44.3 3.5 %all-to-all-start.1 = ((bf16[8,2,288,128]{3,2,1,0:T(8,128)(2,1)}), bf16[8,2,288,128]{3,2,1,0:T(8,128)(2,1)S(1)}, u32[]{:S(2)}, u32[]{:S(2)}) async-start(bf16[8,2,288,128]{3,2,1,0:T(8,128)(2,1)} %get-tuple-element.43), calls=%async_computation.1 | async-start | bytes 2359296 | tf_op jit(solution)/shard_map/all_to_all | solution.py:447
  47.8 0.1 collective-permute-start.4
  47.9 0.5 collective-permute-start.5
  48.4 0.1 collective-permute-start.6
  48.5 0.4 collective-permute-start.7
  48.9 1.6 %collective-permute-done.7.refs_8_ = bf16[2,288,128]{2,1,0:T(8,128)(2,1)S(1)} collective-permute-done((bf16[2,288,128]{2,1,0:T(8,128)(2,1)S(1)}, bf16[2,288,128]{2,1,0:T(8,128)(2,1)S(1)}, u32[]{:S(2)}, u32[]{:S(2)}) %collective-permute-start.7) | collective-permute-done | bytes 147488 | tf_op jit(solution)/shard_map/ppermute | solution.py:434
  50.5 0.0 collective-permute-done.4.refs_5_
  50.5 0.0 collective-permute-done.5.refs_6_
  50.5 0.0 collective-permute-done.6.refs_7_
  50.5 0.0 copy-done.3
  50.5 0.0 copy-done.5
  50.5 0.0 copy-done.6
  50.5 0.0 copy-start
  50.6 2.5 %copy-done = bf16[64,64,576]{2,1,0:T(8,128)(2,1)S(1)} copy-done((bf16[64,64,576]{2,1,0:T(8,128)(2,1)S(1)}, bf16[64,64,576]{2,1,0:T(8,128)(2,1)}, u32[]{:S(2)}) %copy-start) | copy-done | bytes 4718616
  53.0 0.0 copy-start.2
  53.0 1.0 copy-done.2
  54.0 0.0 copy-start.4
  54.0 28.5 %attend_first.1 = (f32[4096,512]{1,0:T(8,128)}, f32[4096,128]{1,0:T(8,128)S(1)}) custom-call(s32[81]{0:T(128)S(1)} %copy-done.6, s32[64]{0:T(128)S(1)} %copy-done.3, bf16[4096,576]{1,0:T(8,128)(2,1)S(1)} %bitcast.5, f32[8,1920]{1,0:T(8,128)S(1)} %copy-done.5, bf16[2,576,128]{2,1,0:T(8,128)(2,1)S(1)} %collective-permute-done.refs_0_, ...), custom_call_target="tpu_custom_call" | custom-call | flops 17112760320 | bytes 13107200 | tf_op jit(solution)/shard_map/attend_first/pallas_call | solution.py:384
  82.5 0.0 copy-start.8
  82.5 1.3 %copy-done.8 = f32[4096,128]{1,0:T(8,128)} copy-done((f32[4096,128]{1,0:T(8,128)}, f32[4096,128]{1,0:T(8,128)S(1)}, u32[]{:S(2)}) %copy-start.8) | copy-done | bytes 2097176
  83.8 0.0 all-to-all-done.1.refs_2_
  83.8 0.1 collective-permute-start.8
  83.9 2.7 %collective-permute-done.8.refs_3_ = bf16[8,2,288,128]{3,2,1,0:T(8,128)(2,1)S(1)} collective-permute-done((bf16[8,2,288,128]{3,2,1,0:T(8,128)(2,1)S(1)}, bf16[8,2,288,128]{3,2,1,0:T(8,128)(2,1)S(1)}, u32[]{:S(2)}, u32[]{:S(2)}) %collective-permute-start.8) | collective-permute-done | bytes 1179680 | tf_op jit(solution)/shard_map/ppermute | solution.py:434
  86.7 0.0 copy-done.4
  86.7 0.0 copy-start.1
  86.7 2.5 %copy-done.1 = bf16[64,64,576]{2,1,0:T(8,128)(2,1)S(1)} copy-done((bf16[64,64,576]{2,1,0:T(8,128)(2,1)S(1)}, bf16[64,64,576]{2,1,0:T(8,128)(2,1)}, u32[]{:S(2)}) %copy-start.1) | copy-done | bytes 4718616
  89.2 0.0 copy-start.7
  89.2 3.4 %copy-done.7 = f32[4096,512]{1,0:T(8,128)S(1)} copy-done((f32[4096,512]{1,0:T(8,128)S(1)}, f32[4096,512]{1,0:T(8,128)}, u32[]{:S(2)}) %copy-start.7) | copy-done | bytes 8388632
  92.5 0.0 copy-start.9
  92.5 1.6 %copy-done.9 = f32[4096,128]{1,0:T(8,128)S(1)} copy-done((f32[4096,128]{1,0:T(8,128)S(1)}, f32[4096,128]{1,0:T(8,128)}, u32[]{:S(2)}) %copy-start.9) | copy-done | bytes 2097176
  94.1 12.8 %attend_last.1 = bf16[4096,512]{1,0:T(8,128)(2,1)} custom-call(s32[81]{0:T(128)S(1)} %copy-done.6, s32[64]{0:T(128)S(1)} %copy-done.3, bf16[4096,576]{1,0:T(8,128)(2,1)S(1)} %bitcast.6, f32[8,1920]{1,0:T(8,128)S(1)} %copy-done.4, f32[4096,512]{1,0:T(8,128)S(1)} %copy-done.7, f32[4096,128]{1,0:T(8,128)S(1)} %copy-done.9, ...), custom_call_target="tpu_custom_call" | custom-call | flops 15971909632 | bytes 13107200 | tf_op jit(solution)/shard_map/attend_last/pallas_call | solution.py:384
Async XLA Ops:
  15.2 35.3 %copy-start.3 = (s32[64]{0:T(128)S(1)}, s32[64]{0:T(128)}, u32[]{:S(2)}) copy-start(s32[64]{0:T(128)} %pos.3) | copy-start | bytes 772
  15.2 29.0 %collective-permute-start = (bf16[2,576,128]{2,1,0:T(8,128)(2,1)}, bf16[2,576,128]{2,1,0:T(8,128)(2,1)S(1)}, u32[]{:S(2)}, u32[]{:S(2)}) collective-permute-start(bf16[2,576,128]{2,1,0:T(8,128)(2,1)} %get-tuple-element.26), channel_id=1, source_target_pairs={{0,2},{1,9},{2,0},{3,11},{4,6},{5,13},{6,4},{7,15},{8,10},{9,1},{1... | collective-permute-start | bytes 884744 | tf_op jit(solution)/shard_map/ppermute | solution.py:430
  15.7 28.5 %collective-permute-start.1 = (bf16[2,576,128]{2,1,0:T(8,128)(2,1)}, bf16[2,576,128]{2,1,0:T(8,128)(2,1)S(1)}, u32[]{:S(2)}, u32[]{:S(2)}) collective-permute-start(bf16[2,576,128]{2,1,0:T(8,128)(2,1)} %get-tuple-element.27), channel_id=1, source_target_pairs={{0,10},{1,5},{2,8},{3,7},{4,14},{5,1},{6,12},{7,3},{8,2},{9,13},{1... | collective-permute-start | bytes 884744 | tf_op jit(solution)/shard_map/ppermute | solution.py:430
  16.8 27.5 %collective-permute-start.2 = (bf16[2,576,128]{2,1,0:T(8,128)(2,1)}, bf16[2,576,128]{2,1,0:T(8,128)(2,1)S(1)}, u32[]{:S(2)}, u32[]{:S(2)}) collective-permute-start(bf16[2,576,128]{2,1,0:T(8,128)(2,1)} %get-tuple-element.28), channel_id=1, source_target_pairs={{0,6},{1,13},{2,4},{3,15},{4,2},{5,9},{6,0},{7,11},{8,14},{9,5},{1... | collective-permute-start | bytes 884744 | tf_op jit(solution)/shard_map/ppermute | solution.py:430
  17.9 26.3 %collective-permute-start.3 = (bf16[2,288,128]{2,1,0:T(8,128)(2,1)}, bf16[2,288,128]{2,1,0:T(8,128)(2,1)S(1)}, u32[]{:S(2)}, u32[]{:S(2)}) collective-permute-start(bf16[2,288,128]{2,1,0:T(8,128)(2,1)} %get-tuple-element.29), channel_id=1, source_target_pairs={{0,14},{1,15},{2,12},{3,13},{4,10},{5,11},{6,8},{7,9},{8,6},{9,7},... | collective-permute-start | bytes 442376 | tf_op jit(solution)/shard_map/ppermute | solution.py:430
  19.9 30.6 %copy-start.5 = (f32[8,1920]{1,0:T(8,128)S(1)}, f32[8,1920]{1,0:T(8,128)}, u32[]{:S(2)}) copy-start(f32[8,1920]{1,0:T(8,128)} %get-tuple-element.36.bias) | copy-start | bytes 184324
  20.0 30.6 %copy-start.6 = (s32[81]{0:T(128)S(1)}, s32[81]{0:T(128)}, u32[]{:S(2)}) copy-start(s32[81]{0:T(128)} %get-tuple-element.34.table) | copy-start | bytes 976
  44.3 39.6 %all-to-all-start.1 = ((bf16[8,2,288,128]{3,2,1,0:T(8,128)(2,1)}), bf16[8,2,288,128]{3,2,1,0:T(8,128)(2,1)S(1)}, u32[]{:S(2)}, u32[]{:S(2)}) async-start(bf16[8,2,288,128]{3,2,1,0:T(8,128)(2,1)} %get-tuple-element.43), calls=%async_computation.1 | async-start | bytes 2359296 | tf_op jit(solution)/shard_map/all_to_all | solution.py:447
  47.8 2.7 %collective-permute-start.4 = (bf16[2,576,128]{2,1,0:T(8,128)(2,1)S(1)}, bf16[2,576,128]{2,1,0:T(8,128)(2,1)S(1)}, u32[]{:S(2)}, u32[]{:S(2)}) collective-permute-start(bf16[2,576,128]{2,1,0:T(8,128)(2,1)S(1)} %collective-permute-done.refs_0_), channel_id=1, source_target_pairs={{0,1},{1,0},{2,3},{3,2},{4,5},{5,4},{6,7},{7,6},{8,9},{9,8},{10,11... | collective-permute-start | bytes 884744 | tf_op jit(solution)/shard_map/ppermute | solution.py:434
  47.9 2.6 %collective-permute-start.5 = (bf16[2,576,128]{2,1,0:T(8,128)(2,1)S(1)}, bf16[2,576,128]{2,1,0:T(8,128)(2,1)S(1)}, u32[]{:S(2)}, u32[]{:S(2)}) collective-permute-start(bf16[2,576,128]{2,1,0:T(8,128)(2,1)S(1)} %collective-permute-done.1.refs_1_), channel_id=1, source_target_pairs={{0,1},{1,0},{2,3},{3,2},{4,5},{5,4},{6,7},{7,6},{8,9},{9,8},{10,11... | collective-permute-start | bytes 884744 | tf_op jit(solution)/shard_map/ppermute | solution.py:434
  48.4 2.1 %collective-permute-start.6 = (bf16[2,576,128]{2,1,0:T(8,128)(2,1)S(1)}, bf16[2,576,128]{2,1,0:T(8,128)(2,1)S(1)}, u32[]{:S(2)}, u32[]{:S(2)}) collective-permute-start(bf16[2,576,128]{2,1,0:T(8,128)(2,1)S(1)} %collective-permute-done.2.refs_2_), channel_id=1, source_target_pairs={{0,1},{1,0},{2,3},{3,2},{4,5},{5,4},{6,7},{7,6},{8,9},{9,8},{10,11... | collective-permute-start | bytes 884744 | tf_op jit(solution)/shard_map/ppermute | solution.py:434
  48.5 2.0 %collective-permute-start.7 = (bf16[2,288,128]{2,1,0:T(8,128)(2,1)S(1)}, bf16[2,288,128]{2,1,0:T(8,128)(2,1)S(1)}, u32[]{:S(2)}, u32[]{:S(2)}) collective-permute-start(bf16[2,288,128]{2,1,0:T(8,128)(2,1)S(1)} %collective-permute-done.3.refs_3_), channel_id=1, source_target_pairs={{0,1},{1,0},{2,3},{3,2},{4,5},{5,4},{6,7},{7,6},{8,9},{9,8},{10,11... | collective-permute-start | bytes 442376 | tf_op jit(solution)/shard_map/ppermute | solution.py:434
  50.5 2.5 %copy-start = (bf16[64,64,576]{2,1,0:T(8,128)(2,1)S(1)}, bf16[64,64,576]{2,1,0:T(8,128)(2,1)}, u32[]{:S(2)}) copy-start(bf16[64,64,576]{2,1,0:T(8,128)(2,1)} %param.4) | copy-start | bytes 14155780
  53.0 1.0 copy-start.2
  54.0 32.7 %copy-start.4 = (f32[8,1920]{1,0:T(8,128)S(1)}, f32[8,1920]{1,0:T(8,128)}, u32[]{:S(2)}) copy-start(f32[8,1920]{1,0:T(8,128)} %get-tuple-element.35.bias) | copy-start | bytes 184324
  82.5 1.3 %copy-start.8 = (f32[4096,128]{1,0:T(8,128)}, f32[4096,128]{1,0:T(8,128)S(1)}, u32[]{:S(2)}) copy-start(f32[4096,128]{1,0:T(8,128)S(1)} %get-tuple-element.45.refs_1_) | copy-start | bytes 6291460
  83.8 2.8 %collective-permute-start.8 = (bf16[8,2,288,128]{3,2,1,0:T(8,128)(2,1)S(1)}, bf16[8,2,288,128]{3,2,1,0:T(8,128)(2,1)S(1)}, u32[]{:S(2)}, u32[]{:S(2)}) collective-permute-start(bf16[8,2,288,128]{3,2,1,0:T(8,128)(2,1)S(1)} %all-to-all-done.1.refs_2_), channel_id=1, source_target_pairs={{0,1},{1,0},{2,3},{3,2},{4,5},{5,4},{6,7},{7,6},{8,9},{9,8},{10,11... | collective-permute-start | bytes 3538952 | tf_op jit(solution)/shard_map/ppermute | solution.py:434
  86.7 2.5 %copy-start.1 = (bf16[64,64,576]{2,1,0:T(8,128)(2,1)S(1)}, bf16[64,64,576]{2,1,0:T(8,128)(2,1)}, u32[]{:S(2)}) copy-start(bf16[64,64,576]{2,1,0:T(8,128)(2,1)} %param.4) | copy-start | bytes 14155780
  89.2 3.4 %copy-start.7 = (f32[4096,512]{1,0:T(8,128)S(1)}, f32[4096,512]{1,0:T(8,128)}, u32[]{:S(2)}) copy-start(f32[4096,512]{1,0:T(8,128)} %get-tuple-element.42.refs_0_) | copy-start | bytes 25165828
  92.5 1.6 %copy-start.9 = (f32[4096,128]{1,0:T(8,128)S(1)}, f32[4096,128]{1,0:T(8,128)}, u32[]{:S(2)}) copy-start(f32[4096,128]{1,0:T(8,128)} %copy-done.8) | copy-start | bytes 6291460

commit v9 on v8

--- a/solution.py
+++ b/solution.py
@@ -369,7 +369,7 @@
     pairs = len(pair_places(owners, chunks, kind in ("first", "only")))
     keys = pairs * PAIR
     levels = [n for n in (4, 5, 6, 8) if n < pairs] + [pairs]
-    sub = 512
+    sub = 256 if kind == "last" else 512
     step = 2 * sub
     out_shape = [jax.ShapeDtypeStruct((rows, KVL), jnp.float32), jax.ShapeDtypeStruct((rows, PAIR), jnp.float32)]
     if kind in ("last", "only"):
@@ -396,7 +396,7 @@
                 *[pltpu.VMEM((sub, PAIR), jnp.float32)] * 4,
             ],
         ),
-        compiler_params=pltpu.CompilerParams(vmem_limit_bytes=min(VMEM, (18 << 20) + keys * 10240)),
+        compiler_params=pltpu.CompilerParams(vmem_limit_bytes=VMEM - (4 << 20)),
         cost_estimate=pl.CostEstimate(
             flops=2 * rows * keys * (lat + KVL), bytes_accessed=rows * (lat + 2 * KVL) * 2, transcendentals=rows * keys
         ),

time: 108 us -> 103 us (0.954)
  the two profiles are of different devices: /device:TPU:11 before, /device:TPU:0 now
where the time goes in v9:
time: 103 us; the launch traced here: 102 us
  Pallas kernels  57.6 us (56%)
  starting transfers between devices  15.7 us (15%)
  blocking collectives  13.5 us (13%)
  waiting for transfers between devices  12.2 us (12%)
  local copies, waits for them, and re-layouts  2.64 us (3%)
    pallas_call x2, Pallas kernels, attend(): pl.pallas_call(functools.partial(attend_kernel, owners, capacity, kind, l...  45.4 us
    all_to_all x1, blocking collectives, local(): lax.all_to_all(jnp.broadcast_to(block_ids, (owners, SEL)), 'ctx', split_a...  13.5 us
    pallas_call x2, Pallas kernels, pack(): pl.pallas_call(functools.partial(pack_kernel, capacity, chunks, spread),...  10.7 us
    ppermute x4, waiting for transfers between devices, send(): got.append(lax.ppermute(x, ('ctx', 'head'), moves))  8 us
    ppermute x4, starting transfers between devices, send(): got.append(lax.ppermute(x, ('ctx', 'head'), moves))  6.81 us
    all_to_all x1, starting transfers between devices, local(): late = lax.all_to_all(more, 'ctx', split_axis=0, concat_axis=0, tiled=True)  5.97 us
    ppermute x5, waiting for transfers between devices, swap(): return [lax.ppermute(x, 'head', [(0, 1), (1, 0)]) for x in got]  4.16 us
    ppermute x5, starting transfers between devices, swap(): return [lax.ppermute(x, 'head', [(0, 1), (1, 0)]) for x in got]  2.93 us
  transfers between devices with their start and end apart: 10, of which 4 were waited for; matrix products, arithmetic and copies ran while one was open for 0% of the time, Pallas kernels for 37%

profile of v9, /device:TPU:0, one launch (start us, length us, event | category | flops | bytes accessed | tf_op | source)
XLA Modules:
  0.0 101.7 jit_solution(8606484894605389479)
XLA Ops:
  0.0 0.7 broadcast_in_dim.2
  0.7 13.5 %all_to_all.13 = s32[8,1,32]{2,1,0:T(1,128)} all-to-all(s32[8,1,32]{2,1,0:T(1,128)S(1)} %broadcast_in_dim.2), channel_id=1, replica_groups=mesh['groups'=2,'ctx'=8,'head'=2] {'ctx'}, dimensions={0} | all-to-all | bytes 2048 | tf_op jit(solution)/shard_map/all_to_all | solution.py:418
  14.1 5.0 %pack.2 = (bf16[2,576,128]{2,1,0:T(8,128)(2,1)}, bf16[2,576,128]{2,1,0:T(8,128)(2,1)}, bf16[2,576,128]{2,1,0:T(8,128)(2,1)}, bf16[2,288,128]{2,1,0:T(8,128)(2,1)}) custom-call(s32[8,32]{1,0:T(8,128)} %bitcast.7, bf16[576,4096]{1,0:T(8,128)(2,1)} %bitcast.5), custom_call_target="tpu_custom_call" | custom-call | bytes 18874368 | tf_op jit(solution)/shard_map/pack/pallas_call | solution.py:87
  19.2 0.6 collective-permute-start
  19.8 1.5 %collective-permute-start.1 = (bf16[2,576,128]{2,1,0:T(8,128)(2,1)}, bf16[2,576,128]{2,1,0:T(8,128)(2,1)S(1)}, u32[]{:S(2)}, u32[]{:S(2)}) collective-permute-start(bf16[2,576,128]{2,1,0:T(8,128)(2,1)} %get-tuple-element.27), channel_id=1, source_target_pairs={{0,10},{1,5},{2,8},{3,7},{4,14},{5,1},{6,12},{7,3},{8,2},{9,13},{1... | collective-permute-start | bytes 884744 | tf_op jit(solution)/shard_map/ppermute | solution.py:430
  21.3 0.7 collective-permute-start.2
  22.0 4.0 %collective-permute-start.3 = (bf16[2,288,128]{2,1,0:T(8,128)(2,1)}, bf16[2,288,128]{2,1,0:T(8,128)(2,1)S(1)}, u32[]{:S(2)}, u32[]{:S(2)}) collective-permute-start(bf16[2,288,128]{2,1,0:T(8,128)(2,1)} %get-tuple-element.29), channel_id=1, source_target_pairs={{0,14},{1,15},{2,12},{3,13},{4,10},{5,11},{6,8},{7,9},{8,6},{9,7},... | collective-permute-start | bytes 442376 | tf_op jit(solution)/shard_map/ppermute | solution.py:430
  26.0 1.6 %plan.1 = (s32[81]{0:T(128)}, f32[8,1920]{1,0:T(8,128)}, f32[8,1920]{1,0:T(8,128)}) custom-call(s32[32]{0:T(128)} %bitcast.10), custom_call_target="tpu_custom_call" | custom-call | bytes 1048576 | tf_op jit(solution)/shard_map/plan/pallas_call | solution.py:159
  27.6 5.6 %pack.3 = (bf16[2,576,128]{2,1,0:T(8,128)(2,1)}, bf16[8,2,288,128]{3,2,1,0:T(8,128)(2,1)}) custom-call(s32[8,32]{1,0:T(8,128)} %bitcast.8, bf16[576,4096]{1,0:T(8,128)(2,1)} %bitcast.6), custom_call_target="tpu_custom_call" | custom-call | bytes 18874368 | tf_op jit(solution)/shard_map/pack/pallas_call | solution.py:87
  33.2 7.3 %collective-permute-done.3.refs_3_ = bf16[2,288,128]{2,1,0:T(8,128)(2,1)S(1)} collective-permute-done((bf16[2,288,128]{2,1,0:T(8,128)(2,1)}, bf16[2,288,128]{2,1,0:T(8,128)(2,1)S(1)}, u32[]{:S(2)}, u32[]{:S(2)}) %collective-permute-start.3) | collective-permute-done | bytes 147488 | tf_op jit(solution)/shard_map/ppermute | solution.py:430
  40.5 0.0 copy-start.8
  40.5 0.0 collective-permute-done.refs_0_
  40.6 0.0 copy-start.2
  40.6 0.7 collective-permute-done.1.refs_1_
  41.2 0.0 copy-start.3
  41.2 0.0 collective-permute-done.2.refs_2_
  41.2 0.0 copy-start.4
  41.2 6.0 %all-to-all-start.1 = ((bf16[8,2,288,128]{3,2,1,0:T(8,128)(2,1)}), bf16[8,2,288,128]{3,2,1,0:T(8,128)(2,1)S(1)}, u32[]{:S(2)}, u32[]{:S(2)}) async-start(bf16[8,2,288,128]{3,2,1,0:T(8,128)(2,1)} %get-tuple-element.43), calls=%async_computation.1 | async-start | bytes 2359296 | tf_op jit(solution)/shard_map/all_to_all | solution.py:447
  47.2 1.9 %collective-permute-start.4 = (bf16[2,576,128]{2,1,0:T(8,128)(2,1)S(1)}, bf16[2,576,128]{2,1,0:T(8,128)(2,1)S(1)}, u32[]{:S(2)}, u32[]{:S(2)}) collective-permute-start(bf16[2,576,128]{2,1,0:T(8,128)(2,1)S(1)} %collective-permute-done.refs_0_), channel_id=1, source_target_pairs={{0,1},{1,0},{2,3},{3,2},{4,5},{5,4},{6,7},{7,6},{8,9},{9,8},{10,11... | collective-permute-start | bytes 884744 | tf_op jit(solution)/shard_map/ppermute | solution.py:434
  49.1 0.1 collective-permute-start.5
  49.2 0.4 collective-permute-start.6
  49.6 0.1 collective-permute-start.7
  49.7 1.7 %collective-permute-done.7.refs_8_ = bf16[2,288,128]{2,1,0:T(8,128)(2,1)S(1)} collective-permute-done((bf16[2,288,128]{2,1,0:T(8,128)(2,1)S(1)}, bf16[2,288,128]{2,1,0:T(8,128)(2,1)S(1)}, u32[]{:S(2)}, u32[]{:S(2)}) %collective-permute-start.7) | collective-permute-done | bytes 147488 | tf_op jit(solution)/shard_map/ppermute | solution.py:434
  51.4 0.0 copy-start.9
  51.4 0.0 collective-permute-done.4.refs_5_
  51.4 0.0 copy-start.5
  51.4 0.0 collective-permute-done.5.refs_6_
  51.4 0.0 copy-start.6
  51.4 0.0 collective-permute-done.6.refs_7_
  51.4 0.0 copy-start.7
  51.4 0.0 copy-done.8
  51.4 0.0 copy-done.2
  51.4 0.0 copy-done.3
  51.4 0.0 copy-done.4
  51.4 0.6 copy-done.9
  52.0 0.1 copy-done.5
  52.1 0.1 copy-done.6
  52.2 0.1 copy-done.7
  52.3 30.3 %attend_first.1 = (f32[4096,512]{1,0:T(8,128)}, f32[4096,128]{1,0:T(8,128)}) custom-call(s32[81]{0:T(128)} %get-tuple-element.34.table, s32[64]{0:T(128)} %pos.3, bf16[4096,576]{1,0:T(8,128)(2,1)} %bitcast.11, f32[8,1920]{1,0:T(8,128)} %get-tuple-element.36.bias, bf16[2,576,128]{2,1,0:T(8,128)(2,1)} %copy-done.2, bf16[2,576,128]{2,1,0:T(8,128)(2,1)} %copy-done.3, ...), custom_call_target="tpu_custom_call" | custom-call | flops 17112760320 | bytes 13107200 | tf_op jit(solution)/shard_map/attend_first/pallas_call | solution.py:384
  82.6 0.0 all-to-all-done.1.refs_2_
  82.6 0.0 copy-start
  82.6 0.4 collective-permute-start.8
  83.1 2.5 %collective-permute-done.8.refs_3_ = bf16[8,2,288,128]{3,2,1,0:T(8,128)(2,1)S(1)} collective-permute-done((bf16[8,2,288,128]{3,2,1,0:T(8,128)(2,1)S(1)}, bf16[8,2,288,128]{3,2,1,0:T(8,128)(2,1)S(1)}, u32[]{:S(2)}, u32[]{:S(2)}) %collective-permute-start.8) | collective-permute-done | bytes 1179680 | tf_op jit(solution)/shard_map/ppermute | solution.py:434
  85.5 0.0 copy-start.1
  85.5 0.0 copy-done
  85.5 1.1 %copy-done.1 = bf16[8,2,288,128]{3,2,1,0:T(8,128)(2,1)} copy-done((bf16[8,2,288,128]{3,2,1,0:T(8,128)(2,1)}, bf16[8,2,288,128]{3,2,1,0:T(8,128)(2,1)S(1)}, u32[]{:S(2)}) %copy-start.1) | copy-done | bytes 1179672
  86.6 15.1 %attend_last.1 = bf16[4096,512]{1,0:T(8,128)(2,1)} custom-call(s32[81]{0:T(128)} %get-tuple-element.34.table, s32[64]{0:T(128)} %pos.3, bf16[4096,576]{1,0:T(8,128)(2,1)} %bitcast.12, f32[8,1920]{1,0:T(8,128)} %get-tuple-element.35.bias, f32[4096,512]{1,0:T(8,128)} %get-tuple-element.42.refs_0_, f32[4096,128]{1,0:T(8,128)} %get-tuple-element.45.refs_1_, ...), custom_call_target="tpu_custom_call" | custom-call | flops 15971909632 | bytes 13107200 | tf_op jit(solution)/shard_map/attend_last/pallas_call | solution.py:384
Async XLA Ops:
  19.2 21.4 %collective-permute-start = (bf16[2,576,128]{2,1,0:T(8,128)(2,1)}, bf16[2,576,128]{2,1,0:T(8,128)(2,1)S(1)}, u32[]{:S(2)}, u32[]{:S(2)}) collective-permute-start(bf16[2,576,128]{2,1,0:T(8,128)(2,1)} %get-tuple-element.26), channel_id=1, source_target_pairs={{0,2},{1,9},{2,0},{3,11},{4,6},{5,13},{6,4},{7,15},{8,10},{9,1},{1... | collective-permute-start | bytes 884744 | tf_op jit(solution)/shard_map/ppermute | solution.py:430
  19.8 21.4 %collective-permute-start.1 = (bf16[2,576,128]{2,1,0:T(8,128)(2,1)}, bf16[2,576,128]{2,1,0:T(8,128)(2,1)S(1)}, u32[]{:S(2)}, u32[]{:S(2)}) collective-permute-start(bf16[2,576,128]{2,1,0:T(8,128)(2,1)} %get-tuple-element.27), channel_id=1, source_target_pairs={{0,10},{1,5},{2,8},{3,7},{4,14},{5,1},{6,12},{7,3},{8,2},{9,13},{1... | collective-permute-start | bytes 884744 | tf_op jit(solution)/shard_map/ppermute | solution.py:430
  21.3 20.0 %collective-permute-start.2 = (bf16[2,576,128]{2,1,0:T(8,128)(2,1)}, bf16[2,576,128]{2,1,0:T(8,128)(2,1)S(1)}, u32[]{:S(2)}, u32[]{:S(2)}) collective-permute-start(bf16[2,576,128]{2,1,0:T(8,128)(2,1)} %get-tuple-element.28), channel_id=1, source_target_pairs={{0,6},{1,13},{2,4},{3,15},{4,2},{5,9},{6,0},{7,11},{8,14},{9,5},{1... | collective-permute-start | bytes 884744 | tf_op jit(solution)/shard_map/ppermute | solution.py:430
  22.0 18.6 %collective-permute-start.3 = (bf16[2,288,128]{2,1,0:T(8,128)(2,1)}, bf16[2,288,128]{2,1,0:T(8,128)(2,1)S(1)}, u32[]{:S(2)}, u32[]{:S(2)}) collective-permute-start(bf16[2,288,128]{2,1,0:T(8,128)(2,1)} %get-tuple-element.29), channel_id=1, source_target_pairs={{0,14},{1,15},{2,12},{3,13},{4,10},{5,11},{6,8},{7,9},{8,6},{9,7},... | collective-permute-start | bytes 442376 | tf_op jit(solution)/shard_map/ppermute | solution.py:430
  40.5 10.9 %copy-start.8 = (bf16[2,288,128]{2,1,0:T(8,128)(2,1)}, bf16[2,288,128]{2,1,0:T(8,128)(2,1)S(1)}, u32[]{:S(2)}) copy-start(bf16[2,288,128]{2,1,0:T(8,128)(2,1)S(1)} %collective-permute-done.3.refs_3_) | copy-start | bytes 442372
  40.6 10.9 %copy-start.2 = (bf16[2,576,128]{2,1,0:T(8,128)(2,1)}, bf16[2,576,128]{2,1,0:T(8,128)(2,1)S(1)}, u32[]{:S(2)}) copy-start(bf16[2,576,128]{2,1,0:T(8,128)(2,1)S(1)} %collective-permute-done.refs_0_) | copy-start | bytes 884740
  41.2 10.2 %copy-start.3 = (bf16[2,576,128]{2,1,0:T(8,128)(2,1)}, bf16[2,576,128]{2,1,0:T(8,128)(2,1)S(1)}, u32[]{:S(2)}) copy-start(bf16[2,576,128]{2,1,0:T(8,128)(2,1)S(1)} %collective-permute-done.1.refs_1_) | copy-start | bytes 884740
  41.2 10.2 %copy-start.4 = (bf16[2,576,128]{2,1,0:T(8,128)(2,1)}, bf16[2,576,128]{2,1,0:T(8,128)(2,1)S(1)}, u32[]{:S(2)}) copy-start(bf16[2,576,128]{2,1,0:T(8,128)(2,1)S(1)} %collective-permute-done.2.refs_2_) | copy-start | bytes 884740
  41.2 41.4 %all-to-all-start.1 = ((bf16[8,2,288,128]{3,2,1,0:T(8,128)(2,1)}), bf16[8,2,288,128]{3,2,1,0:T(8,128)(2,1)S(1)}, u32[]{:S(2)}, u32[]{:S(2)}) async-start(bf16[8,2,288,128]{3,2,1,0:T(8,128)(2,1)} %get-tuple-element.43), calls=%async_computation.1 | async-start | bytes 2359296 | tf_op jit(solution)/shard_map/all_to_all | solution.py:447
  47.2 4.2 %collective-permute-start.4 = (bf16[2,576,128]{2,1,0:T(8,128)(2,1)S(1)}, bf16[2,576,128]{2,1,0:T(8,128)(2,1)S(1)}, u32[]{:S(2)}, u32[]{:S(2)}) collective-permute-start(bf16[2,576,128]{2,1,0:T(8,128)(2,1)S(1)} %collective-permute-done.refs_0_), channel_id=1, source_target_pairs={{0,1},{1,0},{2,3},{3,2},{4,5},{5,4},{6,7},{7,6},{8,9},{9,8},{10,11... | collective-permute-start | bytes 884744 | tf_op jit(solution)/shard_map/ppermute | solution.py:434
  49.1 2.3 %collective-permute-start.5 = (bf16[2,576,128]{2,1,0:T(8,128)(2,1)S(1)}, bf16[2,576,128]{2,1,0:T(8,128)(2,1)S(1)}, u32[]{:S(2)}, u32[]{:S(2)}) collective-permute-start(bf16[2,576,128]{2,1,0:T(8,128)(2,1)S(1)} %collective-permute-done.1.refs_1_), channel_id=1, source_target_pairs={{0,1},{1,0},{2,3},{3,2},{4,5},{5,4},{6,7},{7,6},{8,9},{9,8},{10,11... | collective-permute-start | bytes 884744 | tf_op jit(solution)/shard_map/ppermute | solution.py:434
  49.2 2.2 %collective-permute-start.6 = (bf16[2,576,128]{2,1,0:T(8,128)(2,1)S(1)}, bf16[2,576,128]{2,1,0:T(8,128)(2,1)S(1)}, u32[]{:S(2)}, u32[]{:S(2)}) collective-permute-start(bf16[2,576,128]{2,1,0:T(8,128)(2,1)S(1)} %collective-permute-done.2.refs_2_), channel_id=1, source_target_pairs={{0,1},{1,0},{2,3},{3,2},{4,5},{5,4},{6,7},{7,6},{8,9},{9,8},{10,11... | collective-permute-start | bytes 884744 | tf_op jit(solution)/shard_map/ppermute | solution.py:434
  49.6 1.8 %collective-permute-start.7 = (bf16[2,288,128]{2,1,0:T(8,128)(2,1)S(1)}, bf16[2,288,128]{2,1,0:T(8,128)(2,1)S(1)}, u32[]{:S(2)}, u32[]{:S(2)}) collective-permute-start(bf16[2,288,128]{2,1,0:T(8,128)(2,1)S(1)} %collective-permute-done.3.refs_3_), channel_id=1, source_target_pairs={{0,1},{1,0},{2,3},{3,2},{4,5},{5,4},{6,7},{7,6},{8,9},{9,8},{10,11... | collective-permute-start | bytes 442376 | tf_op jit(solution)/shard_map/ppermute | solution.py:434
  51.4 0.7 copy-start.9
  51.4 0.8 copy-start.5
  51.4 0.9 copy-start.6
  51.4 0.9 copy-start.7
  82.6 2.9 %copy-start = (bf16[8,2,288,128]{3,2,1,0:T(8,128)(2,1)}, bf16[8,2,288,128]{3,2,1,0:T(8,128)(2,1)S(1)}, u32[]{:S(2)}) copy-start(bf16[8,2,288,128]{3,2,1,0:T(8,128)(2,1)S(1)} %all-to-all-done.1.refs_2_) | copy-start | bytes 3538948
  82.6 2.9 %collective-permute-start.8 = (bf16[8,2,288,128]{3,2,1,0:T(8,128)(2,1)S(1)}, bf16[8,2,288,128]{3,2,1,0:T(8,128)(2,1)S(1)}, u32[]{:S(2)}, u32[]{:S(2)}) collective-permute-start(bf16[8,2,288,128]{3,2,1,0:T(8,128)(2,1)S(1)} %all-to-all-done.1.refs_2_), channel_id=1, source_target_pairs={{0,1},{1,0},{2,3},{3,2},{4,5},{5,4},{6,7},{7,6},{8,9},{9,8},{10,11... | collective-permute-start | bytes 3538952 | tf_op jit(solution)/shard_map/ppermute | solution.py:434
  85.5 1.1 %copy-start.1 = (bf16[8,2,288,128]{3,2,1,0:T(8,128)(2,1)}, bf16[8,2,288,128]{3,2,1,0:T(8,128)(2,1)S(1)}, u32[]{:S(2)}) copy-start(bf16[8,2,288,128]{3,2,1,0:T(8,128)(2,1)S(1)} %collective-permute-done.8.refs_3_) | copy-start | bytes 3538948

commit v10 on v8

--- a/solution.py
+++ b/solution.py
@@ -98,7 +98,7 @@
                 pltpu.SemaphoreType.DMA,
             ],
         ),
-        compiler_params=pltpu.CompilerParams(vmem_limit_bytes=VMEM),
+        compiler_params=pltpu.CompilerParams(vmem_limit_bytes=24 << 20 if spread else VMEM),
         cost_estimate=pl.CostEstimate(flops=0, bytes_accessed=8 * lat * tokens, transcendentals=0),
         name="pack",
     )(ids, cache_t)
@@ -396,7 +396,7 @@
                 *[pltpu.VMEM((sub, PAIR), jnp.float32)] * 4,
             ],
         ),
-        compiler_params=pltpu.CompilerParams(vmem_limit_bytes=min(VMEM, (18 << 20) + keys * 10240)),
+        compiler_params=pltpu.CompilerParams(vmem_limit_bytes=VMEM if kind == "last" else min(VMEM, (18 << 20) + keys * 10240)),
         cost_estimate=pl.CostEstimate(
             flops=2 * rows * keys * (lat + KVL), bytes_accessed=rows * (lat + 2 * KVL) * 2, transcendentals=rows * keys
         ),

time: 108 us -> 103 us (0.954)
  the two profiles are of different devices: /device:TPU:11 before, /device:TPU:0 now
where the time goes in v10:
time: 103 us
  Pallas kernels  54.9 us (53%)
  starting transfers between devices  15.3 us (15%)
  blocking collectives  13.6 us (13%)
  waiting for transfers between devices  11.3 us (11%)
  local copies, waits for them, and re-layouts  7.95 us (8%)
    pallas_call x2, Pallas kernels, attend(): pl.pallas_call(functools.partial(attend_kernel, owners, capacity, kind, l...  44.1 us
    all_to_all x1, blocking collectives, local(): lax.all_to_all(jnp.broadcast_to(block_ids, (owners, SEL)), 'ctx', split_a...  13.6 us
    pallas_call x2, Pallas kernels, pack(): pl.pallas_call(functools.partial(pack_kernel, capacity, chunks, spread),...  9.31 us
    unnamed x18, local copies, waits for them, and re-layouts  7.3 us
    ppermute x4, waiting for transfers between devices, send(): got.append(lax.ppermute(x, ('ctx', 'head'), moves))  7.12 us
    ppermute x4, starting transfers between devices, send(): got.append(lax.ppermute(x, ('ctx', 'head'), moves))  6.81 us
    all_to_all x1, starting transfers between devices, local(): late = lax.all_to_all(more, 'ctx', split_axis=0, concat_axis=0, tiled=True)  5.93 us
    ppermute x5, waiting for transfers between devices, swap(): return [lax.ppermute(x, 'head', [(0, 1), (1, 0)]) for x in got]  4.17 us
  transfers between devices with their start and end apart: 10, of which 4 were waited for; matrix products, arithmetic and copies ran while one was open for 0% of the time, Pallas kernels for 33%

profile of v10, /device:TPU:0, one launch (start us, length us, event | category | flops | bytes accessed | tf_op | source)
XLA Modules:
  0.0 103.2 jit_solution(150587637814638971)
XLA Ops:
  0.0 0.7 broadcast_in_dim.2
  0.7 13.6 %all_to_all.13 = s32[8,1,32]{2,1,0:T(1,128)} all-to-all(s32[8,1,32]{2,1,0:T(1,128)S(1)} %broadcast_in_dim.2), channel_id=1, replica_groups=mesh['groups'=2,'ctx'=8,'head'=2] {'ctx'}, dimensions={0} | all-to-all | bytes 2048 | tf_op jit(solution)/shard_map/all_to_all | solution.py:418
  14.3 0.0 copy-start.1
  14.3 5.1 %pack.2 = (bf16[2,576,128]{2,1,0:T(8,128)(2,1)}, bf16[2,576,128]{2,1,0:T(8,128)(2,1)}, bf16[2,576,128]{2,1,0:T(8,128)(2,1)}, bf16[2,288,128]{2,1,0:T(8,128)(2,1)}) custom-call(s32[8,32]{1,0:T(8,128)} %bitcast.7, bf16[576,4096]{1,0:T(8,128)(2,1)} %bitcast.5), custom_call_target="tpu_custom_call" | custom-call | bytes 18874368 | tf_op jit(solution)/shard_map/pack/pallas_call | solution.py:87
  19.4 0.0 copy-start.3
  19.4 0.6 collective-permute-start
  20.1 1.5 %collective-permute-start.1 = (bf16[2,576,128]{2,1,0:T(8,128)(2,1)}, bf16[2,576,128]{2,1,0:T(8,128)(2,1)S(1)}, u32[]{:S(2)}, u32[]{:S(2)}) collective-permute-start(bf16[2,576,128]{2,1,0:T(8,128)(2,1)} %get-tuple-element.27), channel_id=1, source_target_pairs={{0,10},{1,5},{2,8},{3,7},{4,14},{5,1},{6,12},{7,3},{8,2},{9,13},{1... | collective-permute-start | bytes 884744 | tf_op jit(solution)/shard_map/ppermute | solution.py:430
  21.5 0.5 collective-permute-start.2
  22.1 4.2 %collective-permute-start.3 = (bf16[2,288,128]{2,1,0:T(8,128)(2,1)}, bf16[2,288,128]{2,1,0:T(8,128)(2,1)S(1)}, u32[]{:S(2)}, u32[]{:S(2)}) collective-permute-start(bf16[2,288,128]{2,1,0:T(8,128)(2,1)} %get-tuple-element.29), channel_id=1, source_target_pairs={{0,14},{1,15},{2,12},{3,13},{4,10},{5,11},{6,8},{7,9},{8,6},{9,7},... | collective-permute-start | bytes 442376 | tf_op jit(solution)/shard_map/ppermute | solution.py:430
  26.3 1.6 %plan.1 = (s32[81]{0:T(128)}, f32[8,1920]{1,0:T(8,128)}, f32[8,1920]{1,0:T(8,128)}) custom-call(s32[32]{0:T(128)} %bitcast.12), custom_call_target="tpu_custom_call" | custom-call | bytes 1048576 | tf_op jit(solution)/shard_map/plan/pallas_call | solution.py:159
  27.8 0.0 copy-done.1
  27.8 0.0 copy-start
  27.8 2.3 %copy-done = bf16[4096,576]{0,1:T(8,128)(2,1)S(1)} copy-done((bf16[4096,576]{0,1:T(8,128)(2,1)S(1)}, bf16[4096,576]{0,1:T(8,128)(2,1)}, u32[]{:S(2)}) %copy-start) | copy-done | bytes 4718616
  30.2 0.0 copy-start.4
  30.2 0.0 copy-start.5
  30.2 4.2 %pack.3 = (bf16[2,576,128]{2,1,0:T(8,128)(2,1)S(1)}, bf16[8,2,288,128]{3,2,1,0:T(8,128)(2,1)}) custom-call(s32[8,32]{1,0:T(8,128)S(1)} %bitcast.8, bf16[576,4096]{1,0:T(8,128)(2,1)S(1)} %bitcast.6), custom_call_target="tpu_custom_call" | custom-call | bytes 18874368 | tf_op jit(solution)/shard_map/pack/pallas_call | solution.py:87
  34.4 6.3 %collective-permute-done.3.refs_3_ = bf16[2,288,128]{2,1,0:T(8,128)(2,1)S(1)} collective-permute-done((bf16[2,288,128]{2,1,0:T(8,128)(2,1)}, bf16[2,288,128]{2,1,0:T(8,128)(2,1)S(1)}, u32[]{:S(2)}, u32[]{:S(2)}) %collective-permute-start.3) | collective-permute-done | bytes 147488 | tf_op jit(solution)/shard_map/ppermute | solution.py:430
  40.7 0.0 collective-permute-done.refs_0_
  40.7 0.8 collective-permute-done.1.refs_1_
  41.5 0.0 collective-permute-done.2.refs_2_
  41.5 5.9 %all-to-all-start.1 = ((bf16[8,2,288,128]{3,2,1,0:T(8,128)(2,1)}), bf16[8,2,288,128]{3,2,1,0:T(8,128)(2,1)S(1)}, u32[]{:S(2)}, u32[]{:S(2)}) async-start(bf16[8,2,288,128]{3,2,1,0:T(8,128)(2,1)} %get-tuple-element.43), calls=%async_computation.1 | async-start | bytes 2359296 | tf_op jit(solution)/shard_map/all_to_all | solution.py:447
  47.4 1.6 %collective-permute-start.4 = (bf16[2,576,128]{2,1,0:T(8,128)(2,1)S(1)}, bf16[2,576,128]{2,1,0:T(8,128)(2,1)S(1)}, u32[]{:S(2)}, u32[]{:S(2)}) collective-permute-start(bf16[2,576,128]{2,1,0:T(8,128)(2,1)S(1)} %collective-permute-done.refs_0_), channel_id=1, source_target_pairs={{0,1},{1,0},{2,3},{3,2},{4,5},{5,4},{6,7},{7,6},{8,9},{9,8},{10,11... | collective-permute-start | bytes 884744 | tf_op jit(solution)/shard_map/ppermute | solution.py:434
  49.0 0.1 collective-permute-start.5
  49.1 0.4 collective-permute-start.6
  49.5 0.1 collective-permute-start.7
  49.6 1.7 %collective-permute-done.7.refs_8_ = bf16[2,288,128]{2,1,0:T(8,128)(2,1)S(1)} collective-permute-done((bf16[2,288,128]{2,1,0:T(8,128)(2,1)S(1)}, bf16[2,288,128]{2,1,0:T(8,128)(2,1)S(1)}, u32[]{:S(2)}, u32[]{:S(2)}) %collective-permute-start.7) | collective-permute-done | bytes 147488 | tf_op jit(solution)/shard_map/ppermute | solution.py:434
  51.3 0.0 collective-permute-done.4.refs_5_
  51.3 0.0 collective-permute-done.5.refs_6_
  51.3 0.0 collective-permute-done.6.refs_7_
  51.3 0.0 copy-done.3
  51.3 0.0 copy-done.4
  51.3 0.0 copy-done.5
  51.3 0.0 copy-start.2
  51.3 2.5 %copy-done.2 = bf16[64,64,576]{2,1,0:T(8,128)(2,1)S(1)} copy-done((bf16[64,64,576]{2,1,0:T(8,128)(2,1)S(1)}, bf16[64,64,576]{2,1,0:T(8,128)(2,1)}, u32[]{:S(2)}) %copy-start.2) | copy-done | bytes 4718616
  53.8 28.7 %attend_first.1 = (f32[4096,512]{1,0:T(8,128)}, f32[4096,128]{1,0:T(8,128)S(1)}) custom-call(s32[81]{0:T(128)S(1)} %copy-done.5, s32[64]{0:T(128)S(1)} %copy-done.3, bf16[4096,576]{1,0:T(8,128)(2,1)S(1)} %bitcast.10, f32[8,1920]{1,0:T(8,128)S(1)} %copy-done.4, bf16[2,576,128]{2,1,0:T(8,128)(2,1)S(1)} %collective-permute-done.refs_0_, ...), custom_call_target="tpu_custom_call" | custom-call | flops 17112760320 | bytes 13107200 | tf_op jit(solution)/shard_map/attend_first/pallas_call | solution.py:384
  82.5 0.0 copy-start.6
  82.5 1.4 %copy-done.6 = f32[4096,128]{1,0:T(8,128)} copy-done((f32[4096,128]{1,0:T(8,128)}, f32[4096,128]{1,0:T(8,128)S(1)}, u32[]{:S(2)}) %copy-start.6) | copy-done | bytes 2097176
  83.9 0.0 all-to-all-done.1.refs_2_
  83.9 0.0 copy-start.7
  83.9 0.4 collective-permute-start.8
  84.3 2.5 %collective-permute-done.8.refs_3_ = bf16[8,2,288,128]{3,2,1,0:T(8,128)(2,1)S(1)} collective-permute-done((bf16[8,2,288,128]{3,2,1,0:T(8,128)(2,1)S(1)}, bf16[8,2,288,128]{3,2,1,0:T(8,128)(2,1)S(1)}, u32[]{:S(2)}, u32[]{:S(2)}) %collective-permute-start.8) | collective-permute-done | bytes 1179680 | tf_op jit(solution)/shard_map/ppermute | solution.py:434
  86.8 0.0 copy-start.8
  86.8 0.0 copy-done.7
  86.8 1.1 %copy-done.8 = bf16[8,2,288,128]{3,2,1,0:T(8,128)(2,1)} copy-done((bf16[8,2,288,128]{3,2,1,0:T(8,128)(2,1)}, bf16[8,2,288,128]{3,2,1,0:T(8,128)(2,1)S(1)}, u32[]{:S(2)}) %copy-start.8) | copy-done | bytes 1179672
  87.8 15.4 %attend_last.1 = bf16[4096,512]{1,0:T(8,128)(2,1)} custom-call(s32[81]{0:T(128)} %get-tuple-element.34.table, s32[64]{0:T(128)} %pos.3, bf16[4096,576]{1,0:T(8,128)(2,1)} %bitcast.9, f32[8,1920]{1,0:T(8,128)} %get-tuple-element.35.bias, f32[4096,512]{1,0:T(8,128)} %get-tuple-element.42.refs_0_, f32[4096,128]{1,0:T(8,128)} %copy-done.6, ...), custom_call_target="tpu_custom_call" | custom-call | flops 15971909632 | bytes 13107200 | tf_op jit(solution)/shard_map/attend_last/pallas_call | solution.py:384
Async XLA Ops:
  14.3 13.5 %copy-start.1 = (s32[8,1,32]{2,1,0:T(1,128)S(1)}, s32[8,1,32]{2,1,0:T(1,128)}, u32[]{:S(2)}) copy-start(s32[8,1,32]{2,1,0:T(1,128)} %all_to_all.13) | copy-start | bytes 3076
  19.4 31.9 %copy-start.3 = (s32[64]{0:T(128)S(1)}, s32[64]{0:T(128)}, u32[]{:S(2)}) copy-start(s32[64]{0:T(128)} %pos.3) | copy-start | bytes 772
  19.4 21.2 %collective-permute-start = (bf16[2,576,128]{2,1,0:T(8,128)(2,1)}, bf16[2,576,128]{2,1,0:T(8,128)(2,1)S(1)}, u32[]{:S(2)}, u32[]{:S(2)}) collective-permute-start(bf16[2,576,128]{2,1,0:T(8,128)(2,1)} %get-tuple-element.26), channel_id=1, source_target_pairs={{0,2},{1,9},{2,0},{3,11},{4,6},{5,13},{6,4},{7,15},{8,10},{9,1},{1... | collective-permute-start | bytes 884744 | tf_op jit(solution)/shard_map/ppermute | solution.py:430
  20.1 21.4 %collective-permute-start.1 = (bf16[2,576,128]{2,1,0:T(8,128)(2,1)}, bf16[2,576,128]{2,1,0:T(8,128)(2,1)S(1)}, u32[]{:S(2)}, u32[]{:S(2)}) collective-permute-start(bf16[2,576,128]{2,1,0:T(8,128)(2,1)} %get-tuple-element.27), channel_id=1, source_target_pairs={{0,10},{1,5},{2,8},{3,7},{4,14},{5,1},{6,12},{7,3},{8,2},{9,13},{1... | collective-permute-start | bytes 884744 | tf_op jit(solution)/shard_map/ppermute | solution.py:430
  21.5 20.0 %collective-permute-start.2 = (bf16[2,576,128]{2,1,0:T(8,128)(2,1)}, bf16[2,576,128]{2,1,0:T(8,128)(2,1)S(1)}, u32[]{:S(2)}, u32[]{:S(2)}) collective-permute-start(bf16[2,576,128]{2,1,0:T(8,128)(2,1)} %get-tuple-element.28), channel_id=1, source_target_pairs={{0,6},{1,13},{2,4},{3,15},{4,2},{5,9},{6,0},{7,11},{8,14},{9,5},{1... | collective-permute-start | bytes 884744 | tf_op jit(solution)/shard_map/ppermute | solution.py:430
  22.1 18.6 %collective-permute-start.3 = (bf16[2,288,128]{2,1,0:T(8,128)(2,1)}, bf16[2,288,128]{2,1,0:T(8,128)(2,1)S(1)}, u32[]{:S(2)}, u32[]{:S(2)}) collective-permute-start(bf16[2,288,128]{2,1,0:T(8,128)(2,1)} %get-tuple-element.29), channel_id=1, source_target_pairs={{0,14},{1,15},{2,12},{3,13},{4,10},{5,11},{6,8},{7,9},{8,6},{9,7},... | collective-permute-start | bytes 442376 | tf_op jit(solution)/shard_map/ppermute | solution.py:430
  27.8 2.3 %copy-start = (bf16[4096,576]{0,1:T(8,128)(2,1)S(1)}, bf16[4096,576]{0,1:T(8,128)(2,1)}, u32[]{:S(2)}) copy-start(bf16[4096,576]{0,1:T(8,128)(2,1)} %param.5) | copy-start | bytes 14155780
  30.2 21.1 %copy-start.4 = (f32[8,1920]{1,0:T(8,128)S(1)}, f32[8,1920]{1,0:T(8,128)}, u32[]{:S(2)}) copy-start(f32[8,1920]{1,0:T(8,128)} %get-tuple-element.36.bias) | copy-start | bytes 184324
  30.2 21.2 %copy-start.5 = (s32[81]{0:T(128)S(1)}, s32[81]{0:T(128)}, u32[]{:S(2)}) copy-start(s32[81]{0:T(128)} %get-tuple-element.34.table) | copy-start | bytes 976
  41.5 42.4 %all-to-all-start.1 = ((bf16[8,2,288,128]{3,2,1,0:T(8,128)(2,1)}), bf16[8,2,288,128]{3,2,1,0:T(8,128)(2,1)S(1)}, u32[]{:S(2)}, u32[]{:S(2)}) async-start(bf16[8,2,288,128]{3,2,1,0:T(8,128)(2,1)} %get-tuple-element.43), calls=%async_computation.1 | async-start | bytes 2359296 | tf_op jit(solution)/shard_map/all_to_all | solution.py:447
  47.4 3.9 %collective-permute-start.4 = (bf16[2,576,128]{2,1,0:T(8,128)(2,1)S(1)}, bf16[2,576,128]{2,1,0:T(8,128)(2,1)S(1)}, u32[]{:S(2)}, u32[]{:S(2)}) collective-permute-start(bf16[2,576,128]{2,1,0:T(8,128)(2,1)S(1)} %collective-permute-done.refs_0_), channel_id=1, source_target_pairs={{0,1},{1,0},{2,3},{3,2},{4,5},{5,4},{6,7},{7,6},{8,9},{9,8},{10,11... | collective-permute-start | bytes 884744 | tf_op jit(solution)/shard_map/ppermute | solution.py:434
  49.0 2.3 %collective-permute-start.5 = (bf16[2,576,128]{2,1,0:T(8,128)(2,1)S(1)}, bf16[2,576,128]{2,1,0:T(8,128)(2,1)S(1)}, u32[]{:S(2)}, u32[]{:S(2)}) collective-permute-start(bf16[2,576,128]{2,1,0:T(8,128)(2,1)S(1)} %collective-permute-done.1.refs_1_), channel_id=1, source_target_pairs={{0,1},{1,0},{2,3},{3,2},{4,5},{5,4},{6,7},{7,6},{8,9},{9,8},{10,11... | collective-permute-start | bytes 884744 | tf_op jit(solution)/shard_map/ppermute | solution.py:434
  49.1 2.2 %collective-permute-start.6 = (bf16[2,576,128]{2,1,0:T(8,128)(2,1)S(1)}, bf16[2,576,128]{2,1,0:T(8,128)(2,1)S(1)}, u32[]{:S(2)}, u32[]{:S(2)}) collective-permute-start(bf16[2,576,128]{2,1,0:T(8,128)(2,1)S(1)} %collective-permute-done.2.refs_2_), channel_id=1, source_target_pairs={{0,1},{1,0},{2,3},{3,2},{4,5},{5,4},{6,7},{7,6},{8,9},{9,8},{10,11... | collective-permute-start | bytes 884744 | tf_op jit(solution)/shard_map/ppermute | solution.py:434
  49.5 1.8 %collective-permute-start.7 = (bf16[2,288,128]{2,1,0:T(8,128)(2,1)S(1)}, bf16[2,288,128]{2,1,0:T(8,128)(2,1)S(1)}, u32[]{:S(2)}, u32[]{:S(2)}) collective-permute-start(bf16[2,288,128]{2,1,0:T(8,128)(2,1)S(1)} %collective-permute-done.3.refs_3_), channel_id=1, source_target_pairs={{0,1},{1,0},{2,3},{3,2},{4,5},{5,4},{6,7},{7,6},{8,9},{9,8},{10,11... | collective-permute-start | bytes 442376 | tf_op jit(solution)/shard_map/ppermute | solution.py:434
  51.3 2.5 %copy-start.2 = (bf16[64,64,576]{2,1,0:T(8,128)(2,1)S(1)}, bf16[64,64,576]{2,1,0:T(8,128)(2,1)}, u32[]{:S(2)}) copy-start(bf16[64,64,576]{2,1,0:T(8,128)(2,1)} %param.4) | copy-start | bytes 14155780
  82.5 1.4 %copy-start.6 = (f32[4096,128]{1,0:T(8,128)}, f32[4096,128]{1,0:T(8,128)S(1)}, u32[]{:S(2)}) copy-start(f32[4096,128]{1,0:T(8,128)S(1)} %get-tuple-element.45.refs_1_) | copy-start | bytes 6291460
  83.9 2.9 %copy-start.7 = (bf16[8,2,288,128]{3,2,1,0:T(8,128)(2,1)}, bf16[8,2,288,128]{3,2,1,0:T(8,128)(2,1)S(1)}, u32[]{:S(2)}) copy-start(bf16[8,2,288,128]{3,2,1,0:T(8,128)(2,1)S(1)} %all-to-all-done.1.refs_2_) | copy-start | bytes 3538948
  83.9 2.8 %collective-permute-start.8 = (bf16[8,2,288,128]{3,2,1,0:T(8,128)(2,1)S(1)}, bf16[8,2,288,128]{3,2,1,0:T(8,128)(2,1)S(1)}, u32[]{:S(2)}, u32[]{:S(2)}) collective-permute-start(bf16[8,2,288,128]{3,2,1,0:T(8,128)(2,1)S(1)} %all-to-all-done.1.refs_2_), channel_id=1, source_target_pairs={{0,1},{1,0},{2,3},{3,2},{4,5},{5,4},{6,7},{7,6},{8,9},{9,8},{10,11... | collective-permute-start | bytes 3538952 | tf_op jit(solution)/shard_map/ppermute | solution.py:434
  86.8 1.1 %copy-start.8 = (bf16[8,2,288,128]{3,2,1,0:T(8,128)(2,1)}, bf16[8,2,288,128]{3,2,1,0:T(8,128)(2,1)S(1)}, u32[]{:S(2)}) copy-start(bf16[8,2,288,128]{3,2,1,0:T(8,128)(2,1)S(1)} %collective-permute-done.8.refs_3_) | copy-start | bytes 3538948

commit v11 on v8

--- a/solution.py
+++ b/solution.py
@@ -396,7 +396,7 @@
                 *[pltpu.VMEM((sub, PAIR), jnp.float32)] * 4,
             ],
         ),
-        compiler_params=pltpu.CompilerParams(vmem_limit_bytes=min(VMEM, (18 << 20) + keys * 10240)),
+        compiler_params=pltpu.CompilerParams(vmem_limit_bytes=VMEM),
         cost_estimate=pl.CostEstimate(
             flops=2 * rows * keys * (lat + KVL), bytes_accessed=rows * (lat + 2 * KVL) * 2, transcendentals=rows * keys
         ),

time: 108 us -> 101 us (0.935)
  the two profiles are of different devices: /device:TPU:11 before, /device:TPU:0 now
where the time goes in v11:
time: 101 us; the launch traced here: 100 us
  Pallas kernels  56.3 us (56%)
  starting transfers between devices  15.7 us (16%)
  blocking collectives  13.5 us (13%)
  waiting for transfers between devices  12.2 us (12%)
  local copies, waits for them, and re-layouts  2.64 us (3%)
    pallas_call x2, Pallas kernels, attend(): pl.pallas_call(functools.partial(attend_kernel, owners, capacity, kind, l...  44.1 us
    all_to_all x1, blocking collectives, local(): lax.all_to_all(jnp.broadcast_to(block_ids, (owners, SEL)), 'ctx', split_a...  13.5 us
    pallas_call x2, Pallas kernels, pack(): pl.pallas_call(functools.partial(pack_kernel, capacity, chunks, spread),...  10.7 us
    ppermute x4, waiting for transfers between devices, send(): got.append(lax.ppermute(x, ('ctx', 'head'), moves))  8.01 us
    ppermute x4, starting transfers between devices, send(): got.append(lax.ppermute(x, ('ctx', 'head'), moves))  6.81 us
    all_to_all x1, starting transfers between devices, local(): late = lax.all_to_all(more, 'ctx', split_axis=0, concat_axis=0, tiled=True)  5.95 us
    ppermute x5, waiting for transfers between devices, swap(): return [lax.ppermute(x, 'head', [(0, 1), (1, 0)]) for x in got]  4.16 us
    ppermute x5, starting transfers between devices, swap(): return [lax.ppermute(x, 'head', [(0, 1), (1, 0)]) for x in got]  2.94 us
  transfers between devices with their start and end apart: 10, of which 4 were waited for; matrix products, arithmetic and copies ran while one was open for 0% of the time, Pallas kernels for 37%

profile of v11, /device:TPU:0, one launch (start us, length us, event | category | flops | bytes accessed | tf_op | source)
XLA Modules:
  0.0 100.4 jit_solution(16806399163930961968)
XLA Ops:
  0.0 0.7 broadcast_in_dim.2
  0.7 13.5 %all_to_all.13 = s32[8,1,32]{2,1,0:T(1,128)} all-to-all(s32[8,1,32]{2,1,0:T(1,128)S(1)} %broadcast_in_dim.2), channel_id=1, replica_groups=mesh['groups'=2,'ctx'=8,'head'=2] {'ctx'}, dimensions={0} | all-to-all | bytes 2048 | tf_op jit(solution)/shard_map/all_to_all | solution.py:418
  14.1 5.0 %pack.2 = (bf16[2,576,128]{2,1,0:T(8,128)(2,1)}, bf16[2,576,128]{2,1,0:T(8,128)(2,1)}, bf16[2,576,128]{2,1,0:T(8,128)(2,1)}, bf16[2,288,128]{2,1,0:T(8,128)(2,1)}) custom-call(s32[8,32]{1,0:T(8,128)} %bitcast.7, bf16[576,4096]{1,0:T(8,128)(2,1)} %bitcast.5), custom_call_target="tpu_custom_call" | custom-call | bytes 18874368 | tf_op jit(solution)/shard_map/pack/pallas_call | solution.py:87
  19.2 0.6 collective-permute-start
  19.8 1.5 %collective-permute-start.1 = (bf16[2,576,128]{2,1,0:T(8,128)(2,1)}, bf16[2,576,128]{2,1,0:T(8,128)(2,1)S(1)}, u32[]{:S(2)}, u32[]{:S(2)}) collective-permute-start(bf16[2,576,128]{2,1,0:T(8,128)(2,1)} %get-tuple-element.27), channel_id=1, source_target_pairs={{0,10},{1,5},{2,8},{3,7},{4,14},{5,1},{6,12},{7,3},{8,2},{9,13},{1... | collective-permute-start | bytes 884744 | tf_op jit(solution)/shard_map/ppermute | solution.py:430
  21.3 0.7 collective-permute-start.2
  22.0 4.0 %collective-permute-start.3 = (bf16[2,288,128]{2,1,0:T(8,128)(2,1)}, bf16[2,288,128]{2,1,0:T(8,128)(2,1)S(1)}, u32[]{:S(2)}, u32[]{:S(2)}) collective-permute-start(bf16[2,288,128]{2,1,0:T(8,128)(2,1)} %get-tuple-element.29), channel_id=1, source_target_pairs={{0,14},{1,15},{2,12},{3,13},{4,10},{5,11},{6,8},{7,9},{8,6},{9,7},... | collective-permute-start | bytes 442376 | tf_op jit(solution)/shard_map/ppermute | solution.py:430
  26.0 1.6 %plan.1 = (s32[81]{0:T(128)}, f32[8,1920]{1,0:T(8,128)}, f32[8,1920]{1,0:T(8,128)}) custom-call(s32[32]{0:T(128)} %bitcast.10), custom_call_target="tpu_custom_call" | custom-call | bytes 1048576 | tf_op jit(solution)/shard_map/plan/pallas_call | solution.py:159
  27.6 5.7 %pack.3 = (bf16[2,576,128]{2,1,0:T(8,128)(2,1)}, bf16[8,2,288,128]{3,2,1,0:T(8,128)(2,1)}) custom-call(s32[8,32]{1,0:T(8,128)} %bitcast.8, bf16[576,4096]{1,0:T(8,128)(2,1)} %bitcast.6), custom_call_target="tpu_custom_call" | custom-call | bytes 18874368 | tf_op jit(solution)/shard_map/pack/pallas_call | solution.py:87
  33.2 7.3 %collective-permute-done.3.refs_3_ = bf16[2,288,128]{2,1,0:T(8,128)(2,1)S(1)} collective-permute-done((bf16[2,288,128]{2,1,0:T(8,128)(2,1)}, bf16[2,288,128]{2,1,0:T(8,128)(2,1)S(1)}, u32[]{:S(2)}, u32[]{:S(2)}) %collective-permute-start.3) | collective-permute-done | bytes 147488 | tf_op jit(solution)/shard_map/ppermute | solution.py:430
  40.6 0.0 copy-start.8
  40.6 0.0 collective-permute-done.refs_0_
  40.6 0.0 copy-start.2
  40.6 0.7 collective-permute-done.1.refs_1_
  41.2 0.0 copy-start.3
  41.2 0.0 collective-permute-done.2.refs_2_
  41.2 0.0 copy-start.4
  41.2 5.9 %all-to-all-start.1 = ((bf16[8,2,288,128]{3,2,1,0:T(8,128)(2,1)}), bf16[8,2,288,128]{3,2,1,0:T(8,128)(2,1)S(1)}, u32[]{:S(2)}, u32[]{:S(2)}) async-start(bf16[8,2,288,128]{3,2,1,0:T(8,128)(2,1)} %get-tuple-element.43), calls=%async_computation.1 | async-start | bytes 2359296 | tf_op jit(solution)/shard_map/all_to_all | solution.py:447
  47.2 1.9 %collective-permute-start.4 = (bf16[2,576,128]{2,1,0:T(8,128)(2,1)S(1)}, bf16[2,576,128]{2,1,0:T(8,128)(2,1)S(1)}, u32[]{:S(2)}, u32[]{:S(2)}) collective-permute-start(bf16[2,576,128]{2,1,0:T(8,128)(2,1)S(1)} %collective-permute-done.refs_0_), channel_id=1, source_target_pairs={{0,1},{1,0},{2,3},{3,2},{4,5},{5,4},{6,7},{7,6},{8,9},{9,8},{10,11... | collective-permute-start | bytes 884744 | tf_op jit(solution)/shard_map/ppermute | solution.py:434
  49.1 0.1 collective-permute-start.5
  49.2 0.4 collective-permute-start.6
  49.6 0.1 collective-permute-start.7
  49.7 1.7 %collective-permute-done.7.refs_8_ = bf16[2,288,128]{2,1,0:T(8,128)(2,1)S(1)} collective-permute-done((bf16[2,288,128]{2,1,0:T(8,128)(2,1)S(1)}, bf16[2,288,128]{2,1,0:T(8,128)(2,1)S(1)}, u32[]{:S(2)}, u32[]{:S(2)}) %collective-permute-start.7) | collective-permute-done | bytes 147488 | tf_op jit(solution)/shard_map/ppermute | solution.py:434
  51.4 0.0 copy-start.9
  51.4 0.0 collective-permute-done.4.refs_5_
  51.4 0.0 copy-start.5
  51.4 0.0 collective-permute-done.5.refs_6_
  51.4 0.0 copy-start.6
  51.4 0.0 collective-permute-done.6.refs_7_
  51.4 0.0 copy-start.7
  51.4 0.0 copy-done.8
  51.4 0.0 copy-done.2
  51.4 0.0 copy-done.3
  51.4 0.0 copy-done.4
  51.5 0.6 copy-done.9
  52.0 0.1 copy-done.5
  52.1 0.1 copy-done.6
  52.2 0.1 copy-done.7
  52.3 30.3 %attend_first.1 = (f32[4096,512]{1,0:T(8,128)}, f32[4096,128]{1,0:T(8,128)}) custom-call(s32[81]{0:T(128)} %get-tuple-element.34.table, s32[64]{0:T(128)} %pos.3, bf16[4096,576]{1,0:T(8,128)(2,1)} %bitcast.11, f32[8,1920]{1,0:T(8,128)} %get-tuple-element.36.bias, bf16[2,576,128]{2,1,0:T(8,128)(2,1)} %copy-done.2, bf16[2,576,128]{2,1,0:T(8,128)(2,1)} %copy-done.3, ...), custom_call_target="tpu_custom_call" | custom-call | flops 17112760320 | bytes 13107200 | tf_op jit(solution)/shard_map/attend_first/pallas_call | solution.py:384
  82.6 0.0 all-to-all-done.1.refs_2_
  82.6 0.0 copy-start
  82.6 0.4 collective-permute-start.8
  83.1 2.5 %collective-permute-done.8.refs_3_ = bf16[8,2,288,128]{3,2,1,0:T(8,128)(2,1)S(1)} collective-permute-done((bf16[8,2,288,128]{3,2,1,0:T(8,128)(2,1)S(1)}, bf16[8,2,288,128]{3,2,1,0:T(8,128)(2,1)S(1)}, u32[]{:S(2)}, u32[]{:S(2)}) %collective-permute-start.8) | collective-permute-done | bytes 1179680 | tf_op jit(solution)/shard_map/ppermute | solution.py:434
  85.6 0.0 copy-start.1
  85.6 0.0 copy-done
  85.6 1.1 %copy-done.1 = bf16[8,2,288,128]{3,2,1,0:T(8,128)(2,1)} copy-done((bf16[8,2,288,128]{3,2,1,0:T(8,128)(2,1)}, bf16[8,2,288,128]{3,2,1,0:T(8,128)(2,1)S(1)}, u32[]{:S(2)}) %copy-start.1) | copy-done | bytes 1179672
  86.6 13.8 %attend_last.1 = bf16[4096,512]{1,0:T(8,128)(2,1)} custom-call(s32[81]{0:T(128)} %get-tuple-element.34.table, s32[64]{0:T(128)} %pos.3, bf16[4096,576]{1,0:T(8,128)(2,1)} %bitcast.12, f32[8,1920]{1,0:T(8,128)} %get-tuple-element.35.bias, f32[4096,512]{1,0:T(8,128)} %get-tuple-element.42.refs_0_, f32[4096,128]{1,0:T(8,128)} %get-tuple-element.45.refs_1_, ...), custom_call_target="tpu_custom_call" | custom-call | flops 15971909632 | bytes 13107200 | tf_op jit(solution)/shard_map/attend_last/pallas_call | solution.py:384
Async XLA Ops:
  19.2 21.4 %collective-permute-start = (bf16[2,576,128]{2,1,0:T(8,128)(2,1)}, bf16[2,576,128]{2,1,0:T(8,128)(2,1)S(1)}, u32[]{:S(2)}, u32[]{:S(2)}) collective-permute-start(bf16[2,576,128]{2,1,0:T(8,128)(2,1)} %get-tuple-element.26), channel_id=1, source_target_pairs={{0,2},{1,9},{2,0},{3,11},{4,6},{5,13},{6,4},{7,15},{8,10},{9,1},{1... | collective-permute-start | bytes 884744 | tf_op jit(solution)/shard_map/ppermute | solution.py:430
  19.8 21.4 %collective-permute-start.1 = (bf16[2,576,128]{2,1,0:T(8,128)(2,1)}, bf16[2,576,128]{2,1,0:T(8,128)(2,1)S(1)}, u32[]{:S(2)}, u32[]{:S(2)}) collective-permute-start(bf16[2,576,128]{2,1,0:T(8,128)(2,1)} %get-tuple-element.27), channel_id=1, source_target_pairs={{0,10},{1,5},{2,8},{3,7},{4,14},{5,1},{6,12},{7,3},{8,2},{9,13},{1... | collective-permute-start | bytes 884744 | tf_op jit(solution)/shard_map/ppermute | solution.py:430
  21.3 20.0 %collective-permute-start.2 = (bf16[2,576,128]{2,1,0:T(8,128)(2,1)}, bf16[2,576,128]{2,1,0:T(8,128)(2,1)S(1)}, u32[]{:S(2)}, u32[]{:S(2)}) collective-permute-start(bf16[2,576,128]{2,1,0:T(8,128)(2,1)} %get-tuple-element.28), channel_id=1, source_target_pairs={{0,6},{1,13},{2,4},{3,15},{4,2},{5,9},{6,0},{7,11},{8,14},{9,5},{1... | collective-permute-start | bytes 884744 | tf_op jit(solution)/shard_map/ppermute | solution.py:430
  22.0 18.6 %collective-permute-start.3 = (bf16[2,288,128]{2,1,0:T(8,128)(2,1)}, bf16[2,288,128]{2,1,0:T(8,128)(2,1)S(1)}, u32[]{:S(2)}, u32[]{:S(2)}) collective-permute-start(bf16[2,288,128]{2,1,0:T(8,128)(2,1)} %get-tuple-element.29), channel_id=1, source_target_pairs={{0,14},{1,15},{2,12},{3,13},{4,10},{5,11},{6,8},{7,9},{8,6},{9,7},... | collective-permute-start | bytes 442376 | tf_op jit(solution)/shard_map/ppermute | solution.py:430
  40.6 10.9 %copy-start.8 = (bf16[2,288,128]{2,1,0:T(8,128)(2,1)}, bf16[2,288,128]{2,1,0:T(8,128)(2,1)S(1)}, u32[]{:S(2)}) copy-start(bf16[2,288,128]{2,1,0:T(8,128)(2,1)S(1)} %collective-permute-done.3.refs_3_) | copy-start | bytes 442372
  40.6 10.9 %copy-start.2 = (bf16[2,576,128]{2,1,0:T(8,128)(2,1)}, bf16[2,576,128]{2,1,0:T(8,128)(2,1)S(1)}, u32[]{:S(2)}) copy-start(bf16[2,576,128]{2,1,0:T(8,128)(2,1)S(1)} %collective-permute-done.refs_0_) | copy-start | bytes 884740
  41.2 10.2 %copy-start.3 = (bf16[2,576,128]{2,1,0:T(8,128)(2,1)}, bf16[2,576,128]{2,1,0:T(8,128)(2,1)S(1)}, u32[]{:S(2)}) copy-start(bf16[2,576,128]{2,1,0:T(8,128)(2,1)S(1)} %collective-permute-done.1.refs_1_) | copy-start | bytes 884740
  41.2 10.2 %copy-start.4 = (bf16[2,576,128]{2,1,0:T(8,128)(2,1)}, bf16[2,576,128]{2,1,0:T(8,128)(2,1)S(1)}, u32[]{:S(2)}) copy-start(bf16[2,576,128]{2,1,0:T(8,128)(2,1)S(1)} %collective-permute-done.2.refs_2_) | copy-start | bytes 884740
  41.2 41.4 %all-to-all-start.1 = ((bf16[8,2,288,128]{3,2,1,0:T(8,128)(2,1)}), bf16[8,2,288,128]{3,2,1,0:T(8,128)(2,1)S(1)}, u32[]{:S(2)}, u32[]{:S(2)}) async-start(bf16[8,2,288,128]{3,2,1,0:T(8,128)(2,1)} %get-tuple-element.43), calls=%async_computation.1 | async-start | bytes 2359296 | tf_op jit(solution)/shard_map/all_to_all | solution.py:447
  47.2 4.2 %collective-permute-start.4 = (bf16[2,576,128]{2,1,0:T(8,128)(2,1)S(1)}, bf16[2,576,128]{2,1,0:T(8,128)(2,1)S(1)}, u32[]{:S(2)}, u32[]{:S(2)}) collective-permute-start(bf16[2,576,128]{2,1,0:T(8,128)(2,1)S(1)} %collective-permute-done.refs_0_), channel_id=1, source_target_pairs={{0,1},{1,0},{2,3},{3,2},{4,5},{5,4},{6,7},{7,6},{8,9},{9,8},{10,11... | collective-permute-start | bytes 884744 | tf_op jit(solution)/shard_map/ppermute | solution.py:434
  49.1 2.3 %collective-permute-start.5 = (bf16[2,576,128]{2,1,0:T(8,128)(2,1)S(1)}, bf16[2,576,128]{2,1,0:T(8,128)(2,1)S(1)}, u32[]{:S(2)}, u32[]{:S(2)}) collective-permute-start(bf16[2,576,128]{2,1,0:T(8,128)(2,1)S(1)} %collective-permute-done.1.refs_1_), channel_id=1, source_target_pairs={{0,1},{1,0},{2,3},{3,2},{4,5},{5,4},{6,7},{7,6},{8,9},{9,8},{10,11... | collective-permute-start | bytes 884744 | tf_op jit(solution)/shard_map/ppermute | solution.py:434
  49.2 2.2 %collective-permute-start.6 = (bf16[2,576,128]{2,1,0:T(8,128)(2,1)S(1)}, bf16[2,576,128]{2,1,0:T(8,128)(2,1)S(1)}, u32[]{:S(2)}, u32[]{:S(2)}) collective-permute-start(bf16[2,576,128]{2,1,0:T(8,128)(2,1)S(1)} %collective-permute-done.2.refs_2_), channel_id=1, source_target_pairs={{0,1},{1,0},{2,3},{3,2},{4,5},{5,4},{6,7},{7,6},{8,9},{9,8},{10,11... | collective-permute-start | bytes 884744 | tf_op jit(solution)/shard_map/ppermute | solution.py:434
  49.6 1.8 %collective-permute-start.7 = (bf16[2,288,128]{2,1,0:T(8,128)(2,1)S(1)}, bf16[2,288,128]{2,1,0:T(8,128)(2,1)S(1)}, u32[]{:S(2)}, u32[]{:S(2)}) collective-permute-start(bf16[2,288,128]{2,1,0:T(8,128)(2,1)S(1)} %collective-permute-done.3.refs_3_), channel_id=1, source_target_pairs={{0,1},{1,0},{2,3},{3,2},{4,5},{5,4},{6,7},{7,6},{8,9},{9,8},{10,11... | collective-permute-start | bytes 442376 | tf_op jit(solution)/shard_map/ppermute | solution.py:434
  51.4 0.7 copy-start.9
  51.4 0.8 copy-start.5
  51.4 0.9 copy-start.6
  51.4 0.9 copy-start.7
  82.6 2.9 %copy-start = (bf16[8,2,288,128]{3,2,1,0:T(8,128)(2,1)}, bf16[8,2,288,128]{3,2,1,0:T(8,128)(2,1)S(1)}, u32[]{:S(2)}) copy-start(bf16[8,2,288,128]{3,2,1,0:T(8,128)(2,1)S(1)} %all-to-all-done.1.refs_2_) | copy-start | bytes 3538948
  82.6 2.9 %collective-permute-start.8 = (bf16[8,2,288,128]{3,2,1,0:T(8,128)(2,1)S(1)}, bf16[8,2,288,128]{3,2,1,0:T(8,128)(2,1)S(1)}, u32[]{:S(2)}, u32[]{:S(2)}) collective-permute-start(bf16[8,2,288,128]{3,2,1,0:T(8,128)(2,1)S(1)} %all-to-all-done.1.refs_2_), channel_id=1, source_target_pairs={{0,1},{1,0},{2,3},{3,2},{4,5},{5,4},{6,7},{7,6},{8,9},{9,8},{10,11... | collective-permute-start | bytes 3538952 | tf_op jit(solution)/shard_map/ppermute | solution.py:434
  85.6 1.1 %copy-start.1 = (bf16[8,2,288,128]{3,2,1,0:T(8,128)(2,1)}, bf16[8,2,288,128]{3,2,1,0:T(8,128)(2,1)S(1)}, u32[]{:S(2)}) copy-start(bf16[8,2,288,128]{3,2,1,0:T(8,128)(2,1)S(1)} %collective-permute-done.8.refs_3_) | copy-start | bytes 3538948
